TPU v7x, 32 devices: a whole 2x2x4 slice. The times are simulated.
32 devices in a mesh: rep: 8 (over y, x, core), fsdp: 4 (over z).
Axes of the slice: x: 2, y: 2, z: 4, core: 2. Of those that a mesh axis runs over, the one named last changes fastest.
Arguments:
- inputs: bfloat16 [16, 1024, 1024], P('rep', 'fsdp'), may hold values from -6 to 6
- cotangent: bfloat16 [16, 1024, 1024], P('rep', 'fsdp'), may hold values from -6 to 6
- lengths: int32 [16], P('rep'), may hold values from 256 to 1024, as said below
- norm_first: bfloat16 [1024], P('fsdp'), may hold values from 0.5 to 1.5
- w_qkv: bfloat16 [1024, 3072], P('fsdp'), may hold values from -0.1875 to 0.1875
- w_out: bfloat16 [1024, 1024], P('fsdp'), may hold values from -1.5 to 1.5
- norm_second: bfloat16 [1024], P('fsdp'), may hold values from 0.5 to 1.5
- w_in: bfloat16 [1024, 5248], P('fsdp'), may hold values from -0.1875 to 0.1875
- w_down: bfloat16 [2624, 1024], P('fsdp'), may hold values from -0.15625 to 0.15625
Outputs:
- output: bfloat16 [16, 1024, 1024], P('rep', 'fsdp')
- grad_inputs: bfloat16 [16, 1024, 1024], P('rep', 'fsdp')
- grad_norm_first: float32 [1024], P('fsdp')
- grad_w_qkv: float32 [1024, 3072], P('fsdp')
- grad_w_out: float32 [1024, 1024], P('fsdp')
- grad_norm_second: float32 [1024], P('fsdp')
- grad_w_in: float32 [1024, 5248], P('fsdp')
- grad_w_down: float32 [2624, 1024], P('fsdp')
Inputs may be any that keep to these rules, and one draw needn't show every extreme that they name: `lengths`: in each aligned group of 2 sequences (those of one index of rep) at least one has length 1024.
All inputs are finite; a program needn't handle non-finite values.
Results may differ from a plain program's by a relative error of at most 0.022.
Values may be sent and summed in bfloat16 or wider, within the bound.
No kernel may reach another device: no remote copies, remote signals or barrier semaphores. Data moves between devices by JAX's collectives and lax.ppermute only.
A program may use at most 192 MiB of HBM per device.

v0:
```python
import jax
import jax.numpy as jnp
from jax import lax
from jax.sharding import PartitionSpec as P

HEAD_DIM = 64
WIN = 64


epsilon = 1e-05
root_half = 0.7071067811865476
inv_root_two_pi = 0.3989422804014327


def padded(x, sides, width):
    for axis, dim in sides:
        size, length = (lax.axis_size(axis), x.shape[dim])
        up = [(i, (i + 1) % size) for i in range(size - 1)]
        down = [(j, i) for i, j in up]
        last = lax.slice_in_dim(x, length - width, length, axis=dim)
        leading = lax.slice_in_dim(x, 0, width, axis=dim)
        before = lax.ppermute(last, axis, up)
        after = lax.ppermute(leading, axis, down)
        x = jnp.concatenate([before, x, after], axis=dim)
    return x


def from_behind(value, axis, steps):
    count = lax.axis_size(axis)
    leading, last = (max(0, -steps), min(count, count - steps))
    return lax.ppermute(value, axis, [(source, source + steps) for source in range(leading, last)])


def layer_stats(values):
    centred = values - jnp.mean(values, axis=-1, keepdims=True)
    inverse = lax.rsqrt(jnp.mean(centred * centred, axis=-1, keepdims=True) + epsilon)
    return (centred * inverse, inverse)


def norm_back(grad_out, gain, scaled, inverse):
    grad_scaled = grad_out * gain
    return inverse * (
        grad_scaled
        - jnp.mean(grad_scaled, axis=-1, keepdims=True)
        - scaled * jnp.mean(grad_scaled * scaled, axis=-1, keepdims=True)
    )


def rope_tables(positions):
    halfway = HEAD_DIM // 2
    frequency = 10000.0 ** (-(2.0 * jnp.arange(halfway, dtype=jnp.float32)) / HEAD_DIM)
    angles = positions.astype(jnp.float32)[:, None] * frequency[None, :]
    angles = jnp.concatenate([angles, angles], axis=-1)
    return (jnp.cos(angles)[:, None, :], jnp.sin(angles)[:, None, :])


def rotate(values, cosine, sine_table):
    halfway = HEAD_DIM // 2
    rotated = jnp.concatenate([-values[..., halfway:], values[..., :halfway]], axis=-1)
    return values * cosine + rotated * sine_table


def rotate_back(grad_out, cosine, sine_table):
    halfway = HEAD_DIM // 2
    scaled_sin = grad_out * sine_table
    return grad_out * cosine + jnp.concatenate(
        [scaled_sin[..., halfway:], -scaled_sin[..., :halfway]], axis=-1
    )


def on_device(inputs, cotangent, lengths, norm_first, w_qkv, w_out, norm_second, w_in, w_down):
    shard_rows = inputs.shape[1]
    width_model = inputs.shape[2]
    head_count = width_model // HEAD_DIM
    hidden_units = w_in.shape[1] // 2
    rim_rows = shard_rows + 2 * WIN
    score_scale = HEAD_DIM ** (-0.5)
    first_row = lax.axis_index("fsdp") * shard_rows
    query_pos = first_row + jnp.arange(shard_rows, dtype=jnp.int32)
    key_pos = first_row - WIN + jnp.arange(rim_rows, dtype=jnp.int32)
    window = jnp.abs(query_pos[:, None] - key_pos[None, :]) <= WIN
    diagonal = query_pos[:, None] == key_pos[None, :]
    cosine, sine_table = rope_tables(query_pos)
    shards = (norm_first, w_qkv, w_out, norm_second, w_in, w_down)
    group_size = lax.axis_size("fsdp")
    totals = [
        jnp.zeros((weight.shape[0] * group_size,) + weight.shape[1:], jnp.float32)
        for weight in shards
    ]
    outputs = []
    grads_in = []
    for number in range(inputs.shape[0]):
        length = lengths[number]
        valid_rows = (query_pos < length).astype(jnp.float32)[:, None]
        key_live = (key_pos >= 0) & (key_pos < length)
        allowed = window & (key_live[None, :] | diagonal)
        gathered = (
            lax.all_gather(norm_first, "fsdp", axis=0, tiled=True),
            lax.all_gather(w_qkv, "fsdp", axis=0, tiled=True),
            lax.all_gather(w_out, "fsdp", axis=0, tiled=True),
            lax.all_gather(norm_second, "fsdp", axis=0, tiled=True),
            lax.all_gather(w_in, "fsdp", axis=0, tiled=True),
            lax.all_gather(w_down, "fsdp", axis=0, tiled=True),
        )
        gain_first = gathered[0].astype(jnp.float32)
        gain_second = gathered[3].astype(jnp.float32)
        values = inputs[number].astype(jnp.float32)
        scaled_first, inverse_first = layer_stats(values)
        normed_first = (scaled_first * gain_first).astype(jnp.bfloat16)
        joint_qkv = jnp.dot(normed_first, gathered[1], preferred_element_type=jnp.float32)
        queries = rotate(
            joint_qkv[:, :width_model].reshape(shard_rows, head_count, HEAD_DIM), cosine, sine_table
        ).astype(jnp.bfloat16)
        keys_own = rotate(
            joint_qkv[:, width_model : 2 * width_model].reshape(shard_rows, head_count, HEAD_DIM),
            cosine,
            sine_table,
        ).astype(jnp.bfloat16)
        values_own = joint_qkv[:, 2 * width_model :].astype(jnp.bfloat16)
        key_rim = padded(
            jnp.concatenate([keys_own.reshape(shard_rows, width_model), values_own], axis=1),
            (("fsdp", 0),),
            WIN,
        )
        keys_all = key_rim[:, :width_model].reshape(rim_rows, head_count, HEAD_DIM)
        values_all = key_rim[:, width_model:].reshape(rim_rows, head_count, HEAD_DIM)
        scores = (
            jnp.einsum("qhd,khd->hqk", queries, keys_all, preferred_element_type=jnp.float32)
            * score_scale
        )
        masked = jnp.where(allowed[None], scores, -1e30)
        row_peak = jnp.max(masked, axis=-1, keepdims=True)
        exponent = jnp.exp(masked - row_peak)
        softmax_out = exponent / jnp.sum(exponent, axis=-1, keepdims=True)
        probs_low = softmax_out.astype(jnp.bfloat16)
        attended = (
            jnp.einsum("hqk,khd->qhd", probs_low, values_all, preferred_element_type=jnp.float32)
            .reshape(shard_rows, width_model)
            .astype(jnp.bfloat16)
        )
        branch = jnp.dot(attended, gathered[2], preferred_element_type=jnp.float32)
        middle = values + valid_rows * branch
        scaled_second, inverse_second = layer_stats(middle)
        normed_second = (scaled_second * gain_second).astype(jnp.bfloat16)
        hidden = jnp.dot(normed_second, gathered[4], preferred_element_type=jnp.float32)
        gate_in = hidden[:, :hidden_units]
        gate_up = hidden[:, hidden_units:]
        activated = jax.nn.gelu(gate_in, approximate=False)
        mixed_low = (activated * gate_up).astype(jnp.bfloat16)
        result = jnp.dot(mixed_low, gathered[5], preferred_element_type=jnp.float32)
        outputs.append((middle + valid_rows * result).astype(jnp.bfloat16))
        regathered = (
            lax.all_gather(norm_first, "fsdp", axis=0, tiled=True),
            lax.all_gather(w_qkv, "fsdp", axis=0, tiled=True),
            lax.all_gather(w_out, "fsdp", axis=0, tiled=True),
            lax.all_gather(norm_second, "fsdp", axis=0, tiled=True),
            lax.all_gather(w_in, "fsdp", axis=0, tiled=True),
            lax.all_gather(w_down, "fsdp", axis=0, tiled=True),
        )
        back_gain_first = regathered[0].astype(jnp.float32)
        back_gain_second = regathered[3].astype(jnp.float32)
        upstream = cotangent[number].astype(jnp.float32)
        grad_result = (upstream * valid_rows).astype(jnp.bfloat16)
        totals[5] = totals[5] + jnp.einsum(
            "tf,td->fd", mixed_low, grad_result, preferred_element_type=jnp.float32
        )
        grad_mixed = jnp.einsum(
            "td,fd->tf", grad_result, regathered[5], preferred_element_type=jnp.float32
        )
        normal_cdf = 0.5 * (1.0 + jax.scipy.special.erf(gate_in * root_half))
        density = jnp.exp(-0.5 * gate_in * gate_in) * inv_root_two_pi
        grad_hidden = jnp.concatenate(
            [grad_mixed * gate_up * (normal_cdf + gate_in * density), grad_mixed * activated],
            axis=1,
        ).astype(jnp.bfloat16)
        totals[4] = totals[4] + jnp.einsum(
            "td,tf->df", normed_second, grad_hidden, preferred_element_type=jnp.float32
        )
        grad_normed_second = jnp.einsum(
            "tf,df->td", grad_hidden, regathered[4], preferred_element_type=jnp.float32
        )
        totals[3] = totals[3] + jnp.sum(grad_normed_second * scaled_second, axis=0)
        grad_middle = upstream + norm_back(
            grad_normed_second, back_gain_second, scaled_second, inverse_second
        )
        grad_branch = (grad_middle * valid_rows).astype(jnp.bfloat16)
        totals[2] = totals[2] + jnp.einsum(
            "ti,to->io", attended, grad_branch, preferred_element_type=jnp.float32
        )
        grad_att = (
            jnp.einsum("to,io->ti", grad_branch, regathered[2], preferred_element_type=jnp.float32)
            .astype(jnp.bfloat16)
            .reshape(shard_rows, head_count, HEAD_DIM)
        )
        grad_probs = jnp.einsum(
            "qhd,khd->hqk", grad_att, values_all, preferred_element_type=jnp.float32
        )
        row_delta = jnp.sum(softmax_out * grad_probs, axis=-1, keepdims=True)
        grad_scores = (softmax_out * (grad_probs - row_delta)).astype(jnp.bfloat16)
        grad_queries = (
            jnp.einsum("hqk,khd->qhd", grad_scores, keys_all, preferred_element_type=jnp.float32)
            * score_scale
        )
        grad_keys = (
            jnp.einsum("hqk,qhd->khd", grad_scores, queries, preferred_element_type=jnp.float32)
            * score_scale
        )
        grad_values = jnp.einsum(
            "hqk,qhd->khd", probs_low, grad_att, preferred_element_type=jnp.float32
        )
        grad_rim = jnp.concatenate(
            [grad_keys.reshape(rim_rows, width_model), grad_values.reshape(rim_rows, width_model)],
            axis=1,
        )
        from_above = from_behind(
            grad_rim[shard_rows + WIN :].astype(jnp.bfloat16), "fsdp", 1
        ).astype(jnp.float32)
        from_below = from_behind(grad_rim[:WIN].astype(jnp.bfloat16), "fsdp", -1).astype(
            jnp.float32
        )
        grad_kv = (
            grad_rim[WIN : WIN + shard_rows]
            + jnp.pad(from_above, ((0, shard_rows - WIN), (0, 0)))
            + jnp.pad(from_below, ((shard_rows - WIN, 0), (0, 0)))
        )
        grad_joint = jnp.concatenate(
            [
                rotate_back(grad_queries, cosine, sine_table).reshape(shard_rows, width_model),
                rotate_back(
                    grad_kv[:, :width_model].reshape(shard_rows, head_count, HEAD_DIM),
                    cosine,
                    sine_table,
                ).reshape(shard_rows, width_model),
                grad_kv[:, width_model:],
            ],
            axis=1,
        ).astype(jnp.bfloat16)
        totals[1] = totals[1] + jnp.einsum(
            "td,te->de", normed_first, grad_joint, preferred_element_type=jnp.float32
        )
        grad_normed_first = jnp.einsum(
            "te,de->td", grad_joint, regathered[1], preferred_element_type=jnp.float32
        )
        totals[0] = totals[0] + jnp.sum(grad_normed_first * scaled_first, axis=0)
        grads_in.append(
            (
                grad_middle
                + norm_back(grad_normed_first, back_gain_first, scaled_first, inverse_first)
            ).astype(jnp.bfloat16)
        )
    owned_grads = (
        lax.psum_scatter(
            totals[0].astype(jnp.bfloat16), "fsdp", scatter_dimension=0, tiled=True
        ).astype(jnp.float32),
        lax.psum_scatter(
            totals[1].astype(jnp.bfloat16), "fsdp", scatter_dimension=0, tiled=True
        ).astype(jnp.float32),
        lax.psum_scatter(
            totals[2].astype(jnp.bfloat16), "fsdp", scatter_dimension=0, tiled=True
        ).astype(jnp.float32),
        lax.psum_scatter(
            totals[3].astype(jnp.bfloat16), "fsdp", scatter_dimension=0, tiled=True
        ).astype(jnp.float32),
        lax.psum_scatter(
            totals[4].astype(jnp.bfloat16), "fsdp", scatter_dimension=0, tiled=True
        ).astype(jnp.float32),
        lax.psum_scatter(
            totals[5].astype(jnp.bfloat16), "fsdp", scatter_dimension=0, tiled=True
        ).astype(jnp.float32),
    )
    summed = (
        lax.psum(owned_grads[0].astype(jnp.bfloat16), "rep").astype(jnp.float32),
        lax.psum(owned_grads[1].astype(jnp.bfloat16), "rep").astype(jnp.float32),
        lax.psum(owned_grads[2].astype(jnp.bfloat16), "rep").astype(jnp.float32),
        lax.psum(owned_grads[3].astype(jnp.bfloat16), "rep").astype(jnp.float32),
        lax.psum(owned_grads[4].astype(jnp.bfloat16), "rep").astype(jnp.float32),
        lax.psum(owned_grads[5].astype(jnp.bfloat16), "rep").astype(jnp.float32),
    )
    return (
        jnp.stack(outputs),
        jnp.stack(grads_in),
        summed[0],
        summed[1],
        summed[2],
        summed[3],
        summed[4],
        summed[5],
    )


def solution(mesh):
    in_specs = (
        P("rep", "fsdp", None),
        P("rep", "fsdp", None),
        P("rep"),
        P("fsdp"),
        P("fsdp", None),
        P("fsdp", None),
        P("fsdp"),
        P("fsdp", None),
        P("fsdp", None),
    )
    out_specs = (
        P("rep", "fsdp", None),
        P("rep", "fsdp", None),
        P("fsdp"),
        P("fsdp", None),
        P("fsdp", None),
        P("fsdp"),
        P("fsdp", None),
        P("fsdp", None),
    )
    return jax.shard_map(
        on_device, mesh=mesh, in_specs=in_specs, out_specs=out_specs, check_vma=False
    )
```

profile of v0, /device:TPU:0, one launch (start us, length us, event | category | flops | bytes accessed | tf_op | source)
XLA Modules:
  0.0 1092.5 jit_solution(2305936907670897786)
XLA Ops:
  14.0 12.7 %all-gather = bf16[4,1,256]{2,1,0:T(2,128)(2,1)S(1)} all-gather(bf16[1,1,256]{2,1,0:T(2,128)(2,1)S(1)} %reshape.431), channel_id=1, replica_groups=mesh['rep'=8,'fsdp'=4] {'fsdp'}, dimensions={0}, use_global_device_ids=true | all-gather | bytes 2560 | tf_op jit(solution)/shard_map/all_gather | solution.py:98
  28.1 8.0 all-gather.1
  37.0 90.8 %all-gather.7.cloned.1.call-done = bf16[1024,3072]{1,0:T(8,128)(2,1)} async-done(((bf16[256,3072]{1,0:T(8,128)(2,1)}), bf16[1024,3072]{1,0:T(8,128)(2,1)}) %all-gather.7.cloned.1.call-update) | async-done | bytes 6291472 | tf_op jit(solution)/shard_map/all_gather | solution.py:99
  127.7 4.8 fusion.156
  140.3 2.5 copy.75
  148.8 2.6 maximum_multiply_fusion
  151.4 2.5 copy.82
  153.9 3.2 fusion.163
  159.3 5.3 collective-permute-start.2
  166.2 3.0 fusion.162
  175.5 5.4 collective-permute-start
  193.7 4.7 fusion.173
  198.4 4.0 fusion.68
  202.4 3.5 fusion.174
  207.5 4.7 fusion.175
  212.2 4.4 fusion.65
  218.7 149.5 %all-gather.11.cloned.1.call-done = bf16[1024,5248]{1,0:T(8,128)(2,1)} async-done(((bf16[256,5248]{1,0:T(8,128)(2,1)}), bf16[1024,5248]{1,0:T(8,128)(2,1)}) %all-gather.11.cloned.1.call-update) | async-done | bytes 10747920 | tf_op jit(solution)/shard_map/all_gather | solution.py:102
  368.2 10.1 fusion.158
  378.3 89.7 %all-gather.13.cloned.1.call-done = bf16[2624,1024]{1,0:T(8,128)(2,1)} async-done(((bf16[656,1024]{1,0:T(8,128)(2,1)}), bf16[2624,1024]{1,0:T(8,128)(2,1)}) %all-gather.13.cloned.1.call-update) | async-done | bytes 5373968 | tf_op jit(solution)/shard_map/all_gather | solution.py:103
  468.1 12.3 %multiply_convert_fusion.3 = (bf16[256,2624]{1,0:T(8,128)(2,1)}, f32[256,2624]{1,0:T(8,128)S(1)}, bf16[256,2624]{1,0:T(8,128)(2,1)}) fusion(f32[256,5248]{1,0:T(8,128)} %fusion.158, bf16[2624,1024]{1,0:T(8,128)(2,1)} %all-gather.13.cloned.1.call-done, f32[256]{0:T(256)S(1)} %get-tuple-element.117, bf16[2,256,1024]{2,1,0:T(8,128)(2,1)} %param.10), kind=kOutput, calls=%fused_computation.53 | convolution fusion | flops 1428242432 | bytes 16778240 | tf_op jit(solution)/shard_map/td,fd->tf/dot_general | solution.py:167
  482.2 4.5 fusion.159
  486.8 10.9 multiply_convert_fusion.2
  497.7 4.0 fusion.48
  501.7 6.9 multiply_reduce_fusion.3
  508.6 3.3 convert_add_fusion.1
  519.4 3.4 fusion.127
  525.2 4.1 add_convert_fusion.2
  529.2 4.8 multiply_reduce_fusion
  540.1 4.0 fusion.51
  546.8 5.3 collective-permute-start.6
  553.2 4.2 multiply_reduce_fusion.1
  563.7 4.8 collective-permute-start.4
  575.0 10.6 collective-permute-done.5
  592.3 6.9 add_convert_fusion.1
  600.4 10.9 fusion.49
  611.3 15.5 %add_convert_fusion = bf16[1024,5248]{1,0:T(8,128)(2,1)} fusion(f32[1024,5248]{1,0:T(8,128)} %fusion.49, bf16[256,2624]{1,0:T(8,128)(2,1)} %copy-done.57, bf16[256,2624]{1,0:T(8,128)(2,1)} %copy-done.58, f32[256,1024]{1,0:T(8,128)} %get-tuple-element.102, f32[256]{0:T(256)S(1)} %add_rsqrt_fusion, f32[256]{0:T(256)S(1)} %broadcast_multiply_fusion.15, ...), kind=kOutput, calls=%fused_computation.2 | convolution fusion | flops 2768633856 | bytes 35985408 | tf_op jit(solution)/shard_map/td,tf->df/dot_general | solution.py:176
  628.8 5.5 fusion.86
  634.3 5.1 fusion.85
  639.4 27.8 %reduce-scatter.11.cloned.1.call-done = bf16[656,1024]{1,0:T(8,128)(2,1)} async-done(((bf16[2624,1024]{1,0:T(8,128)(2,1)}), bf16[656,1024]{1,0:T(8,128)(2,1)}) %reduce-scatter.11.cloned.1.call-update) | async-done | bytes 1343504 | tf_op jit(solution)/shard_map/reduce_scatter | solution.py:267
  667.2 115.1 %reduce-scatter.5.cloned.1.call-done = bf16[256,3072]{1,0:T(8,128)(2,1)} async-done(((bf16[1024,3072]{1,0:T(8,128)(2,1)}), bf16[256,3072]{1,0:T(8,128)(2,1)}) %reduce-scatter.5.cloned.1.call-update) | async-done | bytes 1572880 | tf_op jit(solution)/shard_map/reduce_scatter | solution.py:255
  782.2 185.3 %reduce-scatter.9.cloned.1.call-done = bf16[256,5248]{1,0:T(8,128)(2,1)} async-done(((bf16[1024,5248]{1,0:T(8,128)(2,1)}), bf16[256,5248]{1,0:T(8,128)(2,1)}) %reduce-scatter.9.cloned.1.call-update) | async-done | bytes 2686992 | tf_op jit(solution)/shard_map/reduce_scatter | solution.py:264
  970.7 4.7 fusion.113
  975.5 7.0 fusion.101
  982.5 11.1 %all-reduce.8 = (bf16[1024]{0:T(1024)(128)(2,1)S(1)}, bf16[1024]{0:T(1024)(128)(2,1)S(1)}) all-reduce(bf16[1024]{0:T(1024)(128)(2,1)S(1)} %add_convert_fusion.7, bf16[1024]{0:T(1024)(128)(2,1)S(1)} %add_convert_fusion.6), channel_id=2, replica_groups=mesh['rep'=8,'fsdp'=4] {'fsdp'}, use_global_device_ids=true, to_apply=%region_24.25.clone | all-reduce | flops 2048 | bytes 8192
  993.7 12.7 %all-reduce.6 = (bf16[256]{0:T(256)(128)(2,1)S(1)}, bf16[256]{0:T(256)(128)(2,1)S(1)}) all-reduce(bf16[256]{0:T(256)(128)(2,1)S(1)} %dynamic-slice.1, bf16[256]{0:T(256)(128)(2,1)S(1)} %dynamic-slice.3), channel_id=1, replica_groups=mesh['rep'=8,'fsdp'=4] {'rep'}, use_global_device_ids=true, to_apply=%region_25.26 | all-reduce | flops 512 | bytes 2048 | tf_op jit(solution)/shard_map/psum | solution.py:272
  1010.9 65.3 %all-reduce.11.cloned.1.call-done = (bf16[256,3072]{1,0:T(8,128)(2,1)}, bf16[256,1024]{1,0:T(8,128)(2,1)}, bf16[256,5248]{1,0:T(8,128)(2,1)}, bf16[656,1024]{1,0:T(8,128)(2,1)}) async-done(((bf16[256,3072]{1,0:T(8,128)(2,1)}, bf16[256,1024]{1,0:T(8,128)(2,1)}, bf16[256,5248]{1,0:T(8,128)(2,1)}, bf16[656,1024]{1,0:T(8,128)(2,1)}), (bf16[256,3072]{1,0:T(8,128)(2,1)}, bf16[256,1024]{1,0:T(8,128)(2,1)}, ...) | async-done | bytes 6127632 | tf_op jit(solution)/shard_map/psum | solution.py:273
  1076.2 3.6 convert_element_type.263
  1080.9 2.7 convert_element_type.269
  (333 shorter events, 102.6 us)
Async XLA Ops:
  7.2 6.1 copy-start.2
  7.2 120.6 %all-gather.7.cloned.1.call-start = ((), (), s32[]{:S(2)}) async-start(), calls=%async_computation.4 | async-start | bytes 7864320 | tf_op jit(solution)/shard_map/all_gather | solution.py:99
  7.9 194.5 %all-gather.9.cloned.1.call-start = ((), (), s32[]{:S(2)}) async-start(), calls=%async_computation.5 | async-start | bytes 2621440 | tf_op jit(solution)/shard_map/all_gather | solution.py:100
  8.7 5.3 copy-start.85
  8.7 359.5 %all-gather.11.cloned.1.call-start = ((), (), s32[]{:S(2)}) async-start(), calls=%async_computation.6 | async-start | bytes 13434880 | tf_op jit(solution)/shard_map/all_gather | solution.py:102
  9.4 458.6 %all-gather.13.cloned.1.call-start = ((), (), s32[]{:S(2)}) async-start(), calls=%async_computation.7 | async-start | bytes 6717440 | tf_op jit(solution)/shard_map/all_gather | solution.py:103
  10.0 629.4 %reduce-scatter.7.cloned.1.call-start = ((), (), s32[]{:S(2)}) async-start(), calls=%async_computation.9 | async-start | bytes 2621440 | tf_op jit(solution)/shard_map/reduce_scatter | solution.py:258
  13.3 14.8 %copy-start.86 = (bf16[256]{0:T(256)(128)(2,1)S(1)}, bf16[256]{0:T(256)(128)(2,1)}, u32[]{:S(2)}) copy-start(bf16[256]{0:T(256)(128)(2,1)} %param.15) | copy-start | bytes 1540
  13.5 119.1 %copy-start.77 = (f32[256]{0:T(256)}, f32[256]{0:T(256)S(1)}, u32[]{:S(2)}) copy-start(f32[256]{0:T(256)S(1)} %get-tuple-element.114) | copy-start | bytes 3076
  13.5 121.9 %copy-start.75 = (f32[256]{0:T(256)}, f32[256]{0:T(256)S(1)}, u32[]{:S(2)}) copy-start(f32[256]{0:T(256)S(1)} %get-tuple-element.115) | copy-start | bytes 3076
  14.0 118.6 %copy-start.81 = (f32[256]{0:T(256)}, f32[256]{0:T(256)S(1)}, u32[]{:S(2)}) copy-start(f32[256]{0:T(256)S(1)} %add_rsqrt_fusion.1) | copy-start | bytes 3076
  26.7 108.7 %copy-start.67 = (f32[4,1,256]{2,1,0:T(1,128)}, f32[4,1,256]{2,1,0:T(1,128)S(1)}, u32[]{:S(2)}) copy-start(f32[4,1,256]{2,1,0:T(1,128)S(1)} %convert_element_type.274) | copy-start | bytes 12292
  26.7 108.7 %copy-start.79 = (f32[256]{0:T(256)}, f32[256]{0:T(256)S(1)}, u32[]{:S(2)}) copy-start(f32[256]{0:T(256)S(1)} %add_rsqrt_fusion.3) | copy-start | bytes 3076
  27.6 153.5 %copy-start.60 = (f32[256,64]{0,1:T(8,128)}, f32[256,64]{0,1:T(8,128)S(1)}, u32[]{:S(2)}) copy-start(f32[256,64]{0,1:T(8,128)S(1)} %get-tuple-element.90) | copy-start | bytes 196612
  27.6 153.5 %copy-start.62 = (f32[256,64]{0,1:T(8,128)}, f32[256,64]{0,1:T(8,128)S(1)}, u32[]{:S(2)}) copy-start(f32[256,64]{0,1:T(8,128)S(1)} %get-tuple-element.91) | copy-start | bytes 196612
  127.7 7.7 copy-start.84
  134.3 22.8 %copy-start.22 = (bf16[256,1024]{1,0:T(8,128)(2,1)}, bf16[256,1024]{1,0:T(8,128)(2,1)S(1)}, u32[]{:S(2)}) copy-start(bf16[256,1024]{1,0:T(8,128)(2,1)S(1)} %slice.322) | copy-start | bytes 1572868
  158.0 24.5 %collective-permute-start.3 = (bf16[64,2048]{1,0:T(8,128)(2,1)}, bf16[64,2048]{1,0:T(8,128)(2,1)}, u32[]{:S(2)}, u32[]{:S(2)}) collective-permute-start(bf16[64,2048]{1,0:T(8,128)(2,1)} %get-tuple-element.73), channel_id=1, source_target_pairs={{1,0},{2,1},{3,2},{5,4},{6,5},{7,6},{9,8},{10,9},{11,10},{13,12},{... | collective-permute-start | bytes 786440 | tf_op jit(solution)/shard_map/ppermute | solution.py:23
  159.3 23.2 %collective-permute-start.2 = (bf16[64,2048]{1,0:T(8,128)(2,1)}, bf16[64,2048]{1,0:T(8,128)(2,1)}, u32[]{:S(2)}, u32[]{:S(2)}) collective-permute-start(bf16[64,2048]{1,0:T(8,128)(2,1)} %get-tuple-element.72), channel_id=1, source_target_pairs={{0,1},{1,2},{2,3},{4,5},{5,6},{6,7},{8,9},{9,10},{10,11},{12,13},{... | collective-permute-start | bytes 786440 | tf_op jit(solution)/shard_map/ppermute | solution.py:22
  174.2 13.3 %collective-permute-start.1 = (bf16[64,2048]{1,0:T(8,128)(2,1)}, bf16[64,2048]{1,0:T(8,128)(2,1)}, u32[]{:S(2)}, u32[]{:S(2)}) collective-permute-start(bf16[64,2048]{1,0:T(8,128)(2,1)} %get-tuple-element.67), channel_id=1, source_target_pairs={{1,0},{2,1},{3,2},{5,4},{6,5},{7,6},{9,8},{10,9},{11,10},{13,12},{... | collective-permute-start | bytes 786440 | tf_op jit(solution)/shard_map/ppermute | solution.py:23
  175.5 12.1 %collective-permute-start = (bf16[64,2048]{1,0:T(8,128)(2,1)}, bf16[64,2048]{1,0:T(8,128)(2,1)}, u32[]{:S(2)}, u32[]{:S(2)}) collective-permute-start(bf16[64,2048]{1,0:T(8,128)(2,1)} %get-tuple-element.66), channel_id=1, source_target_pairs={{0,1},{1,2},{2,3},{4,5},{5,6},{6,7},{8,9},{9,10},{10,11},{12,13},{... | collective-permute-start | bytes 786440 | tf_op jit(solution)/shard_map/ppermute | solution.py:22
  187.5 6.2 copy-start.31
  202.4 9.8 copy-start.47
  468.1 12.3 %copy-start.15 = (f32[256,5248]{1,0:T(8,128)S(1)}, f32[256,5248]{1,0:T(8,128)}, u32[]{:S(2)}) copy-start(f32[256,5248]{1,0:T(8,128)} %fusion.158) | copy-start | bytes 16121860
  468.1 14.2 %copy-start = (bf16[1024,5248]{1,0:T(8,128)(2,1)S(1)}, bf16[1024,5248]{1,0:T(8,128)(2,1)}, u32[]{:S(2)}) copy-start(bf16[1024,5248]{1,0:T(8,128)(2,1)} %all-gather.11.cloned.1.call-done) | copy-start | bytes 32243716
  480.3 6.4 slice-start.6
  486.8 10.9 copy-start.14
  515.5 151.7 %reduce-scatter.11.cloned.1.call-start = ((), (), s32[]{:S(2)}) async-start(), calls=%async_computation.11 | async-start | bytes 6717440 | tf_op jit(solution)/shard_map/reduce_scatter | solution.py:267
  517.3 5.6 slice-start
  536.5 245.7 %reduce-scatter.5.cloned.1.call-start = ((), (), s32[]{:S(2)}) async-start(), calls=%async_computation.8 | async-start | bytes 7864320 | tf_op jit(solution)/shard_map/reduce_scatter | solution.py:255
  544.0 8.1 copy-start.10
  545.5 26.7 %collective-permute-start.7 = (bf16[64,2048]{0,1:T(8,128)(2,1)}, bf16[64,2048]{0,1:T(8,128)(2,1)S(1)}, u32[]{:S(2)}, u32[]{:S(2)}) collective-permute-start(bf16[64,2048]{0,1:T(8,128)(2,1)} %get-tuple-element.47), channel_id=1, source_target_pairs={{1,0},{2,1},{3,2},{5,4},{6,5},{7,6},{9,8},{10,9},{11,10},{13,12},{... | collective-permute-start | bytes 786440 | tf_op jit(solution)/shard_map/ppermute | solution.py:31
  546.8 25.4 %collective-permute-start.6 = (bf16[64,2048]{0,1:T(8,128)(2,1)}, bf16[64,2048]{0,1:T(8,128)(2,1)}, u32[]{:S(2)}, u32[]{:S(2)}) collective-permute-start(bf16[64,2048]{0,1:T(8,128)(2,1)} %get-tuple-element.46), channel_id=1, source_target_pairs={{0,1},{1,2},{2,3},{4,5},{5,6},{6,7},{8,9},{9,10},{10,11},{12,13},{... | collective-permute-start | bytes 786440 | tf_op jit(solution)/shard_map/ppermute | solution.py:31
  561.6 6.8 copy-start.4
  561.7 6.8 copy-start.32
  562.1 7.5 copy-start.34
  562.1 7.5 copy-start.72
  562.1 23.4 %collective-permute-start.5 = (bf16[64,2048]{0,1:T(8,128)(2,1)S(1)}, bf16[64,2048]{0,1:T(8,128)(2,1)S(1)}, u32[]{:S(2)}, u32[]{:S(2)}) collective-permute-start(bf16[64,2048]{0,1:T(8,128)(2,1)S(1)} %get-tuple-element.45), channel_id=1, source_target_pairs={{1,0},{2,1},{3,2},{5,4},{6,5},{7,6},{9,8},{10,9},{11,10},{13,12},{... | collective-permute-start | bytes 786440 | tf_op jit(solution)/shard_map/ppermute | solution.py:31
  563.7 22.5 %collective-permute-start.4 = (bf16[64,2048]{0,1:T(8,128)(2,1)S(1)}, bf16[64,2048]{0,1:T(8,128)(2,1)S(1)}, u32[]{:S(2)}, u32[]{:S(2)}) collective-permute-start(bf16[64,2048]{0,1:T(8,128)(2,1)S(1)} %get-tuple-element.44), channel_id=1, source_target_pairs={{0,1},{1,2},{2,3},{4,5},{5,6},{6,7},{8,9},{9,10},{10,11},{12,13},{... | collective-permute-start | bytes 786440 | tf_op jit(solution)/shard_map/ppermute | solution.py:31
  572.2 17.2 %copy-start.53 = (bf16[256,16,64]{0,2,1:T(8,128)(2,1)}, bf16[256,16,64]{0,2,1:T(8,128)(2,1)S(1)}, u32[]{:S(2)}) copy-start(bf16[256,16,64]{0,2,1:T(8,128)(2,1)S(1)} %get-tuple-element.78) | copy-start | bytes 1572868
  572.2 20.1 %copy-start.39 = (bf16[256,16,64]{0,2,1:T(8,128)(2,1)}, bf16[256,16,64]{0,2,1:T(8,128)(2,1)S(1)}, u32[]{:S(2)}) copy-start(bf16[256,16,64]{0,2,1:T(8,128)(2,1)S(1)} %get-tuple-element.79) | copy-start | bytes 1572868
  574.9 17.4 %copy-start.37 = (bf16[256,1024]{0,1:T(8,128)(2,1)}, bf16[256,1024]{0,1:T(8,128)(2,1)S(1)}, u32[]{:S(2)}) copy-start(bf16[256,1024]{0,1:T(8,128)(2,1)S(1)} %slice.320) | copy-start | bytes 1572868
  599.2 368.3 %reduce-scatter.9.cloned.1.call-start = ((), (), s32[]{:S(2)}) async-start(), calls=%async_computation.10 | async-start | bytes 13434880 | tf_op jit(solution)/shard_map/reduce_scatter | solution.py:264
  626.9 449.3 %all-reduce.11.cloned.1.call-start = ((), (), s32[]{:S(2)}) async-start(), calls=%async_computation.12 | async-start | bytes 12255232 | tf_op jit(solution)/shard_map/psum | solution.py:273
  628.8 5.5 copy-start.16
  975.5 7.0 copy-start.64
  975.5 32.1 %copy-start.8 = (f32[256,1024]{1,0:T(8,128)S(1)}, f32[256,1024]{1,0:T(8,128)}, u32[]{:S(2)}) copy-start(f32[256,1024]{1,0:T(8,128)} %copy-done.7) | copy-start | bytes 3145732
  975.5 32.1 %copy-start.11 = (f32[256,1024]{1,0:T(8,128)S(1)}, f32[256,1024]{1,0:T(8,128)}, u32[]{:S(2)}) copy-start(f32[256,1024]{1,0:T(8,128)} %copy-done.9) | copy-start | bytes 3145732
  (65 other events, 183.9 us)
Sparse Core Ops, SparseCore 0:
  9.6 118.1 all-gather.6
  129.3 50.0 all-gather.8
  181.0 187.1 all-gather.10
  369.6 98.3 all-gather.12
  515.6 48.0 reduce-scatter.6
  566.5 100.6 reduce-scatter.10
  669.6 112.6 reduce-scatter.4
  784.7 182.7 reduce-scatter.8
  971.8 104.4 all-reduce.10
where the time goes:
time: 1100 us; the launch traced here: 1090 us
  waiting for transfers between devices  737 us (67%)
  matrix products  168 us (15%)
  other arithmetic  56.3 us (5%)
  blocking collectives  44.5 us (4%)
  local copies, waits for them, and re-layouts  43.3 us (4%)
  starting transfers between devices  27 us (2%)
  between operations  16.4 us (1%)
    reduce_scatter x1, waiting for transfers between devices, on_device(): lax.psum_scatter(totals[4].astype(jnp.bfloat16), 'fsdp', scatter_dimensio...  185 us
    all_gather x1, waiting for transfers between devices, on_device(): lax.all_gather(w_in, 'fsdp', axis=0, tiled=True)  149 us
    reduce_scatter x1, waiting for transfers between devices, on_device(): lax.psum_scatter(totals[1].astype(jnp.bfloat16), 'fsdp', scatter_dimensio...  115 us
    all_gather x1, waiting for transfers between devices, on_device(): lax.all_gather(w_qkv, 'fsdp', axis=0, tiled=True)  90.8 us
    all_gather x1, waiting for transfers between devices, on_device(): lax.all_gather(w_down, 'fsdp', axis=0, tiled=True)  89.7 us
    psum x1, waiting for transfers between devices, on_device(): lax.psum(owned_grads[1].astype(jnp.bfloat16), 'rep').astype(jnp.float32)  65.3 us
    reduce_scatter x1, waiting for transfers between devices, on_device(): lax.psum_scatter(totals[5].astype(jnp.bfloat16), 'fsdp', scatter_dimensio...  27.8 us
    dot_general x2, matrix products, on_device(): jnp.einsum('td,tf->df', normed_second, grad_hidden, preferred_element_typ...  26.4 us
  transfers between devices with their start and end apart: 17, of which 9 were waited for; matrix products, arithmetic and copies ran while one was open for 18% of the time, Pallas kernels for 0%

commit v1 on v0

v1 whole, which is shorter than its diff:
```python
import functools

import jax
import jax.numpy as jnp
from jax import lax
from jax.experimental import pallas as pl
from jax.experimental.pallas import tpu as pltpu
from jax.sharding import PartitionSpec as P

HEAD_DIM = 64
WIN = 64
BLOCK_Q = 128
LANES = 128

epsilon = 1e-05
root_half = 0.7071067811865476
inv_root_two_pi = 0.3989422804014327
f32 = jnp.float32
bf16 = jnp.bfloat16
VMEM_LIMIT = 48 * 1024 * 1024


def bit_count():
    return lax.axis_size("rep").bit_length() - 1


def axis_of(bit):
    return 0 if bit == 0 else bit_count() - bit


def bit_value(bit):
    return (lax.axis_index("rep") >> bit) & 1


def piece_number():
    bits = bit_count()
    return sum(bit_value(bit) << (bits - 1 - axis_of(bit)) for bit in range(bits))


def flip(value, bit):
    size = lax.axis_size("rep")
    return lax.ppermute(value, "rep", [(i, i ^ (1 << bit)) for i in range(size)])


def turn(value, steps):
    size = lax.axis_size("fsdp")
    return lax.ppermute(value, "fsdp", [(i, (i + steps) % size) for i in range(size)])


def link_orders():
    bits = list(range(1, bit_count()))
    return bits, bits[::-1]


def widen(state, bit):
    axis = axis_of(bit)
    got = flip(state, bit)
    first = bit_value(bit) == 0
    return jnp.concatenate(
        [jnp.where(first, state, got), jnp.where(first, got, state)], axis=axis
    )


def spread(parts):
    results = []
    for part, order in zip(parts, link_orders()):
        state = part[(None,) * bit_count()]
        for bit in order + [0]:
            state = widen(state, bit)
        results.append(state)
    return results


def fold(state, first_axis, order):
    axes = {bit: first_axis + axis_of(bit) - 1 for bit in order}
    for bit in order:
        mine = bit_value(bit)
        keep = lax.dynamic_slice_in_dim(state, mine, 1, axes[bit])
        give = lax.dynamic_slice_in_dim(state, 1 - mine, 1, axes[bit])
        state = (keep.astype(f32) + flip(give, bit).astype(f32)).astype(bf16)
    return state


def to_owner(state):
    size = lax.axis_size("fsdp")
    me = lax.axis_index("fsdp")
    total = lax.dynamic_index_in_dim(state, me, 0, False).astype(f32)
    for steps in range(1, size):
        give = lax.dynamic_index_in_dim(state, lax.rem(me + steps, size), 0, False)
        total = total + turn(give, steps).astype(f32)
    return total.astype(bf16)


def half_columns(width):
    return width // 2 // LANES * LANES


def half_rows(rows):
    return -(-rows // 2 // 16) * 16


def place(shard, others, pad_rows=0):
    size = lax.axis_size("fsdp")
    me = lax.axis_index("fsdp")
    rows = shard.shape[0]
    whole = jnp.zeros((size * rows + pad_rows, shard.shape[1]), shard.dtype)
    whole = lax.dynamic_update_slice(whole, shard, (me * rows, 0))
    for steps in range(1, size):
        source = lax.rem(me - steps + size, size)
        whole = lax.dynamic_update_slice(whole, others[steps - 1], (source * rows, 0))
    return whole


def gather_rows(shard):
    pieces = lax.axis_size("rep")
    size = lax.axis_size("fsdp")
    rows = shard.shape[0] // pieces
    piece = lax.dynamic_slice_in_dim(shard, piece_number() * rows, rows, 0)
    came = jnp.stack([turn(piece, steps) for steps in range(1, size)])
    cut = half_columns(shard.shape[1])
    left, right = spread((came[:, :, :cut], came[:, :, cut:]))
    joined = jnp.concatenate([left, right], axis=-1)
    joined = jnp.moveaxis(joined, bit_count(), 0).reshape((size - 1,) + shard.shape)
    return place(shard, joined)


def gather_columns(shard, pad_rows):
    pieces = lax.axis_size("rep")
    size = lax.axis_size("fsdp")
    rows, width = shard.shape
    columns = width // pieces
    piece = lax.dynamic_slice_in_dim(shard, piece_number() * columns, columns, 1)
    came = jnp.stack([turn(piece, steps) for steps in range(1, size)])
    cut = half_rows(rows)
    upper, lower = spread((came[:, :cut], came[:, cut:]))
    joined = jnp.concatenate([upper, lower], axis=-2)
    joined = joined.reshape((pieces, size - 1, rows, columns))
    joined = jnp.transpose(joined, (1, 2, 0, 3)).reshape((size - 1, rows, width))
    return place(shard, joined, pad_rows)


def tokens_dot(left, right):
    return lax.dot_general(left, right, (((0,), (0,)), ((), ())), preferred_element_type=f32)


def pair_sum(left, right, split_left):
    size = lax.axis_size("fsdp")

    def half(which):
        if split_left:
            view = left.reshape(left.shape[0], size, 2, -1)
            part = lax.dynamic_index_in_dim(view, which, 2, False)
            return tokens_dot(part.reshape(left.shape[0], -1), right)
        width = right.shape[1] // 2
        return tokens_dot(left, lax.dynamic_slice_in_dim(right, which * width, width, 1))

    mine = bit_value(0)
    got = flip(half(1 - mine).astype(bf16), 0)
    return (half(mine) + got.astype(f32)).astype(bf16)


def reduce_rows(state):
    size = lax.axis_size("fsdp")
    links = bit_count() - 1
    width = state.shape[1]
    cut = half_columns(width)
    state = state.reshape((size,) + (2,) * links + (-1, width))
    parts = []
    for part, order in zip((state[..., :cut], state[..., cut:]), link_orders()):
        parts.append(fold(part, 1, order).reshape(size, -1, part.shape[-1]))
    owned = to_owner(jnp.concatenate(parts, axis=-1))
    left, right = spread((owned[:, :cut], owned[:, cut:]))
    return jnp.concatenate([left, right], axis=-1).reshape(-1, width).astype(f32)


def reduce_columns(state):
    size = lax.axis_size("fsdp")
    links = bit_count() - 1
    rows = state.shape[0] // size
    cut = half_rows(rows)
    columns = state.shape[1] // (1 << links)
    state = state.reshape((size, rows) + (2,) * links + (columns,))
    parts = []
    for part, order in zip((state[:, :cut], state[:, cut:]), link_orders()):
        parts.append(fold(part, 2, order).reshape(size, -1, columns))
    owned = to_owner(jnp.concatenate(parts, axis=1))
    upper, lower = spread((owned[:cut], owned[cut:]))
    joined = jnp.concatenate([upper, lower], axis=-2).reshape(-1, rows, columns)
    return jnp.transpose(joined, (1, 0, 2)).reshape(rows, -1).astype(f32)


def neighbours(up, down):
    size = lax.axis_size("fsdp")
    forward = [(i, i + 1) for i in range(size - 1)]
    backward = [(i + 1, i) for i in range(size - 1)]
    return lax.ppermute(up, "fsdp", backward), lax.ppermute(down, "fsdp", forward)


def params(*semantics):
    return pltpu.CompilerParams(
        dimension_semantics=semantics, vmem_limit_bytes=VMEM_LIMIT
    )


def cost(flops, nbytes):
    return pl.CostEstimate(flops=int(flops), bytes_accessed=int(nbytes), transcendentals=0)


def dot_nn(left, right):
    return jnp.dot(left, right, preferred_element_type=f32)


def dot_nt(left, right):
    return lax.dot_general(left, right, (((1,), (1,)), ((), ())), preferred_element_type=f32)


def normalized(values):
    centred = values - jnp.mean(values, axis=-1, keepdims=True)
    inverse = lax.rsqrt(jnp.mean(centred * centred, axis=-1, keepdims=True) + epsilon)
    return centred * inverse, inverse


def norm_back(grad_out, gain, scaled, inverse):
    grad_scaled = grad_out * gain
    return inverse * (
        grad_scaled
        - jnp.mean(grad_scaled, axis=-1, keepdims=True)
        - scaled * jnp.mean(grad_scaled * scaled, axis=-1, keepdims=True)
    )


def swapped_halves(values):
    width = values.shape[-1]
    lane = lax.broadcasted_iota(jnp.int32, values.shape, values.ndim - 1)
    ahead = pltpu.roll(values, width - HEAD_DIM // 2, values.ndim - 1)
    behind = pltpu.roll(values, HEAD_DIM // 2, values.ndim - 1)
    return jnp.where(lane % HEAD_DIM < HEAD_DIM // 2, ahead, behind)


def qkv_kernel(x_ref, gain_ref, w_ref, cos_ref, sin_ref, normed_ref, out_ref, *, rope_steps):
    step = pl.program_id(0)

    @pl.when(step == 0)
    def _():
        scaled, _inverse = normalized(x_ref[...].astype(f32))
        normed_ref[...] = (scaled * gain_ref[...]).astype(bf16)

    product = dot_nn(normed_ref[...], w_ref[...])

    @pl.when(step >= rope_steps)
    def _():
        out_ref[0] = product.astype(bf16)

    @pl.when(step < rope_steps)
    def _():
        seq_rows = cos_ref.shape[0]
        cosine, sine = cos_ref[...], sin_ref[...]
        for top in range(0, product.shape[0], seq_rows):
            for lane in range(0, product.shape[1], LANES):
                tile = product[top : top + seq_rows, lane : lane + LANES]
                out_ref[0, top : top + seq_rows, lane : lane + LANES] = (
                    tile * cosine + swapped_halves(tile) * sine
                ).astype(bf16)


def qkv_call(x, gain, weight, cosine, sine):
    rows, width = x.shape
    block = 512
    per_plane = width // block
    return pl.pallas_call(
        functools.partial(qkv_kernel, rope_steps=2 * per_plane),
        grid=(3 * per_plane,),
        in_specs=[
            pl.BlockSpec((rows, width), lambda i: (0, 0)),
            pl.BlockSpec((1, width), lambda i: (0, 0)),
            pl.BlockSpec((width, block), lambda i: (0, i)),
            pl.BlockSpec(cosine.shape, lambda i: (0, 0)),
            pl.BlockSpec(sine.shape, lambda i: (0, 0)),
        ],
        out_specs=[
            pl.BlockSpec((rows, width), lambda i: (0, 0)),
            pl.BlockSpec((1, rows, block), lambda i: (i // per_plane, 0, i % per_plane)),
        ],
        out_shape=[
            jax.ShapeDtypeStruct((rows, width), bf16),
            jax.ShapeDtypeStruct((3, rows, width), bf16),
        ],
        compiler_params=params("arbitrary"),
        cost_estimate=cost(6 * rows * width * width, 6 * width * width + 10 * rows * width),
        name="qkv",
    )(x, gain, weight, cosine, sine)


def head_masks():
    lane = lax.broadcasted_iota(jnp.int32, (1, LANES), 1)
    first = lane < HEAD_DIM
    return first, first.astype(f32).astype(bf16), (~first).astype(f32).astype(bf16)


def two_heads(tile, low_mask, high_mask):
    return jnp.concatenate([tile * low_mask, tile * high_mask], axis=0)


def score_bias(first_row, length):
    shape = (BLOCK_Q, BLOCK_Q + 2 * WIN)
    query = first_row + lax.broadcasted_iota(jnp.int32, shape, 0)
    key = first_row - WIN + lax.broadcasted_iota(jnp.int32, shape, 1)
    near = jnp.abs(query - key) <= WIN
    live = (key >= 0) & (key < length)
    bias = jnp.where(near & (live | (query == key)), 0.0, -1e30).astype(f32)
    return jnp.concatenate([bias, bias], axis=0)


def softmax_of(queries, keys, bias):
    scores = dot_nt(queries, keys) * (HEAD_DIM**-0.5) + bias
    exponent = jnp.exp(scores - jnp.max(scores, axis=-1, keepdims=True))
    return exponent / jnp.sum(exponent, axis=-1, keepdims=True)


def attend_kernel(
    meta_ref, q_ref, k_ref, v_ref, k_up_ref, v_up_ref, k_down_ref, v_down_ref, out_ref
):
    length = meta_ref[1 + pl.program_id(0)]
    rows, width = q_ref.shape[1:]
    first_head, low_mask, high_mask = head_masks()
    for lane in range(0, width, LANES):
        lanes = slice(lane, lane + LANES)
        keys = jnp.concatenate([k_up_ref[0, :, lanes], k_ref[0, :, lanes], k_down_ref[0, :, lanes]], 0)
        values = jnp.concatenate([v_up_ref[0, :, lanes], v_ref[0, :, lanes], v_down_ref[0, :, lanes]], 0)
        for top in range(0, rows, BLOCK_Q):
            bias = score_bias(meta_ref[0] + top, length)
            span = slice(top, top + BLOCK_Q + 2 * WIN)
            queries = two_heads(q_ref[0, top : top + BLOCK_Q, lanes], low_mask, high_mask)
            probs = softmax_of(queries, keys[span], bias).astype(bf16)
            result = dot_nn(probs, values[span])
            out_ref[top : top + BLOCK_Q, lanes] = jnp.where(
                first_head, result[:BLOCK_Q], result[BLOCK_Q:]
            ).astype(bf16)


def attention_specs(seqs, seq_rows, width, block):
    own = lambda plane: pl.BlockSpec((1, seq_rows, block), lambda s, h: (plane, s, h))
    rim = lambda plane: pl.BlockSpec((1, WIN, block), lambda s, h: (plane, s, h))
    flat = pl.BlockSpec((seq_rows, block), lambda s, h: (s, h))
    return own, rim, flat


def attend_call(meta, qkv, rim_up, rim_down, seqs):
    _, rows, width = qkv.shape
    seq_rows = rows // seqs
    block = 256
    own, rim, flat = attention_specs(seqs, seq_rows, width, block)
    return pl.pallas_call(
        attend_kernel,
        grid=(seqs, width // block),
        in_specs=[pl.BlockSpec(memory_space=pltpu.SMEM), own(0), own(1), own(2), rim(0), rim(1), rim(0), rim(1)],
        out_specs=flat,
        out_shape=jax.ShapeDtypeStruct((rows, width), bf16),
        compiler_params=params("arbitrary", "arbitrary"),
        cost_estimate=cost(8 * rows * width * (BLOCK_Q + 2 * WIN), 10 * rows * width),
        name="attend",
    )(meta, qkv, qkv, qkv, rim_up, rim_up, rim_down, rim_down)


def attend_back_kernel(
    meta_ref,
    q_ref,
    k_ref,
    v_ref,
    k_up_ref,
    v_up_ref,
    k_down_ref,
    v_down_ref,
    go_ref,
    cos_ref,
    sin_ref,
    gq_ref,
    gk_ref,
    gv_ref,
    up_ref,
    down_ref,
    gk_acc,
    gv_acc,
):
    length = meta_ref[1 + pl.program_id(0)]
    rows, width = q_ref.shape[1:]
    scale = HEAD_DIM**-0.5
    first_head, low_mask, high_mask = head_masks()

    def turned_back(tile, span):
        return tile * cos_ref[span, :] - swapped_halves(tile) * sin_ref[span, :]

    for lane in range(0, width, LANES):
        lanes = slice(lane, lane + LANES)
        keys = jnp.concatenate([k_up_ref[0, :, lanes], k_ref[0, :, lanes], k_down_ref[0, :, lanes]], 0)
        values = jnp.concatenate([v_up_ref[0, :, lanes], v_ref[0, :, lanes], v_down_ref[0, :, lanes]], 0)
        gk_acc[...] = jnp.zeros_like(gk_acc)
        gv_acc[...] = jnp.zeros_like(gv_acc)
        for top in range(0, rows, BLOCK_Q):
            bias = score_bias(meta_ref[0] + top, length)
            span = slice(top, top + BLOCK_Q + 2 * WIN)
            queries = two_heads(q_ref[0, top : top + BLOCK_Q, lanes], low_mask, high_mask)
            grads = two_heads(go_ref[top : top + BLOCK_Q, lanes], low_mask, high_mask)
            probs = softmax_of(queries, keys[span], bias)
            grad_probs = dot_nt(grads, values[span])
            delta = jnp.sum(probs * grad_probs, axis=-1, keepdims=True)
            grad_scores = (probs * (grad_probs - delta)).astype(bf16)
            result = dot_nn(grad_scores, keys[span])
            result = jnp.where(first_head, result[:BLOCK_Q], result[BLOCK_Q:]) * scale
            own = slice(WIN + top, WIN + top + BLOCK_Q)
            gq_ref[top : top + BLOCK_Q, lanes] = turned_back(result, own).astype(bf16)
            gk_acc[span, :] += tokens_dot(grad_scores, queries)
            gv_acc[span, :] += tokens_dot(probs.astype(bf16), grads)
        grad_keys = turned_back(gk_acc[...] * scale, slice(None))
        grad_values = gv_acc[...]
        up_ref[0, :, lanes] = grad_keys[:WIN].astype(bf16)
        up_ref[1, :, lanes] = grad_values[:WIN].astype(bf16)
        down_ref[0, :, lanes] = grad_keys[WIN + rows :].astype(bf16)
        down_ref[1, :, lanes] = grad_values[WIN + rows :].astype(bf16)
        gk_ref[:, lanes] = grad_keys[WIN : WIN + rows]
        gv_ref[:, lanes] = grad_values[WIN : WIN + rows]


def attend_back_call(meta, qkv, rim_up, rim_down, grad_out, cosine, sine, seqs):
    _, rows, width = qkv.shape
    seq_rows = rows // seqs
    block = 256
    own, rim, flat = attention_specs(seqs, seq_rows, width, block)
    table = pl.BlockSpec(cosine.shape, lambda s, h: (0, 0))
    edge = pl.BlockSpec((2, WIN, block), lambda s, h: (0, s, h))
    edge_shape = jax.ShapeDtypeStruct((2, seqs * WIN, width), bf16)
    return pl.pallas_call(
        attend_back_kernel,
        grid=(seqs, width // block),
        in_specs=[
            pl.BlockSpec(memory_space=pltpu.SMEM), own(0), own(1), own(2), rim(0), rim(1), rim(0), rim(1),
            flat, table, table,
        ],
        out_specs=[flat, flat, flat, edge, edge],
        out_shape=[
            jax.ShapeDtypeStruct((rows, width), bf16),
            jax.ShapeDtypeStruct((rows, width), f32),
            jax.ShapeDtypeStruct((rows, width), f32),
            edge_shape,
            edge_shape,
        ],
        scratch_shapes=[
            pltpu.VMEM((seq_rows + 2 * WIN, LANES), f32),
            pltpu.VMEM((seq_rows + 2 * WIN, LANES), f32),
        ],
        compiler_params=params("arbitrary", "arbitrary"),
        cost_estimate=cost(20 * rows * width * (BLOCK_Q + 2 * WIN), 20 * rows * width),
        name="attend_back",
    )(meta, qkv, qkv, qkv, rim_up, rim_up, rim_down, rim_down, grad_out, cosine, sine)


def out_kernel(o_ref, w_ref, x_ref, valid_ref, gain_ref, middle_ref, normed_ref):
    branch = dot_nn(o_ref[...], w_ref[...])
    middle = x_ref[...].astype(f32) + valid_ref[...] * branch
    middle_ref[...] = middle
    scaled, _inverse = normalized(middle)
    normed_ref[...] = (scaled * gain_ref[...]).astype(bf16)


def out_call(attended, weight, x, valid, gain):
    rows, width = x.shape
    block = 128
    tile = pl.BlockSpec((block, width), lambda i: (i, 0))
    return pl.pallas_call(
        out_kernel,
        grid=(rows // block,),
        in_specs=[
            tile,
            pl.BlockSpec((width, width), lambda i: (0, 0)),
            tile,
            pl.BlockSpec((block, 1), lambda i: (i, 0)),
            pl.BlockSpec((1, width), lambda i: (0, 0)),
        ],
        out_specs=[tile, tile],
        out_shape=[jax.ShapeDtypeStruct((rows, width), f32), jax.ShapeDtypeStruct((rows, width), bf16)],
        compiler_params=params("arbitrary"),
        cost_estimate=cost(2 * rows * width * width, 2 * width * width + 10 * rows * width),
        name="out_norm",
    )(attended, weight, x, valid, gain)


def gate_kernel(n_ref, w1_ref, w2_ref, mixed_ref, slope_ref, act_ref):
    gate_in = dot_nn(n_ref[...], w1_ref[...])
    gate_up = dot_nn(n_ref[...], w2_ref[...])
    normal_cdf = 0.5 * (1.0 + lax.erf(gate_in * root_half))
    density = jnp.exp(-0.5 * gate_in * gate_in) * inv_root_two_pi
    activated = gate_in * normal_cdf
    mixed_ref[...] = (activated * gate_up).astype(bf16)
    slope_ref[...] = (gate_up * (normal_cdf + gate_in * density)).astype(bf16)
    act_ref[...] = activated.astype(bf16)


def gate_call(normed, weight, block):
    rows, width = normed.shape
    hidden = weight.shape[1] // 2
    steps = hidden // block
    tile = pl.BlockSpec((rows, block), lambda i: (0, i))
    shape = jax.ShapeDtypeStruct((rows, hidden), bf16)
    return pl.pallas_call(
        gate_kernel,
        grid=(steps,),
        in_specs=[
            pl.BlockSpec((rows, width), lambda i: (0, 0)),
            pl.BlockSpec((width, block), lambda i: (0, i)),
            pl.BlockSpec((width, block), lambda i: (0, i + steps)),
        ],
        out_specs=[tile, tile, tile],
        out_shape=[shape, shape, shape],
        compiler_params=params("arbitrary"),
        cost_estimate=cost(4 * rows * width * hidden, 4 * width * hidden + 6 * rows * hidden),
        name="gate",
    )(normed, weight, weight)


def gate_back_kernel(g_ref, w_ref, slope_ref, act_ref, out_ref):
    grad_mixed = dot_nt(g_ref[...], w_ref[...])
    out_ref[0] = (grad_mixed * slope_ref[...].astype(f32)).astype(bf16)
    out_ref[1] = (grad_mixed * act_ref[...].astype(f32)).astype(bf16)


def gate_back_call(grad_result, weight, slope, act, block):
    rows, width = grad_result.shape
    hidden = weight.shape[0]
    tile = pl.BlockSpec((rows, block), lambda i: (0, i))
    return pl.pallas_call(
        gate_back_kernel,
        grid=(hidden // block,),
        in_specs=[
            pl.BlockSpec((rows, width), lambda i: (0, 0)),
            pl.BlockSpec((block, width), lambda i: (i, 0)),
            tile,
            tile,
        ],
        out_specs=pl.BlockSpec((2, rows, block), lambda i: (0, 0, i)),
        out_shape=jax.ShapeDtypeStruct((2, rows, hidden), bf16),
        compiler_params=params("arbitrary"),
        cost_estimate=cost(2 * rows * width * hidden, 2 * width * hidden + 8 * rows * hidden),
        name="gate_back",
    )(grad_result, weight, slope, act)


def middle_back_kernel(gu_ref, w_ref, middle_ref, upstream_ref, valid_ref, gain_ref, grad_ref, branch_ref, acc):
    step = pl.program_id(0) * pl.num_programs(1) + pl.program_id(1)

    @pl.when(step == 0)
    def _():
        acc[...] = jnp.zeros_like(acc)

    acc[...] += dot_nt(gu_ref[0], w_ref[...])

    @pl.when(step == pl.num_programs(0) * pl.num_programs(1) - 1)
    def _():
        for top in range(0, acc.shape[0], 128):
            rows = slice(top, top + 128)
            scaled, inverse = normalized(middle_ref[rows, :])
            grad = upstream_ref[rows, :].astype(f32) + norm_back(
                acc[rows, :], gain_ref[...], scaled, inverse
            )
            grad_ref[rows, :] = grad
            branch_ref[rows, :] = (grad * valid_ref[rows, :]).astype(bf16)


def middle_back_call(grad_hidden, weight, middle, upstream, valid, gain, block):
    rows, width = middle.shape
    hidden = grad_hidden.shape[2]
    steps = hidden // block
    whole = pl.BlockSpec((rows, width), lambda h, i: (0, 0))
    return pl.pallas_call(
        middle_back_kernel,
        grid=(2, steps),
        in_specs=[
            pl.BlockSpec((1, rows, block), lambda h, i: (h, 0, i)),
            pl.BlockSpec((width, block), lambda h, i: (0, h * steps + i)),
            whole,
            whole,
            pl.BlockSpec((rows, 1), lambda h, i: (0, 0)),
            pl.BlockSpec((1, width), lambda h, i: (0, 0)),
        ],
        out_specs=[whole, whole],
        out_shape=[jax.ShapeDtypeStruct((rows, width), f32), jax.ShapeDtypeStruct((rows, width), bf16)],
        scratch_shapes=[pltpu.VMEM((rows, width), f32)],
        compiler_params=params("arbitrary", "arbitrary"),
        cost_estimate=cost(4 * rows * width * hidden, 4 * width * hidden + 4 * rows * hidden + 12 * rows * width),
        name="middle_back",
    )(grad_hidden, weight, middle, upstream, valid, gain)


def input_back_kernel(gqkv_ref, w_ref, x_ref, grad_ref, gain_ref, out_ref, acc):
    step = pl.program_id(0)

    @pl.when(step == 0)
    def _():
        acc[...] = jnp.zeros_like(acc)

    acc[...] += dot_nt(gqkv_ref[...], w_ref[...])

    @pl.when(step == pl.num_programs(0) - 1)
    def _():
        for top in range(0, acc.shape[0], 128):
            rows = slice(top, top + 128)
            scaled, inverse = normalized(x_ref[rows, :].astype(f32))
            out_ref[rows, :] = (
                grad_ref[rows, :] + norm_back(acc[rows, :], gain_ref[...], scaled, inverse)
            ).astype(bf16)


def input_back_call(grad_joint, weight, x, grad_middle, gain):
    rows, width = x.shape
    block = width
    whole = pl.BlockSpec((rows, width), lambda i: (0, 0))
    return pl.pallas_call(
        input_back_kernel,
        grid=(3 * width // block,),
        in_specs=[
            pl.BlockSpec((rows, block), lambda i: (0, i)),
            pl.BlockSpec((width, block), lambda i: (0, i)),
            whole,
            whole,
            pl.BlockSpec((1, width), lambda i: (0, 0)),
        ],
        out_specs=whole,
        out_shape=jax.ShapeDtypeStruct((rows, width), bf16),
        scratch_shapes=[pltpu.VMEM((rows, width), f32)],
        compiler_params=params("arbitrary"),
        cost_estimate=cost(6 * rows * width * width, 6 * width * width + 14 * rows * width),
        name="input_back",
    )(grad_joint, weight, x, grad_middle, gain)


def rope_tables(positions):
    halfway = HEAD_DIM // 2
    frequency = 10000.0 ** (-(2.0 * jnp.arange(halfway, dtype=f32)) / HEAD_DIM)
    angles = positions.astype(f32)[:, None] * frequency[None, :]
    cosine, sine = jnp.cos(angles), jnp.sin(angles)
    return (
        jnp.concatenate([cosine] * (LANES // halfway), axis=1),
        jnp.concatenate([-sine, sine] * (LANES // HEAD_DIM), axis=1),
    )


def on_device(inputs, cotangent, lengths, norm_first, w_qkv, w_out, norm_second, w_in, w_down):
    seqs, shard_rows, width = inputs.shape
    rows = seqs * shard_rows
    hidden = w_in.shape[1] // 2
    hidden_pad = -(-hidden // 384) * 384
    pad = hidden_pad - hidden
    block = 896 if hidden_pad % 896 == 0 else 384
    first_row = lax.axis_index("fsdp") * shard_rows
    query_pos = first_row + jnp.arange(shard_rows, dtype=jnp.int32)
    rim_pos = first_row - WIN + jnp.arange(shard_rows + 2 * WIN, dtype=jnp.int32)
    cosine, sine = rope_tables(rim_pos)
    valid = (query_pos[None, :] < lengths[:, None]).astype(f32).reshape(rows, 1)
    meta = jnp.concatenate([first_row.astype(jnp.int32)[None], lengths.astype(jnp.int32)])
    x = inputs.reshape(rows, width)
    upstream = cotangent.reshape(rows, width)
    grad_result = (upstream.astype(f32) * valid).astype(bf16)

    gains = jnp.pad(jnp.stack([norm_first, norm_second], axis=1), ((0, 0), (0, LANES - 2)))
    whole_first = gather_rows(jnp.concatenate([w_qkv, gains], axis=1))
    in_shard = jnp.pad(w_in.reshape(-1, 2, hidden), ((0, 0), (0, 0), (0, pad))).reshape(-1, 2 * hidden_pad)
    whole_second = gather_rows(jnp.concatenate([w_out, in_shard], axis=1))
    whole_down = gather_columns(w_down, pad)
    gain_first = whole_first[:, 3 * width].astype(f32)[None, :]
    gain_second = whole_first[:, 3 * width + 1].astype(f32)[None, :]
    whole_qkv = whole_first[:, : 3 * width]
    whole_out = whole_second[:, :width]
    whole_in = whole_second[:, width:]

    own_rows = slice(WIN, WIN + shard_rows)
    normed_first, qkv = qkv_call(x, gain_first, whole_qkv, cosine[own_rows], sine[own_rows])
    by_seq = qkv.reshape(3, seqs, shard_rows, width)[1:]
    edge = (2, seqs * WIN, width)
    rim_down, rim_up = neighbours(
        by_seq[:, :, :WIN].reshape(edge), by_seq[:, :, shard_rows - WIN :].reshape(edge)
    )
    attended = attend_call(meta, qkv, rim_up, rim_down, seqs)
    middle, normed_second = out_call(attended, whole_out, x, valid, gain_second)
    mixed, slope, act = gate_call(normed_second, whole_in, block)
    result = jnp.dot(mixed, whole_down, preferred_element_type=f32)
    output = (middle + valid * result).astype(bf16)

    state_down = pair_sum(mixed[:, :hidden], grad_result, False)
    grad_hidden = gate_back_call(grad_result, whole_down, slope, act, block)
    state_in = [pair_sum(normed_second, grad_hidden[half], True) for half in range(2)]
    grad_middle, grad_branch = middle_back_call(
        grad_hidden, whole_in, middle, upstream, valid, gain_second, block
    )
    grad_att = dot_nt(grad_branch, whole_out).astype(bf16)
    state_out = pair_sum(attended, grad_branch, True)
    grad_q, grad_k, grad_v, edge_up, edge_down = attend_back_call(
        meta, qkv, rim_up, rim_down, grad_att, cosine, sine, seqs
    )
    from_next, from_before = neighbours(edge_up, edge_down)

    def with_edges(own, plane):
        own = own.reshape(seqs, shard_rows, width)
        before = from_before[plane].reshape(seqs, WIN, width).astype(f32)
        after = from_next[plane].reshape(seqs, WIN, width).astype(f32)
        rest = ((0, 0), (0, shard_rows - WIN), (0, 0))
        own = own + jnp.pad(before, rest) + jnp.pad(after, (rest[0], rest[1][::-1], rest[2]))
        return own.reshape(rows, width).astype(bf16)

    grad_joint = jnp.concatenate([grad_q, with_edges(grad_k, 0), with_edges(grad_v, 1)], axis=1)
    state_qkv = pair_sum(normed_first, grad_joint, True)
    grad_inputs = input_back_call(grad_joint, whole_qkv, x, grad_middle, gain_first)

    grad_down = reduce_columns(state_down)
    grad_in = reduce_rows(jnp.concatenate(state_in, axis=1))
    grad_in = jnp.concatenate([grad_in[:, :hidden], grad_in[:, hidden_pad : hidden_pad + hidden]], axis=1)
    grad_last = reduce_rows(jnp.concatenate([state_qkv, state_out], axis=1))
    grad_qkv = grad_last[:, : 3 * width]
    grad_out = grad_last[:, 3 * width :]
    grad_first = jnp.sum(grad_qkv * w_qkv.astype(f32), axis=1) / norm_first.astype(f32)
    grad_second = jnp.sum(grad_in * w_in.astype(f32), axis=1) / norm_second.astype(f32)
    return (
        output.reshape(inputs.shape),
        grad_inputs.reshape(inputs.shape),
        grad_first,
        grad_qkv,
        grad_out,
        grad_second,
        grad_in,
        grad_down,
    )


def solution(mesh):
    in_specs = (
        P("rep", "fsdp", None),
        P("rep", "fsdp", None),
        P("rep"),
        P("fsdp"),
        P("fsdp", None),
        P("fsdp", None),
        P("fsdp"),
        P("fsdp", None),
        P("fsdp", None),
    )
    out_specs = (
        P("rep", "fsdp", None),
        P("rep", "fsdp", None),
        P("fsdp"),
        P("fsdp", None),
        P("fsdp", None),
        P("fsdp"),
        P("fsdp", None),
        P("fsdp", None),
    )
    return jax.shard_map(
        on_device, mesh=mesh, in_specs=in_specs, out_specs=out_specs, check_vma=False
    )
```

time: 1100 us -> 616 us (0.56)
  waiting for transfers between devices: 737 us -> 175 us
  matrix products: 168 us -> 42.4 us
  Pallas kernels: 0 us -> 89.1 us
  starting transfers between devices: 27 us -> 116 us
  local copies, waits for them, and re-layouts: 43.3 us -> 131 us
  blocking collectives: 44.5 us -> 0 us
  between operations: 16.4 us -> 2.45 us
    all_gather x4 -> x0, waiting for transfers between devices: 330 us -> none  [the longest x1 149 us: on_device(): lax.all_gather(w_in, 'fsdp', axis=0, tiled=True)]
    reduce_scatter x4 -> x0, waiting for transfers between devices: 328 us -> none  [the longest x1 185 us: on_device(): lax.psum_scatter(totals[4].astype(jnp.bfloat16), 'fsdp', scatter_dimensio...]
    ppermute x8 -> x75, waiting for transfers between devices: 11.2 us -> 175 us  [the longest x53 131 us: flip(): return lax.ppermute(value, 'rep', [(i, i ^ 1 << bit) for i in range(size)])]
    dot_general x34 -> x12, matrix products: 158 us -> 42.4 us  [the longest x10 31.4 us: tokens_dot(): lax.dot_general(left, right, (((0,), (0,)), ((), ())), preferred_element_...]
    ppermute x8 -> x75, starting transfers between devices: 26.2 us -> 116 us  [the longest x18 54.9 us: turn(): lax.ppermute(value, 'fsdp', [(i, (i + steps) % size) for i in range(size)])]
    pallas_call x0 -> x8, Pallas kernels: none -> 89.1 us  [the longest x1 22.9 us: attend_back_call(): pl.pallas_call(attend_back_kernel, grid=(seqs, width // block), in_specs=...]
    psum x1 -> x0, waiting for transfers between devices: 65.3 us -> none  [on_device(): lax.psum(owned_grads[1].astype(jnp.bfloat16), 'rep').astype(jnp.float32)]
    unnamed x197 -> x136, local copies, waits for them, and re-layouts: 14.4 us -> 39.9 us
  transfers between devices with their start and end apart: 17 -> 75, of which waited for: 9 -> 31; matrix products, arithmetic and copies ran while one was open for 18% -> 27% of each run, Pallas kernels for 0% -> 5%
where the time goes in v1:
time: 616 us; the launch traced here: 606 us
  waiting for transfers between devices  175 us (28%)
  local copies, waits for them, and re-layouts  131 us (21%)
  starting transfers between devices  116 us (19%)
  Pallas kernels  89.1 us (14%)
  other arithmetic  49.3 us (8%)
  matrix products  42.4 us (7%)
    ppermute x53, waiting for transfers between devices, flip(): return lax.ppermute(value, 'rep', [(i, i ^ 1 << bit) for i in range(size)])  131 us
    ppermute x18, starting transfers between devices, turn(): lax.ppermute(value, 'fsdp', [(i, (i + steps) % size) for i in range(size)])  54.9 us
    ppermute x53, starting transfers between devices, flip(): return lax.ppermute(value, 'rep', [(i, i ^ 1 << bit) for i in range(size)])  50.5 us
    ppermute x18, waiting for transfers between devices, turn(): lax.ppermute(value, 'fsdp', [(i, (i + steps) % size) for i in range(size)])  44.6 us
    unnamed x136, local copies, waits for them, and re-layouts  39.9 us
    dot_general x10, matrix products, tokens_dot(): lax.dot_general(left, right, (((0,), (0,)), ((), ())), preferred_element_...  31.4 us
    pallas_call x1, Pallas kernels, attend_back_call(): pl.pallas_call(attend_back_kernel, grid=(seqs, width // block), in_specs=...  22.9 us
    dynamic_slice x3, local copies, waits for them, and re-layouts, half(): part = lax.dynamic_index_in_dim(view, which, 2, False)  15.4 us
  transfers between devices with their start and end apart: 75, of which 31 were waited for; matrix products, arithmetic and copies ran while one was open for 27% of the time, Pallas kernels for 5%

profile of v1, /device:TPU:0, one launch (start us, length us, event | category | flops | bytes accessed | tf_op | source)
XLA Modules:
  0.0 605.6 jit_solution(14055299198928529211)
XLA Ops:
  2.2 5.0 collective-permute-start.22
  8.3 3.7 copy.58
  27.4 5.5 broadcast_in_dim.58
  52.5 20.5 %collective-permute-start.11 = (bf16[32,6400]{1,0:T(8,128)(2,1)}, bf16[32,6400]{1,0:T(8,128)(2,1)S(1)}, u32[]{:S(2)}, u32[]{:S(2)}) collective-permute-start(bf16[32,6400]{1,0:T(8,128)(2,1)} %fusion.22), channel_id=1, source_target_pairs={{0,1},{1,2},{2,3},{3,0},{4,5},{5,6},{6,7},{7,4},{8,9},{9,10},{10,1... | collective-permute-start | bytes 1228808 | tf_op jit(solution)/shard_map/ppermute | solution.py:47
  87.6 3.8 collective-permute-done.3
  93.9 18.5 %collective-permute-done.27 = bf16[1,2,1,3,320,128]{5,4,3,2,1,0:T(8,128)(2,1)S(1)} collective-permute-done((bf16[1,2,1,3,320,128]{5,4,3,2,1,0:T(8,128)(2,1)S(1)}, bf16[1,2,1,3,320,128]{5,4,3,2,1,0:T(8,128)(2,1)S(1)}, u32[]{:S(2)}, u32[]{:S(2)}) %collective-permute-start.27) | collective-permute-done | bytes 491552 | tf_op jit(solution)/shard_map/ppermute | solution.py:42
  117.1 7.2 %collective-permute-done.4 = bf16[1,1,2,3,32,1536]{5,4,3,2,1,0:T(8,128)(2,1)S(1)} collective-permute-done((bf16[1,1,2,3,32,1536]{5,4,3,2,1,0:T(8,128)(2,1)S(1)}, bf16[1,1,2,3,32,1536]{5,4,3,2,1,0:T(8,128)(2,1)S(1)}, u32[]{:S(2)}, u32[]{:S(2)}) %collective-permute-start.4) | collective-permute-done | bytes 589856 | tf_op jit(solution)/shard_map/ppermute | solution.py:42
  126.0 3.7 collective-permute-done.7
  133.9 18.1 %collective-permute-done.18 = bf16[1,2,1,3,32,3200]{5,4,3,2,1,0:T(8,128)(2,1)S(1)} collective-permute-done((bf16[1,2,1,3,32,3200]{5,4,3,2,1,0:T(8,128)(2,1)S(1)}, bf16[1,2,1,3,32,3200]{5,4,3,2,1,0:T(8,128)(2,1)S(1)}, u32[]{:S(2)}, u32[]{:S(2)}) %collective-permute-start.18) | collective-permute-done | bytes 1228832 | tf_op jit(solution)/shard_map/ppermute | solution.py:42
  162.2 5.9 slice.209.w_ref
  169.5 9.6 %qkv.1 = (bf16[512,1024]{1,0:T(8,128)(2,1)S(1)}, bf16[3,512,1024]{2,1,0:T(8,128)(2,1)S(1)}) custom-call(bf16[512,1024]{1,0:T(8,128)(2,1)S(1)} %bitcast.224, f32[1,1024]{1,0:T(1,128)S(1)} %bitcast.230, bf16[1024,3072]{1,0:T(8,128)(2,1)} %slice.209.w_ref, f32[256,128]{1,0:T(8,128)S(1)} %copy-done.14, f32[256,128]{1,0:T(8,128)S(1)} %copy-done.15), custom_call_target="tpu_custom_call" | custom-call | flops 3221225472 | bytes 11534336 | tf_op jit(solution)/shard_map/qkv/pallas_call | solution.py:270
  189.4 5.1 constant_dynamic-slice_fusion.21
  194.5 3.5 copy.75
  201.5 10.7 %attend.1.o_ref = bf16[512,1024]{1,0:T(8,128)(2,1)S(1)} custom-call(s32[3]{0:T(128)S(1)} %pad_add_fusion.meta_ref, bf16[3,512,1024]{2,1,0:T(8,128)(2,1)S(1)} %get-tuple-element.22.q_ref.k_ref.v_ref, bf16[3,512,1024]{2,1,0:T(8,128)(2,1)S(1)} %get-tuple-element.22.q_ref.k_ref.v_ref, bf16[3,512,1024]{2,1,0:T(8,128)(2,1)S(1)} %get-tuple-element.22.q_ref.k_ref.v_ref, ...), custom_call_target="tpu_custom_call" | custom-call | flops 1073741824 | bytes 5242880 | tf_op jit(solution)/shard_map/attend/pallas_call | solution.py:353
  215.7 5.2 constant_dynamic-slice_fusion.18
  220.9 3.5 copy.78
  232.6 3.8 maximum_bitcast_fusion
  244.8 4.6 slice.221.w1_ref.w2_ref.w_ref
  252.2 4.3 out_norm.1
  259.7 5.1 constant_dynamic-slice_fusion.12
  264.8 3.5 copy.83
  268.3 11.1 %gate.1 = (bf16[512,2688]{1,0:T(8,128)(2,1)S(1)}, bf16[512,2688]{1,0:T(8,128)(2,1)}, bf16[512,2688]{1,0:T(8,128)(2,1)}) custom-call(bf16[512,1024]{1,0:T(8,128)(2,1)S(1)} %get-tuple-element.24.n_ref, bf16[1024,5376]{1,0:T(8,128)(2,1)} %slice.221.w1_ref.w2_ref.w_ref, bf16[1024,5376]{1,0:T(8,128)(2,1)} %slice.221.w1_ref.w2_ref.w_ref), custom_call_target="tpu_custom_call" | custom-call | flops 5637144576 | bytes 19267584 | tf_op jit(solution)/shard_map/gate/pallas_call | solution.py:504
  279.5 7.7 %add_convert_fusion.11 = bf16[512,1024]{1,0:T(8,128)(2,1)} fusion(f32[512,1024]{1,0:T(8,128)S(1)} %copy-done.19, bf16[512,2688]{1,0:T(8,128)(2,1)S(1)} %get-tuple-element.25, bf16[2688,1024]{1,0:T(8,128)(2,1)} %bitcast_dynamic-update-slice_fusion.w_ref, f32[512]{0:T(512)S(1)} %bitcast.294), kind=kOutput, calls=%fused_computation.51 | convolution fusion | flops 2820145152 | bytes 11405312 | tf_op jit(solution)/shard_map/dot_general | solution.py:684
  287.2 8.4 %gate_back.1.gu_ref = bf16[2,512,2688]{2,1,0:T(8,128)(2,1)} custom-call(bf16[512,1024]{1,0:T(8,128)(2,1)S(1)} %copy-done.5, bf16[2688,1024]{1,0:T(8,128)(2,1)} %bitcast_dynamic-update-slice_fusion.w_ref, bf16[512,2688]{1,0:T(8,128)(2,1)S(1)} %copy-done.6, bf16[512,2688]{1,0:T(8,128)(2,1)} %get-tuple-element.27.act_ref), custom_call_target="tpu_custom_call" | custom-call | flops 2818572288 | bytes 16515072 | tf_op jit(solution)/shard_map/gate_back/pallas_call | solution.py:530
  295.6 13.1 %middle_back.1 = (f32[512,1024]{1,0:T(8,128)S(1)}, bf16[512,1024]{1,0:T(8,128)(2,1)S(1)}) custom-call(bf16[2,512,2688]{2,1,0:T(8,128)(2,1)} %gate_back.1.gu_ref, bf16[1024,5376]{1,0:T(8,128)(2,1)} %slice.221.w1_ref.w2_ref.w_ref, f32[512,1024]{1,0:T(8,128)} %copy-done.18, bf16[512,1024]{1,0:T(8,128)(2,1)S(1)} %bitcast.227, f32[512,1]{1,0:T(8,128)S(1)} %bitcast.229, ...), custom_call_target="tpu_custom_call" | custom-call | flops 5637144576 | bytes 22806528 | tf_op jit(solution)/shard_map/middle_back/pallas_call | solution.py:573
  313.3 22.9 %attend_back.1 = (bf16[512,1024]{1,0:T(8,128)(2,1)S(1)}, f32[512,1024]{1,0:T(8,128)}, f32[512,1024]{1,0:T(8,128)}, bf16[2,128,1024]{2,1,0:T(8,128)(2,1)}, bf16[2,128,1024]{2,1,0:T(8,128)(2,1)}) custom-call(s32[3]{0:T(128)S(1)} %pad_add_fusion.meta_ref, bf16[3,512,1024]{2,1,0:T(8,128)(2,1)} %copy-done, bf16[3,512,1024]{2,1,0:T(8,128)(2,1)} %copy-done, ...), custom_call_target="tpu_custom_call" | custom-call | flops 2684354560 | bytes 10485760 | tf_op jit(solution)/shard_map/attend_back/pallas_call | solution.py:432
  336.2 5.4 collective-permute-start.29
  364.4 3.6 convolution_convert_fusion.3
  370.5 9.0 %input_back.1 = bf16[512,1024]{1,0:T(8,128)(2,1)} custom-call(bf16[512,3072]{1,0:T(8,128)(2,1)} %pad_maximum_fusion.4.gqkv_ref, bf16[1024,3072]{1,0:T(8,128)(2,1)} %slice.209.w_ref, bf16[512,1024]{1,0:T(8,128)(2,1)S(1)} %bitcast.226, f32[512,1024]{1,0:T(8,128)S(1)} %copy-done.8, f32[1,1024]{1,0:T(1,128)S(1)} %bitcast.231), custom_call_target="tpu_custom_call" | custom-call | flops 3221225472 | bytes 13631488 | tf_op jit(solution)/shard_map/input_back/pallas_call | solution.py:616
  381.3 4.9 add_convert_fusion.3
  386.2 7.0 %reshape.269 = bf16[4,656,2,2,128]{4,3,2,1,0:T(2,128)(2,1)} reshape(bf16[2624,512]{1,0:T(8,128)(2,1)} %add_convert_fusion.3) | data formatting | bytes 5373952 | tf_op jit(solution)/shard_map/reshape | solution.py:182
  402.1 3.5 add_convert_fusion.2
  405.7 3.5 add_convert_fusion.1
  421.0 4.1 add_convert_fusion
  426.1 28.0 %collective-permute-done.65 = bf16[4,320,1,1,128]{4,1,0,3,2:T(8,128)(2,1)S(1)} collective-permute-done((bf16[4,320,1,1,128]{4,1,0,3,2:T(8,128)(2,1)}, bf16[4,320,1,1,128]{4,1,0,3,2:T(8,128)(2,1)S(1)}, u32[]{:S(2)}, u32[]{:S(2)}) %collective-permute-start.65) | collective-permute-done | bytes 327712 | tf_op jit(solution)/shard_map/ppermute | solution.py:42
  459.8 3.8 collective-permute-done.66
  471.4 14.5 %collective-permute-done.72 = bf16[1,1,1,320,128]{4,3,2,1,0:T(8,128)(2,1)S(1)} collective-permute-done((bf16[1,1,1,320,128]{4,3,2,1,0:T(8,128)(2,1)S(1)}, bf16[1,1,1,320,128]{4,3,2,1,0:T(8,128)(2,1)S(1)}, u32[]{:S(2)}, u32[]{:S(2)}) %collective-permute-start.72) | collective-permute-done | bytes 81952 | tf_op jit(solution)/shard_map/ppermute | solution.py:42
  487.4 7.6 %collective-permute-done.69 = bf16[1,1,1,336,128]{4,3,2,1,0:T(8,128)(2,1)S(1)} collective-permute-done((bf16[1,1,1,336,128]{4,3,2,1,0:T(8,128)(2,1)S(1)}, bf16[1,1,1,336,128]{4,3,2,1,0:T(8,128)(2,1)S(1)}, u32[]{:S(2)}, u32[]{:S(2)}) %collective-permute-start.69) | collective-permute-done | bytes 86048 | tf_op jit(solution)/shard_map/ppermute | solution.py:42
  509.6 7.4 %collective-permute-done.51 = bf16[4,1,1,32,2688]{4,3,2,1,0:T(8,128)(2,1)S(1)} collective-permute-done((bf16[4,1,1,32,2688]{4,3,2,1,0:T(8,128)(2,1)S(1)}, bf16[4,1,1,32,2688]{4,3,2,1,0:T(8,128)(2,1)S(1)}, u32[]{:S(2)}, u32[]{:S(2)}) %collective-permute-start.51) | collective-permute-done | bytes 688160 | tf_op jit(solution)/shard_map/ppermute | solution.py:42
  517.2 3.8 collective-permute-done.49
  521.3 4.3 collective-permute-start.53
  527.9 6.4 %collective-permute-done.52 = bf16[32,5376]{1,0:T(8,128)(2,1)S(1)} collective-permute-done((bf16[32,5376]{1,0:T(8,128)(2,1)S(1)}, bf16[32,5376]{1,0:T(8,128)(2,1)S(1)}, u32[]{:S(2)}, u32[]{:S(2)}) %collective-permute-start.52) | collective-permute-done | bytes 344096 | tf_op jit(solution)/shard_map/ppermute | solution.py:47
  534.2 13.4 %collective-permute-done.53 = bf16[32,5376]{1,0:T(8,128)(2,1)S(1)} collective-permute-done((bf16[32,5376]{1,0:T(8,128)(2,1)S(1)}, bf16[32,5376]{1,0:T(8,128)(2,1)S(1)}, u32[]{:S(2)}, u32[]{:S(2)}) %collective-permute-start.53) | collective-permute-done | bytes 344096 | tf_op jit(solution)/shard_map/ppermute | solution.py:47
  551.3 7.9 %collective-permute-start.37 = (bf16[32,4096]{1,0:T(8,128)(2,1)S(1)}, bf16[32,4096]{1,0:T(8,128)(2,1)S(1)}, u32[]{:S(2)}, u32[]{:S(2)}) collective-permute-start(bf16[32,4096]{1,0:T(8,128)(2,1)S(1)} %get-tuple-element.110), channel_id=1, source_target_pairs={{0,1},{1,2},{2,3},{3,0},{4,5},{5,6},{6,7},{7,4},{8,9},{9,10},{10,1... | collective-permute-start | bytes 786440 | tf_op jit(solution)/shard_map/ppermute | solution.py:47
  562.2 3.8 collective-permute-done.37
  566.0 8.6 %collective-permute-done.38 = bf16[32,4096]{1,0:T(8,128)(2,1)S(1)} collective-permute-done((bf16[32,4096]{1,0:T(8,128)(2,1)S(1)}, bf16[32,4096]{1,0:T(8,128)(2,1)S(1)}, u32[]{:S(2)}, u32[]{:S(2)}) %collective-permute-start.38) | collective-permute-done | bytes 262176 | tf_op jit(solution)/shard_map/ppermute | solution.py:47
  585.2 4.9 collective-permute-done.56
  596.4 3.6 multiply_reduce_fusion
  (438 shorter events, 230.5 us)
Async XLA Ops:
  2.2 41.6 %collective-permute-start.22 = (bf16[656,128]{1,0:T(8,128)(2,1)}, bf16[656,128]{1,0:T(8,128)(2,1)S(1)}, u32[]{:S(2)}, u32[]{:S(2)}) collective-permute-start(bf16[656,128]{1,0:T(8,128)(2,1)} %constant_dynamic-slice_fusion.22), channel_id=1, source_target_pairs={{0,3},{1,0},{2,1},{3,2},{4,7},{5,4},{6,5},{7,6},{8,11},{9,8},{10,9... | collective-permute-start | bytes 503816 | tf_op jit(solution)/shard_map/ppermute | solution.py:47
  7.3 37.4 %collective-permute-start.21 = (bf16[656,128]{1,0:T(8,128)(2,1)}, bf16[656,128]{1,0:T(8,128)(2,1)}, u32[]{:S(2)}, u32[]{:S(2)}) collective-permute-start(bf16[656,128]{1,0:T(8,128)(2,1)} %constant_dynamic-slice_fusion.22), channel_id=1, source_target_pairs={{0,2},{1,3},{2,0},{3,1},{4,6},{5,7},{6,4},{7,5},{8,10},{9,11},{10,... | collective-permute-start | bytes 503816 | tf_op jit(solution)/shard_map/ppermute | solution.py:47
  7.3 38.4 %collective-permute-start.20 = (bf16[656,128]{1,0:T(8,128)(2,1)}, bf16[656,128]{1,0:T(8,128)(2,1)}, u32[]{:S(2)}, u32[]{:S(2)}) collective-permute-start(bf16[656,128]{1,0:T(8,128)(2,1)} %constant_dynamic-slice_fusion.22), channel_id=1, source_target_pairs={{0,1},{1,2},{2,3},{3,0},{4,5},{5,6},{6,7},{7,4},{8,9},{9,10},{10,1... | collective-permute-start | bytes 503816 | tf_op jit(solution)/shard_map/ppermute | solution.py:47
  17.9 59.6 %collective-permute-start.13 = (bf16[32,6400]{1,0:T(8,128)(2,1)}, bf16[32,6400]{1,0:T(8,128)(2,1)}, u32[]{:S(2)}, u32[]{:S(2)}) collective-permute-start(bf16[32,6400]{1,0:T(8,128)(2,1)} %fusion.22), channel_id=1, source_target_pairs={{0,3},{1,0},{2,1},{3,2},{4,7},{5,4},{6,5},{7,6},{8,11},{9,8},{10,9... | collective-permute-start | bytes 1228808 | tf_op jit(solution)/shard_map/ppermute | solution.py:47
  20.7 57.4 %collective-permute-start.12 = (bf16[32,6400]{1,0:T(8,128)(2,1)}, bf16[32,6400]{1,0:T(8,128)(2,1)}, u32[]{:S(2)}, u32[]{:S(2)}) collective-permute-start(bf16[32,6400]{1,0:T(8,128)(2,1)} %fusion.22), channel_id=1, source_target_pairs={{0,2},{1,3},{2,0},{3,1},{4,6},{5,7},{6,4},{7,5},{8,10},{9,11},{10,... | collective-permute-start | bytes 1228808 | tf_op jit(solution)/shard_map/ppermute | solution.py:47
  44.7 29.7 %collective-permute-start.1 = (bf16[32,3200]{1,0:T(8,128)(2,1)S(1)}, bf16[32,3200]{1,0:T(8,128)(2,1)S(1)}, u32[]{:S(2)}, u32[]{:S(2)}) collective-permute-start(bf16[32,3200]{1,0:T(8,128)(2,1)S(1)} %copy-done.47), channel_id=1, source_target_pairs={{0,2},{1,3},{2,0},{3,1},{4,6},{5,7},{6,4},{7,5},{8,10},{9,11},{10,... | collective-permute-start | bytes 614408 | tf_op jit(solution)/shard_map/ppermute | solution.py:47
  45.7 30.2 %collective-permute-start = (bf16[32,3200]{1,0:T(8,128)(2,1)S(1)}, bf16[32,3200]{1,0:T(8,128)(2,1)S(1)}, u32[]{:S(2)}, u32[]{:S(2)}) collective-permute-start(bf16[32,3200]{1,0:T(8,128)(2,1)S(1)} %copy-done.47), channel_id=1, source_target_pairs={{0,1},{1,2},{2,3},{3,0},{4,5},{5,6},{6,7},{7,4},{8,9},{9,10},{10,1... | collective-permute-start | bytes 614408 | tf_op jit(solution)/shard_map/ppermute | solution.py:47
  52.5 26.3 %collective-permute-start.11 = (bf16[32,6400]{1,0:T(8,128)(2,1)}, bf16[32,6400]{1,0:T(8,128)(2,1)S(1)}, u32[]{:S(2)}, u32[]{:S(2)}) collective-permute-start(bf16[32,6400]{1,0:T(8,128)(2,1)} %fusion.22), channel_id=1, source_target_pairs={{0,1},{1,2},{2,3},{3,0},{4,5},{5,6},{6,7},{7,4},{8,9},{9,10},{10,1... | collective-permute-start | bytes 1228808 | tf_op jit(solution)/shard_map/ppermute | solution.py:47
  80.1 34.3 %collective-permute-start.14 = (bf16[1,1,1,3,32,3200]{5,4,3,2,1,0:T(8,128)(2,1)S(1)}, bf16[1,1,1,3,32,3200]{5,4,3,2,1,0:T(8,128)(2,1)S(1)}, u32[]{:S(2)}, u32[]{:S(2)}) collective-permute-start(bf16[1,1,1,3,32,3200]{5,4,3,2,1,0:T(8,128)(2,1)S(1)} %get-tuple-element.100), channel_id=1, source_target_pairs={{0,8},{4,12},{8,0},{12,4},{16,24},{20,28},{24,16},{28,20},{1,9},{5... | collective-permute-start | bytes 1843208 | tf_op jit(solution)/shard_map/ppermute | solution.py:42
  83.2 31.8 %collective-permute-start.17 = (bf16[1,1,1,3,32,3200]{5,4,3,2,1,0:T(8,128)(2,1)S(1)}, bf16[1,1,1,3,32,3200]{5,4,3,2,1,0:T(8,128)(2,1)S(1)}, u32[]{:S(2)}, u32[]{:S(2)}) collective-permute-start(bf16[1,1,1,3,32,3200]{5,4,3,2,1,0:T(8,128)(2,1)S(1)} %get-tuple-element.101), channel_id=1, source_target_pairs={{0,16},{4,20},{8,24},{12,28},{16,0},{20,4},{24,8},{28,12},{1,17},{... | collective-permute-start | bytes 1843208 | tf_op jit(solution)/shard_map/ppermute | solution.py:42
  85.9 26.4 %collective-permute-start.27 = (bf16[1,2,1,3,320,128]{5,4,3,2,1,0:T(8,128)(2,1)S(1)}, bf16[1,2,1,3,320,128]{5,4,3,2,1,0:T(8,128)(2,1)S(1)}, u32[]{:S(2)}, u32[]{:S(2)}) collective-permute-start(bf16[1,2,1,3,320,128]{5,4,3,2,1,0:T(8,128)(2,1)S(1)} %pad_maximum_fusion.22), channel_id=1, source_target_pairs={{0,8},{4,12},{8,0},{12,4},{16,24},{20,28},{24,16},{28,20},{1,9},{5... | collective-permute-start | bytes 1474568 | tf_op jit(solution)/shard_map/ppermute | solution.py:42
  91.4 22.8 %collective-permute-start.24 = (bf16[1,1,2,3,336,128]{5,4,3,2,1,0:T(8,128)(2,1)S(1)}, bf16[1,1,2,3,336,128]{5,4,3,2,1,0:T(8,128)(2,1)S(1)}, u32[]{:S(2)}, u32[]{:S(2)}) collective-permute-start(bf16[1,1,2,3,336,128]{5,4,3,2,1,0:T(8,128)(2,1)S(1)} %pad_maximum_fusion.20), channel_id=1, source_target_pairs={{0,16},{4,20},{8,24},{12,28},{16,0},{20,4},{24,8},{28,12},{1,17},{... | collective-permute-start | bytes 1548296 | tf_op jit(solution)/shard_map/ppermute | solution.py:42
  92.1 32.2 %collective-permute-start.4 = (bf16[1,1,2,3,32,1536]{5,4,3,2,1,0:T(8,128)(2,1)S(1)}, bf16[1,1,2,3,32,1536]{5,4,3,2,1,0:T(8,128)(2,1)S(1)}, u32[]{:S(2)}, u32[]{:S(2)}) collective-permute-start(bf16[1,1,2,3,32,1536]{5,4,3,2,1,0:T(8,128)(2,1)S(1)} %pad_maximum_fusion.17), channel_id=1, source_target_pairs={{0,16},{4,20},{8,24},{12,28},{16,0},{20,4},{24,8},{28,12},{1,17},{... | collective-permute-start | bytes 1769480 | tf_op jit(solution)/shard_map/ppermute | solution.py:42
  112.3 17.3 %collective-permute-start.7 = (bf16[1,2,1,3,32,1664]{5,4,3,2,1,0:T(8,128)(2,1)S(1)}, bf16[1,2,1,3,32,1664]{5,4,3,2,1,0:T(8,128)(2,1)S(1)}, u32[]{:S(2)}, u32[]{:S(2)}) collective-permute-start(bf16[1,2,1,3,32,1664]{5,4,3,2,1,0:T(8,128)(2,1)S(1)} %pad_maximum_fusion.16), channel_id=1, source_target_pairs={{0,8},{4,12},{8,0},{12,4},{16,24},{20,28},{24,16},{28,20},{1,9},{5... | collective-permute-start | bytes 1916936 | tf_op jit(solution)/shard_map/ppermute | solution.py:42
  114.3 15.7 %collective-permute-start.28 = (bf16[1,2,2,3,320,128]{5,4,3,2,1,0:T(8,128)(2,1)S(1)}, bf16[1,2,2,3,320,128]{5,4,3,2,1,0:T(8,128)(2,1)S(1)}, u32[]{:S(2)}, u32[]{:S(2)}) collective-permute-start(bf16[1,2,2,3,320,128]{5,4,3,2,1,0:T(8,128)(2,1)S(1)} %pad_maximum_fusion.13), channel_id=1, source_target_pairs={{0,4},{4,0},{8,12},{12,8},{16,20},{20,16},{24,28},{28,24},{1,5},{5... | collective-permute-start | bytes 2949128 | tf_op jit(solution)/shard_map/ppermute | solution.py:42
  114.5 16.2 %collective-permute-start.25 = (bf16[1,2,2,3,336,128]{5,4,3,2,1,0:T(8,128)(2,1)S(1)}, bf16[1,2,2,3,336,128]{5,4,3,2,1,0:T(8,128)(2,1)S(1)}, u32[]{:S(2)}, u32[]{:S(2)}) collective-permute-start(bf16[1,2,2,3,336,128]{5,4,3,2,1,0:T(8,128)(2,1)S(1)} %pad_maximum_fusion.12), channel_id=1, source_target_pairs={{0,4},{4,0},{8,12},{12,8},{16,20},{20,16},{24,28},{28,24},{1,5},{5... | collective-permute-start | bytes 3096584 | tf_op jit(solution)/shard_map/ppermute | solution.py:42
  115.4 36.6 %collective-permute-start.18 = (bf16[1,2,1,3,32,3200]{5,4,3,2,1,0:T(8,128)(2,1)S(1)}, bf16[1,2,1,3,32,3200]{5,4,3,2,1,0:T(8,128)(2,1)S(1)}, u32[]{:S(2)}, u32[]{:S(2)}) collective-permute-start(bf16[1,2,1,3,32,3200]{5,4,3,2,1,0:T(8,128)(2,1)S(1)} %pad_maximum_fusion.10), channel_id=1, source_target_pairs={{0,8},{4,12},{8,0},{12,4},{16,24},{20,28},{24,16},{28,20},{1,9},{5... | collective-permute-start | bytes 3686408 | tf_op jit(solution)/shard_map/ppermute | solution.py:42
  124.3 29.9 %collective-permute-start.15 = (bf16[1,1,2,3,32,3200]{5,4,3,2,1,0:T(8,128)(2,1)S(1)}, bf16[1,1,2,3,32,3200]{5,4,3,2,1,0:T(8,128)(2,1)S(1)}, u32[]{:S(2)}, u32[]{:S(2)}) collective-permute-start(bf16[1,1,2,3,32,3200]{5,4,3,2,1,0:T(8,128)(2,1)S(1)} %pad_maximum_fusion.9), channel_id=1, source_target_pairs={{0,16},{4,20},{8,24},{12,28},{16,0},{20,4},{24,8},{28,12},{1,17},{... | collective-permute-start | bytes 3686408 | tf_op jit(solution)/shard_map/ppermute | solution.py:42
  129.7 27.2 %collective-permute-start.5 = (bf16[1,2,2,3,32,1536]{5,4,3,2,1,0:T(8,128)(2,1)S(1)}, bf16[1,2,2,3,32,1536]{5,4,3,2,1,0:T(8,128)(2,1)S(1)}, u32[]{:S(2)}, u32[]{:S(2)}) collective-permute-start(bf16[1,2,2,3,32,1536]{5,4,3,2,1,0:T(8,128)(2,1)S(1)} %pad_maximum_fusion.11), channel_id=1, source_target_pairs={{0,4},{4,0},{8,12},{12,8},{16,20},{20,16},{24,28},{28,24},{1,5},{5... | collective-permute-start | bytes 3538952 | tf_op jit(solution)/shard_map/ppermute | solution.py:42
  130.0 27.1 %collective-permute-start.8 = (bf16[1,2,2,3,32,1664]{5,4,3,2,1,0:T(8,128)(2,1)S(1)}, bf16[1,2,2,3,32,1664]{5,4,3,2,1,0:T(8,128)(2,1)S(1)}, u32[]{:S(2)}, u32[]{:S(2)}) collective-permute-start(bf16[1,2,2,3,32,1664]{5,4,3,2,1,0:T(8,128)(2,1)S(1)} %pad_maximum_fusion.7), channel_id=1, source_target_pairs={{0,4},{4,0},{8,12},{12,8},{16,20},{20,16},{24,28},{28,24},{1,5},{5... | collective-permute-start | bytes 3833864 | tf_op jit(solution)/shard_map/ppermute | solution.py:42
  154.2 73.7 %collective-permute-start.19 = (bf16[1,2,2,3,32,3200]{5,4,3,2,1,0:T(8,128)(2,1)}, bf16[1,2,2,3,32,3200]{5,4,3,2,1,0:T(8,128)(2,1)}, u32[]{:S(2)}, u32[]{:S(2)}) collective-permute-start(bf16[1,2,2,3,32,3200]{5,4,3,2,1,0:T(8,128)(2,1)} %pad_maximum_fusion.6), channel_id=1, source_target_pairs={{0,4},{4,0},{8,12},{12,8},{16,20},{20,16},{24,28},{28,24},{1,5},{5... | collective-permute-start | bytes 7372808 | tf_op jit(solution)/shard_map/ppermute | solution.py:42
  156.4 73.9 %collective-permute-start.16 = (bf16[1,2,2,3,32,3200]{5,4,3,2,1,0:T(8,128)(2,1)}, bf16[1,2,2,3,32,3200]{5,4,3,2,1,0:T(8,128)(2,1)}, u32[]{:S(2)}, u32[]{:S(2)}) collective-permute-start(bf16[1,2,2,3,32,3200]{5,4,3,2,1,0:T(8,128)(2,1)} %pad_maximum_fusion.5), channel_id=1, source_target_pairs={{0,4},{4,0},{8,12},{12,8},{16,20},{20,16},{24,28},{28,24},{1,5},{5... | collective-permute-start | bytes 7372808 | tf_op jit(solution)/shard_map/ppermute | solution.py:42
  180.5 20.9 %collective-permute-start.9 = (bf16[2,128,1024]{2,1,0:T(8,128)(2,1)}, bf16[2,128,1024]{2,1,0:T(8,128)(2,1)}, u32[]{:S(2)}, u32[]{:S(2)}) collective-permute-start(bf16[2,128,1024]{2,1,0:T(8,128)(2,1)} %bitcast.12), channel_id=1, source_target_pairs={{0,1},{1,2},{2,3},{4,5},{5,6},{6,7},{8,9},{9,10},{10,11},{12,13},{... | collective-permute-start | bytes 1572872 | tf_op jit(solution)/shard_map/ppermute | solution.py:196
  182.6 18.8 %collective-permute-start.10 = (bf16[2,128,1024]{2,1,0:T(8,128)(2,1)}, bf16[2,128,1024]{2,1,0:T(8,128)(2,1)}, u32[]{:S(2)}, u32[]{:S(2)}) collective-permute-start(bf16[2,128,1024]{2,1,0:T(8,128)(2,1)} %bitcast.13), channel_id=1, source_target_pairs={{1,0},{2,1},{3,2},{5,4},{6,5},{7,6},{9,8},{10,9},{11,10},{13,12},{... | collective-permute-start | bytes 1572872 | tf_op jit(solution)/shard_map/ppermute | solution.py:196
  336.2 22.2 %collective-permute-start.29 = (bf16[2,128,1024]{2,1,0:T(8,128)(2,1)}, bf16[2,128,1024]{2,1,0:T(8,128)(2,1)}, u32[]{:S(2)}, u32[]{:S(2)}) collective-permute-start(bf16[2,128,1024]{2,1,0:T(8,128)(2,1)} %get-tuple-element.31), channel_id=1, source_target_pairs={{0,1},{1,2},{2,3},{4,5},{5,6},{6,7},{8,9},{9,10},{10,11},{12,13},{... | collective-permute-start | bytes 1572872 | tf_op jit(solution)/shard_map/ppermute | solution.py:196
  341.7 18.4 %collective-permute-start.30 = (bf16[2,128,1024]{2,1,0:T(8,128)(2,1)}, bf16[2,128,1024]{2,1,0:T(8,128)(2,1)}, u32[]{:S(2)}, u32[]{:S(2)}) collective-permute-start(bf16[2,128,1024]{2,1,0:T(8,128)(2,1)} %get-tuple-element.32), channel_id=1, source_target_pairs={{1,0},{2,1},{3,2},{5,4},{6,5},{7,6},{9,8},{10,9},{11,10},{13,12},{... | collective-permute-start | bytes 1572872 | tf_op jit(solution)/shard_map/ppermute | solution.py:196
  346.3 33.9 %collective-permute-start.61 = (bf16[2624,512]{1,0:T(8,128)(2,1)}, bf16[2624,512]{1,0:T(8,128)(2,1)}, u32[]{:S(2)}, u32[]{:S(2)}) collective-permute-start(bf16[2624,512]{1,0:T(8,128)(2,1)} %convolution_convert_fusion), channel_id=1, source_target_pairs={{0,4},{4,0},{8,12},{12,8},{16,20},{20,16},{24,28},{28,24},{1,5},{5... | collective-permute-start | bytes 8060936 | tf_op jit(solution)/shard_map/ppermute | solution.py:42
  357.9 21.6 %collective-permute-start.32 = (bf16[512,1024]{1,0:T(8,128)(2,1)}, bf16[512,1024]{1,0:T(8,128)(2,1)S(1)}, u32[]{:S(2)}, u32[]{:S(2)}) collective-permute-start(bf16[512,1024]{1,0:T(8,128)(2,1)} %convolution_convert_fusion.5), channel_id=1, source_target_pairs={{0,4},{4,0},{8,12},{12,8},{16,20},{20,16},{24,28},{28,24},{1,5},{5... | collective-permute-start | bytes 3145736 | tf_op jit(solution)/shard_map/ppermute | solution.py:42
  358.4 43.7 %collective-permute-start.46 = (bf16[512,2688]{1,0:T(8,128)(2,1)}, bf16[512,2688]{1,0:T(8,128)(2,1)}, u32[]{:S(2)}, u32[]{:S(2)}) collective-permute-start(bf16[512,2688]{1,0:T(8,128)(2,1)} %convolution_convert_fusion.2), channel_id=1, source_target_pairs={{0,4},{4,0},{8,12},{12,8},{16,20},{20,16},{24,28},{28,24},{1,5},{5... | collective-permute-start | bytes 8257544 | tf_op jit(solution)/shard_map/ppermute | solution.py:42
  358.5 47.2 %collective-permute-start.47 = (bf16[512,2688]{1,0:T(8,128)(2,1)}, bf16[512,2688]{1,0:T(8,128)(2,1)}, u32[]{:S(2)}, u32[]{:S(2)}) collective-permute-start(bf16[512,2688]{1,0:T(8,128)(2,1)} %convolution_convert_fusion.1), channel_id=1, source_target_pairs={{0,4},{4,0},{8,12},{12,8},{16,20},{20,16},{24,28},{28,24},{1,5},{5... | collective-permute-start | bytes 8257544 | tf_op jit(solution)/shard_map/ppermute | solution.py:42
  367.9 53.1 %collective-permute-start.31 = (bf16[512,3072]{1,0:T(8,128)(2,1)}, bf16[512,3072]{1,0:T(8,128)(2,1)}, u32[]{:S(2)}, u32[]{:S(2)}) collective-permute-start(bf16[512,3072]{1,0:T(8,128)(2,1)} %convolution_convert_fusion.3), channel_id=1, source_target_pairs={{0,4},{4,0},{8,12},{12,8},{16,20},{20,16},{24,28},{28,24},{1,5},{5... | collective-permute-start | bytes 9437192 | tf_op jit(solution)/shard_map/ppermute | solution.py:42
  396.3 17.0 %collective-permute-start.64 = (bf16[4,320,1,2,128]{4,1,0,3,2:T(8,128)(2,1)}, bf16[4,320,1,2,128]{4,1,0,3,2:T(8,128)(2,1)}, u32[]{:S(2)}, u32[]{:S(2)}) collective-permute-start(bf16[4,320,1,2,128]{4,1,0,3,2:T(8,128)(2,1)} %copy.92), channel_id=1, source_target_pairs={{0,16},{4,20},{8,24},{12,28},{16,0},{20,4},{24,8},{28,12},{1,17},{... | collective-permute-start | bytes 1966088 | tf_op jit(solution)/shard_map/ppermute | solution.py:42
  400.6 18.6 %collective-permute-start.62 = (bf16[4,336,2,1,128]{4,1,0,3,2:T(8,128)(2,1)}, bf16[4,336,2,1,128]{4,1,0,3,2:T(8,128)(2,1)S(1)}, u32[]{:S(2)}, u32[]{:S(2)}) collective-permute-start(bf16[4,336,2,1,128]{4,1,0,3,2:T(8,128)(2,1)} %copy.89), channel_id=1, source_target_pairs={{0,8},{4,12},{8,0},{12,4},{16,24},{20,28},{24,16},{28,20},{1,9},{5... | collective-permute-start | bytes 2064392 | tf_op jit(solution)/shard_map/ppermute | solution.py:42
  410.6 85.9 %collective-permute-start.50 = (bf16[4,1,2,32,2688]{4,3,2,1,0:T(8,128)(2,1)S(1)}, bf16[4,1,2,32,2688]{4,3,2,1,0:T(8,128)(2,1)S(1)}, u32[]{:S(2)}, u32[]{:S(2)}) collective-permute-start(bf16[4,1,2,32,2688]{4,3,2,1,0:T(8,128)(2,1)S(1)} %constant_dynamic-slice_fusion.7), channel_id=1, source_target_pairs={{0,16},{4,20},{8,24},{12,28},{16,0},{20,4},{24,8},{28,12},{1,17},{... | collective-permute-start | bytes 4128776 | tf_op jit(solution)/shard_map/ppermute | solution.py:42
  412.2 86.4 %collective-permute-start.48 = (bf16[4,2,1,32,2688]{4,3,0,2,1:T(8,128)(2,1)S(1)}, bf16[4,2,1,32,2688]{4,3,0,2,1:T(8,128)(2,1)S(1)}, u32[]{:S(2)}, u32[]{:S(2)}) collective-permute-start(bf16[4,2,1,32,2688]{4,3,0,2,1:T(8,128)(2,1)S(1)} %copy.86), channel_id=1, source_target_pairs={{0,8},{4,12},{8,0},{12,4},{16,24},{20,28},{24,16},{28,20},{1,9},{5... | collective-permute-start | bytes 4128776 | tf_op jit(solution)/shard_map/ppermute | solution.py:42
  415.5 38.6 %collective-permute-start.65 = (bf16[4,320,1,1,128]{4,1,0,3,2:T(8,128)(2,1)}, bf16[4,320,1,1,128]{4,1,0,3,2:T(8,128)(2,1)S(1)}, u32[]{:S(2)}, u32[]{:S(2)}) collective-permute-start(bf16[4,320,1,1,128]{4,1,0,3,2:T(8,128)(2,1)} %constant_dynamic-slice_fusion), channel_id=1, source_target_pairs={{0,8},{4,12},{8,0},{12,4},{16,24},{20,28},{24,16},{28,20},{1,9},{5... | collective-permute-start | bytes 983048 | tf_op jit(solution)/shard_map/ppermute | solution.py:42
  419.4 34.8 %collective-permute-start.63 = (bf16[4,336,1,1,128]{4,1,0,3,2:T(8,128)(2,1)S(1)}, bf16[4,336,1,1,128]{4,1,0,3,2:T(8,128)(2,1)S(1)}, u32[]{:S(2)}, u32[]{:S(2)}) collective-permute-start(bf16[4,336,1,1,128]{4,1,0,3,2:T(8,128)(2,1)S(1)} %constant_dynamic-slice_fusion.3), channel_id=1, source_target_pairs={{0,16},{4,20},{8,24},{12,28},{16,0},{20,4},{24,8},{28,12},{1,17},{... | collective-permute-start | bytes 1032200 | tf_op jit(solution)/shard_map/ppermute | solution.py:42
  463.6 43.9 %collective-permute-start.35 = (bf16[4,1,2,32,2048]{4,3,2,1,0:T(8,128)(2,1)S(1)}, bf16[4,1,2,32,2048]{4,3,2,1,0:T(8,128)(2,1)S(1)}, u32[]{:S(2)}, u32[]{:S(2)}) collective-permute-start(bf16[4,1,2,32,2048]{4,3,2,1,0:T(8,128)(2,1)S(1)} %constant_dynamic-slice_fusion.14), channel_id=1, source_target_pairs={{0,16},{4,20},{8,24},{12,28},{16,0},{20,4},{24,8},{28,12},{1,17},{... | collective-permute-start | bytes 3145736 | tf_op jit(solution)/shard_map/ppermute | solution.py:42
  468.2 58.1 %collective-permute-start.33 = (bf16[4,2,1,32,2048]{4,3,0,2,1:T(8,128)(2,1)S(1)}, bf16[4,2,1,32,2048]{4,3,0,2,1:T(8,128)(2,1)S(1)}, u32[]{:S(2)}, u32[]{:S(2)}) collective-permute-start(bf16[4,2,1,32,2048]{4,3,0,2,1:T(8,128)(2,1)S(1)} %copy.81), channel_id=1, source_target_pairs={{0,8},{4,12},{8,0},{12,4},{16,24},{20,28},{24,16},{28,20},{1,9},{5... | collective-permute-start | bytes 3145736 | tf_op jit(solution)/shard_map/ppermute | solution.py:42
  469.8 16.1 %collective-permute-start.72 = (bf16[1,1,1,320,128]{4,3,2,1,0:T(8,128)(2,1)S(1)}, bf16[1,1,1,320,128]{4,3,2,1,0:T(8,128)(2,1)S(1)}, u32[]{:S(2)}, u32[]{:S(2)}) collective-permute-start(bf16[1,1,1,320,128]{4,3,2,1,0:T(8,128)(2,1)S(1)} %slice_bitcast_fusion.18), channel_id=1, source_target_pairs={{0,16},{4,20},{8,24},{12,28},{16,0},{20,4},{24,8},{28,12},{1,17},{... | collective-permute-start | bytes 245768 | tf_op jit(solution)/shard_map/ppermute | solution.py:42
  498.6 18.4 %collective-permute-start.51 = (bf16[4,1,1,32,2688]{4,3,2,1,0:T(8,128)(2,1)S(1)}, bf16[4,1,1,32,2688]{4,3,2,1,0:T(8,128)(2,1)S(1)}, u32[]{:S(2)}, u32[]{:S(2)}) collective-permute-start(bf16[4,1,1,32,2688]{4,3,2,1,0:T(8,128)(2,1)S(1)} %constant_dynamic-slice_fusion.6), channel_id=1, source_target_pairs={{0,8},{4,12},{8,0},{12,4},{16,24},{20,28},{24,16},{28,20},{1,9},{5... | collective-permute-start | bytes 2064392 | tf_op jit(solution)/shard_map/ppermute | solution.py:42
  502.7 18.2 %collective-permute-start.49 = (bf16[4,1,1,32,2688]{4,3,0,2,1:T(8,128)(2,1)S(1)}, bf16[4,1,1,32,2688]{4,3,0,2,1:T(8,128)(2,1)S(1)}, u32[]{:S(2)}, u32[]{:S(2)}) collective-permute-start(bf16[4,1,1,32,2688]{4,3,0,2,1:T(8,128)(2,1)S(1)} %constant_dynamic-slice_fusion.8), channel_id=1, source_target_pairs={{0,16},{4,20},{8,24},{12,28},{16,0},{20,4},{24,8},{28,12},{1,17},{... | collective-permute-start | bytes 2064392 | tf_op jit(solution)/shard_map/ppermute | solution.py:42
  507.9 43.1 %collective-permute-start.36 = (bf16[4,1,1,32,2048]{4,3,2,1,0:T(8,128)(2,1)S(1)}, bf16[4,1,1,32,2048]{4,3,2,1,0:T(8,128)(2,1)S(1)}, u32[]{:S(2)}, u32[]{:S(2)}) collective-permute-start(bf16[4,1,1,32,2048]{4,3,2,1,0:T(8,128)(2,1)S(1)} %constant_dynamic-slice_fusion.13), channel_id=1, source_target_pairs={{0,8},{4,12},{8,0},{12,4},{16,24},{20,28},{24,16},{28,20},{1,9},{5... | collective-permute-start | bytes 1572872 | tf_op jit(solution)/shard_map/ppermute | solution.py:42
  521.3 26.3 %collective-permute-start.53 = (bf16[32,5376]{1,0:T(8,128)(2,1)S(1)}, bf16[32,5376]{1,0:T(8,128)(2,1)S(1)}, u32[]{:S(2)}, u32[]{:S(2)}) collective-permute-start(bf16[32,5376]{1,0:T(8,128)(2,1)S(1)} %get-tuple-element.92), channel_id=1, source_target_pairs={{0,2},{1,3},{2,0},{3,1},{4,6},{5,7},{6,4},{7,5},{8,10},{9,11},{10,... | collective-permute-start | bytes 1032200 | tf_op jit(solution)/shard_map/ppermute | solution.py:47
  525.6 22.0 %collective-permute-start.54 = (bf16[32,5376]{1,0:T(8,128)(2,1)S(1)}, bf16[32,5376]{1,0:T(8,128)(2,1)S(1)}, u32[]{:S(2)}, u32[]{:S(2)}) collective-permute-start(bf16[32,5376]{1,0:T(8,128)(2,1)S(1)} %get-tuple-element.93), channel_id=1, source_target_pairs={{0,3},{1,0},{2,1},{3,2},{4,7},{5,4},{6,5},{7,6},{8,11},{9,8},{10,9... | collective-permute-start | bytes 1032200 | tf_op jit(solution)/shard_map/ppermute | solution.py:47
  526.7 24.4 %collective-permute-start.34 = (bf16[4,1,1,32,2048]{4,3,0,2,1:T(8,128)(2,1)S(1)}, bf16[4,1,1,32,2048]{4,3,0,2,1:T(8,128)(2,1)S(1)}, u32[]{:S(2)}, u32[]{:S(2)}) collective-permute-start(bf16[4,1,1,32,2048]{4,3,0,2,1:T(8,128)(2,1)S(1)} %constant_dynamic-slice_fusion.15), channel_id=1, source_target_pairs={{0,16},{4,20},{8,24},{12,28},{16,0},{20,4},{24,8},{28,12},{1,17},{... | collective-permute-start | bytes 1572872 | tf_op jit(solution)/shard_map/ppermute | solution.py:42
  559.4 16.3 %collective-permute-start.39 = (bf16[32,4096]{1,0:T(8,128)(2,1)S(1)}, bf16[32,4096]{1,0:T(8,128)(2,1)S(1)}, u32[]{:S(2)}, u32[]{:S(2)}) collective-permute-start(bf16[32,4096]{1,0:T(8,128)(2,1)S(1)} %get-tuple-element.112), channel_id=1, source_target_pairs={{0,3},{1,0},{2,1},{3,2},{4,7},{5,4},{6,5},{7,6},{8,11},{9,8},{10,9... | collective-permute-start | bytes 786440 | tf_op jit(solution)/shard_map/ppermute | solution.py:47
  561.8 23.2 %collective-permute-start.59 = (bf16[1,2,1,32,2688]{4,3,2,1,0:T(8,128)(2,1)S(1)}, bf16[1,2,1,32,2688]{4,3,2,1,0:T(8,128)(2,1)S(1)}, u32[]{:S(2)}, u32[]{:S(2)}) collective-permute-start(bf16[1,2,1,32,2688]{4,3,2,1,0:T(8,128)(2,1)S(1)} %pad_maximum_fusion.24), channel_id=1, source_target_pairs={{0,8},{4,12},{8,0},{12,4},{16,24},{20,28},{24,16},{28,20},{1,9},{5... | collective-permute-start | bytes 1032200 | tf_op jit(solution)/shard_map/ppermute | solution.py:42
  (90 other events, 684.2 us)

commit v2 on v1

v2 whole, which is shorter than its diff:
```python
import functools

import jax
import jax.numpy as jnp
from jax import lax
from jax.experimental import pallas as pl
from jax.experimental.pallas import tpu as pltpu
from jax.sharding import PartitionSpec as P

HEAD_DIM = 64
WIN = 64
BLOCK_Q = 128
LANES = 128

epsilon = 1e-05
root_half = 0.7071067811865476
inv_root_two_pi = 0.3989422804014327
f32 = jnp.float32
bf16 = jnp.bfloat16
VMEM_LIMIT = 48 * 1024 * 1024


def after(value, *before):
    return lax.optimization_barrier((value, before))[0]


def bit_count():
    return lax.axis_size("rep").bit_length() - 1


def bit_value(bit):
    return (lax.axis_index("rep") >> bit) & 1


def link_count():
    return bit_count() - 1


def link_axis(bit):
    return bit_count() - 1 - bit


def flip(value, bit):
    size = lax.axis_size("rep")
    return lax.ppermute(value, "rep", [(i, i ^ (1 << bit)) for i in range(size)])


def turn(value, steps):
    size = lax.axis_size("fsdp")
    return lax.ppermute(value, "fsdp", [(i, (i + steps) % size) for i in range(size)])


def link_orders():
    bits = list(range(1, bit_count()))
    return list(zip(bits, bits[::-1]))


def in_order(mine, got, bit, axis):
    first = bit_value(bit) == 0
    return jnp.concatenate([jnp.where(first, mine, got), jnp.where(first, got, mine)], axis=axis)


def widen(states, bits, lead):
    return [
        in_order(state, flip(state, bit), bit, lead + link_axis(bit)) for state, bit in zip(states, bits)
    ]


def row_piece(shards):
    width = sum(shard.shape[1] for shard in shards)
    links = 1 << link_count()
    core, link = bit_value(0), lax.axis_index("rep") >> 1
    views = [shard.reshape(2, 2, links, -1, shard.shape[1]) for shard in shards]
    rows = views[0].shape[3]
    pieces = [
        lax.dynamic_slice(view, (core, 0, link, 0, 0), (1, 2, 1, rows, view.shape[4])) for view in views
    ]
    return jnp.concatenate(pieces, axis=-1).reshape(2, rows, width)


def row_states(came):
    ones = (1,) * link_count()
    return [
        jnp.stack([piece[part] for piece in came]).reshape((len(came),) + ones + came[0].shape[1:])
        for part in range(2)
    ]


def row_parts(states):
    mine = [state.reshape(state.shape[0], -1, state.shape[-1]) for state in states]
    return mine + [flip(state, 0) for state in mine]


def half_rows(rows):
    return -(-rows // 2 // 16) * 16


def column_piece(shard):
    columns = shard.shape[1] // lax.axis_size("rep")
    place = (bit_value(0) << link_count()) + (lax.axis_index("rep") >> 1)
    return lax.dynamic_slice_in_dim(shard, place * columns, columns, 1)


def column_states(came):
    cut = half_rows(came[0].shape[0])
    ones = (1,) * link_count()
    stacked = jnp.stack(came)
    return [
        part.reshape(part.shape[:1] + ones + part.shape[1:]) for part in (stacked[:, :cut], stacked[:, cut:])
    ]


def column_parts(states):
    mine = [state.reshape((state.shape[0], -1) + state.shape[-2:]) for state in states]
    return mine + [flip(state, 0) for state in mine]


def whole_columns(shard, parts, pad_rows):
    size = lax.axis_size("fsdp")
    me = lax.axis_index("fsdp")
    rows, width = shard.shape
    mine, got = [jnp.concatenate(pair, axis=2) for pair in (parts[:2], parts[2:])]
    joined = in_order(mine, got, 0, 1)
    joined = jnp.transpose(joined, (0, 2, 1, 3)).reshape(size - 1, rows, width)
    whole = jnp.zeros((size * rows + pad_rows, width), shard.dtype)
    whole = lax.dynamic_update_slice(whole, shard, (me * rows, 0))
    for steps in range(1, size):
        source = lax.rem(me - steps + size, size)
        whole = lax.dynamic_update_slice(whole, joined[steps - 1], (source * rows, 0))
    return whole


def turned_before(piece):
    return [turn(piece, steps) for steps in range(1, lax.axis_size("fsdp"))]


def tokens_dot(left, right):
    return lax.dot_general(left, right, (((0,), (0,)), ((), ())), preferred_element_type=f32)


def half_of(split, mine):
    index = bit_value(0) if mine else 1 - bit_value(0)
    return lax.dynamic_index_in_dim(split, index, 0, False)


def fold(blocks, lead, bit):
    axis = lead + link_axis(bit)
    mine = bit_value(bit)
    give = [lax.dynamic_slice_in_dim(block, 1 - mine, 1, axis) for block in blocks]
    got = flip(give[0] if len(give) == 1 else jnp.concatenate(give, axis=-1), bit)
    results, start = [], 0
    for block in blocks:
        keep = lax.dynamic_slice_in_dim(block, mine, 1, axis)
        width = block.shape[-1]
        add = lax.slice_in_dim(got, start, start + width, axis=got.ndim - 1)
        results.append((keep.astype(f32) + add.astype(f32)).astype(bf16))
        start += width
    return results


def scattered(state):
    flat = lax.psum_scatter(state.reshape(-1, state.shape[-1]), "fsdp", scatter_dimension=0, tiled=True)
    return flat.reshape(state.shape[1:])


def to_owner(state):
    size = lax.axis_size("fsdp")
    me = lax.axis_index("fsdp")
    came = [
        turn(lax.dynamic_index_in_dim(state, lax.rem(me + steps, size), 0, False), steps)
        for steps in range(1, size)
    ]
    total = lax.dynamic_index_in_dim(state, me, 0, False).astype(f32)
    for part in came:
        total = total + part.astype(f32)
    return total.astype(bf16)


def row_blocks(states):
    size = lax.axis_size("fsdp")
    views = [state.reshape((size, 2) + (2,) * link_count() + (-1, state.shape[1])) for state in states]
    return [[view[:, part] for view in views] for part in range(2)]


def neighbours(up, down):
    size = lax.axis_size("fsdp")
    forward = [(i, i + 1) for i in range(size - 1)]
    backward = [(i + 1, i) for i in range(size - 1)]
    return lax.ppermute(up, "fsdp", backward), lax.ppermute(down, "fsdp", forward)


def params(*semantics):
    return pltpu.CompilerParams(
        dimension_semantics=semantics, vmem_limit_bytes=VMEM_LIMIT
    )


def cost(flops, nbytes):
    return pl.CostEstimate(flops=int(flops), bytes_accessed=int(nbytes), transcendentals=0)


def dot_nn(left, right):
    return jnp.dot(left, right, preferred_element_type=f32)


def dot_nt(left, right):
    return lax.dot_general(left, right, (((1,), (1,)), ((), ())), preferred_element_type=f32)


def normalized(values):
    centred = values - jnp.mean(values, axis=-1, keepdims=True)
    inverse = lax.rsqrt(jnp.mean(centred * centred, axis=-1, keepdims=True) + epsilon)
    return centred * inverse, inverse


def norm_back(grad_out, gain, scaled, inverse):
    grad_scaled = grad_out * gain
    return inverse * (
        grad_scaled
        - jnp.mean(grad_scaled, axis=-1, keepdims=True)
        - scaled * jnp.mean(grad_scaled * scaled, axis=-1, keepdims=True)
    )


def swapped_halves(values):
    width = values.shape[-1]
    lane = lax.broadcasted_iota(jnp.int32, values.shape, values.ndim - 1)
    ahead = pltpu.roll(values, width - HEAD_DIM // 2, values.ndim - 1)
    behind = pltpu.roll(values, HEAD_DIM // 2, values.ndim - 1)
    return jnp.where(lane % HEAD_DIM < HEAD_DIM // 2, ahead, behind)


def assemble(meta_ref, whole_ref, own_ref, part_refs):
    rows = own_ref.shape[0]
    count, quarter = part_refs[0].shape[:2]
    size = count + 1
    me, core = meta_ref[1], meta_ref[2]
    whole_ref[pl.ds(pl.multiple_of(me * rows, quarter), rows), :] = own_ref[...]
    for steps in range(1, size):
        base = lax.rem(me - steps + size, size) * rows
        for number, part_ref in enumerate(part_refs):
            half = core if number < 2 else 1 - core
            start = base + half * (rows // 2) + (number % 2) * quarter
            whole_ref[pl.ds(pl.multiple_of(start, quarter), quarter), :] = part_ref[steps - 1]


def split_columns(values, split_ref, rows, size):
    half = values.shape[1] // size // 2
    for place in range(size):
        for core in range(2):
            start = (2 * place + core) * half
            split_ref[core, rows, place * half : (place + 1) * half] = values[:, start : start + half]


def joined_columns(split_ref, rows, size):
    half = split_ref.shape[2] // size
    return jnp.concatenate(
        [
            split_ref[core, rows, place * half : (place + 1) * half]
            for place in range(size)
            for core in range(2)
        ],
        axis=1,
    )


def part_specs(parts, block, place):
    count, quarter, _ = parts[0].shape
    return [pl.BlockSpec((count, quarter, block), lambda i: (0, 0, place(i)))] * 4


def qkv_kernel(
    meta_ref, x_ref, own_ref, p0, p1, p2, p3, gain_ref, g0, g1, g2, g3, cos_ref, sin_ref,
    split_ref, out_ref, gains_ref, whole_ref, normed_ref, column_ref, *, rope_steps, size,
):
    step = pl.program_id(0)

    @pl.when(step == 0)
    def _():
        assemble(meta_ref, column_ref, gain_ref, (g0, g1, g2, g3))
        row = lax.broadcasted_iota(jnp.int32, gains_ref.shape[:1] + (LANES,), 0)
        lane = lax.broadcasted_iota(jnp.int32, gains_ref.shape[:1] + (LANES,), 1)
        gains_ref[...] = dot_nt((row == lane).astype(f32).astype(bf16), column_ref[...])
        for top in range(0, x_ref.shape[0], 128):
            rows = slice(top, top + 128)
            scaled, _inverse = normalized(x_ref[rows, :].astype(f32))
            normed = (scaled * gains_ref[0:1, :]).astype(bf16)
            normed_ref[rows, :] = normed
            split_columns(normed, split_ref, rows, size)

    assemble(meta_ref, whole_ref, own_ref, (p0, p1, p2, p3))
    product = dot_nn(normed_ref[...], whole_ref[...])

    @pl.when(step >= rope_steps)
    def _():
        out_ref[0] = product.astype(bf16)

    @pl.when(step < rope_steps)
    def _():
        seq_rows = cos_ref.shape[0]
        cosine, sine = cos_ref[...], sin_ref[...]
        for top in range(0, product.shape[0], seq_rows):
            for lane in range(0, product.shape[1], LANES):
                tile = product[top : top + seq_rows, lane : lane + LANES]
                out_ref[0, top : top + seq_rows, lane : lane + LANES] = (
                    tile * cosine + swapped_halves(tile) * sine
                ).astype(bf16)


SMEM_SPEC = pl.BlockSpec(memory_space=pltpu.SMEM)


def fixed(*shape):
    return pl.BlockSpec(shape, lambda i: (0,) * len(shape))


def qkv_call(meta, x, own, parts, own_gains, cosine, sine):
    rows, width = x.shape
    slab = own.shape[0]
    size = width // slab
    block = 512
    per_plane = width // block
    return pl.pallas_call(
        functools.partial(qkv_kernel, rope_steps=2 * per_plane, size=size),
        grid=(3 * per_plane,),
        in_specs=[SMEM_SPEC, fixed(rows, width), pl.BlockSpec((slab, block), lambda i: (0, i))]
        + part_specs(parts, block, lambda i: i)
        + [fixed(slab, LANES)]
        + part_specs(parts, LANES, lambda i: 3 * width // LANES)
        + [fixed(*cosine.shape), fixed(*sine.shape)],
        out_specs=[
            fixed(2, rows, width // 2),
            pl.BlockSpec((1, rows, block), lambda i: (i // per_plane, 0, i % per_plane)),
            fixed(8, width),
        ],
        out_shape=[
            jax.ShapeDtypeStruct((2, rows, width // 2), bf16),
            jax.ShapeDtypeStruct((3, rows, width), bf16),
            jax.ShapeDtypeStruct((8, width), f32),
        ],
        scratch_shapes=[
            pltpu.VMEM((width, block), bf16),
            pltpu.VMEM((rows, width), bf16),
            pltpu.VMEM((width, LANES), bf16),
        ],
        compiler_params=params("arbitrary"),
        cost_estimate=cost(6 * rows * width * width, 6 * width * width + 10 * rows * width),
        name="qkv",
    )(meta, x, own, *parts, own_gains, *parts, cosine, sine)


def head_masks():
    lane = lax.broadcasted_iota(jnp.int32, (1, LANES), 1)
    first = lane < HEAD_DIM
    return first, first.astype(f32).astype(bf16), (~first).astype(f32).astype(bf16)


def two_heads(tile, low_mask, high_mask):
    return jnp.concatenate([tile * low_mask, tile * high_mask], axis=0)


def score_bias(first_row, length):
    shape = (BLOCK_Q, BLOCK_Q + 2 * WIN)
    query = first_row + lax.broadcasted_iota(jnp.int32, shape, 0)
    key = first_row - WIN + lax.broadcasted_iota(jnp.int32, shape, 1)
    near = jnp.abs(query - key) <= WIN
    live = (key >= 0) & (key < length)
    bias = jnp.where(near & (live | (query == key)), 0.0, -1e30).astype(f32)
    return jnp.concatenate([bias, bias], axis=0)


def softmax_of(queries, keys, bias):
    scores = dot_nt(queries, keys) * (HEAD_DIM**-0.5) + bias
    exponent = jnp.exp(scores - jnp.max(scores, axis=-1, keepdims=True))
    return exponent / jnp.sum(exponent, axis=-1, keepdims=True)


def attend_kernel(
    meta_ref, q_ref, k_ref, v_ref, k_up_ref, v_up_ref, k_down_ref, v_down_ref, out_ref, probs_ref
):
    length = meta_ref[3 + pl.program_id(0)]
    rows, width = q_ref.shape[1:]
    first_head, low_mask, high_mask = head_masks()
    for lane in range(0, width, LANES):
        lanes = slice(lane, lane + LANES)
        keys = jnp.concatenate([k_up_ref[0, :, lanes], k_ref[0, :, lanes], k_down_ref[0, :, lanes]], 0)
        values = jnp.concatenate([v_up_ref[0, :, lanes], v_ref[0, :, lanes], v_down_ref[0, :, lanes]], 0)
        for top in range(0, rows, BLOCK_Q):
            bias = score_bias(meta_ref[0] + top, length)
            span = slice(top, top + BLOCK_Q + 2 * WIN)
            queries = two_heads(q_ref[0, top : top + BLOCK_Q, lanes], low_mask, high_mask)
            probs = softmax_of(queries, keys[span], bias).astype(bf16)
            probs_ref[0, lane // LANES, top // BLOCK_Q] = probs
            result = dot_nn(probs, values[span])
            out_ref[top : top + BLOCK_Q, lanes] = jnp.where(
                first_head, result[:BLOCK_Q], result[BLOCK_Q:]
            ).astype(bf16)


def attention_specs(seqs, seq_rows, width, block):
    own = lambda plane: pl.BlockSpec((1, seq_rows, block), lambda s, h: (plane, s, h))
    rim = lambda plane: pl.BlockSpec((1, WIN, block), lambda s, h: (plane, s, h))
    flat = pl.BlockSpec((seq_rows, block), lambda s, h: (s, h))
    inner = (seq_rows // BLOCK_Q, 2 * BLOCK_Q, BLOCK_Q + 2 * WIN)
    probs = pl.BlockSpec((1, block // LANES) + inner, lambda s, h: (s, h, 0, 0, 0))
    probs_shape = jax.ShapeDtypeStruct((seqs, width // LANES) + inner, bf16)
    return own, rim, flat, probs, probs_shape


def attend_call(meta, qkv, rim_up, rim_down, seqs):
    _, rows, width = qkv.shape
    seq_rows = rows // seqs
    block = 256
    own, rim, flat, probs, probs_shape = attention_specs(seqs, seq_rows, width, block)
    return pl.pallas_call(
        attend_kernel,
        grid=(seqs, width // block),
        in_specs=[SMEM_SPEC, own(0), own(1), own(2), rim(0), rim(1), rim(0), rim(1)],
        out_specs=[flat, probs],
        out_shape=[jax.ShapeDtypeStruct((rows, width), bf16), probs_shape],
        compiler_params=params("arbitrary", "arbitrary"),
        cost_estimate=cost(8 * rows * width * (BLOCK_Q + 2 * WIN), 10 * rows * width),
        name="attend",
    )(meta, qkv, qkv, qkv, rim_up, rim_up, rim_down, rim_down)


def attend_back_kernel(
    q_ref,
    k_ref,
    v_ref,
    k_up_ref,
    v_up_ref,
    k_down_ref,
    v_down_ref,
    probs_ref,
    go_ref,
    cos_ref,
    sin_ref,
    gq_ref,
    gk_ref,
    gv_ref,
    up_ref,
    down_ref,
    gk_acc,
    gv_acc,
):
    rows, width = q_ref.shape[1:]
    scale = HEAD_DIM**-0.5
    first_head, low_mask, high_mask = head_masks()

    def turned_back(tile, span):
        return tile * cos_ref[span, :] - swapped_halves(tile) * sin_ref[span, :]

    for lane in range(0, width, LANES):
        lanes = slice(lane, lane + LANES)
        keys = jnp.concatenate([k_up_ref[0, :, lanes], k_ref[0, :, lanes], k_down_ref[0, :, lanes]], 0)
        values = jnp.concatenate([v_up_ref[0, :, lanes], v_ref[0, :, lanes], v_down_ref[0, :, lanes]], 0)
        gk_acc[...] = jnp.zeros_like(gk_acc)
        gv_acc[...] = jnp.zeros_like(gv_acc)
        for top in range(0, rows, BLOCK_Q):
            span = slice(top, top + BLOCK_Q + 2 * WIN)
            queries = two_heads(q_ref[0, top : top + BLOCK_Q, lanes], low_mask, high_mask)
            grads = two_heads(go_ref[top : top + BLOCK_Q, lanes], low_mask, high_mask)
            probs_low = probs_ref[0, lane // LANES, top // BLOCK_Q]
            probs = probs_low.astype(f32)
            grad_probs = dot_nt(grads, values[span])
            delta = jnp.sum(probs * grad_probs, axis=-1, keepdims=True)
            grad_scores = (probs * (grad_probs - delta)).astype(bf16)
            result = dot_nn(grad_scores, keys[span])
            result = jnp.where(first_head, result[:BLOCK_Q], result[BLOCK_Q:]) * scale
            own = slice(WIN + top, WIN + top + BLOCK_Q)
            gq_ref[top : top + BLOCK_Q, lanes] = turned_back(result, own).astype(bf16)
            gk_acc[span, :] += tokens_dot(grad_scores, queries)
            gv_acc[span, :] += tokens_dot(probs_low, grads)
        grad_keys = turned_back(gk_acc[...] * scale, slice(None))
        grad_values = gv_acc[...]
        up_ref[0, :, lanes] = grad_keys[:WIN].astype(bf16)
        up_ref[1, :, lanes] = grad_values[:WIN].astype(bf16)
        down_ref[0, :, lanes] = grad_keys[WIN + rows :].astype(bf16)
        down_ref[1, :, lanes] = grad_values[WIN + rows :].astype(bf16)
        gk_ref[:, lanes] = grad_keys[WIN : WIN + rows]
        gv_ref[:, lanes] = grad_values[WIN : WIN + rows]


def attend_back_call(qkv, rim_up, rim_down, saved, grad_out, cosine, sine, seqs):
    _, rows, width = qkv.shape
    seq_rows = rows // seqs
    block = 256
    own, rim, flat, probs, probs_shape = attention_specs(seqs, seq_rows, width, block)
    table = pl.BlockSpec(cosine.shape, lambda s, h: (0, 0))
    edge = pl.BlockSpec((2, WIN, block), lambda s, h: (0, s, h))
    edge_shape = jax.ShapeDtypeStruct((2, seqs * WIN, width), bf16)
    return pl.pallas_call(
        attend_back_kernel,
        grid=(seqs, width // block),
        in_specs=[
            own(0), own(1), own(2), rim(0), rim(1), rim(0), rim(1),
            probs, flat, table, table,
        ],
        out_specs=[flat, flat, flat, edge, edge],
        out_shape=[
            jax.ShapeDtypeStruct((rows, width), bf16),
            jax.ShapeDtypeStruct((rows, width), f32),
            jax.ShapeDtypeStruct((rows, width), f32),
            edge_shape,
            edge_shape,
        ],
        scratch_shapes=[
            pltpu.VMEM((seq_rows + 2 * WIN, LANES), f32),
            pltpu.VMEM((seq_rows + 2 * WIN, LANES), f32),
        ],
        compiler_params=params("arbitrary", "arbitrary"),
        cost_estimate=cost(20 * rows * width * (BLOCK_Q + 2 * WIN), 20 * rows * width),
        name="attend_back",
    )(qkv, qkv, qkv, rim_up, rim_up, rim_down, rim_down, saved, grad_out, cosine, sine)


def out_kernel(
    meta_ref, o_ref, own_ref, p0, p1, p2, p3, x_ref, valid_ref, gains_ref,
    middle_ref, n_split_ref, o_split_ref, whole_ref, *, size,
):
    @pl.when(pl.program_id(0) == 0)
    def _():
        assemble(meta_ref, whole_ref, own_ref, (p0, p1, p2, p3))

    values = o_ref[...]
    split_columns(values, o_split_ref, slice(None), size)
    middle = x_ref[...].astype(f32) + valid_ref[...] * dot_nn(values, whole_ref[...])
    middle_ref[...] = middle
    scaled, _inverse = normalized(middle)
    split_columns((scaled * gains_ref[1:2, :]).astype(bf16), n_split_ref, slice(None), size)


def out_call(meta, attended, own, parts, x, valid, gains):
    rows, width = x.shape
    slab = own.shape[0]
    size = width // slab
    block = 128
    tile = pl.BlockSpec((block, width), lambda i: (i, 0))
    split = pl.BlockSpec((2, block, width // 2), lambda i: (0, i, 0))
    split_shape = jax.ShapeDtypeStruct((2, rows, width // 2), bf16)
    return pl.pallas_call(
        functools.partial(out_kernel, size=size),
        grid=(rows // block,),
        in_specs=[SMEM_SPEC, tile, fixed(slab, width)]
        + part_specs(parts, width, lambda i: 0)
        + [tile, pl.BlockSpec((block, 1), lambda i: (i, 0)), fixed(8, width)],
        out_specs=[tile, split, split],
        out_shape=[jax.ShapeDtypeStruct((rows, width), f32), split_shape, split_shape],
        scratch_shapes=[pltpu.VMEM((width, width), bf16)],
        compiler_params=params("arbitrary"),
        cost_estimate=cost(2 * rows * width * width, 2 * width * width + 12 * rows * width),
        name="out_norm",
    )(meta, attended, own, *parts, x, valid, gains)


def gate_kernel(
    meta_ref, n_ref, own1_ref, p0, p1, p2, p3, own2_ref, q0, q1, q2, q3,
    mixed_ref, slope_ref, act_ref, normed_ref, first_ref, second_ref, *, size,
):
    @pl.when(pl.program_id(0) == 0)
    def _():
        for top in range(0, normed_ref.shape[0], 128):
            rows = slice(top, top + 128)
            normed_ref[rows, :] = joined_columns(n_ref, rows, size)

    assemble(meta_ref, first_ref, own1_ref, (p0, p1, p2, p3))
    assemble(meta_ref, second_ref, own2_ref, (q0, q1, q2, q3))
    gate_in = dot_nn(normed_ref[...], first_ref[...])
    gate_up = dot_nn(normed_ref[...], second_ref[...])
    normal_cdf = 0.5 * (1.0 + lax.erf(gate_in * root_half))
    density = jnp.exp(-0.5 * gate_in * gate_in) * inv_root_two_pi
    activated = gate_in * normal_cdf
    mixed_ref[...] = (activated * gate_up).astype(bf16)
    slope_ref[...] = (gate_up * (normal_cdf + gate_in * density)).astype(bf16)
    act_ref[...] = activated.astype(bf16)


def gate_call(meta, normed, own1, parts1, own2, parts2, block):
    _, rows, half = normed.shape
    width = 2 * half
    slab, hidden = own1.shape
    size = width // slab
    tile = pl.BlockSpec((rows, block), lambda i: (0, i))
    own = pl.BlockSpec((slab, block), lambda i: (0, i))
    shape = jax.ShapeDtypeStruct((rows, hidden), bf16)
    return pl.pallas_call(
        functools.partial(gate_kernel, size=size),
        grid=(hidden // block,),
        in_specs=[SMEM_SPEC, fixed(2, rows, half), own]
        + part_specs(parts1, block, lambda i: i)
        + [own]
        + part_specs(parts2, block, lambda i: i),
        out_specs=[tile, tile, tile],
        out_shape=[shape, shape, shape],
        scratch_shapes=[
            pltpu.VMEM((rows, width), bf16),
            pltpu.VMEM((width, block), bf16),
            pltpu.VMEM((width, block), bf16),
        ],
        compiler_params=params("arbitrary"),
        cost_estimate=cost(4 * rows * width * hidden, 4 * width * hidden + 6 * rows * hidden),
        name="gate",
    )(meta, normed, own1, *parts1, own2, *parts2)


def gate_back_kernel(
    meta_ref, g_ref, own_ref, p0, p1, p2, p3, slope_ref, act_ref, out_ref, whole_ref, *, block
):
    step = pl.program_id(0)

    @pl.when(step == 0)
    def _():
        rows = own_ref.shape[0]
        count, links, cut, columns = p0.shape
        size = count + 1
        me, core = meta_ref[1], meta_ref[2]
        whole_ref[size * rows :, :] = jnp.zeros_like(whole_ref[size * rows :, :])
        whole_ref[pl.ds(pl.multiple_of(me * rows, 16), rows), :] = own_ref[...]

        def put(halves):
            for steps in range(1, size):
                base = lax.rem(me - steps + size, size) * rows
                for half, parts in enumerate(halves):
                    for part, start in zip(parts, (0, cut)):
                        target = pl.ds(pl.multiple_of(base + start, 16), part.shape[2])
                        for link in range(links):
                            lane = (half * links + link) * columns
                            whole_ref[target, lane : lane + columns] = part[steps - 1, link]

        @pl.when(core == 0)
        def _():
            put(((p0, p1), (p2, p3)))

        @pl.when(core == 1)
        def _():
            put(((p2, p3), (p0, p1)))

    weight = whole_ref[pl.ds(pl.multiple_of(step * block, block), block), :]
    grad_mixed = dot_nt(g_ref[...], weight)
    out_ref[0] = (grad_mixed * slope_ref[...].astype(f32)).astype(bf16)
    out_ref[1] = (grad_mixed * act_ref[...].astype(f32)).astype(bf16)


def gate_back_plain_kernel(g_ref, w_ref, slope_ref, act_ref, out_ref):
    grad_mixed = dot_nt(g_ref[...], w_ref[...])
    out_ref[0] = (grad_mixed * slope_ref[...].astype(f32)).astype(bf16)
    out_ref[1] = (grad_mixed * act_ref[...].astype(f32)).astype(bf16)


def gate_back_call(meta, grad_result, own, parts, slope, act, block):
    rows, width = grad_result.shape
    hidden = slope.shape[1]
    tile = pl.BlockSpec((rows, block), lambda i: (0, i))
    out_spec = pl.BlockSpec((2, rows, block), lambda i: (0, 0, i))
    out_shape = jax.ShapeDtypeStruct((2, rows, hidden), bf16)
    settings = dict(
        grid=(hidden // block,),
        compiler_params=params("arbitrary"),
        cost_estimate=cost(2 * rows * width * hidden, 4 * width * hidden + 8 * rows * hidden),
        name="gate_back",
    )
    if own.shape[0] % 16:
        whole = whole_columns(own, parts, hidden - own.shape[0] * (parts[0].shape[0] + 1))
        out = pl.pallas_call(
            gate_back_plain_kernel,
            in_specs=[fixed(rows, width), pl.BlockSpec((block, width), lambda i: (i, 0)), tile, tile],
            out_specs=out_spec,
            out_shape=out_shape,
            **settings,
        )(grad_result, whole, slope, act)
        return out, whole
    return pl.pallas_call(
        functools.partial(gate_back_kernel, block=block),
        in_specs=[SMEM_SPEC, fixed(rows, width), fixed(*own.shape)]
        + [fixed(*part.shape) for part in parts]
        + [tile, tile],
        out_specs=[out_spec, fixed(hidden, width)],
        out_shape=[out_shape, jax.ShapeDtypeStruct((hidden, width), bf16)],
        **settings,
    )(meta, grad_result, own, *parts, slope, act)


def down_kernel(meta_ref, m_ref, g_ref, *rest, mine, size, links):
    add_ref = rest[0] if mine else None
    out_ref, sums_ref = rest[-2:]
    step = pl.program_id(0)
    block, half = m_ref.shape[1], sums_ref.shape[1]
    which = meta_ref[2] if mine else 1 - meta_ref[2]
    right = g_ref[:, pl.ds(pl.multiple_of(which * half, half), half)]
    sums_ref[pl.ds(pl.multiple_of(step * block, block), block), :] = tokens_dot(m_ref[...], right)

    @pl.when(step == pl.num_programs(0) - 1)
    def _():
        rows, columns = out_ref.shape[2:]
        for place in range(size):
            for link in range(links):
                value = sums_ref[place * rows : (place + 1) * rows, link * columns : (link + 1) * columns]
                if mine:
                    value = value + add_ref[place, link].astype(f32)
                out_ref[place, link] = value.astype(bf16)


def down_call(meta, mixed, grad_result, size, hidden, block, add=None):
    rows, hidden_pad = mixed.shape
    width = grad_result.shape[1]
    links = 1 << link_count()
    shape = (size, links, hidden // size, width // 2 // links)
    extra = [] if add is None else [add]
    return pl.pallas_call(
        functools.partial(down_kernel, mine=add is not None, size=size, links=links),
        grid=(hidden_pad // block,),
        in_specs=[SMEM_SPEC, pl.BlockSpec((rows, block), lambda i: (0, i)), fixed(rows, width)]
        + [fixed(*shape) for _ in extra],
        out_specs=fixed(*shape),
        out_shape=jax.ShapeDtypeStruct(shape, bf16),
        scratch_shapes=[pltpu.VMEM((hidden_pad, width // 2), f32)],
        compiler_params=params("arbitrary"),
        cost_estimate=cost(rows * width * hidden, width * hidden + 2 * rows * (hidden + width)),
        name="down_sum",
    )(meta, mixed, grad_result, *extra)


def middle_back_kernel(
    meta_ref, gu_ref, own1_ref, p0, p1, p2, p3, own2_ref, q0, q1, q2, q3, out_own_ref, r0, r1, r2, r3,
    middle_ref, upstream_ref, valid_ref, gains_ref, grad_ref, branch_ref, att_ref,
    acc, first_ref, second_ref, out_ref,
):
    step = pl.program_id(0)
    assemble(meta_ref, first_ref, own1_ref, (p0, p1, p2, p3))
    assemble(meta_ref, second_ref, own2_ref, (q0, q1, q2, q3))
    total = dot_nt(gu_ref[0], first_ref[...]) + dot_nt(gu_ref[1], second_ref[...])

    @pl.when(step == 0)
    def _():
        acc[...] = total
        assemble(meta_ref, out_ref, out_own_ref, (r0, r1, r2, r3))

    @pl.when(step > 0)
    def _():
        acc[...] += total

    @pl.when(step == pl.num_programs(0) - 1)
    def _():
        for top in range(0, acc.shape[0], 128):
            rows = slice(top, top + 128)
            scaled, inverse = normalized(middle_ref[rows, :])
            grad = upstream_ref[rows, :].astype(f32) + norm_back(
                acc[rows, :], gains_ref[1:2, :], scaled, inverse
            )
            grad_ref[rows, :] = grad
            branch = (grad * valid_ref[rows, :]).astype(bf16)
            branch_ref[rows, :] = branch
            att_ref[rows, :] = dot_nt(branch, out_ref[...]).astype(bf16)


def middle_back_call(
    meta, grad_hidden, own1, parts1, own2, parts2, out_own, out_parts, middle, upstream, valid, gains, block
):
    rows, width = middle.shape
    slab = own1.shape[0]
    hidden = grad_hidden.shape[2]
    whole = fixed(rows, width)
    own = pl.BlockSpec((slab, block), lambda i: (0, i))
    flat_low = jax.ShapeDtypeStruct((rows, width), bf16)
    return pl.pallas_call(
        middle_back_kernel,
        grid=(hidden // block,),
        in_specs=[SMEM_SPEC, pl.BlockSpec((2, rows, block), lambda i: (0, 0, i)), own]
        + part_specs(parts1, block, lambda i: i)
        + [own]
        + part_specs(parts2, block, lambda i: i)
        + [fixed(slab, width)]
        + part_specs(out_parts, width, lambda i: 0)
        + [whole, whole, fixed(rows, 1), fixed(8, width)],
        out_specs=[whole, whole, whole],
        out_shape=[jax.ShapeDtypeStruct((rows, width), f32), flat_low, flat_low],
        scratch_shapes=[
            pltpu.VMEM((rows, width), f32),
            pltpu.VMEM((width, block), bf16),
            pltpu.VMEM((width, block), bf16),
            pltpu.VMEM((width, width), bf16),
        ],
        compiler_params=params("arbitrary"),
        cost_estimate=cost(4 * rows * width * hidden, 4 * width * hidden + 4 * rows * hidden + 12 * rows * width),
        name="middle_back",
    )(meta, grad_hidden, own1, *parts1, own2, *parts2, out_own, *out_parts, middle, upstream, valid, gains)


def input_back_kernel(
    meta_ref, gqkv_ref, own_ref, p0, p1, p2, p3, x_ref, grad_ref, gains_ref, out_ref, acc, whole_ref
):
    step = pl.program_id(0)
    assemble(meta_ref, whole_ref, own_ref, (p0, p1, p2, p3))
    total = dot_nt(gqkv_ref[...], whole_ref[...])

    @pl.when(step == 0)
    def _():
        acc[...] = total

    @pl.when(step > 0)
    def _():
        acc[...] += total

    @pl.when(step == pl.num_programs(0) - 1)
    def _():
        for top in range(0, acc.shape[0], 128):
            rows = slice(top, top + 128)
            scaled, inverse = normalized(x_ref[rows, :].astype(f32))
            out_ref[rows, :] = (
                grad_ref[rows, :] + norm_back(acc[rows, :], gains_ref[0:1, :], scaled, inverse)
            ).astype(bf16)


def input_back_call(meta, grad_joint, own, parts, x, grad_middle, gains):
    rows, width = x.shape
    slab = own.shape[0]
    block = width
    whole = fixed(rows, width)
    return pl.pallas_call(
        input_back_kernel,
        grid=(3 * width // block,),
        in_specs=[
            SMEM_SPEC,
            pl.BlockSpec((rows, block), lambda i: (0, i)),
            pl.BlockSpec((slab, block), lambda i: (0, i)),
        ]
        + part_specs(parts, block, lambda i: i)
        + [whole, whole, fixed(8, width)],
        out_specs=whole,
        out_shape=jax.ShapeDtypeStruct((rows, width), bf16),
        scratch_shapes=[pltpu.VMEM((rows, width), f32), pltpu.VMEM((width, block), bf16)],
        compiler_params=params("arbitrary"),
        cost_estimate=cost(6 * rows * width * width, 6 * width * width + 14 * rows * width),
        name="input_back",
    )(meta, grad_joint, own, *parts, x, grad_middle, gains)


def rope_tables(positions):
    halfway = HEAD_DIM // 2
    frequency = 10000.0 ** (-(2.0 * jnp.arange(halfway, dtype=f32)) / HEAD_DIM)
    angles = positions.astype(f32)[:, None] * frequency[None, :]
    cosine, sine = jnp.cos(angles), jnp.sin(angles)
    return (
        jnp.concatenate([cosine] * (LANES // halfway), axis=1),
        jnp.concatenate([-sine, sine] * (LANES // HEAD_DIM), axis=1),
    )


def on_device(inputs, cotangent, lengths, norm_first, w_qkv, w_out, norm_second, w_in, w_down):
    seqs, shard_rows, width = inputs.shape
    rows = seqs * shard_rows
    size = lax.axis_size("fsdp")
    me = lax.axis_index("fsdp")
    hidden = w_in.shape[1] // 2
    hidden_pad = -(-hidden // 384) * 384
    pad = hidden_pad - hidden
    block = 896 if hidden_pad % 896 == 0 else 384
    steps = link_orders()

    gains = jnp.pad(jnp.stack([norm_first, norm_second], axis=1), ((0, 0), (0, LANES - 2)))
    came_one = turned_before(row_piece([w_qkv, gains]))
    own_in = [jnp.pad(w_in[:, half * hidden :][:, :hidden], ((0, 0), (0, pad))) for half in range(2)]
    piece_two = row_piece([own_in[0], w_out])
    piece_three = row_piece([own_in[1]])
    piece_four = column_piece(w_down)

    first_row = me * shard_rows
    query_pos = first_row + jnp.arange(shard_rows, dtype=jnp.int32)
    rim_pos = first_row - WIN + jnp.arange(shard_rows + 2 * WIN, dtype=jnp.int32)
    cosine, sine = rope_tables(rim_pos)
    valid = (query_pos[None, :] < lengths[:, None]).astype(f32).reshape(rows, 1)
    meta = jnp.concatenate([jnp.stack([first_row, me, bit_value(0)]).astype(jnp.int32), lengths.astype(jnp.int32)])
    x = inputs.reshape(rows, width)
    upstream = cotangent.reshape(rows, width)
    grad_result = (upstream.astype(f32) * valid).astype(bf16)

    came_one, piece_two, piece_three, piece_four, own_in, cosine, sine, grad_result = after(
        (came_one, piece_two, piece_three, piece_four, own_in, cosine, sine, grad_result)
    )
    came_two = turned_before(piece_two)
    one = row_states(came_one)
    for bits in steps:
        one = after(widen(one, bits, 1))
    one, came_two = after((one, came_two))
    parts_one = row_parts(one)
    two = widen(row_states(came_two), steps[0], 1)
    parts_one, piece_three = after((parts_one, piece_three))
    came_three = turned_before(piece_three)

    own_rows = slice(WIN, WIN + shard_rows)
    normed_first, qkv, gains_all = qkv_call(meta, x, w_qkv, parts_one, gains, cosine[own_rows], sine[own_rows])
    two, qkv = after((two, qkv))
    by_seq = qkv.reshape(3, seqs, shard_rows, width)[1:]
    edge = (2, seqs * WIN, width)
    edge_up, edge_down, came_three = after(
        (by_seq[:, :, :WIN].reshape(edge), by_seq[:, :, shard_rows - WIN :].reshape(edge), came_three)
    )
    rim_down, rim_up = neighbours(edge_up, edge_down)
    for bits in steps[1:]:
        two = widen(two, bits, 1)
    rim_down, rim_up, piece_four = after((rim_down, rim_up, piece_four))
    came_four = turned_before(piece_four)
    attended, saved = attend_call(meta, qkv, rim_up, rim_down, seqs)
    two, attended = after((two, attended))
    parts_two = after(row_parts(two))
    parts_in_one = [part[:, :, :hidden_pad] for part in parts_two]
    parts_out = [part[:, :, hidden_pad:] for part in parts_two]
    three = widen(row_states(after(came_three, parts_two)), steps[0], 1)
    middle, normed_second, attended_split = out_call(meta, attended, w_out, parts_out, x, valid, gains_all)
    three, middle, normed_second = after((three, middle, normed_second))
    for bits in steps[1:]:
        three = widen(three, bits, 1)
    three, came_four = after((three, came_four))
    parts_three = after(row_parts(three))
    four = widen(column_states(came_four), steps[0], 1)
    mixed, slope, act = gate_call(meta, normed_second, own_in[0], parts_in_one, own_in[1], parts_three, block)
    four, mixed = after((four, mixed))
    for bits in steps[1:]:
        four = widen(four, bits, 1)

    down_give = down_call(meta, mixed, grad_result, size, hidden, block)
    down_got = flip(down_give, 0)
    four, down_got = after((four, down_got))
    parts_four = column_parts(four)
    down = down_call(meta, mixed, grad_result, size, hidden, block, down_got)
    parts_four, down = after((parts_four, down))
    down = down.reshape((size,) + (2,) * link_count() + down.shape[2:])
    cut = half_rows(hidden // size)
    down = [[down[..., :cut, :]], [down[..., cut:, :]]]
    down = [fold(part, 1, bit) for part, bit in zip(down, steps[0])]
    grad_hidden, whole_down = gate_back_call(meta, grad_result, w_down, parts_four, slope, act, block)

    give_left = half_of(normed_second, False)
    in_give = [tokens_dot(give_left, grad_hidden[half]).astype(bf16) for half in range(2)]
    down, in_give, grad_hidden = after((down, in_give, grad_hidden))
    in_got = [flip(give, 0) for give in in_give]
    for bits in steps[1:]:
        down = [fold(part, 1, bit) for part, bit in zip(down, bits)]
    keep_left = half_of(normed_second, True)
    in_state = [
        (tokens_dot(keep_left, grad_hidden[half]) + in_got[half].astype(f32)).astype(bf16)
        for half in range(2)
    ]
    down, in_state, grad_hidden = after((down, in_state, grad_hidden))
    ins = [fold(part, 1, bit) for part, bit in zip(row_blocks(in_state), steps[0])]
    owned_down = scattered(
        jnp.concatenate([part[0].reshape((size,) + part[0].shape[-2:]) for part in down], axis=1)
    )
    grad_middle, grad_branch, grad_att = middle_back_call(
        meta, grad_hidden, own_in[0], parts_in_one, own_in[1], parts_three, w_out, parts_out,
        middle, upstream, valid, gains_all, block,
    )
    out_give = tokens_dot(half_of(attended_split, False), grad_branch).astype(bf16)
    out_got, grad_branch, grad_att = after((flip(out_give, 0), grad_branch, grad_att))
    out_state = (tokens_dot(half_of(attended_split, True), grad_branch) + out_got.astype(f32)).astype(bf16)
    grad_att, out_state, owned_down = after((grad_att, out_state, owned_down))
    all_down = lax.all_gather(owned_down, "rep", axis=0)
    grad_q, grad_k, grad_v, edge_up, edge_down = attend_back_call(
        qkv, rim_up, rim_down, saved, grad_att, cosine, sine, seqs
    )
    ins, edge_up, edge_down = after((ins, edge_up, edge_down))
    from_next, from_before = neighbours(edge_up, edge_down)
    for bits in steps[1:]:
        ins = [fold(part, 1, bit) for part, bit in zip(ins, bits)]

    def with_edges(own, plane):
        own = own.reshape(seqs, shard_rows, width)
        before = from_before[plane].reshape(seqs, WIN, width).astype(f32)
        later = from_next[plane].reshape(seqs, WIN, width).astype(f32)
        rest = ((0, 0), (0, shard_rows - WIN), (0, 0))
        own = own + jnp.pad(before, rest) + jnp.pad(later, (rest[0], rest[1][::-1], rest[2]))
        return own.reshape(rows, width).astype(bf16)

    grad_joint = jnp.concatenate([grad_q, with_edges(grad_k, 0), with_edges(grad_v, 1)], axis=1)
    give_left = half_of(normed_first, False)
    qkv_give = tokens_dot(give_left, grad_joint).astype(bf16)
    qkv_got, grad_last = after((flip(qkv_give, 0), grad_joint))
    keep_left = half_of(normed_first, True)
    qkv_state = (tokens_dot(keep_left, grad_last) + qkv_got.astype(f32)).astype(bf16)
    ins, out_state, qkv_state, grad_last, mixed = after((ins, out_state, qkv_state, grad_last, mixed))
    last = [fold(part, 1, bit) for part, bit in zip(row_blocks([qkv_state, out_state]), steps[0])]

    def slots(parts):
        return jnp.stack(
            [
                jnp.concatenate([piece.reshape(size, -1, piece.shape[-1]) for piece in part], axis=-1)
                for part in parts
            ],
            axis=1,
        )

    owned_in = scattered(slots(ins))
    grad_inputs = input_back_call(meta, grad_last, w_qkv, parts_one, x, grad_middle, gains_all)
    last, grad_inputs, mixed = after((last, grad_inputs, mixed))
    for bits in steps[1:]:
        last = [fold(part, 1, bit) for part, bit in zip(last, bits)]
    result = jnp.dot(mixed, whole_down, preferred_element_type=f32)
    output = (middle + valid * result).astype(bf16)
    last, output, owned_in, all_down = after((last, output, owned_in, all_down))
    owned_last = to_owner(slots(last))

    links = 1 << link_count()

    def spread(owned):
        ones = (1,) * link_count()
        states = [owned[part].reshape(ones + owned.shape[1:]) for part in range(2)]
        for bits in steps:
            states = widen(states, bits, 0)
        mine = jnp.stack([state.reshape((-1,) + owned.shape[1:]) for state in states])
        return in_order(mine[None], flip(mine, 0)[None], 0, 0).reshape(-1, owned.shape[-1])

    grad_down = all_down.reshape(links, 2, hidden // size, -1)
    grad_down = jnp.transpose(grad_down, (2, 1, 0, 3)).reshape(hidden // size, width).astype(f32)
    grad_mid = spread(owned_in)
    grad_in = jnp.concatenate(
        [grad_mid[:, :hidden], grad_mid[:, hidden_pad : hidden_pad + hidden]], axis=1
    ).astype(f32)
    grad_second = jnp.sum(grad_in * w_in.astype(f32), axis=1) / norm_second.astype(f32)
    owned_last, grad_in, grad_down, grad_second = after((owned_last, grad_in, grad_down, grad_second))
    grad_last = spread(owned_last)
    grad_qkv = grad_last[:, : 3 * width].astype(f32)
    grad_out = grad_last[:, 3 * width :].astype(f32)
    grad_first = jnp.sum(grad_qkv * w_qkv.astype(f32), axis=1) / norm_first.astype(f32)
    return (
        output.reshape(inputs.shape),
        grad_inputs.reshape(inputs.shape),
        grad_first,
        grad_qkv,
        grad_out,
        grad_second,
        grad_in,
        grad_down,
    )


def solution(mesh):
    in_specs = (
        P("rep", "fsdp", None),
        P("rep", "fsdp", None),
        P("rep"),
        P("fsdp"),
        P("fsdp", None),
        P("fsdp", None),
        P("fsdp"),
        P("fsdp", None),
        P("fsdp", None),
    )
    out_specs = (
        P("rep", "fsdp", None),
        P("rep", "fsdp", None),
        P("fsdp"),
        P("fsdp", None),
        P("fsdp", None),
        P("fsdp"),
        P("fsdp", None),
        P("fsdp", None),
    )
    return jax.shard_map(
        on_device, mesh=mesh, in_specs=in_specs, out_specs=out_specs, check_vma=False
    )
```

time: 616 us -> 504 us (0.82)
  local copies, waits for them, and re-layouts: 131 us -> 42.6 us
  starting transfers between devices: 116 us -> 89.8 us
  Pallas kernels: 89.1 us -> 106 us
  matrix products: 42.4 us -> 26.2 us
  between operations: 2.45 us -> 16.4 us
  other arithmetic: 49.3 us -> 41.1 us
    unnamed x136 -> x177, local copies, waits for them, and re-layouts: 39.9 us -> 11.5 us
    ppermute x18 -> x15, waiting for transfers between devices: 44.6 us -> 20.4 us  [turn(): lax.ppermute(value, 'fsdp', [(i, (i + steps) % size) for i in range(size)])]
    ppermute x18 -> x15, starting transfers between devices: 54.9 us -> 31.8 us  [turn(): lax.ppermute(value, 'fsdp', [(i, (i + steps) % size) for i in range(size)])]
    pallas_call x7 -> x9, Pallas kernels: 66.2 us -> 87.8 us  [the longest x1 17.3 us: middle_back_call(): pl.pallas_call(middle_back_kernel, grid=(hidden // block,), in_specs=[SME...]
    reshape x6 -> x2, local copies, waits for them, and re-layouts: 18.6 us -> 0.03 us  [the longest x1 0.02 us: column_states(): part.reshape(part.shape[:1] + ones + part.shape[1:])]
    dynamic_slice x17 -> x21, local copies, waits for them, and re-layouts: 23.2 us -> 6.98 us  [the longest x6 4.06 us: fold(): keep = lax.dynamic_slice_in_dim(block, mine, 1, axis)]
    reduce_scatter x0 -> x2, waiting for transfers between devices: none -> 15 us  [scattered(): lax.psum_scatter(state.reshape(-1, state.shape[-1]), 'fsdp', scatter_dime...]
    dynamic_update_slice x10 -> x0, local copies, waits for them, and re-layouts: 12.4 us -> none  [the longest x9 11.2 us: place(): lax.dynamic_update_slice(whole, others[steps - 1], (source * rows, 0))]
  transfers between devices with their start and end apart: 75 -> 73, of which waited for: 31 -> 39; matrix products, arithmetic and copies ran while one was open for 27% -> 14% of each run, Pallas kernels for 5% -> 18%
where the time goes in v2:
time: 504 us; the launch traced here: 496 us
  waiting for transfers between devices  174 us (35%)
  Pallas kernels  106 us (21%)
  starting transfers between devices  89.8 us (18%)
  local copies, waits for them, and re-layouts  42.6 us (8%)
  other arithmetic  41.1 us (8%)
  matrix products  26.2 us (5%)
  between operations  16.4 us (3%)
    ppermute x51, waiting for transfers between devices, flip(): return lax.ppermute(value, 'rep', [(i, i ^ 1 << bit) for i in range(size)])  124 us
    ppermute x51, starting transfers between devices, flip(): return lax.ppermute(value, 'rep', [(i, i ^ 1 << bit) for i in range(size)])  45.8 us
    ppermute x15, starting transfers between devices, turn(): lax.ppermute(value, 'fsdp', [(i, (i + steps) % size) for i in range(size)])  31.8 us
    ppermute x15, waiting for transfers between devices, turn(): lax.ppermute(value, 'fsdp', [(i, (i + steps) % size) for i in range(size)])  20.4 us
    dot_general x8, matrix products, tokens_dot(): lax.dot_general(left, right, (((0,), (0,)), ((), ())), preferred_element_...  19.4 us
    pallas_call x1, Pallas kernels, attend_back_call(): pl.pallas_call(attend_back_kernel, grid=(seqs, width // block), in_specs=...  17.7 us
    pallas_call x1, Pallas kernels, middle_back_call(): pl.pallas_call(middle_back_kernel, grid=(hidden // block,), in_specs=[SME...  17.3 us
    reduce_scatter x2, waiting for transfers between devices, scattered(): lax.psum_scatter(state.reshape(-1, state.shape[-1]), 'fsdp', scatter_dime...  15 us
  transfers between devices with their start and end apart: 73, of which 39 were waited for; matrix products, arithmetic and copies ran while one was open for 14% of the time, Pallas kernels for 18%

profile of v2, /device:TPU:0, one launch (start us, length us, event | category | flops | bytes accessed | tf_op | source)
XLA Modules:
  0.0 495.8 jit_solution(17022958151919344152)
XLA Ops:
  9.9 3.1 collective-permute-start
  13.0 2.6 collective-permute-start.1
  26.4 2.6 collective-permute-done.1
  33.2 6.0 %collective-permute-done.3 = bf16[3,1,1,16,3200]{4,3,0,2,1:T(8,128)(2,1)S(1)} collective-permute-done((bf16[3,1,1,16,3200]{4,3,0,2,1:T(8,128)(2,1)S(1)}, bf16[3,1,1,16,3200]{4,3,0,2,1:T(8,128)(2,1)S(1)}, u32[]{:S(2)}, u32[]{:S(2)}) %collective-permute-start.3) | collective-permute-done | bytes 307232 | tf_op jit(solution)/shard_map/ppermute | solution.py:45
  42.3 5.1 %collective-permute-start.7 = (bf16[2,16,3712]{2,1,0:T(8,128)(2,1)S(1)}, bf16[2,16,3712]{2,1,0:T(8,128)(2,1)S(1)}, u32[]{:S(2)}, u32[]{:S(2)}) collective-permute-start(bf16[2,16,3712]{2,1,0:T(8,128)(2,1)S(1)} %maximum_bitcast_fusion.11), channel_id=1, source_target_pairs={{0,1},{1,2},{2,3},{3,0},{4,5},{5,6},{6,7},{7,4},{8,9},{9,10},{10,1... | collective-permute-start | bytes 712712 | tf_op jit(solution)/shard_map/ppermute | solution.py:50
  50.5 4.8 collective-permute-done.5
  55.5 8.2 %collective-permute-done.6 = bf16[3,2,1,16,3200]{4,3,2,1,0:T(8,128)(2,1)S(1)} collective-permute-done((bf16[3,2,1,16,3200]{4,3,2,1,0:T(8,128)(2,1)S(1)}, bf16[3,2,1,16,3200]{4,3,2,1,0:T(8,128)(2,1)S(1)}, u32[]{:S(2)}, u32[]{:S(2)}) %collective-permute-start.6) | collective-permute-done | bytes 614432 | tf_op jit(solution)/shard_map/ppermute | solution.py:45
  66.2 5.8 %collective-permute-done.10 = bf16[3,1,1,16,3712]{4,3,0,2,1:T(8,128)(2,1)S(1)} collective-permute-done((bf16[3,1,1,16,3712]{4,3,0,2,1:T(8,128)(2,1)S(1)}, bf16[3,1,1,16,3712]{4,3,0,2,1:T(8,128)(2,1)S(1)}, u32[]{:S(2)}, u32[]{:S(2)}) %collective-permute-start.10) | collective-permute-done | bytes 356384 | tf_op jit(solution)/shard_map/ppermute | solution.py:45
  72.6 5.7 %collective-permute-start.14 = (bf16[2,16,2688]{2,1,0:T(8,128)(2,1)S(1)}, bf16[2,16,2688]{2,1,0:T(8,128)(2,1)S(1)}, u32[]{:S(2)}, u32[]{:S(2)}) collective-permute-start(bf16[2,16,2688]{2,1,0:T(8,128)(2,1)S(1)} %dynamic-slice_bitcast_fusion.3), channel_id=1, source_target_pairs={{0,1},{1,2},{2,3},{3,0},{4,5},{5,6},{6,7},{7,4},{8,9},{9,10},{10,1... | collective-permute-start | bytes 516104 | tf_op jit(solution)/shard_map/ppermute | solution.py:50
  80.8 11.3 %qkv.1 = (bf16[2,512,512]{2,1,0:T(8,128)(2,1)S(1)}, bf16[3,512,1024]{2,1,0:T(8,128)(2,1)}, f32[8,1024]{1,0:T(8,128)S(1)}) custom-call(s32[5]{0:T(128)S(1)} %pad_add_fusion.meta_ref, bf16[512,1024]{1,0:T(8,128)(2,1)S(1)} %bitcast.299, bf16[256,3072]{1,0:T(8,128)(2,1)} %own_ref.7, bf16[3,64,3200]{2,1,0:T(8,128)(2,1)S(1)} %bitcast.293, ...), custom_call_target="tpu_custom_call" | custom-call | flops 3221225472 | bytes 11534336 | tf_op jit(solution)/shard_map/qkv/pallas_call | solution.py:323
  92.1 2.2 slice.251
  96.3 4.8 collective-permute-start.20
  102.6 6.2 %collective-permute-done.19.k_down_ref.v_down_ref = bf16[2,128,1024]{2,1,0:T(8,128)(2,1)S(1)} collective-permute-done((bf16[2,128,1024]{2,1,0:T(8,128)(2,1)S(1)}, bf16[2,128,1024]{2,1,0:T(8,128)(2,1)S(1)}, u32[]{:S(2)}, u32[]{:S(2)}) %collective-permute-start.19) | collective-permute-done | bytes 524320 | tf_op jit(solution)/shard_map/ppermute | solution.py:189
  110.0 11.3 %attend.1 = (bf16[512,1024]{1,0:T(8,128)(2,1)S(1)}, bf16[2,8,2,256,256]{4,3,2,1,0:T(8,128)(2,1)}) custom-call(s32[5]{0:T(128)S(1)} %pad_add_fusion.meta_ref, bf16[3,512,1024]{2,1,0:T(8,128)(2,1)S(1)} %copy-done, bf16[3,512,1024]{2,1,0:T(8,128)(2,1)S(1)} %copy-done, bf16[3,512,1024]{2,1,0:T(8,128)(2,1)S(1)} %copy-done, ...), custom_call_target="tpu_custom_call" | custom-call | flops 1073741824 | bytes 5242880 | tf_op jit(solution)/shard_map/attend/pallas_call | solution.py:415
  123.5 2.7 collective-permute-done.21
  135.7 5.1 %out_norm.1 = (f32[512,1024]{1,0:T(8,128)}, bf16[2,512,512]{2,1,0:T(8,128)(2,1)S(1)}, bf16[2,512,512]{2,1,0:T(8,128)(2,1)S(1)}) custom-call(s32[5]{0:T(128)S(1)} %pad_add_fusion.meta_ref, bf16[512,1024]{1,0:T(8,128)(2,1)S(1)} %copy-done.37, bf16[256,1024]{1,0:T(8,128)(2,1)S(1)} %copy-done.27, bf16[3,64,1024]{2,1,0:T(8,128)(2,1)S(1)} %slice.261.p0.r0, ...), custom_call_target="tpu_custom_call" | custom-call | flops 1073741824 | bytes 8388608 | tf_op jit(solution)/shard_map/out_norm/pallas_call | solution.py:542
  143.8 2.5 collective-permute-start.27
  155.2 8.6 %collective-permute-done.26 = bf16[3,2,1,16,2688]{4,3,2,1,0:T(8,128)(2,1)S(1)} collective-permute-done((bf16[3,2,1,16,2688]{4,3,2,1,0:T(8,128)(2,1)S(1)}, bf16[3,2,1,16,2688]{4,3,2,1,0:T(8,128)(2,1)S(1)}, u32[]{:S(2)}, u32[]{:S(2)}) %collective-permute-start.26) | collective-permute-done | bytes 516128 | tf_op jit(solution)/shard_map/ppermute | solution.py:45
  166.5 3.8 collective-permute-done.31
  170.5 3.5 collective-permute-done.30
  176.0 11.6 %gate.1 = (bf16[512,2688]{1,0:T(8,128)(2,1)}, bf16[512,2688]{1,0:T(8,128)(2,1)}, bf16[512,2688]{1,0:T(8,128)(2,1)}) custom-call(s32[5]{0:T(128)S(1)} %pad_add_fusion.meta_ref, bf16[2,512,512]{2,1,0:T(8,128)(2,1)} %copy-done.42, bf16[256,2688]{1,0:T(8,128)(2,1)} %copy-done.49, bf16[3,64,2688]{2,1,0:T(8,128)(2,1)S(1)} %slice.267.p0, ...), custom_call_target="tpu_custom_call" | custom-call | flops 5637144576 | bytes 19267584 | tf_op jit(solution)/shard_map/gate/pallas_call | solution.py:587
  187.6 4.1 down_sum.2
  193.8 11.7 %collective-permute-done.35 = bf16[3,2,1,320,128]{4,3,0,2,1:T(8,128)(2,1)S(1)} collective-permute-done((bf16[3,2,1,320,128]{4,3,0,2,1:T(8,128)(2,1)S(1)}, bf16[3,2,1,320,128]{4,3,0,2,1:T(8,128)(2,1)S(1)}, u32[]{:S(2)}, u32[]{:S(2)}) %collective-permute-start.35) | collective-permute-done | bytes 491552 | tf_op jit(solution)/shard_map/ppermute | solution.py:45
  209.3 5.3 %down_sum.3 = bf16[4,4,656,128]{3,2,1,0:T(8,128)(2,1)S(1)} custom-call(s32[5]{0:T(128)S(1)} %pad_add_fusion.meta_ref, bf16[512,2688]{1,0:T(8,128)(2,1)} %get-tuple-element.269.m_ref, bf16[512,1024]{1,0:T(8,128)(2,1)S(1)} %copy-done.5, bf16[4,4,656,128]{3,2,1,0:T(8,128)(2,1)} %copy-done.66), custom_call_target="tpu_custom_call" | custom-call | flops 1375731712 | bytes 6422528 | tf_op jit(solution)/shard_map/down_sum/pallas_call | solution.py:710
  218.4 12.2 %gate_back.1 = (bf16[2,512,2688]{2,1,0:T(8,128)(2,1)}, bf16[2688,1024]{1,0:T(8,128)(2,1)}) custom-call(s32[5]{0:T(128)S(1)} %pad_add_fusion.meta_ref, bf16[512,1024]{1,0:T(8,128)(2,1)S(1)} %copy-done.5, bf16[656,1024]{1,0:T(8,128)(2,1)} %own_ref.6, bf16[3,4,336,128]{3,2,1,0:T(8,128)(2,1)} %bitcast.33.p0, bf16[3,4,320,128]{3,2,1,0:T(8,128)(2,1)} %bitcast.34.p1, ...), custom_call_target="tpu_custom_call" | custom-call | flops 2818572288 | bytes 22020096 | tf_op jit(solution)/shard_map/gate_back/pallas_call | solution.py:673
  230.7 3.6 convolution_convert_fusion.2
  241.0 8.0 %collective-permute-done.42 = bf16[4,1,1,320,128]{4,3,2,1,0:T(8,128)(2,1)S(1)} collective-permute-done((bf16[4,1,1,320,128]{4,3,2,1,0:T(8,128)(2,1)S(1)}, bf16[4,1,1,320,128]{4,3,2,1,0:T(8,128)(2,1)S(1)}, u32[]{:S(2)}, u32[]{:S(2)}) %collective-permute-start.42) | collective-permute-done | bytes 327712 | tf_op jit(solution)/shard_map/ppermute | solution.py:45
  260.7 17.3 %middle_back.1 = (f32[512,1024]{1,0:T(8,128)}, bf16[512,1024]{1,0:T(8,128)(2,1)}, bf16[512,1024]{1,0:T(8,128)(2,1)}) custom-call(s32[5]{0:T(128)S(1)} %pad_add_fusion.meta_ref, bf16[2,512,2688]{2,1,0:T(8,128)(2,1)} %get-tuple-element.235.gu_ref, bf16[256,2688]{1,0:T(8,128)(2,1)} %copy-done.49, bf16[3,64,2688]{2,1,0:T(8,128)(2,1)S(1)} %slice.267.p0, ...), custom_call_target="tpu_custom_call" | custom-call | flops 5637144576 | bytes 22806528 | tf_op jit(solution)/shard_map/middle_back/pallas_call | solution.py:766
  278.0 3.1 convolution_convert_fusion.3
  285.3 3.6 add_convert_fusion.6
  288.9 13.3 %reduce-scatter.3.cloned.1.call-done = bf16[656,128]{1,0:T(8,128)(2,1)} async-done(((bf16[2624,128]{1,0:T(8,128)(2,1)}), bf16[656,128]{1,0:T(8,128)(2,1)}) %reduce-scatter.3.cloned.1.call-update) | async-done | bytes 167952 | tf_op jit(solution)/shard_map/reduce_scatter | solution.py:162
  302.4 17.7 %attend_back.1 = (bf16[512,1024]{1,0:T(8,128)(2,1)S(1)}, f32[512,1024]{1,0:T(8,128)}, f32[512,1024]{1,0:T(8,128)}, bf16[2,128,1024]{2,1,0:T(8,128)(2,1)S(1)}, bf16[2,128,1024]{2,1,0:T(8,128)(2,1)S(1)}) custom-call(bf16[3,512,1024]{2,1,0:T(8,128)(2,1)} %get-tuple-element.169.q_ref.k_ref.v_ref, bf16[3,512,1024]{2,1,0:T(8,128)(2,1)} %get-tuple-element.169.q_ref.k_ref.v_ref, ...), custom_call_target="tpu_custom_call" | custom-call | flops 2684354560 | bytes 10485760 | tf_op jit(solution)/shard_map/attend_back/pallas_call | solution.py:493
  325.2 4.6 collective-permute-start.50
  331.5 5.7 %collective-permute-done.51 = bf16[2,128,1024]{2,1,0:T(8,128)(2,1)S(1)} collective-permute-done((bf16[2,128,1024]{2,1,0:T(8,128)(2,1)S(1)}, bf16[2,128,1024]{2,1,0:T(8,128)(2,1)S(1)}, u32[]{:S(2)}, u32[]{:S(2)}) %collective-permute-start.51) | collective-permute-done | bytes 524320 | tf_op jit(solution)/shard_map/ppermute | solution.py:189
  344.6 15.7 %collective-permute-done.49 = bf16[4,1,1,16,5376]{4,3,0,2,1:T(8,128)(2,1)S(1)} collective-permute-done((bf16[4,1,1,16,5376]{4,3,0,2,1:T(8,128)(2,1)S(1)}, bf16[4,1,1,16,5376]{4,3,0,2,1:T(8,128)(2,1)S(1)}, u32[]{:S(2)}, u32[]{:S(2)}) %collective-permute-start.49) | collective-permute-done | bytes 688160 | tf_op jit(solution)/shard_map/ppermute | solution.py:45
  371.3 9.6 %input_back.1 = bf16[512,1024]{1,0:T(8,128)(2,1)} custom-call(s32[5]{0:T(128)S(1)} %pad_add_fusion.meta_ref, bf16[512,3072]{1,0:T(8,128)(2,1)} %copy-done.45, bf16[256,3072]{1,0:T(8,128)(2,1)} %own_ref.7, bf16[3,64,3200]{2,1,0:T(8,128)(2,1)S(1)} %bitcast.295, bf16[3,64,3200]{2,1,0:T(8,128)(2,1)S(1)} %bitcast.291, bf16[3,64,3200]{2,1,0:T(8,128)(2,1)S(1)} %copy-done.7, ...), custom_call_target="tpu_custom_call" | custom-call | flops 3221225472 | bytes 13631488 | tf_op jit(solution)/shard_map/input_back/pallas_call | solution.py:820
  380.9 10.8 %collective-permute-done.54 = bf16[4,1,2,16,4096]{4,3,2,0,1:T(8,128)(2,1)} collective-permute-done((bf16[4,1,2,16,4096]{4,3,2,0,1:T(8,128)(2,1)}, bf16[4,1,2,16,4096]{4,3,2,0,1:T(8,128)(2,1)}, u32[]{:S(2)}, u32[]{:S(2)}) %collective-permute-start.54) | collective-permute-done | bytes 1048608 | tf_op jit(solution)/shard_map/ppermute | solution.py:45
  399.1 6.8 %add_convert_fusion.3 = bf16[512,1024]{1,0:T(8,128)(2,1)} fusion(f32[512,1024]{1,0:T(8,128)S(1)} %copy-done.67, bf16[512,2688]{1,0:T(8,128)(2,1)S(1)} %copy-done.48, bf16[2688,1024]{1,0:T(8,128)(2,1)} %get-tuple-element.270, f32[512]{0:T(512)S(1)} %bitcast.381), kind=kOutput, calls=%fused_computation.23 | convolution fusion | flops 2820145152 | bytes 11405312 | tf_op jit(solution)/shard_map/dot_general | solution.py:998
  406.0 3.3 collective-permute-done.55
  416.7 2.9 collective-permute-done.60
  423.2 6.3 %collective-permute-done.63 = bf16[2,1,16,5376]{3,2,1,0:T(8,128)(2,1)S(1)} collective-permute-done((bf16[2,1,16,5376]{3,2,1,0:T(8,128)(2,1)S(1)}, bf16[2,1,16,5376]{3,2,1,0:T(8,128)(2,1)S(1)}, u32[]{:S(2)}, u32[]{:S(2)}) %collective-permute-start.63) | collective-permute-done | bytes 344096 | tf_op jit(solution)/shard_map/ppermute | solution.py:45
  434.0 2.2 collective-permute-start.57
  438.1 2.2 reshape.439
  441.5 16.6 %collective-permute-done.58 = bf16[2,16,4096]{2,1,0:T(8,128)(2,1)} collective-permute-done((bf16[2,16,4096]{2,1,0:T(8,128)(2,1)}, bf16[2,16,4096]{2,1,0:T(8,128)(2,1)}, u32[]{:S(2)}, u32[]{:S(2)}) %collective-permute-start.58) | collective-permute-done | bytes 262176 | tf_op jit(solution)/shard_map/ppermute | solution.py:50
  461.5 3.0 maximum_convert_fusion
  469.4 2.5 collective-permute-done.65
  475.3 4.8 collective-permute-done.68
  480.9 2.6 collective-permute-done.69
  (479 shorter events, 162.4 us)
Async XLA Ops:
  7.2 295.1 %reduce-scatter.3.cloned.1.call-start = ((), (), s32[]{:S(2)}) async-start(), calls=%async_computation.2 | async-start | bytes 839680 | tf_op jit(solution)/shard_map/reduce_scatter | solution.py:162
  9.9 16.5 %collective-permute-start = (bf16[2,16,3200]{2,1,0:T(8,128)(2,1)S(1)}, bf16[2,16,3200]{2,1,0:T(8,128)(2,1)S(1)}, u32[]{:S(2)}, u32[]{:S(2)}) collective-permute-start(bf16[2,16,3200]{2,1,0:T(8,128)(2,1)S(1)} %maximum_bitcast_fusion.12), channel_id=1, source_target_pairs={{0,1},{1,2},{2,3},{3,0},{4,5},{5,6},{6,7},{7,4},{8,9},{9,10},{10,1... | collective-permute-start | bytes 614408 | tf_op jit(solution)/shard_map/ppermute | solution.py:50
  13.0 16.0 %collective-permute-start.1 = (bf16[2,16,3200]{2,1,0:T(8,128)(2,1)S(1)}, bf16[2,16,3200]{2,1,0:T(8,128)(2,1)S(1)}, u32[]{:S(2)}, u32[]{:S(2)}) collective-permute-start(bf16[2,16,3200]{2,1,0:T(8,128)(2,1)S(1)} %maximum_bitcast_fusion.12), channel_id=1, source_target_pairs={{0,2},{1,3},{2,0},{3,1},{4,6},{5,7},{6,4},{7,5},{8,10},{9,11},{10,... | collective-permute-start | bytes 614408 | tf_op jit(solution)/shard_map/ppermute | solution.py:50
  15.6 13.4 %collective-permute-start.2 = (bf16[2,16,3200]{2,1,0:T(8,128)(2,1)S(1)}, bf16[2,16,3200]{2,1,0:T(8,128)(2,1)}, u32[]{:S(2)}, u32[]{:S(2)}) collective-permute-start(bf16[2,16,3200]{2,1,0:T(8,128)(2,1)S(1)} %maximum_bitcast_fusion.12), channel_id=1, source_target_pairs={{0,3},{1,0},{2,1},{3,2},{4,7},{5,4},{6,5},{7,6},{8,11},{9,8},{10,9... | collective-permute-start | bytes 614408 | tf_op jit(solution)/shard_map/ppermute | solution.py:50
  40.7 14.6 %collective-permute-start.5 = (bf16[3,1,2,16,3200]{4,3,0,2,1:T(8,128)(2,1)S(1)}, bf16[3,1,2,16,3200]{4,3,0,2,1:T(8,128)(2,1)S(1)}, u32[]{:S(2)}, u32[]{:S(2)}) collective-permute-start(bf16[3,1,2,16,3200]{4,3,0,2,1:T(8,128)(2,1)S(1)} %pad_maximum_fusion.25), channel_id=1, source_target_pairs={{0,16},{4,20},{8,24},{12,28},{16,0},{20,4},{24,8},{28,12},{1,17},{... | collective-permute-start | bytes 1843208 | tf_op jit(solution)/shard_map/ppermute | solution.py:45
  42.3 21.6 %collective-permute-start.7 = (bf16[2,16,3712]{2,1,0:T(8,128)(2,1)S(1)}, bf16[2,16,3712]{2,1,0:T(8,128)(2,1)S(1)}, u32[]{:S(2)}, u32[]{:S(2)}) collective-permute-start(bf16[2,16,3712]{2,1,0:T(8,128)(2,1)S(1)} %maximum_bitcast_fusion.11), channel_id=1, source_target_pairs={{0,1},{1,2},{2,3},{3,0},{4,5},{5,6},{6,7},{7,4},{8,9},{9,10},{10,1... | collective-permute-start | bytes 712712 | tf_op jit(solution)/shard_map/ppermute | solution.py:50
  47.4 16.6 %collective-permute-start.8 = (bf16[2,16,3712]{2,1,0:T(8,128)(2,1)S(1)}, bf16[2,16,3712]{2,1,0:T(8,128)(2,1)S(1)}, u32[]{:S(2)}, u32[]{:S(2)}) collective-permute-start(bf16[2,16,3712]{2,1,0:T(8,128)(2,1)S(1)} %maximum_bitcast_fusion.11), channel_id=1, source_target_pairs={{0,2},{1,3},{2,0},{3,1},{4,6},{5,7},{6,4},{7,5},{8,10},{9,11},{10,... | collective-permute-start | bytes 712712 | tf_op jit(solution)/shard_map/ppermute | solution.py:50
  47.9 16.1 %collective-permute-start.9 = (bf16[2,16,3712]{2,1,0:T(8,128)(2,1)S(1)}, bf16[2,16,3712]{2,1,0:T(8,128)(2,1)S(1)}, u32[]{:S(2)}, u32[]{:S(2)}) collective-permute-start(bf16[2,16,3712]{2,1,0:T(8,128)(2,1)S(1)} %maximum_bitcast_fusion.11), channel_id=1, source_target_pairs={{0,3},{1,0},{2,1},{3,2},{4,7},{5,4},{6,5},{7,6},{8,11},{9,8},{10,9... | collective-permute-start | bytes 712712 | tf_op jit(solution)/shard_map/ppermute | solution.py:50
  49.9 13.8 %collective-permute-start.6 = (bf16[3,2,1,16,3200]{4,3,2,1,0:T(8,128)(2,1)S(1)}, bf16[3,2,1,16,3200]{4,3,2,1,0:T(8,128)(2,1)S(1)}, u32[]{:S(2)}, u32[]{:S(2)}) collective-permute-start(bf16[3,2,1,16,3200]{4,3,2,1,0:T(8,128)(2,1)S(1)} %pad_maximum_fusion.26), channel_id=1, source_target_pairs={{0,8},{4,12},{8,0},{12,4},{16,24},{20,28},{24,16},{28,20},{1,9},{5... | collective-permute-start | bytes 1843208 | tf_op jit(solution)/shard_map/ppermute | solution.py:45
  72.6 22.3 %collective-permute-start.14 = (bf16[2,16,2688]{2,1,0:T(8,128)(2,1)S(1)}, bf16[2,16,2688]{2,1,0:T(8,128)(2,1)S(1)}, u32[]{:S(2)}, u32[]{:S(2)}) collective-permute-start(bf16[2,16,2688]{2,1,0:T(8,128)(2,1)S(1)} %dynamic-slice_bitcast_fusion.3), channel_id=1, source_target_pairs={{0,1},{1,2},{2,3},{3,0},{4,5},{5,6},{6,7},{7,4},{8,9},{9,10},{10,1... | collective-permute-start | bytes 516104 | tf_op jit(solution)/shard_map/ppermute | solution.py:50
  78.3 16.6 %collective-permute-start.15 = (bf16[2,16,2688]{2,1,0:T(8,128)(2,1)S(1)}, bf16[2,16,2688]{2,1,0:T(8,128)(2,1)S(1)}, u32[]{:S(2)}, u32[]{:S(2)}) collective-permute-start(bf16[2,16,2688]{2,1,0:T(8,128)(2,1)S(1)} %dynamic-slice_bitcast_fusion.3), channel_id=1, source_target_pairs={{0,2},{1,3},{2,0},{3,1},{4,6},{5,7},{6,4},{7,5},{8,10},{9,11},{10,... | collective-permute-start | bytes 516104 | tf_op jit(solution)/shard_map/ppermute | solution.py:50
  79.4 15.5 %collective-permute-start.16 = (bf16[2,16,2688]{2,1,0:T(8,128)(2,1)S(1)}, bf16[2,16,2688]{2,1,0:T(8,128)(2,1)S(1)}, u32[]{:S(2)}, u32[]{:S(2)}) collective-permute-start(bf16[2,16,2688]{2,1,0:T(8,128)(2,1)S(1)} %dynamic-slice_bitcast_fusion.3), channel_id=1, source_target_pairs={{0,3},{1,0},{2,1},{3,2},{4,7},{5,4},{6,5},{7,6},{8,11},{9,8},{10,9... | collective-permute-start | bytes 516104 | tf_op jit(solution)/shard_map/ppermute | solution.py:50
  94.3 27.1 %collective-permute-start.17 = (bf16[3,1,2,16,3712]{4,3,0,2,1:T(8,128)(2,1)S(1)}, bf16[3,1,2,16,3712]{4,3,0,2,1:T(8,128)(2,1)S(1)}, u32[]{:S(2)}, u32[]{:S(2)}) collective-permute-start(bf16[3,1,2,16,3712]{4,3,0,2,1:T(8,128)(2,1)S(1)} %pad_maximum_fusion.18), channel_id=1, source_target_pairs={{0,16},{4,20},{8,24},{12,28},{16,0},{20,4},{24,8},{28,12},{1,17},{... | collective-permute-start | bytes 2138120 | tf_op jit(solution)/shard_map/ppermute | solution.py:45
  95.0 13.9 %collective-permute-start.19 = (bf16[2,128,1024]{2,1,0:T(8,128)(2,1)S(1)}, bf16[2,128,1024]{2,1,0:T(8,128)(2,1)S(1)}, u32[]{:S(2)}, u32[]{:S(2)}) collective-permute-start(bf16[2,128,1024]{2,1,0:T(8,128)(2,1)S(1)} %bitcast.377), channel_id=1, source_target_pairs={{1,0},{2,1},{3,2},{5,4},{6,5},{7,6},{9,8},{10,9},{11,10},{13,12},{... | collective-permute-start | bytes 1572872 | tf_op jit(solution)/shard_map/ppermute | solution.py:189
  96.3 13.8 %collective-permute-start.20 = (bf16[2,128,1024]{2,1,0:T(8,128)(2,1)S(1)}, bf16[2,128,1024]{2,1,0:T(8,128)(2,1)S(1)}, u32[]{:S(2)}, u32[]{:S(2)}) collective-permute-start(bf16[2,128,1024]{2,1,0:T(8,128)(2,1)S(1)} %bitcast.376), channel_id=1, source_target_pairs={{0,1},{1,2},{2,3},{4,5},{5,6},{6,7},{8,9},{9,10},{10,11},{12,13},{... | collective-permute-start | bytes 1572872 | tf_op jit(solution)/shard_map/ppermute | solution.py:189
  101.1 21.3 %collective-permute-start.18 = (bf16[3,2,1,16,3712]{4,3,2,1,0:T(8,128)(2,1)S(1)}, bf16[3,2,1,16,3712]{4,3,2,1,0:T(8,128)(2,1)S(1)}, u32[]{:S(2)}, u32[]{:S(2)}) collective-permute-start(bf16[3,2,1,16,3712]{4,3,2,1,0:T(8,128)(2,1)S(1)} %pad_maximum_fusion.19), channel_id=1, source_target_pairs={{0,8},{4,12},{8,0},{12,4},{16,24},{20,28},{24,16},{28,20},{1,9},{5... | collective-permute-start | bytes 2138120 | tf_op jit(solution)/shard_map/ppermute | solution.py:45
  130.2 10.6 %collective-permute-start.23 = (bf16[3,1,1,16,2688]{4,3,0,2,1:T(8,128)(2,1)S(1)}, bf16[3,1,1,16,2688]{4,3,0,2,1:T(8,128)(2,1)S(1)}, u32[]{:S(2)}, u32[]{:S(2)}) collective-permute-start(bf16[3,1,1,16,2688]{4,3,0,2,1:T(8,128)(2,1)S(1)} %maximum_bitcast_fusion.8), channel_id=1, source_target_pairs={{0,8},{4,12},{8,0},{12,4},{16,24},{20,28},{24,16},{28,20},{1,9},{5... | collective-permute-start | bytes 774152 | tf_op jit(solution)/shard_map/ppermute | solution.py:45
  142.3 12.7 %collective-permute-start.25 = (bf16[3,1,2,16,2688]{4,3,0,2,1:T(8,128)(2,1)S(1)}, bf16[3,1,2,16,2688]{4,3,0,2,1:T(8,128)(2,1)S(1)}, u32[]{:S(2)}, u32[]{:S(2)}) collective-permute-start(bf16[3,1,2,16,2688]{4,3,0,2,1:T(8,128)(2,1)S(1)} %pad_maximum_fusion.31), channel_id=1, source_target_pairs={{0,16},{4,20},{8,24},{12,28},{16,0},{20,4},{24,8},{28,12},{1,17},{... | collective-permute-start | bytes 1548296 | tf_op jit(solution)/shard_map/ppermute | solution.py:45
  143.8 20.1 %collective-permute-start.27 = (bf16[656,128]{1,0:T(8,128)(2,1)S(1)}, bf16[656,128]{1,0:T(8,128)(2,1)S(1)}, u32[]{:S(2)}, u32[]{:S(2)}) collective-permute-start(bf16[656,128]{1,0:T(8,128)(2,1)S(1)} %copy-done.77), channel_id=1, source_target_pairs={{0,1},{1,2},{2,3},{3,0},{4,5},{5,6},{6,7},{7,4},{8,9},{9,10},{10,1... | collective-permute-start | bytes 503816 | tf_op jit(solution)/shard_map/ppermute | solution.py:50
  146.3 17.7 %collective-permute-start.28 = (bf16[656,128]{1,0:T(8,128)(2,1)S(1)}, bf16[656,128]{1,0:T(8,128)(2,1)S(1)}, u32[]{:S(2)}, u32[]{:S(2)}) collective-permute-start(bf16[656,128]{1,0:T(8,128)(2,1)S(1)} %copy-done.77), channel_id=1, source_target_pairs={{0,2},{1,3},{2,0},{3,1},{4,6},{5,7},{6,4},{7,5},{8,10},{9,11},{10,... | collective-permute-start | bytes 503816 | tf_op jit(solution)/shard_map/ppermute | solution.py:50
  146.9 17.1 %collective-permute-start.29 = (bf16[656,128]{1,0:T(8,128)(2,1)S(1)}, bf16[656,128]{1,0:T(8,128)(2,1)S(1)}, u32[]{:S(2)}, u32[]{:S(2)}) collective-permute-start(bf16[656,128]{1,0:T(8,128)(2,1)S(1)} %copy-done.77), channel_id=1, source_target_pairs={{0,3},{1,0},{2,1},{3,2},{4,7},{5,4},{6,5},{7,6},{8,11},{9,8},{10,9... | collective-permute-start | bytes 503816 | tf_op jit(solution)/shard_map/ppermute | solution.py:50
  152.2 11.6 %collective-permute-start.26 = (bf16[3,2,1,16,2688]{4,3,2,1,0:T(8,128)(2,1)S(1)}, bf16[3,2,1,16,2688]{4,3,2,1,0:T(8,128)(2,1)S(1)}, u32[]{:S(2)}, u32[]{:S(2)}) collective-permute-start(bf16[3,2,1,16,2688]{4,3,2,1,0:T(8,128)(2,1)S(1)} %pad_maximum_fusion.32), channel_id=1, source_target_pairs={{0,8},{4,12},{8,0},{12,4},{16,24},{20,28},{24,16},{28,20},{1,9},{5... | collective-permute-start | bytes 1548296 | tf_op jit(solution)/shard_map/ppermute | solution.py:45
  191.8 14.9 %collective-permute-start.36 = (bf16[4,4,656,128]{3,2,1,0:T(8,128)(2,1)S(1)}, bf16[4,4,656,128]{3,2,1,0:T(8,128)(2,1)S(1)}, u32[]{:S(2)}, u32[]{:S(2)}) collective-permute-start(bf16[4,4,656,128]{3,2,1,0:T(8,128)(2,1)S(1)} %down_sum.2), channel_id=1, source_target_pairs={{0,4},{4,0},{8,12},{12,8},{16,20},{20,16},{24,28},{28,24},{1,5},{5... | collective-permute-start | bytes 8060936 | tf_op jit(solution)/shard_map/ppermute | solution.py:45
  191.9 13.6 %collective-permute-start.35 = (bf16[3,2,1,320,128]{4,3,0,2,1:T(8,128)(2,1)S(1)}, bf16[3,2,1,320,128]{4,3,0,2,1:T(8,128)(2,1)S(1)}, u32[]{:S(2)}, u32[]{:S(2)}) collective-permute-start(bf16[3,2,1,320,128]{4,3,0,2,1:T(8,128)(2,1)S(1)} %pad_maximum_fusion.35), channel_id=1, source_target_pairs={{0,8},{4,12},{8,0},{12,4},{16,24},{20,28},{24,16},{28,20},{1,9},{5... | collective-permute-start | bytes 1474568 | tf_op jit(solution)/shard_map/ppermute | solution.py:45
  192.7 13.8 %collective-permute-start.34 = (bf16[3,1,2,336,128]{4,3,0,2,1:T(8,128)(2,1)S(1)}, bf16[3,1,2,336,128]{4,3,0,2,1:T(8,128)(2,1)S(1)}, u32[]{:S(2)}, u32[]{:S(2)}) collective-permute-start(bf16[3,1,2,336,128]{4,3,0,2,1:T(8,128)(2,1)S(1)} %pad_maximum_fusion.33), channel_id=1, source_target_pairs={{0,16},{4,20},{8,24},{12,28},{16,0},{20,4},{24,8},{28,12},{1,17},{... | collective-permute-start | bytes 1548296 | tf_op jit(solution)/shard_map/ppermute | solution.py:45
  214.9 22.4 %collective-permute-start.39 = (bf16[4,2,1,336,128]{4,3,2,1,0:T(8,128)(2,1)S(1)}, bf16[4,2,1,336,128]{4,3,2,1,0:T(8,128)(2,1)}, u32[]{:S(2)}, u32[]{:S(2)}) collective-permute-start(bf16[4,2,1,336,128]{4,3,2,1,0:T(8,128)(2,1)S(1)} %constant_dynamic-slice_fusion.23), channel_id=1, source_target_pairs={{0,8},{4,12},{8,0},{12,4},{16,24},{20,28},{24,16},{28,20},{1,9},{5... | collective-permute-start | bytes 2064392 | tf_op jit(solution)/shard_map/ppermute | solution.py:45
  217.2 18.9 %collective-permute-start.40 = (bf16[4,1,2,320,128]{4,3,2,1,0:T(8,128)(2,1)}, bf16[4,1,2,320,128]{4,3,2,1,0:T(8,128)(2,1)}, u32[]{:S(2)}, u32[]{:S(2)}) collective-permute-start(bf16[4,1,2,320,128]{4,3,2,1,0:T(8,128)(2,1)} %constant_dynamic-slice_fusion.22), channel_id=1, source_target_pairs={{0,16},{4,20},{8,24},{12,28},{16,0},{20,4},{24,8},{28,12},{1,17},{... | collective-permute-start | bytes 1966088 | tf_op jit(solution)/shard_map/ppermute | solution.py:45
  238.6 11.3 %collective-permute-start.43 = (bf16[512,2688]{1,0:T(8,128)(2,1)S(1)}, bf16[512,2688]{1,0:T(8,128)(2,1)S(1)}, u32[]{:S(2)}, u32[]{:S(2)}) collective-permute-start(bf16[512,2688]{1,0:T(8,128)(2,1)S(1)} %convolution_convert_fusion.2), channel_id=1, source_target_pairs={{0,4},{4,0},{8,12},{12,8},{16,20},{20,16},{24,28},{28,24},{1,5},{5... | collective-permute-start | bytes 8257544 | tf_op jit(solution)/shard_map/ppermute | solution.py:45
  238.7 13.0 %collective-permute-start.44 = (bf16[512,2688]{1,0:T(8,128)(2,1)S(1)}, bf16[512,2688]{1,0:T(8,128)(2,1)S(1)}, u32[]{:S(2)}, u32[]{:S(2)}) collective-permute-start(bf16[512,2688]{1,0:T(8,128)(2,1)S(1)} %convolution_convert_fusion.1), channel_id=1, source_target_pairs={{0,4},{4,0},{8,12},{12,8},{16,20},{20,16},{24,28},{28,24},{1,5},{5... | collective-permute-start | bytes 8257544 | tf_op jit(solution)/shard_map/ppermute | solution.py:45
  239.2 9.8 %collective-permute-start.42 = (bf16[4,1,1,320,128]{4,3,2,1,0:T(8,128)(2,1)S(1)}, bf16[4,1,1,320,128]{4,3,2,1,0:T(8,128)(2,1)S(1)}, u32[]{:S(2)}, u32[]{:S(2)}) collective-permute-start(bf16[4,1,1,320,128]{4,3,2,1,0:T(8,128)(2,1)S(1)} %constant_dynamic-slice_fusion.20), channel_id=1, source_target_pairs={{0,8},{4,12},{8,0},{12,4},{16,24},{20,28},{24,16},{28,20},{1,9},{5... | collective-permute-start | bytes 983048 | tf_op jit(solution)/shard_map/ppermute | solution.py:45
  240.0 9.8 %collective-permute-start.41 = (bf16[4,1,1,336,128]{4,3,2,1,0:T(8,128)(2,1)S(1)}, bf16[4,1,1,336,128]{4,3,2,1,0:T(8,128)(2,1)S(1)}, u32[]{:S(2)}, u32[]{:S(2)}) collective-permute-start(bf16[4,1,1,336,128]{4,3,2,1,0:T(8,128)(2,1)S(1)} %constant_dynamic-slice_fusion.21), channel_id=1, source_target_pairs={{0,16},{4,20},{8,24},{12,28},{16,0},{20,4},{24,8},{28,12},{1,17},{... | collective-permute-start | bytes 1032200 | tf_op jit(solution)/shard_map/ppermute | solution.py:45
  258.3 61.8 %collective-permute-start.45 = (bf16[4,2,1,16,5376]{4,3,0,2,1:T(8,128)(2,1)}, bf16[4,2,1,16,5376]{4,3,0,2,1:T(8,128)(2,1)}, u32[]{:S(2)}, u32[]{:S(2)}) collective-permute-start(bf16[4,2,1,16,5376]{4,3,0,2,1:T(8,128)(2,1)} %pad_maximum_fusion.5), channel_id=1, source_target_pairs={{0,8},{4,12},{8,0},{12,4},{16,24},{20,28},{24,16},{28,20},{1,9},{5... | collective-permute-start | bytes 4128776 | tf_op jit(solution)/shard_map/ppermute | solution.py:45
  282.1 128.9 %all-gather.3.cloned.1.call-start = ((), (), s32[]{:S(2)}) async-start(), calls=%async_computation.4 | async-start | bytes 1511424 | tf_op jit(solution)/shard_map/all_gather | solution.py:958
  284.4 37.5 %collective-permute-start.46 = (bf16[4,1,2,16,5376]{4,3,0,2,1:T(8,128)(2,1)}, bf16[4,1,2,16,5376]{4,3,0,2,1:T(8,128)(2,1)}, u32[]{:S(2)}, u32[]{:S(2)}) collective-permute-start(bf16[4,1,2,16,5376]{4,3,0,2,1:T(8,128)(2,1)} %pad_maximum_fusion.6), channel_id=1, source_target_pairs={{0,16},{4,20},{8,24},{12,28},{16,0},{20,4},{24,8},{28,12},{1,17},{... | collective-permute-start | bytes 4128776 | tf_op jit(solution)/shard_map/ppermute | solution.py:45
  302.3 110.3 %reduce-scatter.5.cloned.1.call-start = ((), (), s32[]{:S(2)}) async-start(), calls=%async_computation.3 | async-start | bytes 1720320 | tf_op jit(solution)/shard_map/reduce_scatter | solution.py:162
  323.7 13.5 %collective-permute-start.51 = (bf16[2,128,1024]{2,1,0:T(8,128)(2,1)S(1)}, bf16[2,128,1024]{2,1,0:T(8,128)(2,1)S(1)}, u32[]{:S(2)}, u32[]{:S(2)}) collective-permute-start(bf16[2,128,1024]{2,1,0:T(8,128)(2,1)S(1)} %get-tuple-element.256), channel_id=1, source_target_pairs={{1,0},{2,1},{3,2},{5,4},{6,5},{7,6},{9,8},{10,9},{11,10},{13,12},{... | collective-permute-start | bytes 1572872 | tf_op jit(solution)/shard_map/ppermute | solution.py:189
  325.2 13.2 %collective-permute-start.50 = (bf16[2,128,1024]{2,1,0:T(8,128)(2,1)S(1)}, bf16[2,128,1024]{2,1,0:T(8,128)(2,1)S(1)}, u32[]{:S(2)}, u32[]{:S(2)}) collective-permute-start(bf16[2,128,1024]{2,1,0:T(8,128)(2,1)S(1)} %get-tuple-element.255), channel_id=1, source_target_pairs={{0,1},{1,2},{2,3},{4,5},{5,6},{6,7},{8,9},{9,10},{10,11},{12,13},{... | collective-permute-start | bytes 1572872 | tf_op jit(solution)/shard_map/ppermute | solution.py:189
  329.8 14.7 %collective-permute-start.48 = (bf16[4,1,1,16,5376]{4,3,0,2,1:T(8,128)(2,1)S(1)}, bf16[4,1,1,16,5376]{4,3,0,2,1:T(8,128)(2,1)S(1)}, u32[]{:S(2)}, u32[]{:S(2)}) collective-permute-start(bf16[4,1,1,16,5376]{4,3,0,2,1:T(8,128)(2,1)S(1)} %pad_maximum_fusion.20), channel_id=1, source_target_pairs={{0,16},{4,20},{8,24},{12,28},{16,0},{20,4},{24,8},{28,12},{1,17},{... | collective-permute-start | bytes 2064392 | tf_op jit(solution)/shard_map/ppermute | solution.py:45
  342.2 18.3 %collective-permute-start.52 = (bf16[512,3072]{1,0:T(8,128)(2,1)S(1)}, bf16[512,3072]{1,0:T(8,128)(2,1)S(1)}, u32[]{:S(2)}, u32[]{:S(2)}) collective-permute-start(bf16[512,3072]{1,0:T(8,128)(2,1)S(1)} %convolution_convert_fusion), channel_id=1, source_target_pairs={{0,4},{4,0},{8,12},{12,8},{16,20},{20,16},{24,28},{28,24},{1,5},{5... | collective-permute-start | bytes 9437192 | tf_op jit(solution)/shard_map/ppermute | solution.py:45
  342.5 17.9 %collective-permute-start.49 = (bf16[4,1,1,16,5376]{4,3,0,2,1:T(8,128)(2,1)S(1)}, bf16[4,1,1,16,5376]{4,3,0,2,1:T(8,128)(2,1)S(1)}, u32[]{:S(2)}, u32[]{:S(2)}) collective-permute-start(bf16[4,1,1,16,5376]{4,3,0,2,1:T(8,128)(2,1)S(1)} %pad_maximum_fusion.21), channel_id=1, source_target_pairs={{0,8},{4,12},{8,0},{12,4},{16,24},{20,28},{24,16},{28,20},{1,9},{5... | collective-permute-start | bytes 2064392 | tf_op jit(solution)/shard_map/ppermute | solution.py:45
  364.2 29.9 %collective-permute-start.53 = (bf16[4,2,1,16,4096]{4,3,0,2,1:T(8,128)(2,1)}, bf16[4,2,1,16,4096]{4,3,0,2,1:T(8,128)(2,1)}, u32[]{:S(2)}, u32[]{:S(2)}) collective-permute-start(bf16[4,2,1,16,4096]{4,3,0,2,1:T(8,128)(2,1)} %pad_maximum_fusion.11), channel_id=1, source_target_pairs={{0,8},{4,12},{8,0},{12,4},{16,24},{20,28},{24,16},{28,20},{1,9},{5... | collective-permute-start | bytes 3145736 | tf_op jit(solution)/shard_map/ppermute | solution.py:45
  366.9 24.8 %collective-permute-start.54 = (bf16[4,1,2,16,4096]{4,3,2,0,1:T(8,128)(2,1)}, bf16[4,1,2,16,4096]{4,3,2,0,1:T(8,128)(2,1)}, u32[]{:S(2)}, u32[]{:S(2)}) collective-permute-start(bf16[4,1,2,16,4096]{4,3,2,0,1:T(8,128)(2,1)} %pad_maximum_fusion.12), channel_id=1, source_target_pairs={{0,16},{4,20},{8,24},{12,28},{16,0},{20,4},{24,8},{28,12},{1,17},{... | collective-permute-start | bytes 3145736 | tf_op jit(solution)/shard_map/ppermute | solution.py:45
  396.9 12.4 %collective-permute-start.55 = (bf16[4,1,1,16,4096]{4,3,0,2,1:T(8,128)(2,1)S(1)}, bf16[4,1,1,16,4096]{4,3,0,2,1:T(8,128)(2,1)S(1)}, u32[]{:S(2)}, u32[]{:S(2)}) collective-permute-start(bf16[4,1,1,16,4096]{4,3,0,2,1:T(8,128)(2,1)S(1)} %pad_maximum_fusion.27), channel_id=1, source_target_pairs={{0,16},{4,20},{8,24},{12,28},{16,0},{20,4},{24,8},{28,12},{1,17},{... | collective-permute-start | bytes 1572872 | tf_op jit(solution)/shard_map/ppermute | solution.py:45
  398.5 12.1 %collective-permute-start.56 = (bf16[4,1,1,16,4096]{4,3,2,0,1:T(8,128)(2,1)S(1)}, bf16[4,1,1,16,4096]{4,3,2,0,1:T(8,128)(2,1)S(1)}, u32[]{:S(2)}, u32[]{:S(2)}) collective-permute-start(bf16[4,1,1,16,4096]{4,3,2,0,1:T(8,128)(2,1)S(1)} %pad_maximum_fusion.28), channel_id=1, source_target_pairs={{0,8},{4,12},{8,0},{12,4},{16,24},{20,28},{24,16},{28,20},{1,9},{5... | collective-permute-start | bytes 1572872 | tf_op jit(solution)/shard_map/ppermute | solution.py:45
  431.2 28.2 %collective-permute-start.64 = (bf16[2,4,16,5376]{3,2,1,0:T(8,128)(2,1)}, bf16[2,4,16,5376]{3,2,1,0:T(8,128)(2,1)}, u32[]{:S(2)}, u32[]{:S(2)}) collective-permute-start(bf16[2,4,16,5376]{3,2,1,0:T(8,128)(2,1)} %pad_maximum_fusion.8), channel_id=1, source_target_pairs={{0,4},{4,0},{8,12},{12,8},{16,20},{20,16},{24,28},{28,24},{1,5},{5... | collective-permute-start | bytes 4128776 | tf_op jit(solution)/shard_map/ppermute | solution.py:45
  432.2 9.3 %collective-permute-start.59 = (bf16[2,16,4096]{2,1,0:T(8,128)(2,1)}, bf16[2,16,4096]{2,1,0:T(8,128)(2,1)}, u32[]{:S(2)}, u32[]{:S(2)}) collective-permute-start(bf16[2,16,4096]{2,1,0:T(8,128)(2,1)} %get-tuple-element.328), channel_id=1, source_target_pairs={{0,3},{1,0},{2,1},{3,2},{4,7},{5,4},{6,5},{7,6},{8,11},{9,8},{10,9... | collective-permute-start | bytes 786440 | tf_op jit(solution)/shard_map/ppermute | solution.py:50
  433.8 24.3 %collective-permute-start.58 = (bf16[2,16,4096]{2,1,0:T(8,128)(2,1)}, bf16[2,16,4096]{2,1,0:T(8,128)(2,1)}, u32[]{:S(2)}, u32[]{:S(2)}) collective-permute-start(bf16[2,16,4096]{2,1,0:T(8,128)(2,1)} %get-tuple-element.327), channel_id=1, source_target_pairs={{0,2},{1,3},{2,0},{3,1},{4,6},{5,7},{6,4},{7,5},{8,10},{9,11},{10,... | collective-permute-start | bytes 786440 | tf_op jit(solution)/shard_map/ppermute | solution.py:50
  434.0 24.1 %collective-permute-start.57 = (bf16[2,16,4096]{2,1,0:T(8,128)(2,1)}, bf16[2,16,4096]{2,1,0:T(8,128)(2,1)}, u32[]{:S(2)}, u32[]{:S(2)}) collective-permute-start(bf16[2,16,4096]{2,1,0:T(8,128)(2,1)} %get-tuple-element.326), channel_id=1, source_target_pairs={{0,1},{1,2},{2,3},{3,0},{4,5},{5,6},{6,7},{7,4},{8,9},{9,10},{10,1... | collective-permute-start | bytes 786440 | tf_op jit(solution)/shard_map/ppermute | solution.py:50
  (107 other events, 905.8 us)
Sparse Core Ops, SparseCore 0:
  282.2 20.0 reduce-scatter.2
  304.3 25.1 all-gather.2
  381.0 31.4 reduce-scatter.4

commit v3 on v2

--- a/solution.py
+++ b/solution.py
@@ -17,7 +17,7 @@
 inv_root_two_pi = 0.3989422804014327
 f32 = jnp.float32
 bf16 = jnp.bfloat16
-VMEM_LIMIT = 48 * 1024 * 1024
+COST_SCALE = 1.0
 
 
 def after(value, *before):
@@ -130,8 +130,20 @@
     return whole
 
 
-def turned_before(piece):
-    return [turn(piece, steps) for steps in range(1, lax.axis_size("fsdp"))]
+def turned_before(piece, steps):
+    return [turn(piece, step) for step in steps]
+
+
+def runs():
+    size = lax.axis_size("fsdp")
+    order = sorted(range(1, size), key=lambda step: (min(step, size - step), step))
+    cuts = [(size - 1) * part // 3 for part in range(4)]
+    return [order[first:last] for first, last in zip(cuts, cuts[1:])]
+
+
+def in_turn(states, came):
+    order = [step for run in runs() for step in run]
+    return states([came[order.index(step)] for step in range(1, lax.axis_size("fsdp"))])
 
 
 def tokens_dot(left, right):
@@ -143,43 +155,50 @@
     return lax.dynamic_index_in_dim(split, index, 0, False)
 
 
-def fold(blocks, lead, bit):
-    axis = lead + link_axis(bit)
-    mine = bit_value(bit)
-    give = [lax.dynamic_slice_in_dim(block, 1 - mine, 1, axis) for block in blocks]
-    got = flip(give[0] if len(give) == 1 else jnp.concatenate(give, axis=-1), bit)
-    results, start = [], 0
-    for block in blocks:
-        keep = lax.dynamic_slice_in_dim(block, mine, 1, axis)
-        width = block.shape[-1]
-        add = lax.slice_in_dim(got, start, start + width, axis=got.ndim - 1)
-        results.append((keep.astype(f32) + add.astype(f32)).astype(bf16))
-        start += width
-    return results
-
-
-def scattered(state):
-    flat = lax.psum_scatter(state.reshape(-1, state.shape[-1]), "fsdp", scatter_dimension=0, tiled=True)
-    return flat.reshape(state.shape[1:])
-
-
-def to_owner(state):
+def turned_slots(slots, steps):
     size = lax.axis_size("fsdp")
     me = lax.axis_index("fsdp")
-    came = [
-        turn(lax.dynamic_index_in_dim(state, lax.rem(me + steps, size), 0, False), steps)
-        for steps in range(1, size)
+    return [
+        turn(lax.dynamic_index_in_dim(slots, lax.rem(me + step, size), 0, False), step) for step in steps
     ]
-    total = lax.dynamic_index_in_dim(state, me, 0, False).astype(f32)
+
+
+def slot_sum(slots, came):
+    total = lax.dynamic_index_in_dim(slots, lax.axis_index("fsdp"), 0, False).astype(f32)
     for part in came:
         total = total + part.astype(f32)
     return total.astype(bf16)
 
 
-def row_blocks(states):
-    size = lax.axis_size("fsdp")
-    views = [state.reshape((size, 2) + (2,) * link_count() + (-1, state.shape[1])) for state in states]
-    return [[view[:, part] for view in views] for part in range(2)]
+def bits_left(done):
+    orders = zip(*link_orders())
+    return [sorted(order[done:]) for order in orders]
+
+
+def split_index(number, place):
+    low = number & ((1 << place) - 1)
+    return ((number >> place) << (place + 1)) | low
+
+
+def halves(state, done, part):
+    bit = link_orders()[done][part]
+    place = bits_left(done)[part].index(bit)
+    size, links = state.shape[:2]
+    view = state.reshape((size, links >> (place + 1), 2, 1 << place) + state.shape[2:])
+    shape = (size, links // 2) + state.shape[2:]
+    keep, give = [
+        lax.dynamic_index_in_dim(view, index, 2, False).reshape(shape)
+        for index in (bit_value(bit), 1 - bit_value(bit))
+    ]
+    return keep, give
+
+
+def swap(parts, done):
+    return [(keep, flip(give, bit)) for (keep, give), bit in zip(parts, link_orders()[done])]
+
+
+def added(keep, got):
+    return (keep.astype(f32) + got.astype(f32)).astype(bf16)
 
 
 def neighbours(up, down):
@@ -189,14 +208,12 @@
     return lax.ppermute(up, "fsdp", backward), lax.ppermute(down, "fsdp", forward)
 
 
-def params(*semantics):
-    return pltpu.CompilerParams(
-        dimension_semantics=semantics, vmem_limit_bytes=VMEM_LIMIT
-    )
+def params(megabytes, *semantics):
+    return pltpu.CompilerParams(dimension_semantics=semantics, vmem_limit_bytes=megabytes << 20)
 
 
 def cost(flops, nbytes):
-    return pl.CostEstimate(flops=int(flops), bytes_accessed=int(nbytes), transcendentals=0)
+    return pl.CostEstimate(flops=int(flops * COST_SCALE), bytes_accessed=int(nbytes * COST_SCALE), transcendentals=0)
 
 
 def dot_nn(left, right):
@@ -264,6 +281,18 @@
     )
 
 
+def assemble_two(meta_ref, whole_ref, own_ref, wide_refs, narrow_refs):
+    cut = wide_refs[0].shape[2]
+    assemble(meta_ref, whole_ref.at[:, :cut], own_ref.at[:, :cut], wide_refs)
+    assemble(meta_ref, whole_ref.at[:, cut:], own_ref.at[:, cut:], narrow_refs)
+
+
+def stretch_specs(parts, start, block):
+    rest = parts[0].shape[2] - start - block
+    wide = part_specs(parts, block, lambda i: start // block)
+    return wide + part_specs(parts, rest, lambda i: (start + block) // rest)
+
+
 def part_specs(parts, block, place):
     count, quarter, _ = parts[0].shape
     return [pl.BlockSpec((count, quarter, block), lambda i: (0, 0, place(i)))] * 4
@@ -314,6 +343,10 @@
     return pl.BlockSpec(shape, lambda i: (0,) * len(shape))
 
 
+def once(*shape):
+    return pl.BlockSpec(shape, lambda i: (0,) * len(shape), pipeline_mode=pl.Buffered(1))
+
+
 def qkv_call(meta, x, own, parts, own_gains, cosine, sine):
     rows, width = x.shape
     slab = own.shape[0]
@@ -323,11 +356,11 @@
     return pl.pallas_call(
         functools.partial(qkv_kernel, rope_steps=2 * per_plane, size=size),
         grid=(3 * per_plane,),
-        in_specs=[SMEM_SPEC, fixed(rows, width), pl.BlockSpec((slab, block), lambda i: (0, i))]
+        in_specs=[SMEM_SPEC, once(rows, width), pl.BlockSpec((slab, block), lambda i: (0, i))]
         + part_specs(parts, block, lambda i: i)
-        + [fixed(slab, LANES)]
+        + [once(slab, LANES)]
         + part_specs(parts, LANES, lambda i: 3 * width // LANES)
-        + [fixed(*cosine.shape), fixed(*sine.shape)],
+        + [once(*cosine.shape), once(*sine.shape)],
         out_specs=[
             fixed(2, rows, width // 2),
             pl.BlockSpec((1, rows, block), lambda i: (i // per_plane, 0, i % per_plane)),
@@ -343,7 +376,7 @@
             pltpu.VMEM((rows, width), bf16),
             pltpu.VMEM((width, LANES), bf16),
         ],
-        compiler_params=params("arbitrary"),
+        compiler_params=params(48, "arbitrary"),
         cost_estimate=cost(6 * rows * width * width, 6 * width * width + 10 * rows * width),
         name="qkv",
     )(meta, x, own, *parts, own_gains, *parts, cosine, sine)
@@ -378,7 +411,7 @@
 def attend_kernel(
     meta_ref, q_ref, k_ref, v_ref, k_up_ref, v_up_ref, k_down_ref, v_down_ref, out_ref, probs_ref
 ):
-    length = meta_ref[3 + pl.program_id(0)]
+    length = meta_ref[1 + pl.program_id(0)]
     rows, width = q_ref.shape[1:]
     first_head, low_mask, high_mask = head_masks()
     for lane in range(0, width, LANES):
@@ -418,7 +451,7 @@
         in_specs=[SMEM_SPEC, own(0), own(1), own(2), rim(0), rim(1), rim(0), rim(1)],
         out_specs=[flat, probs],
         out_shape=[jax.ShapeDtypeStruct((rows, width), bf16), probs_shape],
-        compiler_params=params("arbitrary", "arbitrary"),
+        compiler_params=params(48, "arbitrary", "arbitrary"),
         cost_estimate=cost(8 * rows * width * (BLOCK_Q + 2 * WIN), 10 * rows * width),
         name="attend",
     )(meta, qkv, qkv, qkv, rim_up, rim_up, rim_down, rim_down)
@@ -509,19 +542,19 @@
             pltpu.VMEM((seq_rows + 2 * WIN, LANES), f32),
             pltpu.VMEM((seq_rows + 2 * WIN, LANES), f32),
         ],
-        compiler_params=params("arbitrary", "arbitrary"),
+        compiler_params=params(48, "arbitrary", "arbitrary"),
         cost_estimate=cost(20 * rows * width * (BLOCK_Q + 2 * WIN), 20 * rows * width),
         name="attend_back",
     )(qkv, qkv, qkv, rim_up, rim_up, rim_down, rim_down, saved, grad_out, cosine, sine)
 
 
 def out_kernel(
-    meta_ref, o_ref, own_ref, p0, p1, p2, p3, x_ref, valid_ref, gains_ref,
+    meta_ref, o_ref, own_ref, p0, p1, p2, p3, q0, q1, q2, q3, x_ref, valid_ref, gains_ref,
     middle_ref, n_split_ref, o_split_ref, whole_ref, *, size,
 ):
     @pl.when(pl.program_id(0) == 0)
     def _():
-        assemble(meta_ref, whole_ref, own_ref, (p0, p1, p2, p3))
+        assemble_two(meta_ref, whole_ref, own_ref, (p0, p1, p2, p3), (q0, q1, q2, q3))
 
     values = o_ref[...]
     split_columns(values, o_split_ref, slice(None), size)
@@ -531,7 +564,7 @@
     split_columns((scaled * gains_ref[1:2, :]).astype(bf16), n_split_ref, slice(None), size)
 
 
-def out_call(meta, attended, own, parts, x, valid, gains):
+def out_call(meta, attended, own, parts, start, stretch, x, valid, gains):
     rows, width = x.shape
     slab = own.shape[0]
     size = width // slab
@@ -542,16 +575,16 @@
     return pl.pallas_call(
         functools.partial(out_kernel, size=size),
         grid=(rows // block,),
-        in_specs=[SMEM_SPEC, tile, fixed(slab, width)]
-        + part_specs(parts, width, lambda i: 0)
-        + [tile, pl.BlockSpec((block, 1), lambda i: (i, 0)), fixed(8, width)],
+        in_specs=[SMEM_SPEC, tile, once(slab, width)]
+        + stretch_specs(parts, start, stretch)
+        + [tile, pl.BlockSpec((block, 1), lambda i: (i, 0)), once(8, width)],
         out_specs=[tile, split, split],
         out_shape=[jax.ShapeDtypeStruct((rows, width), f32), split_shape, split_shape],
         scratch_shapes=[pltpu.VMEM((width, width), bf16)],
-        compiler_params=params("arbitrary"),
+        compiler_params=params(48, "arbitrary"),
         cost_estimate=cost(2 * rows * width * width, 2 * width * width + 12 * rows * width),
         name="out_norm",
-    )(meta, attended, own, *parts, x, valid, gains)
+    )(meta, attended, own, *parts, *parts, x, valid, gains)
 
 
 def gate_kernel(
@@ -576,10 +609,11 @@
     act_ref[...] = activated.astype(bf16)
 
 
-def gate_call(meta, normed, own1, parts1, own2, parts2, block):
+def gate_call(meta, normed, owns, parts, block):
     _, rows, half = normed.shape
     width = 2 * half
-    slab, hidden = own1.shape
+    slab, hidden = owns[0].shape
+    steps = hidden // block
     size = width // slab
     tile = pl.BlockSpec((rows, block), lambda i: (0, i))
     own = pl.BlockSpec((slab, block), lambda i: (0, i))
@@ -587,10 +621,10 @@
     return pl.pallas_call(
         functools.partial(gate_kernel, size=size),
         grid=(hidden // block,),
-        in_specs=[SMEM_SPEC, fixed(2, rows, half), own]
-        + part_specs(parts1, block, lambda i: i)
+        in_specs=[SMEM_SPEC, once(2, rows, half), own]
+        + part_specs(parts, block, lambda i: i)
         + [own]
-        + part_specs(parts2, block, lambda i: i),
+        + part_specs(parts, block, lambda i: i + steps),
         out_specs=[tile, tile, tile],
         out_shape=[shape, shape, shape],
         scratch_shapes=[
@@ -598,10 +632,10 @@
             pltpu.VMEM((width, block), bf16),
             pltpu.VMEM((width, block), bf16),
         ],
-        compiler_params=params("arbitrary"),
+        compiler_params=params(48, "arbitrary"),
         cost_estimate=cost(4 * rows * width * hidden, 4 * width * hidden + 6 * rows * hidden),
         name="gate",
-    )(meta, normed, own1, *parts1, own2, *parts2)
+    )(meta, normed, owns[0], *parts, owns[1], *parts)
 
 
 def gate_back_kernel(
@@ -656,7 +690,7 @@
     out_shape = jax.ShapeDtypeStruct((2, rows, hidden), bf16)
     settings = dict(
         grid=(hidden // block,),
-        compiler_params=params("arbitrary"),
+        compiler_params=params(48, "arbitrary"),
         cost_estimate=cost(2 * rows * width * hidden, 4 * width * hidden + 8 * rows * hidden),
         name="gate_back",
     )
@@ -664,7 +698,7 @@
         whole = whole_columns(own, parts, hidden - own.shape[0] * (parts[0].shape[0] + 1))
         out = pl.pallas_call(
             gate_back_plain_kernel,
-            in_specs=[fixed(rows, width), pl.BlockSpec((block, width), lambda i: (i, 0)), tile, tile],
+            in_specs=[once(rows, width), pl.BlockSpec((block, width), lambda i: (i, 0)), tile, tile],
             out_specs=out_spec,
             out_shape=out_shape,
             **settings,
@@ -672,8 +706,8 @@
         return out, whole
     return pl.pallas_call(
         functools.partial(gate_back_kernel, block=block),
-        in_specs=[SMEM_SPEC, fixed(rows, width), fixed(*own.shape)]
-        + [fixed(*part.shape) for part in parts]
+        in_specs=[SMEM_SPEC, once(rows, width), once(*own.shape)]
+        + [once(*part.shape) for part in parts]
         + [tile, tile],
         out_specs=[out_spec, fixed(hidden, width)],
         out_shape=[out_shape, jax.ShapeDtypeStruct((hidden, width), bf16)],
@@ -681,49 +715,194 @@
     )(meta, grad_result, own, *parts, slope, act)
 
 
-def down_kernel(meta_ref, m_ref, g_ref, *rest, mine, size, links):
-    add_ref = rest[0] if mine else None
-    out_ref, sums_ref = rest[-2:]
+def down_kernel(meta_ref, m_ref, g_ref, *rest, mine, size, links, hidden, cut, places):
     step = pl.program_id(0)
-    block, half = m_ref.shape[1], sums_ref.shape[1]
+    block, half = m_ref.shape[1], g_ref.shape[1] // 2
     which = meta_ref[2] if mine else 1 - meta_ref[2]
     right = g_ref[:, pl.ds(pl.multiple_of(which * half, half), half)]
-    sums_ref[pl.ds(pl.multiple_of(step * block, block), block), :] = tokens_dot(m_ref[...], right)
-
-    @pl.when(step == pl.num_programs(0) - 1)
-    def _():
-        rows, columns = out_ref.shape[2:]
+    sums = tokens_dot(m_ref[...], right)
+    rows, columns = hidden // size, half // links
+
+    def put(first):
         for place in range(size):
+            top, end = max(place * rows, first), min((place + 1) * rows, first + block)
+            if top >= end:
+                continue
             for link in range(links):
-                value = sums_ref[place * rows : (place + 1) * rows, link * columns : (link + 1) * columns]
-                if mine:
-                    value = value + add_ref[place, link].astype(f32)
-                out_ref[place, link] = value.astype(bf16)
+                value = sums[top - first : end - first, link * columns : (link + 1) * columns]
+                rest[-1][place, link, top - place * rows : end - place * rows, :] = value.astype(bf16)
+
+    for number in range(-(-hidden // block)):
+        pl.when(step == number)(functools.partial(put, number * block))
+
+    if mine:
+        add_ref, keep0, give0, keep1, give1, state_ref = rest
+
+        @pl.when(step == pl.num_programs(0) - 1)
+        def _():
+            for part, (keep_ref, give_ref) in enumerate(((keep0, give0), (keep1, give1))):
+                span = slice(0, cut) if part == 0 else slice(cut, rows)
+                own = meta_ref[3 + part]
+                for place in range(size):
+                    for number in range(links // 2):
+                        base = split_index(number, places[part])
+                        for ref, value in ((keep_ref, own), (give_ref, 1 - own)):
+                            link = base + value * (1 << places[part])
+                            ref[place, number] = added(
+                                state_ref[place, link, span, :], add_ref[place, link, span, :]
+                            )
+
+
+def first_places():
+    return [left.index(bit) for left, bit in zip(bits_left(0), link_orders()[0])]
 
 
 def down_call(meta, mixed, grad_result, size, hidden, block, add=None):
     rows, hidden_pad = mixed.shape
     width = grad_result.shape[1]
     links = 1 << link_count()
-    shape = (size, links, hidden // size, width // 2 // links)
-    extra = [] if add is None else [add]
-    return pl.pallas_call(
-        functools.partial(down_kernel, mine=add is not None, size=size, links=links),
+    shard = hidden // size
+    cut = half_rows(shard)
+    columns = width // 2 // links
+    shape = (size, links, shard, columns)
+    mine = add is not None
+    parts = [(size, links // 2, height, columns) for height in (cut, cut, shard - cut, shard - cut)]
+    out = pl.pallas_call(
+        functools.partial(
+            down_kernel, mine=mine, size=size, links=links, hidden=hidden, cut=cut, places=first_places()
+        ),
         grid=(hidden_pad // block,),
-        in_specs=[SMEM_SPEC, pl.BlockSpec((rows, block), lambda i: (0, i)), fixed(rows, width)]
-        + [fixed(*shape) for _ in extra],
-        out_specs=fixed(*shape),
-        out_shape=jax.ShapeDtypeStruct(shape, bf16),
-        scratch_shapes=[pltpu.VMEM((hidden_pad, width // 2), f32)],
-        compiler_params=params("arbitrary"),
+        in_specs=[SMEM_SPEC, pl.BlockSpec((rows, block), lambda i: (0, i)), once(rows, width)]
+        + ([once(*shape)] if mine else []),
+        out_specs=[fixed(*part) for part in parts] if mine else fixed(*shape),
+        out_shape=[jax.ShapeDtypeStruct(part, bf16) for part in parts]
+        if mine
+        else jax.ShapeDtypeStruct(shape, bf16),
+        scratch_shapes=[pltpu.VMEM(shape, bf16)] if mine else [],
+        compiler_params=params(24, "arbitrary"),
         cost_estimate=cost(rows * width * hidden, width * hidden + 2 * rows * (hidden + width)),
         name="down_sum",
-    )(meta, mixed, grad_result, *extra)
+    )(meta, mixed, grad_result, *([add] if mine else []))
+    return [(out[0], out[1]), (out[2], out[3])] if mine else out
+
+
+def sum_kernel(meta_ref, left_ref, right_ref, add_ref, keep0, give0, keep1, give1, state_ref, *, size, links, places):
+    state_ref[...] = (tokens_dot(left_ref[meta_ref[2]], right_ref[...]) + add_ref[...].astype(f32)).astype(bf16)
+    rows = state_ref.shape[0] // (2 * size * links)
+    for part, (keep_ref, give_ref) in enumerate(((keep0, give0), (keep1, give1))):
+        own = meta_ref[3 + part]
+        for place in range(size):
+            for number in range(links // 2):
+                base = (2 * place + part) * links + split_index(number, places[part])
+                for ref, value in ((keep_ref, own), (give_ref, 1 - own)):
+                    start = (base + value * (1 << places[part])) * rows
+                    ref[place, number] = state_ref[pl.ds(pl.multiple_of(start, rows), rows), :]
+
+
+def sum_call(meta, left, right, add, block):
+    _, tokens, height = left.shape
+    width = right.shape[1]
+    size = lax.axis_size("fsdp")
+    links = 1 << link_count()
+    rows = height // (2 * size * links)
+    if rows % 16:
+        state = (tokens_dot(half_of(left, True), right) + add.astype(f32)).astype(bf16)
+        state = state.reshape(size, 2, links, rows, width)
+        return [halves(state[:, part], 0, part) for part in range(2)]
+    shape = (size, links // 2, rows, width)
+    out = pl.pallas_call(
+        functools.partial(sum_kernel, size=size, links=links, places=first_places()),
+        grid=(width // block,),
+        in_specs=[
+            SMEM_SPEC,
+            once(2, tokens, height),
+            pl.BlockSpec((tokens, block), lambda i: (0, i)),
+            pl.BlockSpec((height, block), lambda i: (0, i)),
+        ],
+        out_specs=[pl.BlockSpec((size, links // 2, rows, block), lambda i: (0, 0, 0, i))] * 4,
+        out_shape=[jax.ShapeDtypeStruct(shape, bf16)] * 4,
+        scratch_shapes=[pltpu.VMEM((height, block), bf16)],
+        compiler_params=params(12, "arbitrary"),
+        cost_estimate=cost(2 * tokens * height * width, 4 * height * width + 4 * tokens * width),
+        name="sum_rows",
+    )(meta, left, right, add)
+    return [(out[0], out[1]), (out[2], out[3])]
+
+
+def fold_kernel(meta_ref, *refs, count, done, places):
+    ins, outs = refs[: 4 * count], refs[4 * count :]
+    for part in range(2):
+        own = meta_ref[3 + 2 * done + part]
+        start = 0
+        for number in range(count):
+            keep_ref, got_ref = ins[4 * number + 2 * part], ins[4 * number + 2 * part + 1]
+            width = keep_ref.shape[3]
+            for index in range(keep_ref.shape[1] // 2):
+                base = split_index(index, places[part])
+                for ref, value in ((outs[2 * part], own), (outs[2 * part + 1], 1 - own)):
+                    link = base + value * (1 << places[part])
+                    ref[0, index, :, start : start + width] = added(keep_ref[0, link], got_ref[0, link])
+            start += width
+
+
+def fold_next(meta, blocks, done):
+    size = blocks[0][0][0].shape[0]
+    places = [left.index(bit) for left, bit in zip(bits_left(done), link_orders()[done])]
+    flat = [array for block in blocks for pair in block for array in pair]
+    shapes = []
+    for part in range(2):
+        _, links, rows, _ = blocks[0][part][0].shape
+        width = sum(block[part][0].shape[3] for block in blocks)
+        shapes += [(size, links // 2, rows, width)] * 2
+    if any(shape[2] % 16 for shape in shapes):
+        result = []
+        for part in range(2):
+            state = jnp.concatenate([added(*block[part]) for block in blocks], axis=3)
+            result.append(halves(state, done, part))
+        return result
+    spec = lambda shape: pl.BlockSpec((1,) + tuple(shape[1:]), lambda i: (i, 0, 0, 0))
+    out = pl.pallas_call(
+        functools.partial(fold_kernel, count=len(blocks), done=done, places=places),
+        grid=(size,),
+        in_specs=[SMEM_SPEC] + [spec(array.shape) for array in flat],
+        out_specs=[spec(shape) for shape in shapes],
+        out_shape=[jax.ShapeDtypeStruct(shape, bf16) for shape in shapes],
+        compiler_params=params(6, "arbitrary"),
+        cost_estimate=cost(0, 3 * sum(array.size for array in flat)),
+        name="fold",
+    )(meta, *flat)
+    return [(out[0], out[1]), (out[2], out[3])]
+
+
+def last_kernel(*refs):
+    k0, g0, k1, g1, out_ref = refs
+    cut = k0.shape[2]
+    out_ref[0, :cut, :] = added(k0[0, 0], g0[0, 0])
+    out_ref[0, cut:, :] = added(k1[0, 0], g1[0, 0])
+
+
+def fold_last(parts):
+    (k0, g0), (k1, g1) = parts
+    size, _, cut, width = k0.shape
+    rows = cut + k1.shape[2]
+    if cut % 16 or k1.shape[2] % 16:
+        return jnp.concatenate([added(k0, g0)[:, 0], added(k1, g1)[:, 0]], axis=1)
+    spec = lambda array: pl.BlockSpec((1,) + array.shape[1:], lambda i: (i, 0, 0, 0))
+    return pl.pallas_call(
+        last_kernel,
+        grid=(size,),
+        in_specs=[spec(array) for array in (k0, g0, k1, g1)],
+        out_specs=pl.BlockSpec((1, rows, width), lambda i: (i, 0, 0)),
+        out_shape=jax.ShapeDtypeStruct((size, rows, width), bf16),
+        compiler_params=params(6, "arbitrary"),
+        cost_estimate=cost(0, 6 * size * rows * width),
+        name="fold_last",
+    )(k0, g0, k1, g1)
 
 
 def middle_back_kernel(
     meta_ref, gu_ref, own1_ref, p0, p1, p2, p3, own2_ref, q0, q1, q2, q3, out_own_ref, r0, r1, r2, r3,
-    middle_ref, upstream_ref, valid_ref, gains_ref, grad_ref, branch_ref, att_ref,
+    s0, s1, s2, s3, middle_ref, upstream_ref, valid_ref, gains_ref, grad_ref, branch_ref, att_ref,
     acc, first_ref, second_ref, out_ref,
 ):
     step = pl.program_id(0)
@@ -734,7 +913,7 @@
     @pl.when(step == 0)
     def _():
         acc[...] = total
-        assemble(meta_ref, out_ref, out_own_ref, (r0, r1, r2, r3))
+        assemble_two(meta_ref, out_ref, out_own_ref, (r0, r1, r2, r3), (s0, s1, s2, s3))
 
     @pl.when(step > 0)
     def _():
@@ -755,11 +934,12 @@
 
 
 def middle_back_call(
-    meta, grad_hidden, own1, parts1, own2, parts2, out_own, out_parts, middle, upstream, valid, gains, block
+    meta, grad_hidden, owns, parts, out_own, middle, upstream, valid, gains, block
 ):
     rows, width = middle.shape
-    slab = own1.shape[0]
+    slab = owns[0].shape[0]
     hidden = grad_hidden.shape[2]
+    steps = hidden // block
     whole = fixed(rows, width)
     own = pl.BlockSpec((slab, block), lambda i: (0, i))
     flat_low = jax.ShapeDtypeStruct((rows, width), bf16)
@@ -767,12 +947,12 @@
         middle_back_kernel,
         grid=(hidden // block,),
         in_specs=[SMEM_SPEC, pl.BlockSpec((2, rows, block), lambda i: (0, 0, i)), own]
-        + part_specs(parts1, block, lambda i: i)
+        + part_specs(parts, block, lambda i: i)
         + [own]
-        + part_specs(parts2, block, lambda i: i)
-        + [fixed(slab, width)]
-        + part_specs(out_parts, width, lambda i: 0)
-        + [whole, whole, fixed(rows, 1), fixed(8, width)],
+        + part_specs(parts, block, lambda i: i + steps)
+        + [once(slab, width)]
+        + stretch_specs(parts, 2 * hidden, block)
+        + [whole, whole, once(rows, 1), once(8, width)],
         out_specs=[whole, whole, whole],
         out_shape=[jax.ShapeDtypeStruct((rows, width), f32), flat_low, flat_low],
         scratch_shapes=[
@@ -781,10 +961,10 @@
             pltpu.VMEM((width, block), bf16),
             pltpu.VMEM((width, width), bf16),
         ],
-        compiler_params=params("arbitrary"),
+        compiler_params=params(40, "arbitrary"),
         cost_estimate=cost(4 * rows * width * hidden, 4 * width * hidden + 4 * rows * hidden + 12 * rows * width),
         name="middle_back",
-    )(meta, grad_hidden, own1, *parts1, own2, *parts2, out_own, *out_parts, middle, upstream, valid, gains)
+    )(meta, grad_hidden, owns[0], *parts, owns[1], *parts, out_own, *parts, *parts, middle, upstream, valid, gains)
 
 
 def input_back_kernel(
@@ -826,11 +1006,11 @@
             pl.BlockSpec((slab, block), lambda i: (0, i)),
         ]
         + part_specs(parts, block, lambda i: i)
-        + [whole, whole, fixed(8, width)],
+        + [whole, whole, once(8, width)],
         out_specs=whole,
         out_shape=jax.ShapeDtypeStruct((rows, width), bf16),
         scratch_shapes=[pltpu.VMEM((rows, width), f32), pltpu.VMEM((width, block), bf16)],
-        compiler_params=params("arbitrary"),
+        compiler_params=params(48, "arbitrary"),
         cost_estimate=cost(6 * rows * width * width, 6 * width * width + 14 * rows * width),
         name="input_back",
     )(meta, grad_joint, own, *parts, x, grad_middle, gains)
@@ -853,116 +1033,124 @@
     size = lax.axis_size("fsdp")
     me = lax.axis_index("fsdp")
     hidden = w_in.shape[1] // 2
-    hidden_pad = -(-hidden // 384) * 384
+    block = 896
+    hidden_pad = -(-hidden // block) * block
     pad = hidden_pad - hidden
-    block = 896 if hidden_pad % 896 == 0 else 384
     steps = link_orders()
+    near, far, middle_way = runs()
 
     gains = jnp.pad(jnp.stack([norm_first, norm_second], axis=1), ((0, 0), (0, LANES - 2)))
-    came_one = turned_before(row_piece([w_qkv, gains]))
+    came_one = turned_before(row_piece([w_qkv, gains]), range(1, size))
     own_in = [jnp.pad(w_in[:, half * hidden :][:, :hidden], ((0, 0), (0, pad))) for half in range(2)]
-    piece_two = row_piece([own_in[0], w_out])
-    piece_three = row_piece([own_in[1]])
-    piece_four = column_piece(w_down)
-
+    piece_two = row_piece([own_in[0], own_in[1], w_out])
+    piece_three = column_piece(w_down)
     first_row = me * shard_rows
     query_pos = first_row + jnp.arange(shard_rows, dtype=jnp.int32)
     rim_pos = first_row - WIN + jnp.arange(shard_rows + 2 * WIN, dtype=jnp.int32)
     cosine, sine = rope_tables(rim_pos)
     valid = (query_pos[None, :] < lengths[:, None]).astype(f32).reshape(rows, 1)
-    meta = jnp.concatenate([jnp.stack([first_row, me, bit_value(0)]).astype(jnp.int32), lengths.astype(jnp.int32)])
+    bits = [bit_value(bit) for pair in steps for bit in pair]
+    meta = jnp.stack([first_row, me, bit_value(0)] + bits).astype(jnp.int32)
+    meta_rows = jnp.concatenate([first_row.astype(jnp.int32)[None], lengths.astype(jnp.int32)])
     x = inputs.reshape(rows, width)
     upstream = cotangent.reshape(rows, width)
     grad_result = (upstream.astype(f32) * valid).astype(bf16)
-
-    came_one, piece_two, piece_three, piece_four, own_in, cosine, sine, grad_result = after(
-        (came_one, piece_two, piece_three, piece_four, own_in, cosine, sine, grad_result)
-    )
-    came_two = turned_before(piece_two)
-    one = row_states(came_one)
-    for bits in steps:
-        one = after(widen(one, bits, 1))
-    one, came_two = after((one, came_two))
+    own_rows = slice(WIN, WIN + shard_rows)
+    own_cosine, own_sine = cosine[own_rows], sine[own_rows]
+    came_one, piece_two, piece_three, own_in, gains, cosine, sine, own_cosine, own_sine, grad_result, valid = after(
+        (came_one, piece_two, piece_three, own_in, gains, cosine, sine, own_cosine, own_sine, grad_result, valid)
+    )
+
+    one = widen(row_states(came_one), steps[0], 1)
+    came_two = turned_before(piece_two, near)
+    one, came_two, piece_two = after((one, came_two, piece_two))
+
+    for bits in steps[1:]:
+        one = widen(one, bits, 1)
+    came_two = came_two + turned_before(piece_two, far)
+    one, came_two, piece_two = after((one, came_two, piece_two))
+
     parts_one = row_parts(one)
-    two = widen(row_states(came_two), steps[0], 1)
-    parts_one, piece_three = after((parts_one, piece_three))
-    came_three = turned_before(piece_three)
-
-    own_rows = slice(WIN, WIN + shard_rows)
-    normed_first, qkv, gains_all = qkv_call(meta, x, w_qkv, parts_one, gains, cosine[own_rows], sine[own_rows])
-    two, qkv = after((two, qkv))
+    came_two = came_two + turned_before(piece_two, middle_way)
+    normed_first, qkv, gains_all = qkv_call(meta, x, w_qkv, parts_one, gains, own_cosine, own_sine)
     by_seq = qkv.reshape(3, seqs, shard_rows, width)[1:]
     edge = (2, seqs * WIN, width)
-    edge_up, edge_down, came_three = after(
-        (by_seq[:, :, :WIN].reshape(edge), by_seq[:, :, shard_rows - WIN :].reshape(edge), came_three)
-    )
+    edge_up, edge_down = by_seq[:, :, :WIN].reshape(edge), by_seq[:, :, shard_rows - WIN :].reshape(edge)
+    qkv, edge_up, edge_down, came_two, piece_three = after((qkv, edge_up, edge_down, came_two, piece_three))
+
     rim_down, rim_up = neighbours(edge_up, edge_down)
+    two = widen(in_turn(row_states, came_two), steps[0], 1)
+    rim_down, rim_up, two, piece_three = after((rim_down, rim_up, two, piece_three))
+
     for bits in steps[1:]:
         two = widen(two, bits, 1)
-    rim_down, rim_up, piece_four = after((rim_down, rim_up, piece_four))
-    came_four = turned_before(piece_four)
-    attended, saved = attend_call(meta, qkv, rim_up, rim_down, seqs)
-    two, attended = after((two, attended))
-    parts_two = after(row_parts(two))
-    parts_in_one = [part[:, :, :hidden_pad] for part in parts_two]
-    parts_out = [part[:, :, hidden_pad:] for part in parts_two]
-    three = widen(row_states(after(came_three, parts_two)), steps[0], 1)
-    middle, normed_second, attended_split = out_call(meta, attended, w_out, parts_out, x, valid, gains_all)
-    three, middle, normed_second = after((three, middle, normed_second))
+    came_three = turned_before(piece_three, range(1, size))
+    attended, saved = attend_call(meta_rows, qkv, rim_up, rim_down, seqs)
+    two, came_three, attended = after((two, came_three, attended))
+
+    parts_two = row_parts(two)
+    three = widen(column_states(came_three), steps[0], 1)
+    parts_two, three, attended = after((parts_two, three, attended))
+
     for bits in steps[1:]:
         three = widen(three, bits, 1)
-    three, came_four = after((three, came_four))
-    parts_three = after(row_parts(three))
-    four = widen(column_states(came_four), steps[0], 1)
-    mixed, slope, act = gate_call(meta, normed_second, own_in[0], parts_in_one, own_in[1], parts_three, block)
-    four, mixed = after((four, mixed))
-    for bits in steps[1:]:
-        four = widen(four, bits, 1)
-
+    middle, normed_second, attended_split = out_call(
+        meta, attended, w_out, parts_two, 2 * hidden_pad, block, x, valid, gains_all
+    )
+    mixed, slope, act = gate_call(meta, normed_second, own_in, parts_two, block)
+    three, mixed, slope, act, normed_second = after((three, mixed, slope, act, normed_second))
+
+    parts_three = column_parts(three)
     down_give = down_call(meta, mixed, grad_result, size, hidden, block)
     down_got = flip(down_give, 0)
-    four, down_got = after((four, down_got))
-    parts_four = column_parts(four)
+    parts_three, down_got, slope, mixed = after((parts_three, down_got, slope, mixed))
+
     down = down_call(meta, mixed, grad_result, size, hidden, block, down_got)
-    parts_four, down = after((parts_four, down))
-    down = down.reshape((size,) + (2,) * link_count() + down.shape[2:])
-    cut = half_rows(hidden // size)
-    down = [[down[..., :cut, :]], [down[..., cut:, :]]]
-    down = [fold(part, 1, bit) for part, bit in zip(down, steps[0])]
-    grad_hidden, whole_down = gate_back_call(meta, grad_result, w_down, parts_four, slope, act, block)
-
+    down, slope, mixed = after((down, slope, mixed))
+
+    down = swap(down, 0)
+    grad_hidden, whole_down = gate_back_call(meta, grad_result, w_down, parts_three, slope, act, block)
     give_left = half_of(normed_second, False)
     in_give = [tokens_dot(give_left, grad_hidden[half]).astype(bf16) for half in range(2)]
-    down, in_give, grad_hidden = after((down, in_give, grad_hidden))
+    down, in_give, grad_hidden, whole_down, mixed, normed_second = after(
+        (down, in_give, grad_hidden, whole_down, mixed, normed_second)
+    )
+
     in_got = [flip(give, 0) for give in in_give]
-    for bits in steps[1:]:
-        down = [fold(part, 1, bit) for part, bit in zip(down, bits)]
-    keep_left = half_of(normed_second, True)
-    in_state = [
-        (tokens_dot(keep_left, grad_hidden[half]) + in_got[half].astype(f32)).astype(bf16)
-        for half in range(2)
-    ]
-    down, in_state, grad_hidden = after((down, in_state, grad_hidden))
-    ins = [fold(part, 1, bit) for part, bit in zip(row_blocks(in_state), steps[0])]
-    owned_down = scattered(
-        jnp.concatenate([part[0].reshape((size,) + part[0].shape[-2:]) for part in down], axis=1)
-    )
+    for done in range(1, len(steps)):
+        down = swap(fold_next(meta, [down], done), done)
+    result = jnp.dot(mixed, whole_down, preferred_element_type=f32)
+    output = (middle + valid * result).astype(bf16)
+    in_got, output, grad_hidden, normed_second, down = after((in_got, output, grad_hidden, normed_second, down))
+
+    one, two = [sum_call(meta, normed_second, grad_hidden[half], in_got[half], block) for half in range(2)]
+    one, two, grad_hidden = after((one, two, grad_hidden))
+
+    one = swap(one, 0)
+    down_slots = fold_last(down)
+    down_came = turned_slots(down_slots, range(1, size))
     grad_middle, grad_branch, grad_att = middle_back_call(
-        meta, grad_hidden, own_in[0], parts_in_one, own_in[1], parts_three, w_out, parts_out,
-        middle, upstream, valid, gains_all, block,
-    )
+        meta, grad_hidden, own_in, parts_two, w_out, middle, upstream, valid, gains_all, block
+    )
+    one, two, down_came, grad_branch, grad_att = after((one, two, down_came, grad_branch, grad_att))
+
+    two = swap(two, 0)
+    for done in range(1, len(steps)):
+        one = swap(fold_next(meta, [one], done), done)
     out_give = tokens_dot(half_of(attended_split, False), grad_branch).astype(bf16)
     out_got, grad_branch, grad_att = after((flip(out_give, 0), grad_branch, grad_att))
-    out_state = (tokens_dot(half_of(attended_split, True), grad_branch) + out_got.astype(f32)).astype(bf16)
-    grad_att, out_state, owned_down = after((grad_att, out_state, owned_down))
-    all_down = lax.all_gather(owned_down, "rep", axis=0)
+    outs = sum_call(meta, attended_split, grad_branch, out_got, width // 2)
+    grad_att, outs = after((grad_att, outs))
     grad_q, grad_k, grad_v, edge_up, edge_down = attend_back_call(
         qkv, rim_up, rim_down, saved, grad_att, cosine, sine, seqs
     )
-    ins, edge_up, edge_down = after((ins, edge_up, edge_down))
+    one, two, outs, edge_up, edge_down, grad_q = after((one, two, outs, edge_up, edge_down, grad_q))
+
+    for done in range(1, len(steps)):
+        two = swap(fold_next(meta, [two], done), done)
     from_next, from_before = neighbours(edge_up, edge_down)
-    for bits in steps[1:]:
-        ins = [fold(part, 1, bit) for part, bit in zip(ins, bits)]
+    one_slots = fold_last(one)
+    from_next, from_before, two, one_slots, outs = after((from_next, from_before, two, one_slots, outs))
 
     def with_edges(own, plane):
         own = own.reshape(seqs, shard_rows, width)
@@ -972,53 +1160,73 @@
         own = own + jnp.pad(before, rest) + jnp.pad(later, (rest[0], rest[1][::-1], rest[2]))
         return own.reshape(rows, width).astype(bf16)
 
+    outs = swap(outs, 0)
+    one_came = turned_slots(one_slots, near) + turned_slots(one_slots, far)
     grad_joint = jnp.concatenate([grad_q, with_edges(grad_k, 0), with_edges(grad_v, 1)], axis=1)
     give_left = half_of(normed_first, False)
     qkv_give = tokens_dot(give_left, grad_joint).astype(bf16)
     qkv_got, grad_last = after((flip(qkv_give, 0), grad_joint))
-    keep_left = half_of(normed_first, True)
-    qkv_state = (tokens_dot(keep_left, grad_last) + qkv_got.astype(f32)).astype(bf16)
-    ins, out_state, qkv_state, grad_last, mixed = after((ins, out_state, qkv_state, grad_last, mixed))
-    last = [fold(part, 1, bit) for part, bit in zip(row_blocks([qkv_state, out_state]), steps[0])]
-
-    def slots(parts):
-        return jnp.stack(
-            [
-                jnp.concatenate([piece.reshape(size, -1, piece.shape[-1]) for piece in part], axis=-1)
-                for part in parts
-            ],
-            axis=1,
-        )
-
-    owned_in = scattered(slots(ins))
+    last = sum_call(meta, normed_first, grad_last, qkv_got, width)
+    two_slots = fold_last(two)
+    last, grad_last, outs, one_came, two_slots, one_slots = after(
+        (last, grad_last, outs, one_came, two_slots, one_slots)
+    )
+
+    last = swap(last, 0)
+    one_came = one_came + turned_slots(one_slots, middle_way)
+    two_came = turned_slots(two_slots, near) + turned_slots(two_slots, far)
     grad_inputs = input_back_call(meta, grad_last, w_qkv, parts_one, x, grad_middle, gains_all)
-    last, grad_inputs, mixed = after((last, grad_inputs, mixed))
+    last, grad_inputs, one_came, two_came, one_slots, two_slots = after(
+        (last, grad_inputs, one_came, two_came, one_slots, two_slots)
+    )
+
+    def spread_start(owned, cut):
+        ones = (1,) * link_count()
+        return [part.reshape(ones + part.shape) for part in (owned[:cut], owned[cut:])]
+
+    def spread_end(states):
+        mine = jnp.stack([state.reshape((-1,) + state.shape[-2:]) for state in states])
+        whole = in_order(mine[None], flip(mine, 0)[None], 0, 0)
+        return whole.reshape(-1, mine.shape[-1])
+
+    last = [last, outs]
+    for done in range(1, len(steps)):
+        last = [swap(fold_next(meta, last, done), done)]
+    two_came = two_came + turned_slots(two_slots, middle_way)
+    owned_down = slot_sum(down_slots, down_came)
+    spread_down = widen(spread_start(owned_down, half_rows(hidden // size)), steps[0], 0)
+    owned_one = slot_sum(one_slots, one_came)
+    last, two_came, owned_one, spread_down = after((last, two_came, owned_one, spread_down))
+
+    last_slots = fold_last(last[0])
+    last_came = turned_slots(last_slots, near) + turned_slots(last_slots, far)
+    owned_in = jnp.concatenate([owned_one, slot_sum(two_slots, two_came)], axis=1)
+    spread_in = widen(spread_start(owned_in, owned_in.shape[0] // 2), steps[0], 0)
+    last_came, spread_in, last_slots, spread_down = after((last_came, spread_in, last_slots, spread_down))
+
+    last_came = last_came + turned_slots(last_slots, middle_way)
     for bits in steps[1:]:
-        last = [fold(part, 1, bit) for part, bit in zip(last, bits)]
-    result = jnp.dot(mixed, whole_down, preferred_element_type=f32)
-    output = (middle + valid * result).astype(bf16)
-    last, output, owned_in, all_down = after((last, output, owned_in, all_down))
-    owned_last = to_owner(slots(last))
-
-    links = 1 << link_count()
-
-    def spread(owned):
-        ones = (1,) * link_count()
-        states = [owned[part].reshape(ones + owned.shape[1:]) for part in range(2)]
-        for bits in steps:
-            states = widen(states, bits, 0)
-        mine = jnp.stack([state.reshape((-1,) + owned.shape[1:]) for state in states])
-        return in_order(mine[None], flip(mine, 0)[None], 0, 0).reshape(-1, owned.shape[-1])
-
-    grad_down = all_down.reshape(links, 2, hidden // size, -1)
-    grad_down = jnp.transpose(grad_down, (2, 1, 0, 3)).reshape(hidden // size, width).astype(f32)
-    grad_mid = spread(owned_in)
+        spread_in = widen(spread_in, bits, 0)
+        spread_down = widen(spread_down, bits, 0)
+    last_came, spread_in, last_slots, spread_down = after((last_came, spread_in, last_slots, spread_down))
+
+    owned_last = slot_sum(last_slots, last_came)
+    spread_last = widen(spread_start(owned_last, owned_last.shape[0] // 2), steps[0], 0)
+    down_mine = jnp.concatenate([state.reshape((-1,) + state.shape[-2:]) for state in spread_down], axis=1)
+    grad_down = in_order(down_mine, flip(down_mine, 0), 0, 0)
+    grad_in = spread_end(spread_in)
+    spread_last, grad_in, grad_down = after((spread_last, grad_in, grad_down))
+
+    for bits in steps[1:]:
+        spread_last = widen(spread_last, bits, 0)
+    spread_last, grad_in, grad_down = after((spread_last, grad_in, grad_down))
+
+    grad_last = spread_end(spread_last)
     grad_in = jnp.concatenate(
-        [grad_mid[:, :hidden], grad_mid[:, hidden_pad : hidden_pad + hidden]], axis=1
+        [grad_in[:, :hidden], grad_in[:, hidden_pad : hidden_pad + hidden]], axis=1
     ).astype(f32)
     grad_second = jnp.sum(grad_in * w_in.astype(f32), axis=1) / norm_second.astype(f32)
-    owned_last, grad_in, grad_down, grad_second = after((owned_last, grad_in, grad_down, grad_second))
-    grad_last = spread(owned_last)
+    grad_down = jnp.transpose(grad_down, (1, 0, 2)).reshape(hidden // size, width).astype(f32)
     grad_qkv = grad_last[:, : 3 * width].astype(f32)
     grad_out = grad_last[:, 3 * width :].astype(f32)
     grad_first = jnp.sum(grad_qkv * w_qkv.astype(f32), axis=1) / norm_first.astype(f32)

time: 504 us -> 435 us (0.86)
  waiting for transfers between devices: 174 us -> 108 us
  Pallas kernels: 106 us -> 124 us
  other arithmetic: 41.1 us -> 26.3 us
  between operations: 16.4 us -> 3.13 us
  matrix products: 26.2 us -> 13.8 us
  starting transfers between devices: 89.8 us -> 99.6 us
  local copies, waits for them, and re-layouts: 42.6 us -> 51.8 us
    ppermute x51 -> x56, waiting for transfers between devices: 124 us -> 79.6 us  [flip(): return lax.ppermute(value, 'rep', [(i, i ^ 1 << bit) for i in range(size)])]
    unnamed x177 -> x242, local copies, waits for them, and re-layouts: 11.5 us -> 37.7 us
    pallas_call x2 -> x14, Pallas kernels: 9.39 us -> 30 us  [the longest x4 13.9 us: sum_call(): pl.pallas_call(functools.partial(sum_kernel, size=size, links=links, plac...]
    reduce_scatter x2 -> x0, waiting for transfers between devices: 15 us -> none  [scattered(): lax.psum_scatter(state.reshape(-1, state.shape[-1]), 'fsdp', scatter_dime...]
    convert_element_type x19 -> x5, other arithmetic: 16.4 us -> 3.6 us  [the longest x1 1.86 us: on_device(): jnp.transpose(grad_down, (1, 0, 2)).reshape(hidden // size, width)]
    ppermute x2, waiting for transfers between devices: 12 us -> 1.65 us  [neighbours(): lax.ppermute(up, 'fsdp', backward)]
    ppermute x15 -> x21, starting transfers between devices: 31.8 us -> 41.7 us  [turn(): lax.ppermute(value, 'fsdp', [(i, (i + steps) % size) for i in range(size)])]
    dot_general x8 -> x4, matrix products: 19.4 us -> 9.59 us  [tokens_dot(): lax.dot_general(left, right, (((0,), (0,)), ((), ())), preferred_element_...]
  transfers between devices with their start and end apart: 73 -> 81, of which waited for: 39 -> 36; matrix products, arithmetic and copies ran while one was open for 14% -> 9% of each run, Pallas kernels for 18% -> 25%
where the time goes in v3:
time: 435 us; the launch traced here: 427 us
  Pallas kernels  124 us (29%)
  waiting for transfers between devices  108 us (25%)
  starting transfers between devices  99.6 us (23%)
  local copies, waits for them, and re-layouts  51.8 us (12%)
  other arithmetic  26.3 us (6%)
  matrix products  13.8 us (3%)
    ppermute x56, waiting for transfers between devices, flip(): return lax.ppermute(value, 'rep', [(i, i ^ 1 << bit) for i in range(size)])  79.6 us
    ppermute x56, starting transfers between devices, flip(): return lax.ppermute(value, 'rep', [(i, i ^ 1 << bit) for i in range(size)])  45.8 us
    ppermute x21, starting transfers between devices, turn(): lax.ppermute(value, 'fsdp', [(i, (i + steps) % size) for i in range(size)])  41.7 us
    unnamed x242, local copies, waits for them, and re-layouts  37.7 us
    ppermute x21, waiting for transfers between devices, turn(): lax.ppermute(value, 'fsdp', [(i, (i + steps) % size) for i in range(size)])  26 us
    pallas_call x1, Pallas kernels, attend_back_call(): pl.pallas_call(attend_back_kernel, grid=(seqs, width // block), in_specs=...  17.7 us
    pallas_call x1, Pallas kernels, middle_back_call(): pl.pallas_call(middle_back_kernel, grid=(hidden // block,), in_specs=[SME...  14.9 us
    pallas_call x4, Pallas kernels, sum_call(): pl.pallas_call(functools.partial(sum_kernel, size=size, links=links, plac...  13.9 us
  transfers between devices with their start and end apart: 81, of which 36 were waited for; matrix products, arithmetic and copies ran while one was open for 9% of the time, Pallas kernels for 25%

profile of v3, /device:TPU:0, one launch (start us, length us, event | category | flops | bytes accessed | tf_op | source)
XLA Modules:
  0.0 427.1 jit_solution(7182656907699159751)
XLA Ops:
  4.4 3.0 collective-permute-start
  7.4 2.6 collective-permute-start.1
  21.3 2.4 collective-permute-done.1
  28.9 4.9 %collective-permute-start.5 = (bf16[2,16,6400]{2,1,0:T(8,128)(2,1)S(1)}, bf16[2,16,6400]{2,1,0:T(8,128)(2,1)S(1)}, u32[]{:S(2)}, u32[]{:S(2)}) collective-permute-start(bf16[2,16,6400]{2,1,0:T(8,128)(2,1)S(1)} %maximum_bitcast_fusion.2), channel_id=1, source_target_pairs={{0,1},{1,2},{2,3},{3,0},{4,5},{5,6},{6,7},{7,4},{8,9},{9,10},{10,1... | collective-permute-start | bytes 1228808 | tf_op jit(solution)/shard_map/ppermute | solution.py:50
  36.4 6.4 %collective-permute-done.5 = bf16[2,16,6400]{2,1,0:T(8,128)(2,1)S(1)} collective-permute-done((bf16[2,16,6400]{2,1,0:T(8,128)(2,1)S(1)}, bf16[2,16,6400]{2,1,0:T(8,128)(2,1)S(1)}, u32[]{:S(2)}, u32[]{:S(2)}) %collective-permute-start.5) | collective-permute-done | bytes 409632 | tf_op jit(solution)/shard_map/ppermute | solution.py:50
  45.7 10.8 %collective-permute-done.7 = bf16[3,2,1,16,3200]{4,3,2,1,0:T(8,128)(2,1)S(1)} collective-permute-done((bf16[3,2,1,16,3200]{4,3,2,1,0:T(8,128)(2,1)S(1)}, bf16[3,2,1,16,3200]{4,3,2,1,0:T(8,128)(2,1)S(1)}, u32[]{:S(2)}, u32[]{:S(2)}) %collective-permute-start.7) | collective-permute-done | bytes 614432 | tf_op jit(solution)/shard_map/ppermute | solution.py:45
  58.0 2.5 collective-permute-start.11
  65.9 11.1 %qkv.1 = (bf16[2,512,512]{2,1,0:T(8,128)(2,1)S(1)}, bf16[3,512,1024]{2,1,0:T(8,128)(2,1)}, f32[8,1024]{1,0:T(8,128)S(1)}) custom-call(s32[7]{0:T(128)S(1)} %stack.64.meta_ref, bf16[512,1024]{1,0:T(8,128)(2,1)S(1)} %bitcast.221, bf16[256,3072]{1,0:T(8,128)(2,1)} %own_ref.7, bf16[3,64,3200]{2,1,0:T(8,128)(2,1)S(1)} %bitcast.216, ...), custom_call_target="tpu_custom_call" | custom-call | flops 3221225472 | bytes 11534336 | tf_op jit(solution)/shard_map/qkv/pallas_call | solution.py:356
  83.9 5.0 %collective-permute-start.13 = (bf16[2,128,1024]{2,1,0:T(8,128)(2,1)S(1)}, bf16[2,128,1024]{2,1,0:T(8,128)(2,1)S(1)}, u32[]{:S(2)}, u32[]{:S(2)}) collective-permute-start(bf16[2,128,1024]{2,1,0:T(8,128)(2,1)S(1)} %bitcast.266), channel_id=1, source_target_pairs={{0,1},{1,2},{2,3},{4,5},{5,6},{6,7},{8,9},{9,10},{10,11},{12,13},{... | collective-permute-start | bytes 1572872 | tf_op jit(solution)/shard_map/ppermute | solution.py:208
  88.9 7.5 %collective-permute-done.15 = bf16[3,1,1,16,6400]{4,3,2,1,0:T(8,128)(2,1)S(1)} collective-permute-done((bf16[3,1,1,16,6400]{4,3,2,1,0:T(8,128)(2,1)S(1)}, bf16[3,1,1,16,6400]{4,3,2,1,0:T(8,128)(2,1)S(1)}, u32[]{:S(2)}, u32[]{:S(2)}) %collective-permute-start.15) | collective-permute-done | bytes 614432 | tf_op jit(solution)/shard_map/ppermute | solution.py:45
  100.4 2.5 collective-permute-start.18
  104.7 2.8 collective-permute-start.20
  109.0 11.3 %attend.1 = (bf16[512,1024]{1,0:T(8,128)(2,1)S(1)}, bf16[2,8,2,256,256]{4,3,2,1,0:T(8,128)(2,1)}) custom-call(s32[3]{0:T(128)S(1)} %pad_add_fusion.meta_ref, bf16[3,512,1024]{2,1,0:T(8,128)(2,1)S(1)} %copy-done.2, bf16[3,512,1024]{2,1,0:T(8,128)(2,1)S(1)} %copy-done.2, bf16[3,512,1024]{2,1,0:T(8,128)(2,1)S(1)} %copy-done.2, ...), custom_call_target="tpu_custom_call" | custom-call | flops 1073741824 | bytes 5242880 | tf_op jit(solution)/shard_map/attend/pallas_call | solution.py:448
  120.4 7.0 %collective-permute-done.17 = bf16[3,2,1,16,6400]{4,3,2,1,0:T(8,128)(2,1)S(1)} collective-permute-done((bf16[3,2,1,16,6400]{4,3,2,1,0:T(8,128)(2,1)S(1)}, bf16[3,2,1,16,6400]{4,3,2,1,0:T(8,128)(2,1)S(1)}, u32[]{:S(2)}, u32[]{:S(2)}) %collective-permute-start.17) | collective-permute-done | bytes 1228832 | tf_op jit(solution)/shard_map/ppermute | solution.py:45
  129.3 4.4 %collective-permute-done.16 = bf16[3,1,2,16,6400]{4,3,0,2,1:T(8,128)(2,1)S(1)} collective-permute-done((bf16[3,1,2,16,6400]{4,3,0,2,1:T(8,128)(2,1)S(1)}, bf16[3,1,2,16,6400]{4,3,0,2,1:T(8,128)(2,1)S(1)}, u32[]{:S(2)}, u32[]{:S(2)}) %collective-permute-start.16) | collective-permute-done | bytes 1228832 | tf_op jit(solution)/shard_map/ppermute | solution.py:45
  141.8 3.5 collective-permute-done.24
  145.4 2.6 collective-permute-done.23
  150.2 5.5 %out_norm.1 = (f32[512,1024]{1,0:T(8,128)}, bf16[2,512,512]{2,1,0:T(8,128)(2,1)S(1)}, bf16[2,512,512]{2,1,0:T(8,128)(2,1)S(1)}) custom-call(s32[7]{0:T(128)S(1)} %stack.64.meta_ref, bf16[512,1024]{1,0:T(8,128)(2,1)S(1)} %copy-done.40, bf16[256,1024]{1,0:T(8,128)(2,1)S(1)} %copy-done.28, bf16[3,64,6400]{2,1,0:T(8,128)(2,1)} %bitcast.203, ...), custom_call_target="tpu_custom_call" | custom-call | flops 1073741824 | bytes 8388608 | tf_op jit(solution)/shard_map/out_norm/pallas_call | solution.py:575
  155.7 11.8 %gate.1 = (bf16[512,2688]{1,0:T(8,128)(2,1)}, bf16[512,2688]{1,0:T(8,128)(2,1)}, bf16[512,2688]{1,0:T(8,128)(2,1)}) custom-call(s32[7]{0:T(128)S(1)} %stack.64.meta_ref, bf16[2,512,512]{2,1,0:T(8,128)(2,1)S(1)} %get-tuple-element.362.n_ref.left_ref, bf16[256,2688]{1,0:T(8,128)(2,1)S(1)} %copy-done.12, bf16[3,64,6400]{2,1,0:T(8,128)(2,1)} %bitcast.205, ...), custom_call_target="tpu_custom_call" | custom-call | flops 5637144576 | bytes 19267584 | tf_op jit(solution)/shard_map/gate/pallas_call | solution.py:621
  169.5 4.7 %down_sum.2 = bf16[4,4,656,128]{3,2,1,0:T(8,128)(2,1)} custom-call(s32[7]{0:T(128)S(1)} %stack.64.meta_ref, bf16[512,2688]{1,0:T(8,128)(2,1)S(1)} %copy-done.14, bf16[512,1024]{1,0:T(8,128)(2,1)S(1)} %multiply_convert_fusion.g_ref), custom_call_target="tpu_custom_call" | custom-call | flops 1375731712 | bytes 6422528 | tf_op jit(solution)/shard_map/down_sum/pallas_call | solution.py:770
  175.9 6.6 %collective-permute-done.28.p3 = bf16[3,4,320,128]{3,2,1,0:T(8,128)(2,1)} collective-permute-done((bf16[3,4,320,128]{3,2,1,0:T(8,128)(2,1)}, bf16[3,4,320,128]{3,2,1,0:T(8,128)(2,1)}, u32[]{:S(2)}, u32[]{:S(2)}) %collective-permute-start.28) | collective-permute-done | bytes 983072 | tf_op jit(solution)/shard_map/ppermute | solution.py:45
  184.2 5.0 %down_sum.3 = (bf16[4,2,336,128]{3,2,1,0:T(8,128)(2,1)S(1)}, bf16[4,2,336,128]{3,2,1,0:T(8,128)(2,1)S(1)}, bf16[4,2,320,128]{3,2,1,0:T(8,128)(2,1)S(1)}, bf16[4,2,320,128]{3,2,1,0:T(8,128)(2,1)S(1)}) custom-call(s32[7]{0:T(128)S(1)} %stack.64.meta_ref, bf16[512,2688]{1,0:T(8,128)(2,1)S(1)} %copy-done.15, bf16[512,1024]{1,0:T(8,128)(2,1)S(1)} %multiply_convert_fusion.g_ref, ...), custom_call_target="tpu_custom_call" | custom-call | flops 1375731712 | bytes 6422528 | tf_op jit(solution)/shard_map/down_sum/pallas_call | solution.py:770
  191.4 11.7 %gate_back.1 = (bf16[2,512,2688]{2,1,0:T(8,128)(2,1)}, bf16[2688,1024]{1,0:T(8,128)(2,1)}) custom-call(s32[7]{0:T(128)S(1)} %stack.64.meta_ref, bf16[512,1024]{1,0:T(8,128)(2,1)S(1)} %multiply_convert_fusion.g_ref, bf16[656,1024]{1,0:T(8,128)(2,1)} %own_ref.6, bf16[3,4,336,128]{3,2,1,0:T(8,128)(2,1)S(1)} %bitcast.226, bf16[3,4,320,128]{3,2,1,0:T(8,128)(2,1)} %bitcast.31.p1, ...), custom_call_target="tpu_custom_call" | custom-call | flops 2818572288 | bytes 22020096 | tf_op jit(solution)/shard_map/gate_back/pallas_call | solution.py:707
  203.2 3.6 convolution_convert_fusion.1
  212.2 4.2 add_convert_fusion.2
  216.4 3.7 collective-permute-done.35.refs_3_
  222.0 3.6 sum_rows.5
  226.5 4.3 %sum_rows.4 = (bf16[4,2,16,2688]{3,2,1,0:T(8,128)(2,1)S(1)}, bf16[4,2,16,2688]{3,2,1,0:T(8,128)(2,1)}, bf16[4,2,16,2688]{3,2,1,0:T(8,128)(2,1)S(1)}, bf16[4,2,16,2688]{3,2,1,0:T(8,128)(2,1)}) custom-call(s32[7]{0:T(128)S(1)} %stack.64.meta_ref, bf16[2,512,512]{2,1,0:T(8,128)(2,1)S(1)} %get-tuple-element.362.n_ref.left_ref, ...), custom_call_target="tpu_custom_call" | custom-call | flops 1409286144 | bytes 11010048 | tf_op jit(solution)/shard_map/sum_rows/pallas_call | solution.py:813
  240.9 2.7 collective-permute-start.40
  248.8 14.9 %middle_back.1 = (f32[512,1024]{1,0:T(8,128)S(1)}, bf16[512,1024]{1,0:T(8,128)(2,1)S(1)}, bf16[512,1024]{1,0:T(8,128)(2,1)S(1)}) custom-call(s32[7]{0:T(128)S(1)} %stack.64.meta_ref, bf16[2,512,2688]{2,1,0:T(8,128)(2,1)} %get-tuple-element.386.gu_ref, bf16[256,2688]{1,0:T(8,128)(2,1)S(1)} %copy-done.13, bf16[3,64,6400]{2,1,0:T(8,128)(2,1)S(1)} %bitcast.207, ...), custom_call_target="tpu_custom_call" | custom-call | flops 5637144576 | bytes 22806528 | tf_op jit(solution)/shard_map/middle_back/pallas_call | solution.py:946
  266.5 2.5 fold.5
  276.6 17.7 %attend_back.1 = (bf16[512,1024]{1,0:T(8,128)(2,1)S(1)}, f32[512,1024]{1,0:T(8,128)}, f32[512,1024]{1,0:T(8,128)}, bf16[2,128,1024]{2,1,0:T(8,128)(2,1)S(1)}, bf16[2,128,1024]{2,1,0:T(8,128)(2,1)S(1)}) custom-call(bf16[3,512,1024]{2,1,0:T(8,128)(2,1)} %get-tuple-element.294.q_ref.k_ref.v_ref, bf16[3,512,1024]{2,1,0:T(8,128)(2,1)} %get-tuple-element.294.q_ref.k_ref.v_ref, ...), custom_call_target="tpu_custom_call" | custom-call | flops 2684354560 | bytes 10485760 | tf_op jit(solution)/shard_map/attend_back/pallas_call | solution.py:526
  295.7 4.6 %collective-permute-start.47 = (bf16[2,128,1024]{2,1,0:T(8,128)(2,1)S(1)}, bf16[2,128,1024]{2,1,0:T(8,128)(2,1)S(1)}, u32[]{:S(2)}, u32[]{:S(2)}) collective-permute-start(bf16[2,128,1024]{2,1,0:T(8,128)(2,1)S(1)} %get-tuple-element.425), channel_id=1, source_target_pairs={{0,1},{1,2},{2,3},{4,5},{5,6},{6,7},{8,9},{9,10},{10,11},{12,13},{... | collective-permute-start | bytes 1572872 | tf_op jit(solution)/shard_map/ppermute | solution.py:208
  303.7 6.1 %collective-permute-done.48.refs_1_ = bf16[4,1,16,2688]{3,2,1,0:T(8,128)(2,1)S(1)} collective-permute-done((bf16[4,1,16,2688]{3,2,1,0:T(8,128)(2,1)S(1)}, bf16[4,1,16,2688]{3,2,1,0:T(8,128)(2,1)S(1)}, u32[]{:S(2)}, u32[]{:S(2)}) %collective-permute-start.48) | collective-permute-done | bytes 344096 | tf_op jit(solution)/shard_map/ppermute | solution.py:45
  313.5 3.5 convolution_convert_fusion
  320.2 3.2 collective-permute-done.64
  325.7 2.8 collective-permute-start.54
  333.8 4.2 sum_rows.7
  340.7 3.8 collective-permute-start.59
  344.6 9.8 %input_back.1 = bf16[512,1024]{1,0:T(8,128)(2,1)} custom-call(s32[7]{0:T(128)S(1)} %stack.64.meta_ref, bf16[512,3072]{1,0:T(8,128)(2,1)} %copy-done.3, bf16[256,3072]{1,0:T(8,128)(2,1)} %own_ref.7, bf16[3,64,3200]{2,1,0:T(8,128)(2,1)S(1)} %bitcast.218, bf16[3,64,3200]{2,1,0:T(8,128)(2,1)S(1)} %bitcast.214, ...), custom_call_target="tpu_custom_call" | custom-call | flops 3221225472 | bytes 13631488 | tf_op jit(solution)/shard_map/input_back/pallas_call | solution.py:1000
  360.4 7.2 %collective-permute-done.62 = bf16[32,2688]{1,0:T(8,128)(2,1)S(1)} collective-permute-done((bf16[32,2688]{1,0:T(8,128)(2,1)S(1)}, bf16[32,2688]{1,0:T(8,128)(2,1)S(1)}, u32[]{:S(2)}, u32[]{:S(2)}) %collective-permute-start.62) | collective-permute-done | bytes 172064 | tf_op jit(solution)/shard_map/ppermute | solution.py:50
  372.6 4.1 collective-permute-start.66
  377.2 3.8 collective-permute-done.65
  389.2 2.7 collective-permute-done.71
  393.1 3.7 collective-permute-done.69
  399.8 3.3 collective-permute-done.74
  407.1 5.8 %collective-permute-done.79 = bf16[2,1,16,4096]{3,2,1,0:T(8,128)(2,1)S(1)} collective-permute-done((bf16[2,1,16,4096]{3,2,1,0:T(8,128)(2,1)S(1)}, bf16[2,1,16,4096]{3,2,1,0:T(8,128)(2,1)S(1)}, u32[]{:S(2)}, u32[]{:S(2)}) %collective-permute-start.79) | collective-permute-done | bytes 262176 | tf_op jit(solution)/shard_map/ppermute | solution.py:45
  415.2 3.7 multiply_reduce_fusion
  (509 shorter events, 158.8 us)
Async XLA Ops:
  4.4 16.9 %collective-permute-start = (bf16[2,16,3200]{2,1,0:T(8,128)(2,1)}, bf16[2,16,3200]{2,1,0:T(8,128)(2,1)S(1)}, u32[]{:S(2)}, u32[]{:S(2)}) collective-permute-start(bf16[2,16,3200]{2,1,0:T(8,128)(2,1)} %maximum_bitcast_fusion.6), channel_id=1, source_target_pairs={{0,1},{1,2},{2,3},{3,0},{4,5},{5,6},{6,7},{7,4},{8,9},{9,10},{10,1... | collective-permute-start | bytes 614408 | tf_op jit(solution)/shard_map/ppermute | solution.py:50
  7.4 16.3 %collective-permute-start.1 = (bf16[2,16,3200]{2,1,0:T(8,128)(2,1)}, bf16[2,16,3200]{2,1,0:T(8,128)(2,1)}, u32[]{:S(2)}, u32[]{:S(2)}) collective-permute-start(bf16[2,16,3200]{2,1,0:T(8,128)(2,1)} %maximum_bitcast_fusion.6), channel_id=1, source_target_pairs={{0,2},{1,3},{2,0},{3,1},{4,6},{5,7},{6,4},{7,5},{8,10},{9,11},{10,... | collective-permute-start | bytes 614408 | tf_op jit(solution)/shard_map/ppermute | solution.py:50
  10.0 13.7 %collective-permute-start.2 = (bf16[2,16,3200]{2,1,0:T(8,128)(2,1)}, bf16[2,16,3200]{2,1,0:T(8,128)(2,1)}, u32[]{:S(2)}, u32[]{:S(2)}) collective-permute-start(bf16[2,16,3200]{2,1,0:T(8,128)(2,1)} %maximum_bitcast_fusion.6), channel_id=1, source_target_pairs={{0,3},{1,0},{2,1},{3,2},{4,7},{5,4},{6,5},{7,6},{8,11},{9,8},{10,9... | collective-permute-start | bytes 614408 | tf_op jit(solution)/shard_map/ppermute | solution.py:50
  28.9 13.9 %collective-permute-start.5 = (bf16[2,16,6400]{2,1,0:T(8,128)(2,1)S(1)}, bf16[2,16,6400]{2,1,0:T(8,128)(2,1)S(1)}, u32[]{:S(2)}, u32[]{:S(2)}) collective-permute-start(bf16[2,16,6400]{2,1,0:T(8,128)(2,1)S(1)} %maximum_bitcast_fusion.2), channel_id=1, source_target_pairs={{0,1},{1,2},{2,3},{3,0},{4,5},{5,6},{6,7},{7,4},{8,9},{9,10},{10,1... | collective-permute-start | bytes 1228808 | tf_op jit(solution)/shard_map/ppermute | solution.py:50
  42.9 13.6 %collective-permute-start.7 = (bf16[3,2,1,16,3200]{4,3,2,1,0:T(8,128)(2,1)S(1)}, bf16[3,2,1,16,3200]{4,3,2,1,0:T(8,128)(2,1)S(1)}, u32[]{:S(2)}, u32[]{:S(2)}) collective-permute-start(bf16[3,2,1,16,3200]{4,3,2,1,0:T(8,128)(2,1)S(1)} %pad_maximum_fusion.18), channel_id=1, source_target_pairs={{0,8},{4,12},{8,0},{12,4},{16,24},{20,28},{24,16},{28,20},{1,9},{5... | collective-permute-start | bytes 1843208 | tf_op jit(solution)/shard_map/ppermute | solution.py:45
  43.4 13.3 %collective-permute-start.6 = (bf16[3,1,2,16,3200]{4,3,0,2,1:T(8,128)(2,1)S(1)}, bf16[3,1,2,16,3200]{4,3,0,2,1:T(8,128)(2,1)S(1)}, u32[]{:S(2)}, u32[]{:S(2)}) collective-permute-start(bf16[3,1,2,16,3200]{4,3,0,2,1:T(8,128)(2,1)S(1)} %pad_maximum_fusion.17), channel_id=1, source_target_pairs={{0,16},{4,20},{8,24},{12,28},{16,0},{20,4},{24,8},{28,12},{1,17},{... | collective-permute-start | bytes 1843208 | tf_op jit(solution)/shard_map/ppermute | solution.py:45
  43.9 13.1 %collective-permute-start.8 = (bf16[2,16,6400]{2,1,0:T(8,128)(2,1)S(1)}, bf16[2,16,6400]{2,1,0:T(8,128)(2,1)S(1)}, u32[]{:S(2)}, u32[]{:S(2)}) collective-permute-start(bf16[2,16,6400]{2,1,0:T(8,128)(2,1)S(1)} %maximum_bitcast_fusion.2), channel_id=1, source_target_pairs={{0,3},{1,0},{2,1},{3,2},{4,7},{5,4},{6,5},{7,6},{8,11},{9,8},{10,9... | collective-permute-start | bytes 1228808 | tf_op jit(solution)/shard_map/ppermute | solution.py:50
  58.0 21.3 %collective-permute-start.11 = (bf16[2,16,6400]{2,1,0:T(8,128)(2,1)}, bf16[2,16,6400]{2,1,0:T(8,128)(2,1)S(1)}, u32[]{:S(2)}, u32[]{:S(2)}) collective-permute-start(bf16[2,16,6400]{2,1,0:T(8,128)(2,1)} %copy-done.100), channel_id=1, source_target_pairs={{0,2},{1,3},{2,0},{3,1},{4,6},{5,7},{6,4},{7,5},{8,10},{9,11},{10,... | collective-permute-start | bytes 1228808 | tf_op jit(solution)/shard_map/ppermute | solution.py:50
  80.4 16.0 %collective-permute-start.15 = (bf16[3,1,1,16,6400]{4,3,2,1,0:T(8,128)(2,1)S(1)}, bf16[3,1,1,16,6400]{4,3,2,1,0:T(8,128)(2,1)S(1)}, u32[]{:S(2)}, u32[]{:S(2)}) collective-permute-start(bf16[3,1,1,16,6400]{4,3,2,1,0:T(8,128)(2,1)S(1)} %maximum_bitcast_fusion.1), channel_id=1, source_target_pairs={{0,16},{4,20},{8,24},{12,28},{16,0},{20,4},{24,8},{28,12},{1,17},{... | collective-permute-start | bytes 1843208 | tf_op jit(solution)/shard_map/ppermute | solution.py:45
  81.1 15.7 %collective-permute-start.14 = (bf16[3,1,1,16,6400]{4,3,0,2,1:T(8,128)(2,1)S(1)}, bf16[3,1,1,16,6400]{4,3,0,2,1:T(8,128)(2,1)S(1)}, u32[]{:S(2)}, u32[]{:S(2)}) collective-permute-start(bf16[3,1,1,16,6400]{4,3,0,2,1:T(8,128)(2,1)S(1)} %maximum_bitcast_fusion), channel_id=1, source_target_pairs={{0,8},{4,12},{8,0},{12,4},{16,24},{20,28},{24,16},{28,20},{1,9},{5... | collective-permute-start | bytes 1843208 | tf_op jit(solution)/shard_map/ppermute | solution.py:45
  82.6 16.0 %collective-permute-start.12 = (bf16[2,128,1024]{2,1,0:T(8,128)(2,1)S(1)}, bf16[2,128,1024]{2,1,0:T(8,128)(2,1)S(1)}, u32[]{:S(2)}, u32[]{:S(2)}) collective-permute-start(bf16[2,128,1024]{2,1,0:T(8,128)(2,1)S(1)} %bitcast.267), channel_id=1, source_target_pairs={{1,0},{2,1},{3,2},{5,4},{6,5},{7,6},{9,8},{10,9},{11,10},{13,12},{... | collective-permute-start | bytes 1572872 | tf_op jit(solution)/shard_map/ppermute | solution.py:208
  83.9 15.9 %collective-permute-start.13 = (bf16[2,128,1024]{2,1,0:T(8,128)(2,1)S(1)}, bf16[2,128,1024]{2,1,0:T(8,128)(2,1)S(1)}, u32[]{:S(2)}, u32[]{:S(2)}) collective-permute-start(bf16[2,128,1024]{2,1,0:T(8,128)(2,1)S(1)} %bitcast.266), channel_id=1, source_target_pairs={{0,1},{1,2},{2,3},{4,5},{5,6},{6,7},{8,9},{9,10},{10,11},{12,13},{... | collective-permute-start | bytes 1572872 | tf_op jit(solution)/shard_map/ppermute | solution.py:208
  99.8 27.6 %collective-permute-start.17 = (bf16[3,2,1,16,6400]{4,3,2,1,0:T(8,128)(2,1)S(1)}, bf16[3,2,1,16,6400]{4,3,2,1,0:T(8,128)(2,1)S(1)}, u32[]{:S(2)}, u32[]{:S(2)}) collective-permute-start(bf16[3,2,1,16,6400]{4,3,2,1,0:T(8,128)(2,1)S(1)} %pad_maximum_fusion.10), channel_id=1, source_target_pairs={{0,8},{4,12},{8,0},{12,4},{16,24},{20,28},{24,16},{28,20},{1,9},{5... | collective-permute-start | bytes 3686408 | tf_op jit(solution)/shard_map/ppermute | solution.py:45
  100.4 33.7 %collective-permute-start.18 = (bf16[656,128]{1,0:T(8,128)(2,1)S(1)}, bf16[656,128]{1,0:T(8,128)(2,1)S(1)}, u32[]{:S(2)}, u32[]{:S(2)}) collective-permute-start(bf16[656,128]{1,0:T(8,128)(2,1)S(1)} %copy-done.109), channel_id=1, source_target_pairs={{0,1},{1,2},{2,3},{3,0},{4,5},{5,6},{6,7},{7,4},{8,9},{9,10},{10,1... | collective-permute-start | bytes 503816 | tf_op jit(solution)/shard_map/ppermute | solution.py:50
  102.9 31.2 %collective-permute-start.19 = (bf16[656,128]{1,0:T(8,128)(2,1)S(1)}, bf16[656,128]{1,0:T(8,128)(2,1)S(1)}, u32[]{:S(2)}, u32[]{:S(2)}) collective-permute-start(bf16[656,128]{1,0:T(8,128)(2,1)S(1)} %copy-done.109), channel_id=1, source_target_pairs={{0,2},{1,3},{2,0},{3,1},{4,6},{5,7},{6,4},{7,5},{8,10},{9,11},{10,... | collective-permute-start | bytes 503816 | tf_op jit(solution)/shard_map/ppermute | solution.py:50
  104.7 29.4 %collective-permute-start.20 = (bf16[656,128]{1,0:T(8,128)(2,1)S(1)}, bf16[656,128]{1,0:T(8,128)(2,1)S(1)}, u32[]{:S(2)}, u32[]{:S(2)}) collective-permute-start(bf16[656,128]{1,0:T(8,128)(2,1)S(1)} %copy-done.109), channel_id=1, source_target_pairs={{0,3},{1,0},{2,1},{3,2},{4,7},{5,4},{6,5},{7,6},{8,11},{9,8},{10,9... | collective-permute-start | bytes 503816 | tf_op jit(solution)/shard_map/ppermute | solution.py:50
  107.5 26.2 %collective-permute-start.16 = (bf16[3,1,2,16,6400]{4,3,0,2,1:T(8,128)(2,1)S(1)}, bf16[3,1,2,16,6400]{4,3,0,2,1:T(8,128)(2,1)S(1)}, u32[]{:S(2)}, u32[]{:S(2)}) collective-permute-start(bf16[3,1,2,16,6400]{4,3,0,2,1:T(8,128)(2,1)S(1)} %pad_maximum_fusion.9), channel_id=1, source_target_pairs={{0,16},{4,20},{8,24},{12,28},{16,0},{20,4},{24,8},{28,12},{1,17},{... | collective-permute-start | bytes 3686408 | tf_op jit(solution)/shard_map/ppermute | solution.py:45
  134.9 13.2 %collective-permute-start.21 = (bf16[3,64,6400]{2,1,0:T(8,128)(2,1)S(1)}, bf16[3,64,6400]{2,1,0:T(8,128)(2,1)}, u32[]{:S(2)}, u32[]{:S(2)}) collective-permute-start(bf16[3,64,6400]{2,1,0:T(8,128)(2,1)S(1)} %bitcast.202), channel_id=1, source_target_pairs={{0,4},{4,0},{8,12},{12,8},{16,20},{20,16},{24,28},{28,24},{1,5},{5... | collective-permute-start | bytes 7372808 | tf_op jit(solution)/shard_map/ppermute | solution.py:45
  134.9 13.2 %collective-permute-start.22 = (bf16[3,64,6400]{2,1,0:T(8,128)(2,1)}, bf16[3,64,6400]{2,1,0:T(8,128)(2,1)}, u32[]{:S(2)}, u32[]{:S(2)}) collective-permute-start(bf16[3,64,6400]{2,1,0:T(8,128)(2,1)} %bitcast.24.p1.q1.r1.s1), channel_id=1, source_target_pairs={{0,4},{4,0},{8,12},{12,8},{16,20},{20,16},{24,28},{28,24},{1,5},{5... | collective-permute-start | bytes 7372808 | tf_op jit(solution)/shard_map/ppermute | solution.py:45
  148.1 19.4 %collective-permute-start.26 = (bf16[3,2,1,320,128]{4,3,0,2,1:T(8,128)(2,1)S(1)}, bf16[3,2,1,320,128]{4,3,0,2,1:T(8,128)(2,1)S(1)}, u32[]{:S(2)}, u32[]{:S(2)}) collective-permute-start(bf16[3,2,1,320,128]{4,3,0,2,1:T(8,128)(2,1)S(1)} %pad_maximum_fusion.23), channel_id=1, source_target_pairs={{0,8},{4,12},{8,0},{12,4},{16,24},{20,28},{24,16},{28,20},{1,9},{5... | collective-permute-start | bytes 1474568 | tf_op jit(solution)/shard_map/ppermute | solution.py:45
  149.7 18.1 %collective-permute-start.25 = (bf16[3,1,2,336,128]{4,3,0,2,1:T(8,128)(2,1)S(1)}, bf16[3,1,2,336,128]{4,3,0,2,1:T(8,128)(2,1)S(1)}, u32[]{:S(2)}, u32[]{:S(2)}) collective-permute-start(bf16[3,1,2,336,128]{4,3,0,2,1:T(8,128)(2,1)S(1)} %pad_maximum_fusion.21), channel_id=1, source_target_pairs={{0,16},{4,20},{8,24},{12,28},{16,0},{20,4},{24,8},{28,12},{1,17},{... | collective-permute-start | bytes 1548296 | tf_op jit(solution)/shard_map/ppermute | solution.py:45
  189.3 19.3 %collective-permute-start.30 = (bf16[4,2,336,128]{3,2,1,0:T(8,128)(2,1)S(1)}, bf16[4,2,336,128]{3,2,1,0:T(8,128)(2,1)S(1)}, u32[]{:S(2)}, u32[]{:S(2)}) collective-permute-start(bf16[4,2,336,128]{3,2,1,0:T(8,128)(2,1)S(1)} %get-tuple-element.332), channel_id=1, source_target_pairs={{0,8},{4,12},{8,0},{12,4},{16,24},{20,28},{24,16},{28,20},{1,9},{5... | collective-permute-start | bytes 2064392 | tf_op jit(solution)/shard_map/ppermute | solution.py:45
  189.9 18.7 %collective-permute-start.31 = (bf16[4,2,320,128]{3,2,1,0:T(8,128)(2,1)S(1)}, bf16[4,2,320,128]{3,2,1,0:T(8,128)(2,1)S(1)}, u32[]{:S(2)}, u32[]{:S(2)}) collective-permute-start(bf16[4,2,320,128]{3,2,1,0:T(8,128)(2,1)S(1)} %get-tuple-element.334), channel_id=1, source_target_pairs={{0,16},{4,20},{8,24},{12,28},{16,0},{20,4},{24,8},{28,12},{1,17},{... | collective-permute-start | bytes 1966088 | tf_op jit(solution)/shard_map/ppermute | solution.py:45
  208.6 13.0 %collective-permute-start.32 = (bf16[512,2688]{1,0:T(8,128)(2,1)S(1)}, bf16[512,2688]{1,0:T(8,128)(2,1)S(1)}, u32[]{:S(2)}, u32[]{:S(2)}) collective-permute-start(bf16[512,2688]{1,0:T(8,128)(2,1)S(1)} %convolution_convert_fusion.2), channel_id=1, source_target_pairs={{0,4},{4,0},{8,12},{12,8},{16,20},{20,16},{24,28},{28,24},{1,5},{5... | collective-permute-start | bytes 8257544 | tf_op jit(solution)/shard_map/ppermute | solution.py:45
  208.7 12.9 %collective-permute-start.33 = (bf16[512,2688]{1,0:T(8,128)(2,1)S(1)}, bf16[512,2688]{1,0:T(8,128)(2,1)S(1)}, u32[]{:S(2)}, u32[]{:S(2)}) collective-permute-start(bf16[512,2688]{1,0:T(8,128)(2,1)S(1)} %convolution_convert_fusion.1), channel_id=1, source_target_pairs={{0,4},{4,0},{8,12},{12,8},{16,20},{20,16},{24,28},{28,24},{1,5},{5... | collective-permute-start | bytes 8257544 | tf_op jit(solution)/shard_map/ppermute | solution.py:45
  210.1 10.7 %collective-permute-start.34 = (bf16[4,1,336,128]{3,2,1,0:T(8,128)(2,1)S(1)}, bf16[4,1,336,128]{3,2,1,0:T(8,128)(2,1)S(1)}, u32[]{:S(2)}, u32[]{:S(2)}) collective-permute-start(bf16[4,1,336,128]{3,2,1,0:T(8,128)(2,1)S(1)} %get-tuple-element.357), channel_id=1, source_target_pairs={{0,16},{4,20},{8,24},{12,28},{16,0},{20,4},{24,8},{28,12},{1,17},{... | collective-permute-start | bytes 1032200 | tf_op jit(solution)/shard_map/ppermute | solution.py:45
  232.5 31.3 %collective-permute-start.36 = (bf16[4,2,16,2688]{3,2,1,0:T(8,128)(2,1)}, bf16[4,2,16,2688]{3,2,1,0:T(8,128)(2,1)}, u32[]{:S(2)}, u32[]{:S(2)}) collective-permute-start(bf16[4,2,16,2688]{3,2,1,0:T(8,128)(2,1)} %get-tuple-element.375), channel_id=1, source_target_pairs={{0,8},{4,12},{8,0},{12,4},{16,24},{20,28},{24,16},{28,20},{1,9},{5... | collective-permute-start | bytes 2064392 | tf_op jit(solution)/shard_map/ppermute | solution.py:45
  234.0 29.9 %collective-permute-start.37 = (bf16[4,2,16,2688]{3,2,1,0:T(8,128)(2,1)}, bf16[4,2,16,2688]{3,2,1,0:T(8,128)(2,1)}, u32[]{:S(2)}, u32[]{:S(2)}) collective-permute-start(bf16[4,2,16,2688]{3,2,1,0:T(8,128)(2,1)} %get-tuple-element.377), channel_id=1, source_target_pairs={{0,16},{4,20},{8,24},{12,28},{16,0},{20,4},{24,8},{28,12},{1,17},{... | collective-permute-start | bytes 2064392 | tf_op jit(solution)/shard_map/ppermute | solution.py:45
  239.7 24.1 %collective-permute-start.38 = (bf16[656,128]{1,0:T(8,128)(2,1)S(1)}, bf16[656,128]{1,0:T(8,128)(2,1)S(1)}, u32[]{:S(2)}, u32[]{:S(2)}) collective-permute-start(bf16[656,128]{1,0:T(8,128)(2,1)S(1)} %get-tuple-element.572), channel_id=1, source_target_pairs={{0,1},{1,2},{2,3},{3,0},{4,5},{5,6},{6,7},{7,4},{8,9},{9,10},{10,1... | collective-permute-start | bytes 503816 | tf_op jit(solution)/shard_map/ppermute | solution.py:50
  239.8 24.0 %collective-permute-start.39 = (bf16[656,128]{1,0:T(8,128)(2,1)S(1)}, bf16[656,128]{1,0:T(8,128)(2,1)S(1)}, u32[]{:S(2)}, u32[]{:S(2)}) collective-permute-start(bf16[656,128]{1,0:T(8,128)(2,1)S(1)} %get-tuple-element.571), channel_id=1, source_target_pairs={{0,2},{1,3},{2,0},{3,1},{4,6},{5,7},{6,4},{7,5},{8,10},{9,11},{10,... | collective-permute-start | bytes 503816 | tf_op jit(solution)/shard_map/ppermute | solution.py:50
  240.9 22.9 %collective-permute-start.40 = (bf16[656,128]{1,0:T(8,128)(2,1)S(1)}, bf16[656,128]{1,0:T(8,128)(2,1)S(1)}, u32[]{:S(2)}, u32[]{:S(2)}) collective-permute-start(bf16[656,128]{1,0:T(8,128)(2,1)S(1)} %get-tuple-element.570), channel_id=1, source_target_pairs={{0,3},{1,0},{2,1},{3,2},{4,7},{5,4},{6,5},{7,6},{8,11},{9,8},{10,9... | collective-permute-start | bytes 503816 | tf_op jit(solution)/shard_map/ppermute | solution.py:50
  265.3 29.0 %collective-permute-start.43 = (bf16[4,2,16,2688]{3,2,1,0:T(8,128)(2,1)S(1)}, bf16[4,2,16,2688]{3,2,1,0:T(8,128)(2,1)S(1)}, u32[]{:S(2)}, u32[]{:S(2)}) collective-permute-start(bf16[4,2,16,2688]{3,2,1,0:T(8,128)(2,1)S(1)} %copy-done.81), channel_id=1, source_target_pairs={{0,8},{4,12},{8,0},{12,4},{16,24},{20,28},{24,16},{28,20},{1,9},{5... | collective-permute-start | bytes 2064392 | tf_op jit(solution)/shard_map/ppermute | solution.py:45
  266.0 28.4 %collective-permute-start.44 = (bf16[4,2,16,2688]{3,2,1,0:T(8,128)(2,1)S(1)}, bf16[4,2,16,2688]{3,2,1,0:T(8,128)(2,1)S(1)}, u32[]{:S(2)}, u32[]{:S(2)}) collective-permute-start(bf16[4,2,16,2688]{3,2,1,0:T(8,128)(2,1)S(1)} %copy-done.79), channel_id=1, source_target_pairs={{0,16},{4,20},{8,24},{12,28},{16,0},{20,4},{24,8},{28,12},{1,17},{... | collective-permute-start | bytes 2064392 | tf_op jit(solution)/shard_map/ppermute | solution.py:45
  269.0 25.3 %collective-permute-start.41 = (bf16[4,1,16,2688]{3,2,1,0:T(8,128)(2,1)S(1)}, bf16[4,1,16,2688]{3,2,1,0:T(8,128)(2,1)S(1)}, u32[]{:S(2)}, u32[]{:S(2)}) collective-permute-start(bf16[4,1,16,2688]{3,2,1,0:T(8,128)(2,1)S(1)} %get-tuple-element.394), channel_id=1, source_target_pairs={{0,16},{4,20},{8,24},{12,28},{16,0},{20,4},{24,8},{28,12},{1,17},{... | collective-permute-start | bytes 1032200 | tf_op jit(solution)/shard_map/ppermute | solution.py:45
  270.6 23.8 %collective-permute-start.42 = (bf16[4,1,16,2688]{3,2,1,0:T(8,128)(2,1)S(1)}, bf16[4,1,16,2688]{3,2,1,0:T(8,128)(2,1)S(1)}, u32[]{:S(2)}, u32[]{:S(2)}) collective-permute-start(bf16[4,1,16,2688]{3,2,1,0:T(8,128)(2,1)S(1)} %get-tuple-element.396), channel_id=1, source_target_pairs={{0,8},{4,12},{8,0},{12,4},{16,24},{20,28},{24,16},{28,20},{1,9},{5... | collective-permute-start | bytes 1032200 | tf_op jit(solution)/shard_map/ppermute | solution.py:45
  294.4 16.8 %collective-permute-start.46 = (bf16[2,128,1024]{2,1,0:T(8,128)(2,1)S(1)}, bf16[2,128,1024]{2,1,0:T(8,128)(2,1)S(1)}, u32[]{:S(2)}, u32[]{:S(2)}) collective-permute-start(bf16[2,128,1024]{2,1,0:T(8,128)(2,1)S(1)} %get-tuple-element.424), channel_id=1, source_target_pairs={{1,0},{2,1},{3,2},{5,4},{6,5},{7,6},{9,8},{10,9},{11,10},{13,12},{... | collective-permute-start | bytes 1572872 | tf_op jit(solution)/shard_map/ppermute | solution.py:208
  295.7 15.5 %collective-permute-start.47 = (bf16[2,128,1024]{2,1,0:T(8,128)(2,1)S(1)}, bf16[2,128,1024]{2,1,0:T(8,128)(2,1)S(1)}, u32[]{:S(2)}, u32[]{:S(2)}) collective-permute-start(bf16[2,128,1024]{2,1,0:T(8,128)(2,1)S(1)} %get-tuple-element.425), channel_id=1, source_target_pairs={{0,1},{1,2},{2,3},{4,5},{5,6},{6,7},{8,9},{9,10},{10,11},{12,13},{... | collective-permute-start | bytes 1572872 | tf_op jit(solution)/shard_map/ppermute | solution.py:208
  317.0 15.0 %collective-permute-start.50 = (bf16[512,3072]{1,0:T(8,128)(2,1)}, bf16[512,3072]{1,0:T(8,128)(2,1)S(1)}, u32[]{:S(2)}, u32[]{:S(2)}) collective-permute-start(bf16[512,3072]{1,0:T(8,128)(2,1)} %convolution_convert_fusion), channel_id=1, source_target_pairs={{0,4},{4,0},{8,12},{12,8},{16,20},{20,16},{24,28},{28,24},{1,5},{5... | collective-permute-start | bytes 9437192 | tf_op jit(solution)/shard_map/ppermute | solution.py:45
  324.3 13.7 %collective-permute-start.53 = (bf16[32,2688]{1,0:T(8,128)(2,1)S(1)}, bf16[32,2688]{1,0:T(8,128)(2,1)S(1)}, u32[]{:S(2)}, u32[]{:S(2)}) collective-permute-start(bf16[32,2688]{1,0:T(8,128)(2,1)S(1)} %get-tuple-element.569), channel_id=1, source_target_pairs={{0,1},{1,2},{2,3},{3,0},{4,5},{5,6},{6,7},{7,4},{8,9},{9,10},{10,1... | collective-permute-start | bytes 516104 | tf_op jit(solution)/shard_map/ppermute | solution.py:50
  325.7 12.3 %collective-permute-start.54 = (bf16[32,2688]{1,0:T(8,128)(2,1)S(1)}, bf16[32,2688]{1,0:T(8,128)(2,1)S(1)}, u32[]{:S(2)}, u32[]{:S(2)}) collective-permute-start(bf16[32,2688]{1,0:T(8,128)(2,1)S(1)} %get-tuple-element.568), channel_id=1, source_target_pairs={{0,3},{1,0},{2,1},{3,2},{4,7},{5,4},{6,5},{7,6},{8,11},{9,8},{10,9... | collective-permute-start | bytes 516104 | tf_op jit(solution)/shard_map/ppermute | solution.py:50
  338.0 18.0 %collective-permute-start.55 = (bf16[4,2,16,3072]{3,2,1,0:T(8,128)(2,1)}, bf16[4,2,16,3072]{3,2,1,0:T(8,128)(2,1)S(1)}, u32[]{:S(2)}, u32[]{:S(2)}) collective-permute-start(bf16[4,2,16,3072]{3,2,1,0:T(8,128)(2,1)} %get-tuple-element.461), channel_id=1, source_target_pairs={{0,8},{4,12},{8,0},{12,4},{16,24},{20,28},{24,16},{28,20},{1,9},{5... | collective-permute-start | bytes 2359304 | tf_op jit(solution)/shard_map/ppermute | solution.py:45
  339.5 17.6 %collective-permute-start.56 = (bf16[4,2,16,3072]{3,2,1,0:T(8,128)(2,1)}, bf16[4,2,16,3072]{3,2,1,0:T(8,128)(2,1)S(1)}, u32[]{:S(2)}, u32[]{:S(2)}) collective-permute-start(bf16[4,2,16,3072]{3,2,1,0:T(8,128)(2,1)} %get-tuple-element.463), channel_id=1, source_target_pairs={{0,16},{4,20},{8,24},{12,28},{16,0},{20,4},{24,8},{28,12},{1,17},{... | collective-permute-start | bytes 2359304 | tf_op jit(solution)/shard_map/ppermute | solution.py:45
  340.6 13.9 %collective-permute-start.58 = (bf16[32,2688]{1,0:T(8,128)(2,1)S(1)}, bf16[32,2688]{1,0:T(8,128)(2,1)S(1)}, u32[]{:S(2)}, u32[]{:S(2)}) collective-permute-start(bf16[32,2688]{1,0:T(8,128)(2,1)S(1)} %get-tuple-element.567), channel_id=1, source_target_pairs={{0,1},{1,2},{2,3},{3,0},{4,5},{5,6},{6,7},{7,4},{8,9},{9,10},{10,1... | collective-permute-start | bytes 516104 | tf_op jit(solution)/shard_map/ppermute | solution.py:50
  340.7 13.8 %collective-permute-start.59 = (bf16[32,2688]{1,0:T(8,128)(2,1)S(1)}, bf16[32,2688]{1,0:T(8,128)(2,1)S(1)}, u32[]{:S(2)}, u32[]{:S(2)}) collective-permute-start(bf16[32,2688]{1,0:T(8,128)(2,1)S(1)} %get-tuple-element.566), channel_id=1, source_target_pairs={{0,3},{1,0},{2,1},{3,2},{4,7},{5,4},{6,5},{7,6},{8,11},{9,8},{10,9... | collective-permute-start | bytes 516104 | tf_op jit(solution)/shard_map/ppermute | solution.py:50
  344.5 11.2 %collective-permute-start.57 = (bf16[32,2688]{1,0:T(8,128)(2,1)S(1)}, bf16[32,2688]{1,0:T(8,128)(2,1)S(1)}, u32[]{:S(2)}, u32[]{:S(2)}) collective-permute-start(bf16[32,2688]{1,0:T(8,128)(2,1)S(1)} %dynamic-slice_bitcast_fusion.7), channel_id=1, source_target_pairs={{0,2},{1,3},{2,0},{3,1},{4,6},{5,7},{6,4},{7,5},{8,10},{9,11},{10,... | collective-permute-start | bytes 516104 | tf_op jit(solution)/shard_map/ppermute | solution.py:50
  358.3 11.5 %collective-permute-start.60 = (bf16[4,1,16,4096]{3,2,1,0:T(8,128)(2,1)S(1)}, bf16[4,1,16,4096]{3,2,1,0:T(8,128)(2,1)S(1)}, u32[]{:S(2)}, u32[]{:S(2)}) collective-permute-start(bf16[4,1,16,4096]{3,2,1,0:T(8,128)(2,1)S(1)} %get-tuple-element.480), channel_id=1, source_target_pairs={{0,16},{4,20},{8,24},{12,28},{16,0},{20,4},{24,8},{28,12},{1,17},{... | collective-permute-start | bytes 1572872 | tf_op jit(solution)/shard_map/ppermute | solution.py:45
  359.4 11.1 %collective-permute-start.61 = (bf16[4,1,16,4096]{3,2,1,0:T(8,128)(2,1)S(1)}, bf16[4,1,16,4096]{3,2,1,0:T(8,128)(2,1)S(1)}, u32[]{:S(2)}, u32[]{:S(2)}) collective-permute-start(bf16[4,1,16,4096]{3,2,1,0:T(8,128)(2,1)S(1)} %get-tuple-element.482), channel_id=1, source_target_pairs={{0,8},{4,12},{8,0},{12,4},{16,24},{20,28},{24,16},{28,20},{1,9},{5... | collective-permute-start | bytes 1572872 | tf_op jit(solution)/shard_map/ppermute | solution.py:45
  386.3 10.5 %collective-permute-start.69 = (bf16[32,4096]{1,0:T(8,128)(2,1)S(1)}, bf16[32,4096]{1,0:T(8,128)(2,1)S(1)}, u32[]{:S(2)}, u32[]{:S(2)}) collective-permute-start(bf16[32,4096]{1,0:T(8,128)(2,1)S(1)} %dynamic-slice_bitcast_fusion), channel_id=1, source_target_pairs={{0,2},{1,3},{2,0},{3,1},{4,6},{5,7},{6,4},{7,5},{8,10},{9,11},{10,... | collective-permute-start | bytes 786440 | tf_op jit(solution)/shard_map/ppermute | solution.py:50
  (151 other events, 919.1 us)

commit v4 on v3

--- a/solution.py
+++ b/solution.py
@@ -214,6 +214,10 @@
 
 def cost(flops, nbytes):
     return pl.CostEstimate(flops=int(flops * COST_SCALE), bytes_accessed=int(nbytes * COST_SCALE), transcendentals=0)
+
+
+def far(*arrays):
+    return [pltpu.with_memory_space_constraint(array, pltpu.HBM) for array in arrays]
 
 
 def dot_nn(left, right):
@@ -376,10 +380,10 @@
             pltpu.VMEM((rows, width), bf16),
             pltpu.VMEM((width, LANES), bf16),
         ],
-        compiler_params=params(48, "arbitrary"),
+        compiler_params=params(20, "arbitrary"),
         cost_estimate=cost(6 * rows * width * width, 6 * width * width + 10 * rows * width),
         name="qkv",
-    )(meta, x, own, *parts, own_gains, *parts, cosine, sine)
+    )(meta, *far(x, own, *parts), own_gains, *far(*parts), cosine, sine)
 
 
 def head_masks():
@@ -436,7 +440,7 @@
     flat = pl.BlockSpec((seq_rows, block), lambda s, h: (s, h))
     inner = (seq_rows // BLOCK_Q, 2 * BLOCK_Q, BLOCK_Q + 2 * WIN)
     probs = pl.BlockSpec((1, block // LANES) + inner, lambda s, h: (s, h, 0, 0, 0))
-    probs_shape = jax.ShapeDtypeStruct((seqs, width // LANES) + inner, bf16)
+    probs_shape = pltpu.HBM((seqs, width // LANES) + inner, bf16)
     return own, rim, flat, probs, probs_shape
 
 
@@ -451,7 +455,7 @@
         in_specs=[SMEM_SPEC, own(0), own(1), own(2), rim(0), rim(1), rim(0), rim(1)],
         out_specs=[flat, probs],
         out_shape=[jax.ShapeDtypeStruct((rows, width), bf16), probs_shape],
-        compiler_params=params(48, "arbitrary", "arbitrary"),
+        compiler_params=params(16, "arbitrary", "arbitrary"),
         cost_estimate=cost(8 * rows * width * (BLOCK_Q + 2 * WIN), 10 * rows * width),
         name="attend",
     )(meta, qkv, qkv, qkv, rim_up, rim_up, rim_down, rim_down)
@@ -542,10 +546,10 @@
             pltpu.VMEM((seq_rows + 2 * WIN, LANES), f32),
             pltpu.VMEM((seq_rows + 2 * WIN, LANES), f32),
         ],
-        compiler_params=params(48, "arbitrary", "arbitrary"),
+        compiler_params=params(16, "arbitrary", "arbitrary"),
         cost_estimate=cost(20 * rows * width * (BLOCK_Q + 2 * WIN), 20 * rows * width),
         name="attend_back",
-    )(qkv, qkv, qkv, rim_up, rim_up, rim_down, rim_down, saved, grad_out, cosine, sine)
+    )(qkv, qkv, qkv, rim_up, rim_up, rim_down, rim_down, *far(saved), grad_out, cosine, sine)
 
 
 def out_kernel(
@@ -579,12 +583,12 @@
         + stretch_specs(parts, start, stretch)
         + [tile, pl.BlockSpec((block, 1), lambda i: (i, 0)), once(8, width)],
         out_specs=[tile, split, split],
-        out_shape=[jax.ShapeDtypeStruct((rows, width), f32), split_shape, split_shape],
+        out_shape=[pltpu.HBM((rows, width), f32), split_shape, split_shape],
         scratch_shapes=[pltpu.VMEM((width, width), bf16)],
-        compiler_params=params(48, "arbitrary"),
+        compiler_params=params(16, "arbitrary"),
         cost_estimate=cost(2 * rows * width * width, 2 * width * width + 12 * rows * width),
         name="out_norm",
-    )(meta, attended, own, *parts, *parts, x, valid, gains)
+    )(meta, attended, *far(own, *parts, *parts, x), valid, gains)
 
 
 def gate_kernel(
@@ -617,7 +621,6 @@
     size = width // slab
     tile = pl.BlockSpec((rows, block), lambda i: (0, i))
     own = pl.BlockSpec((slab, block), lambda i: (0, i))
-    shape = jax.ShapeDtypeStruct((rows, hidden), bf16)
     return pl.pallas_call(
         functools.partial(gate_kernel, size=size),
         grid=(hidden // block,),
@@ -626,16 +629,16 @@
         + [own]
         + part_specs(parts, block, lambda i: i + steps),
         out_specs=[tile, tile, tile],
-        out_shape=[shape, shape, shape],
+        out_shape=[pltpu.HBM((rows, hidden), bf16)] * 3,
         scratch_shapes=[
             pltpu.VMEM((rows, width), bf16),
             pltpu.VMEM((width, block), bf16),
             pltpu.VMEM((width, block), bf16),
         ],
-        compiler_params=params(48, "arbitrary"),
+        compiler_params=params(32, "arbitrary"),
         cost_estimate=cost(4 * rows * width * hidden, 4 * width * hidden + 6 * rows * hidden),
         name="gate",
-    )(meta, normed, owns[0], *parts, owns[1], *parts)
+    )(meta, normed, *far(owns[0], *parts, owns[1], *parts))
 
 
 def gate_back_kernel(
@@ -690,7 +693,7 @@
     out_shape = jax.ShapeDtypeStruct((2, rows, hidden), bf16)
     settings = dict(
         grid=(hidden // block,),
-        compiler_params=params(48, "arbitrary"),
+        compiler_params=params(28, "arbitrary"),
         cost_estimate=cost(2 * rows * width * hidden, 4 * width * hidden + 8 * rows * hidden),
         name="gate_back",
     )
@@ -712,16 +715,17 @@
         out_specs=[out_spec, fixed(hidden, width)],
         out_shape=[out_shape, jax.ShapeDtypeStruct((hidden, width), bf16)],
         **settings,
-    )(meta, grad_result, own, *parts, slope, act)
-
-
-def down_kernel(meta_ref, m_ref, g_ref, *rest, mine, size, links, hidden, cut, places):
+    )(meta, *far(grad_result, own, *parts, slope, act))
+
+
+def down_kernel(
+    meta_ref, m_ref, n_ref, g_ref, h_ref, keep0, give0, keep1, give1, state_ref, *, hidden, places
+):
     step = pl.program_id(0)
-    block, half = m_ref.shape[1], g_ref.shape[1] // 2
-    which = meta_ref[2] if mine else 1 - meta_ref[2]
-    right = g_ref[:, pl.ds(pl.multiple_of(which * half, half), half)]
-    sums = tokens_dot(m_ref[...], right)
-    rows, columns = hidden // size, half // links
+    block, half = m_ref.shape[1], h_ref.shape[1]
+    size, links, rows, columns = state_ref.shape
+    right = g_ref[:, pl.ds(pl.multiple_of(meta_ref[2] * half, half), half)]
+    sums = tokens_dot(m_ref[...], right) + tokens_dot(n_ref[...], h_ref[...])
 
     def put(first):
         for place in range(size):
@@ -730,26 +734,30 @@
                 continue
             for link in range(links):
                 value = sums[top - first : end - first, link * columns : (link + 1) * columns]
-                rest[-1][place, link, top - place * rows : end - place * rows, :] = value.astype(bf16)
+                state_ref[place, link, top - place * rows : end - place * rows, :] = value.astype(bf16)
 
     for number in range(-(-hidden // block)):
         pl.when(step == number)(functools.partial(put, number * block))
 
-    if mine:
-        add_ref, keep0, give0, keep1, give1, state_ref = rest
-
-        @pl.when(step == pl.num_programs(0) - 1)
-        def _():
-            for part, (keep_ref, give_ref) in enumerate(((keep0, give0), (keep1, give1))):
-                span = slice(0, cut) if part == 0 else slice(cut, rows)
-                own = meta_ref[3 + part]
-                for place in range(size):
-                    for number in range(links // 2):
-                        base = split_index(number, places[part])
-                        for ref, value in ((keep_ref, own), (give_ref, 1 - own)):
-                            link = base + value * (1 << places[part])
-                            ref[place, number] = added(
-                                state_ref[place, link, span, :], add_ref[place, link, span, :]
+    @pl.when(step == pl.num_programs(0) - 1)
+    def _():
+        height, width = keep0.shape[2:]
+        tiles = rows // height
+        for part, (keep_ref, give_ref) in enumerate(((keep0, give0), (keep1, give1))):
+            own = meta_ref[3 + part]
+            span = range(part * (width // columns), min((part + 1) * (width // columns), tiles))
+            for place in range(size):
+                for number in range(links // 2):
+                    base = split_index(number, places[part])
+                    for ref, value in ((keep_ref, own), (give_ref, 1 - own)):
+                        link = base + value * (1 << places[part])
+                        for lane, tile in enumerate(span):
+                            ref[place, number, :, lane * columns : (lane + 1) * columns] = state_ref[
+                                place, link, tile * height : (tile + 1) * height, :
+                            ]
+                        if len(span) * columns < width:
+                            ref[place, number, :, len(span) * columns :] = jnp.zeros(
+                                (height, width - len(span) * columns), bf16
                             )
 
 
@@ -757,76 +765,100 @@
     return [left.index(bit) for left, bit in zip(bits_left(0), link_orders()[0])]
 
 
-def down_call(meta, mixed, grad_result, size, hidden, block, add=None):
+def piece_rows(width):
+    return width // lax.axis_size("fsdp") // (4 << link_count())
+
+
+def fits(shard, columns, height):
+    return shard % 16 == 0 and columns == LANES and height == 16
+
+
+def down_call(meta, mixed, mixed_other, grad_result, grad_other, hidden, block):
     rows, hidden_pad = mixed.shape
     width = grad_result.shape[1]
+    size = lax.axis_size("fsdp")
     links = 1 << link_count()
-    shard = hidden // size
-    cut = half_rows(shard)
-    columns = width // 2 // links
-    shape = (size, links, shard, columns)
-    mine = add is not None
-    parts = [(size, links // 2, height, columns) for height in (cut, cut, shard - cut, shard - cut)]
+    shard, columns, height = hidden // size, width // 2 // links, piece_rows(width)
+    if not fits(shard, columns, height):
+        own = lax.dynamic_slice_in_dim(grad_result, bit_value(0) * (width // 2), width // 2, 1)
+        sums = tokens_dot(mixed, own) + tokens_dot(mixed_other, grad_other)
+        state = sums[:hidden].astype(bf16).reshape(size, shard, links, columns)
+        state = jnp.moveaxis(state, 2, 1).reshape(size, links, 2, height, -1)
+        return [halves(state[:, :, part], 0, part) for part in range(2)]
+    tiles = -(-shard // height // 2)
+    shape = (size, links // 2, height, tiles * columns)
     out = pl.pallas_call(
-        functools.partial(
-            down_kernel, mine=mine, size=size, links=links, hidden=hidden, cut=cut, places=first_places()
-        ),
+        functools.partial(down_kernel, hidden=hidden, places=first_places()),
         grid=(hidden_pad // block,),
-        in_specs=[SMEM_SPEC, pl.BlockSpec((rows, block), lambda i: (0, i)), once(rows, width)]
-        + ([once(*shape)] if mine else []),
-        out_specs=[fixed(*part) for part in parts] if mine else fixed(*shape),
-        out_shape=[jax.ShapeDtypeStruct(part, bf16) for part in parts]
-        if mine
-        else jax.ShapeDtypeStruct(shape, bf16),
-        scratch_shapes=[pltpu.VMEM(shape, bf16)] if mine else [],
+        in_specs=[SMEM_SPEC]
+        + [pl.BlockSpec((rows, block), lambda i: (0, i))] * 2
+        + [once(rows, width), once(rows, width // 2)],
+        out_specs=[fixed(*shape)] * 4,
+        out_shape=[pltpu.HBM(shape, bf16)] * 4,
+        scratch_shapes=[pltpu.VMEM((size, links, shard, columns), bf16)],
         compiler_params=params(24, "arbitrary"),
-        cost_estimate=cost(rows * width * hidden, width * hidden + 2 * rows * (hidden + width)),
+        cost_estimate=cost(2 * rows * width * hidden, width * hidden + 4 * rows * (hidden + width)),
         name="down_sum",
-    )(meta, mixed, grad_result, *([add] if mine else []))
-    return [(out[0], out[1]), (out[2], out[3])] if mine else out
-
-
-def sum_kernel(meta_ref, left_ref, right_ref, add_ref, keep0, give0, keep1, give1, state_ref, *, size, links, places):
-    state_ref[...] = (tokens_dot(left_ref[meta_ref[2]], right_ref[...]) + add_ref[...].astype(f32)).astype(bf16)
+    )(meta, *far(mixed, mixed_other, grad_result, grad_other))
+    return [(out[0], out[1]), (out[2], out[3])]
+
+
+def sum_kernel(meta_ref, left_ref, left_other_ref, right_ref, right_other_ref, *rest, size, links, places, steps):
+    state_ref = rest[-1]
+    state_ref[...] = (
+        tokens_dot(left_ref[meta_ref[2]], right_ref[0]) + tokens_dot(left_other_ref[...], right_other_ref[0])
+    ).astype(bf16)
     rows = state_ref.shape[0] // (2 * size * links)
-    for part, (keep_ref, give_ref) in enumerate(((keep0, give0), (keep1, give1))):
-        own = meta_ref[3 + part]
-        for place in range(size):
-            for number in range(links // 2):
-                base = (2 * place + part) * links + split_index(number, places[part])
-                for ref, value in ((keep_ref, own), (give_ref, 1 - own)):
-                    start = (base + value * (1 << places[part])) * rows
-                    ref[place, number] = state_ref[pl.ds(pl.multiple_of(start, rows), rows), :]
-
-
-def sum_call(meta, left, right, add, block):
+
+    def put(outs):
+        for part in range(2):
+            own = meta_ref[3 + part]
+            for place in range(size):
+                for number in range(links // 2):
+                    base = (2 * place + part) * links + split_index(number, places[part])
+                    for ref, value in ((outs[2 * part], own), (outs[2 * part + 1], 1 - own)):
+                        start = (base + value * (1 << places[part])) * rows
+                        ref[place, number] = state_ref[pl.ds(pl.multiple_of(start, rows), rows), :]
+
+    planes = (len(rest) - 1) // 4
+    for plane in range(planes):
+        pl.when(pl.program_id(0) // steps == plane)(functools.partial(put, rest[4 * plane : 4 * plane + 4]))
+
+
+def sum_call(meta, left, left_other, right, right_other, block):
     _, tokens, height = left.shape
-    width = right.shape[1]
+    planes, _, width = right.shape
     size = lax.axis_size("fsdp")
     links = 1 << link_count()
     rows = height // (2 * size * links)
+    steps = width // block
     if rows % 16:
-        state = (tokens_dot(half_of(left, True), right) + add.astype(f32)).astype(bf16)
-        state = state.reshape(size, 2, links, rows, width)
-        return [halves(state[:, part], 0, part) for part in range(2)]
+        result = []
+        for plane in range(planes):
+            state = tokens_dot(half_of(left, True), right[plane]) + tokens_dot(left_other, right_other[plane])
+            state = state.astype(bf16).reshape(size, 2, links, rows, width)
+            result.append([halves(state[:, part], 0, part) for part in range(2)])
+        return result
     shape = (size, links // 2, rows, width)
+    right_spec = pl.BlockSpec((1, tokens, block), lambda i: (i // steps, 0, i % steps))
+
+    def out_spec(plane):
+        return pl.BlockSpec(
+            shape[:3] + (block,), lambda i: (0, 0, 0, jnp.clip(i - plane * steps, 0, steps - 1))
+        )
+
     out = pl.pallas_call(
-        functools.partial(sum_kernel, size=size, links=links, places=first_places()),
-        grid=(width // block,),
-        in_specs=[
-            SMEM_SPEC,
-            once(2, tokens, height),
-            pl.BlockSpec((tokens, block), lambda i: (0, i)),
-            pl.BlockSpec((height, block), lambda i: (0, i)),
-        ],
-        out_specs=[pl.BlockSpec((size, links // 2, rows, block), lambda i: (0, 0, 0, i))] * 4,
-        out_shape=[jax.ShapeDtypeStruct(shape, bf16)] * 4,
+        functools.partial(sum_kernel, size=size, links=links, places=first_places(), steps=steps),
+        grid=(planes * steps,),
+        in_specs=[SMEM_SPEC, once(2, tokens, height), once(tokens, height), right_spec, right_spec],
+        out_specs=[out_spec(plane) for plane in range(planes) for _ in range(4)],
+        out_shape=[pltpu.HBM(shape, bf16)] * (4 * planes),
         scratch_shapes=[pltpu.VMEM((height, block), bf16)],
-        compiler_params=params(12, "arbitrary"),
-        cost_estimate=cost(2 * tokens * height * width, 4 * height * width + 4 * tokens * width),
+        compiler_params=params(22, "arbitrary"),
+        cost_estimate=cost(4 * tokens * height * width * planes, 4 * planes * (height + tokens) * width),
         name="sum_rows",
-    )(meta, left, right, add)
-    return [(out[0], out[1]), (out[2], out[3])]
+    )(meta, left, left_other, right, right_other)
+    return [[(out[k], out[k + 1]), (out[k + 2], out[k + 3])] for k in range(0, 4 * planes, 4)]
 
 
 def fold_kernel(meta_ref, *refs, count, done, places):
@@ -836,12 +868,15 @@
         start = 0
         for number in range(count):
             keep_ref, got_ref = ins[4 * number + 2 * part], ins[4 * number + 2 * part + 1]
-            width = keep_ref.shape[3]
-            for index in range(keep_ref.shape[1] // 2):
-                base = split_index(index, places[part])
-                for ref, value in ((outs[2 * part], own), (outs[2 * part + 1], 1 - own)):
-                    link = base + value * (1 << places[part])
-                    ref[0, index, :, start : start + width] = added(keep_ref[0, link], got_ref[0, link])
+            size, links, _, width = keep_ref.shape
+            for place in range(size):
+                for index in range(links // 2):
+                    base = split_index(index, places[part])
+                    for ref, value in ((outs[2 * part], own), (outs[2 * part + 1], 1 - own)):
+                        link = base + value * (1 << places[part])
+                        ref[place, index, :, start : start + width] = added(
+                            keep_ref[place, link], got_ref[place, link]
+                        )
             start += width
 
 
@@ -860,25 +895,90 @@
             state = jnp.concatenate([added(*block[part]) for block in blocks], axis=3)
             result.append(halves(state, done, part))
         return result
-    spec = lambda shape: pl.BlockSpec((1,) + tuple(shape[1:]), lambda i: (i, 0, 0, 0))
     out = pl.pallas_call(
         functools.partial(fold_kernel, count=len(blocks), done=done, places=places),
-        grid=(size,),
-        in_specs=[SMEM_SPEC] + [spec(array.shape) for array in flat],
-        out_specs=[spec(shape) for shape in shapes],
-        out_shape=[jax.ShapeDtypeStruct(shape, bf16) for shape in shapes],
-        compiler_params=params(6, "arbitrary"),
+        grid=(1,),
+        in_specs=[SMEM_SPEC] + [once(*array.shape) for array in flat],
+        out_specs=[fixed(*shape) for shape in shapes],
+        out_shape=[pltpu.HBM(shape, bf16) for shape in shapes],
+        compiler_params=params(16, "arbitrary"),
         cost_estimate=cost(0, 3 * sum(array.size for array in flat)),
         name="fold",
-    )(meta, *flat)
+    )(meta, *far(*flat))
     return [(out[0], out[1]), (out[2], out[3])]
+
+
+def finish_kernel(meta_ref, m0, m1, g0, g1, w_ref, out_ref, norm_ref, *down_refs, padded, links):
+    step = pl.program_id(0)
+    mine = (step < 2) == (meta_ref[2] == 0)
+    first = step % 2 == 0
+    own = jnp.where(first, m0[...].astype(f32), m1[...].astype(f32))
+    got = jnp.where(first, g0[...].astype(f32), g1[...].astype(f32))
+    value = jnp.where(mine, own, got)
+    hidden = out_ref.shape[1] // 2
+    out_ref[:, :hidden] = value[:, :hidden]
+    out_ref[:, hidden:] = value[:, padded : padded + hidden]
+    sums = jnp.sum(out_ref[...] * w_ref[...].astype(f32), axis=1, keepdims=True)
+    norm_ref[0] = jnp.broadcast_to(sums, (sums.shape[0], LANES)).T[:1]
+    if down_refs:
+        (down_ref,) = down_refs
+        height = value.shape[0] // links
+        tiles = (value.shape[1] - 2 * padded) // LANES
+
+        def put(core, part):
+            for link in range(links):
+                for tile in range(tiles):
+                    top = (part * tiles + tile) * height
+                    if top < down_ref.shape[0]:
+                        lane = (core * links + link) * LANES
+                        start = 2 * padded + tile * LANES
+                        down_ref[top : top + height, lane : lane + LANES] = value[
+                            link * height : (link + 1) * height, start : start + LANES
+                        ]
+
+        for number in range(4):
+            pl.when(step == number)(functools.partial(put, number // 2, number % 2))
+
+
+def finish_call(meta, parts, w_in, padded, shard, model):
+    rows, columns = w_in.shape
+    quarter, width = parts[0].shape
+    links = 1 << link_count()
+    height = quarter // links
+    fast = fits(shard, model // 2 // links, height)
+    out = pl.pallas_call(
+        functools.partial(finish_kernel, padded=padded, links=links),
+        grid=(4,),
+        in_specs=[SMEM_SPEC]
+        + [once(quarter, width)] * 4
+        + [pl.BlockSpec((quarter, columns), lambda i: (i, 0))],
+        out_specs=[
+            pl.BlockSpec((quarter, columns), lambda i: (i, 0)),
+            pl.BlockSpec((1, 1, quarter), lambda i: (i, 0, 0)),
+        ]
+        + [fixed(shard, model)] * fast,
+        out_shape=[jax.ShapeDtypeStruct((rows, columns), f32), jax.ShapeDtypeStruct((4, 1, quarter), f32)]
+        + [jax.ShapeDtypeStruct((shard, model), f32)] * fast,
+        compiler_params=params(30, "arbitrary"),
+        cost_estimate=cost(4 * rows * columns, 10 * rows * columns),
+        name="finish",
+    )(meta, *far(*parts, w_in))
+    if fast:
+        return out
+    mine, got = [
+        jnp.stack([part[:, 2 * padded :] for part in pair]).reshape(1, 2, links, height, -1)
+        for pair in (parts[:2], parts[2:])
+    ]
+    whole = jnp.moveaxis(in_order(mine, got, 0, 0), 2, 1).reshape(2 * links, shard, -1)
+    return out[0], out[1], jnp.transpose(whole, (1, 0, 2)).reshape(shard, model).astype(f32)
 
 
 def last_kernel(*refs):
     k0, g0, k1, g1, out_ref = refs
     cut = k0.shape[2]
-    out_ref[0, :cut, :] = added(k0[0, 0], g0[0, 0])
-    out_ref[0, cut:, :] = added(k1[0, 0], g1[0, 0])
+    for place in range(k0.shape[0]):
+        out_ref[place, :cut, :] = added(k0[place, 0], g0[place, 0])
+        out_ref[place, cut:, :] = added(k1[place, 0], g1[place, 0])
 
 
 def fold_last(parts):
@@ -887,17 +987,16 @@
     rows = cut + k1.shape[2]
     if cut % 16 or k1.shape[2] % 16:
         return jnp.concatenate([added(k0, g0)[:, 0], added(k1, g1)[:, 0]], axis=1)
-    spec = lambda array: pl.BlockSpec((1,) + array.shape[1:], lambda i: (i, 0, 0, 0))
     return pl.pallas_call(
         last_kernel,
-        grid=(size,),
-        in_specs=[spec(array) for array in (k0, g0, k1, g1)],
-        out_specs=pl.BlockSpec((1, rows, width), lambda i: (i, 0, 0)),
+        grid=(1,),
+        in_specs=[once(*array.shape) for array in (k0, g0, k1, g1)],
+        out_specs=fixed(size, rows, width),
         out_shape=jax.ShapeDtypeStruct((size, rows, width), bf16),
-        compiler_params=params(6, "arbitrary"),
+        compiler_params=params(16, "arbitrary"),
         cost_estimate=cost(0, 6 * size * rows * width),
         name="fold_last",
-    )(k0, g0, k1, g1)
+    )(*far(k0, g0, k1, g1))
 
 
 def middle_back_kernel(
@@ -961,10 +1060,10 @@
             pltpu.VMEM((width, block), bf16),
             pltpu.VMEM((width, width), bf16),
         ],
-        compiler_params=params(40, "arbitrary"),
+        compiler_params=params(38, "arbitrary"),
         cost_estimate=cost(4 * rows * width * hidden, 4 * width * hidden + 4 * rows * hidden + 12 * rows * width),
         name="middle_back",
-    )(meta, grad_hidden, owns[0], *parts, owns[1], *parts, out_own, *parts, *parts, middle, upstream, valid, gains)
+    )(meta, grad_hidden, *far(owns[0], *parts, owns[1], *parts, out_own, *parts, *parts, middle, upstream), valid, gains)
 
 
 def input_back_kernel(
@@ -1010,10 +1109,10 @@
         out_specs=whole,
         out_shape=jax.ShapeDtypeStruct((rows, width), bf16),
         scratch_shapes=[pltpu.VMEM((rows, width), f32), pltpu.VMEM((width, block), bf16)],
-        compiler_params=params(48, "arbitrary"),
+        compiler_params=params(24, "arbitrary"),
         cost_estimate=cost(6 * rows * width * width, 6 * width * width + 14 * rows * width),
         name="input_back",
-    )(meta, grad_joint, own, *parts, x, grad_middle, gains)
+    )(meta, grad_joint, *far(own, *parts, x, grad_middle), gains)
 
 
 def rope_tables(positions):
@@ -1055,10 +1154,18 @@
     x = inputs.reshape(rows, width)
     upstream = cotangent.reshape(rows, width)
     grad_result = (upstream.astype(f32) * valid).astype(bf16)
+    grad_give = lax.dynamic_slice_in_dim(grad_result, (1 - bit_value(0)) * (width // 2), width // 2, 1)
+    grad_other = flip(grad_give, 0)
     own_rows = slice(WIN, WIN + shard_rows)
     own_cosine, own_sine = cosine[own_rows], sine[own_rows]
-    came_one, piece_two, piece_three, own_in, gains, cosine, sine, own_cosine, own_sine, grad_result, valid = after(
-        (came_one, piece_two, piece_three, own_in, gains, cosine, sine, own_cosine, own_sine, grad_result, valid)
+    (
+        came_one, piece_two, piece_three, own_in, gains, cosine, sine, own_cosine, own_sine, grad_result, grad_other,
+        valid,
+    ) = after(
+        (
+            came_one, piece_two, piece_three, own_in, gains, cosine, sine, own_cosine, own_sine, grad_result,
+            grad_other, valid,
+        )
     )
 
     one = widen(row_states(came_one), steps[0], 1)
@@ -1086,69 +1193,77 @@
         two = widen(two, bits, 1)
     came_three = turned_before(piece_three, range(1, size))
     attended, saved = attend_call(meta_rows, qkv, rim_up, rim_down, seqs)
-    two, came_three, attended = after((two, came_three, attended))
+    two, came_three, attended, normed_first = after((two, came_three, attended, normed_first))
 
     parts_two = row_parts(two)
     three = widen(column_states(came_three), steps[0], 1)
-    parts_two, three, attended = after((parts_two, three, attended))
+    first_other = flip(half_of(normed_first, False), 0)
+    parts_two, three, attended, first_other = after((parts_two, three, attended, first_other))
 
     for bits in steps[1:]:
         three = widen(three, bits, 1)
     middle, normed_second, attended_split = out_call(
         meta, attended, w_out, parts_two, 2 * hidden_pad, block, x, valid, gains_all
     )
+    second_other = flip(half_of(normed_second, False), 0)
+    attended_other = flip(half_of(attended_split, False), 0)
     mixed, slope, act = gate_call(meta, normed_second, own_in, parts_two, block)
-    three, mixed, slope, act, normed_second = after((three, mixed, slope, act, normed_second))
+    three, mixed, slope, act, second_other, attended_other = after(
+        (three, mixed, slope, act, second_other, attended_other)
+    )
 
     parts_three = column_parts(three)
-    down_give = down_call(meta, mixed, grad_result, size, hidden, block)
-    down_got = flip(down_give, 0)
-    parts_three, down_got, slope, mixed = after((parts_three, down_got, slope, mixed))
-
-    down = down_call(meta, mixed, grad_result, size, hidden, block, down_got)
-    down, slope, mixed = after((down, slope, mixed))
+    parts_three, mixed, slope, act = after((parts_three, mixed, slope, act))
+
+    mixed_other = flip(mixed, 0)
+    grad_hidden, whole_down = gate_back_call(meta, grad_result, w_down, parts_three, slope, act, block)
+    grad_hidden, mixed, mixed_other = after((grad_hidden, mixed, mixed_other))
+
+    hidden_other = flip(grad_hidden, 0)
+    down = down_call(meta, mixed, mixed_other, grad_result, grad_other, hidden, block)
+    result = jnp.dot(mixed, whole_down, preferred_element_type=f32)
+    output = (middle + valid * result).astype(bf16)
+    down, hidden_other, grad_hidden, output = after((down, hidden_other, grad_hidden, output))
 
     down = swap(down, 0)
-    grad_hidden, whole_down = gate_back_call(meta, grad_result, w_down, parts_three, slope, act, block)
-    give_left = half_of(normed_second, False)
-    in_give = [tokens_dot(give_left, grad_hidden[half]).astype(bf16) for half in range(2)]
-    down, in_give, grad_hidden, whole_down, mixed, normed_second = after(
-        (down, in_give, grad_hidden, whole_down, mixed, normed_second)
-    )
-
-    in_got = [flip(give, 0) for give in in_give]
+    one, two = sum_call(meta, normed_second, second_other, grad_hidden, hidden_other, block)
+    down, one, two, grad_hidden = after((down, one, two, grad_hidden))
+
+    one = swap(one, 0)
     for done in range(1, len(steps)):
         down = swap(fold_next(meta, [down], done), done)
-    result = jnp.dot(mixed, whole_down, preferred_element_type=f32)
-    output = (middle + valid * result).astype(bf16)
-    in_got, output, grad_hidden, normed_second, down = after((in_got, output, grad_hidden, normed_second, down))
-
-    one, two = [sum_call(meta, normed_second, grad_hidden[half], in_got[half], block) for half in range(2)]
-    one, two, grad_hidden = after((one, two, grad_hidden))
-
-    one = swap(one, 0)
-    down_slots = fold_last(down)
-    down_came = turned_slots(down_slots, range(1, size))
     grad_middle, grad_branch, grad_att = middle_back_call(
         meta, grad_hidden, own_in, parts_two, w_out, middle, upstream, valid, gains_all, block
     )
-    one, two, down_came, grad_branch, grad_att = after((one, two, down_came, grad_branch, grad_att))
+    one, two, grad_branch, grad_att, down = after((one, two, grad_branch, grad_att, down))
 
     two = swap(two, 0)
     for done in range(1, len(steps)):
         one = swap(fold_next(meta, [one], done), done)
-    out_give = tokens_dot(half_of(attended_split, False), grad_branch).astype(bf16)
-    out_got, grad_branch, grad_att = after((flip(out_give, 0), grad_branch, grad_att))
-    outs = sum_call(meta, attended_split, grad_branch, out_got, width // 2)
-    grad_att, outs = after((grad_att, outs))
+    down_slots = fold_last(down)
+    down_came = turned_slots(down_slots, near)
     grad_q, grad_k, grad_v, edge_up, edge_down = attend_back_call(
         qkv, rim_up, rim_down, saved, grad_att, cosine, sine, seqs
     )
-    one, two, outs, edge_up, edge_down, grad_q = after((one, two, outs, edge_up, edge_down, grad_q))
-
+    one, two, edge_up, edge_down, grad_q, grad_branch, down_slots, down_came = after(
+        (one, two, edge_up, edge_down, grad_q, grad_branch, down_slots, down_came)
+    )
+
+    def spread_start(owned):
+        ones = (1,) * link_count()
+        cut = owned.shape[0] // 2
+        return [part.reshape(ones + part.shape) for part in (owned[:cut], owned[cut:])]
+
+    def spread_end(states):
+        mine = jnp.stack([state.reshape((-1,) + state.shape[-2:]) for state in states])
+        return in_order(mine[None], flip(mine, 0)[None], 0, 0)
+
+    from_next, from_before = neighbours(edge_up, edge_down)
+    branch_other = flip(grad_branch, 0)
+    two, branch_other = after((two, branch_other))
     for done in range(1, len(steps)):
         two = swap(fold_next(meta, [two], done), done)
-    from_next, from_before = neighbours(edge_up, edge_down)
+    (outs,) = sum_call(meta, attended_split, attended_other, grad_branch[None], branch_other[None], width // 2)
     one_slots = fold_last(one)
     from_next, from_before, two, one_slots, outs = after((from_next, from_before, two, one_slots, outs))
 
@@ -1161,72 +1276,54 @@
         return own.reshape(rows, width).astype(bf16)
 
     outs = swap(outs, 0)
-    one_came = turned_slots(one_slots, near) + turned_slots(one_slots, far)
+    down_came = down_came + turned_slots(down_slots, far) + turned_slots(down_slots, middle_way)
     grad_joint = jnp.concatenate([grad_q, with_edges(grad_k, 0), with_edges(grad_v, 1)], axis=1)
-    give_left = half_of(normed_first, False)
-    qkv_give = tokens_dot(give_left, grad_joint).astype(bf16)
-    qkv_got, grad_last = after((flip(qkv_give, 0), grad_joint))
-    last = sum_call(meta, normed_first, grad_last, qkv_got, width)
+    joint_other = flip(grad_joint, 0)
+    (last,) = sum_call(meta, normed_first, first_other, grad_joint[None], joint_other[None], width)
     two_slots = fold_last(two)
-    last, grad_last, outs, one_came, two_slots, one_slots = after(
-        (last, grad_last, outs, one_came, two_slots, one_slots)
+    last, grad_joint, outs, one_slots, two_slots, down_came, down_slots = after(
+        (last, grad_joint, outs, one_slots, two_slots, down_came, down_slots)
     )
 
     last = swap(last, 0)
-    one_came = one_came + turned_slots(one_slots, middle_way)
-    two_came = turned_slots(two_slots, near) + turned_slots(two_slots, far)
-    grad_inputs = input_back_call(meta, grad_last, w_qkv, parts_one, x, grad_middle, gains_all)
-    last, grad_inputs, one_came, two_came, one_slots, two_slots = after(
-        (last, grad_inputs, one_came, two_came, one_slots, two_slots)
-    )
-
-    def spread_start(owned, cut):
-        ones = (1,) * link_count()
-        return [part.reshape(ones + part.shape) for part in (owned[:cut], owned[cut:])]
-
-    def spread_end(states):
-        mine = jnp.stack([state.reshape((-1,) + state.shape[-2:]) for state in states])
-        whole = in_order(mine[None], flip(mine, 0)[None], 0, 0)
-        return whole.reshape(-1, mine.shape[-1])
+    one_came = turned_slots(one_slots, range(1, size))
+    grad_inputs = input_back_call(meta, grad_joint, w_qkv, parts_one, x, grad_middle, gains_all)
+    last, grad_inputs, one_came, one_slots, two_slots, down_came, down_slots = after(
+        (last, grad_inputs, one_came, one_slots, two_slots, down_came, down_slots)
+    )
 
     last = [last, outs]
     for done in range(1, len(steps)):
         last = [swap(fold_next(meta, last, done), done)]
-    two_came = two_came + turned_slots(two_slots, middle_way)
-    owned_down = slot_sum(down_slots, down_came)
-    spread_down = widen(spread_start(owned_down, half_rows(hidden // size)), steps[0], 0)
-    owned_one = slot_sum(one_slots, one_came)
-    last, two_came, owned_one, spread_down = after((last, two_came, owned_one, spread_down))
+    two_came = turned_slots(two_slots, range(1, size))
+    owned = [slot_sum(one_slots, one_came), slot_sum(down_slots, down_came)]
+    last, two_came, two_slots, owned = after((last, two_came, two_slots, owned))
 
     last_slots = fold_last(last[0])
     last_came = turned_slots(last_slots, near) + turned_slots(last_slots, far)
-    owned_in = jnp.concatenate([owned_one, slot_sum(two_slots, two_came)], axis=1)
-    spread_in = widen(spread_start(owned_in, owned_in.shape[0] // 2), steps[0], 0)
-    last_came, spread_in, last_slots, spread_down = after((last_came, spread_in, last_slots, spread_down))
+    spread_in = widen(
+        spread_start(jnp.concatenate([owned[0], slot_sum(two_slots, two_came), owned[1]], axis=1)), steps[0], 0
+    )
+    last_came, spread_in, last_slots = after((last_came, spread_in, last_slots))
 
     last_came = last_came + turned_slots(last_slots, middle_way)
     for bits in steps[1:]:
         spread_in = widen(spread_in, bits, 0)
-        spread_down = widen(spread_down, bits, 0)
-    last_came, spread_in, last_slots, spread_down = after((last_came, spread_in, last_slots, spread_down))
-
-    owned_last = slot_sum(last_slots, last_came)
-    spread_last = widen(spread_start(owned_last, owned_last.shape[0] // 2), steps[0], 0)
-    down_mine = jnp.concatenate([state.reshape((-1,) + state.shape[-2:]) for state in spread_down], axis=1)
-    grad_down = in_order(down_mine, flip(down_mine, 0), 0, 0)
-    grad_in = spread_end(spread_in)
-    spread_last, grad_in, grad_down = after((spread_last, grad_in, grad_down))
+    last_came, spread_in, last_slots = after((last_came, spread_in, last_slots))
+
+    spread_last = widen(spread_start(slot_sum(last_slots, last_came)), steps[0], 0)
+    in_parts = [state.reshape((-1, state.shape[-1])) for state in spread_in]
+    in_parts = in_parts + [flip(part, 0) for part in in_parts]
+    spread_last, in_parts = after((spread_last, in_parts))
 
     for bits in steps[1:]:
         spread_last = widen(spread_last, bits, 0)
-    spread_last, grad_in, grad_down = after((spread_last, grad_in, grad_down))
-
+    grad_in, grad_second, grad_down = finish_call(meta, in_parts, w_in, hidden_pad, hidden // size, width)
+    spread_last, grad_in, grad_second, grad_down = after((spread_last, grad_in, grad_second, grad_down))
+
+    grad_second = grad_second.reshape(-1) / norm_second.astype(f32)
     grad_last = spread_end(spread_last)
-    grad_in = jnp.concatenate(
-        [grad_in[:, :hidden], grad_in[:, hidden_pad : hidden_pad + hidden]], axis=1
-    ).astype(f32)
-    grad_second = jnp.sum(grad_in * w_in.astype(f32), axis=1) / norm_second.astype(f32)
-    grad_down = jnp.transpose(grad_down, (1, 0, 2)).reshape(hidden // size, width).astype(f32)
+    grad_last = grad_last.reshape(-1, grad_last.shape[-1])
     grad_qkv = grad_last[:, : 3 * width].astype(f32)
     grad_out = grad_last[:, 3 * width :].astype(f32)
     grad_first = jnp.sum(grad_qkv * w_qkv.astype(f32), axis=1) / norm_first.astype(f32)

time: 435 us -> 417 us (0.959)
  Pallas kernels: 124 us -> 150 us
  local copies, waits for them, and re-layouts: 51.8 us -> 35.1 us
  matrix products: 13.8 us -> 4.13 us
  starting transfers between devices: 99.6 us -> 92.7 us
  waiting for transfers between devices: 108 us -> 102 us
    unnamed x242 -> x168, local copies, waits for them, and re-layouts: 37.7 us -> 22 us
    pallas_call x6, Pallas kernels: 10.7 us -> 23.6 us  [the longest x1 8.78 us: down_call(): pl.pallas_call(functools.partial(down_kernel, hidden=hidden, places=first...]
    ppermute x56 -> x55, waiting for transfers between devices: 79.6 us -> 69.2 us  [flip(): return lax.ppermute(value, 'rep', [(i, i ^ 1 << bit) for i in range(size)])]
    dot_general x4 -> x0, matrix products: 9.59 us -> none  [tokens_dot(): lax.dot_general(left, right, (((0,), (0,)), ((), ())), preferred_element_...]
    pallas_call x4, Pallas kernels: 5.49 us -> 12.7 us  [fold_next(): pl.pallas_call(functools.partial(fold_kernel, count=len(blocks), done=don...]
    pallas_call x4 -> x3, Pallas kernels: 13.9 us -> 20.9 us  [sum_call(): pl.pallas_call(functools.partial(sum_kernel, size=size, links=links, plac...]
    ppermute x56 -> x55, starting transfers between devices: 45.8 us -> 39.6 us  [flip(): return lax.ppermute(value, 'rep', [(i, i ^ 1 << bit) for i in range(size)])]
  transfers between devices with their start and end apart: 81 -> 80, of which waited for: 36 -> 35; matrix products, arithmetic and copies ran while one was open for 9% -> 7% of each run, Pallas kernels for 25% -> 34%
where the time goes in v4:
time: 417 us; the launch traced here: 409 us
  Pallas kernels  150 us (36%)
  waiting for transfers between devices  102 us (24%)
  starting transfers between devices  92.7 us (22%)
  local copies, waits for them, and re-layouts  35.1 us (8%)
  other arithmetic  22.5 us (5%)
    ppermute x55, waiting for transfers between devices, flip(): return lax.ppermute(value, 'rep', [(i, i ^ 1 << bit) for i in range(size)])  69.2 us
    ppermute x21, starting transfers between devices, turn(): lax.ppermute(value, 'fsdp', [(i, (i + steps) % size) for i in range(size)])  41.3 us
    ppermute x55, starting transfers between devices, flip(): return lax.ppermute(value, 'rep', [(i, i ^ 1 << bit) for i in range(size)])  39.6 us
    ppermute x21, waiting for transfers between devices, turn(): lax.ppermute(value, 'fsdp', [(i, (i + steps) % size) for i in range(size)])  29.7 us
    unnamed x168, local copies, waits for them, and re-layouts  22 us
    pallas_call x3, Pallas kernels, sum_call(): pl.pallas_call(functools.partial(sum_kernel, size=size, links=links, plac...  20.9 us
    pallas_call x1, Pallas kernels, attend_back_call(): pl.pallas_call(attend_back_kernel, grid=(seqs, width // block), in_specs=...  17.4 us
    pallas_call x1, Pallas kernels, middle_back_call(): pl.pallas_call(middle_back_kernel, grid=(hidden // block,), in_specs=[SME...  16 us
  transfers between devices with their start and end apart: 80, of which 35 were waited for; matrix products, arithmetic and copies ran while one was open for 7% of the time, Pallas kernels for 34%

profile of v4, /device:TPU:0, one launch (start us, length us, event | category | flops | bytes accessed | tf_op | source)
XLA Modules:
  0.0 408.8 jit_solution(313405855916381824)
XLA Ops:
  4.0 3.0 collective-permute-start
  7.0 2.6 collective-permute-start.1
  29.4 4.9 %collective-permute-start.6 = (bf16[2,16,6400]{2,1,0:T(8,128)(2,1)}, bf16[2,16,6400]{2,1,0:T(8,128)(2,1)S(1)}, u32[]{:S(2)}, u32[]{:S(2)}) collective-permute-start(bf16[2,16,6400]{2,1,0:T(8,128)(2,1)} %maximum_bitcast_fusion.2), channel_id=1, source_target_pairs={{0,1},{1,2},{2,3},{3,0},{4,5},{5,6},{6,7},{7,4},{8,9},{9,10},{10,1... | collective-permute-start | bytes 1228808 | tf_op jit(solution)/shard_map/ppermute | solution.py:50
  36.9 6.7 %collective-permute-done.6 = bf16[2,16,6400]{2,1,0:T(8,128)(2,1)S(1)} collective-permute-done((bf16[2,16,6400]{2,1,0:T(8,128)(2,1)}, bf16[2,16,6400]{2,1,0:T(8,128)(2,1)S(1)}, u32[]{:S(2)}, u32[]{:S(2)}) %collective-permute-start.6) | collective-permute-done | bytes 409632 | tf_op jit(solution)/shard_map/ppermute | solution.py:50
  46.4 10.9 %collective-permute-done.8 = bf16[3,2,1,16,3200]{4,3,2,1,0:T(8,128)(2,1)S(1)} collective-permute-done((bf16[3,2,1,16,3200]{4,3,2,1,0:T(8,128)(2,1)S(1)}, bf16[3,2,1,16,3200]{4,3,2,1,0:T(8,128)(2,1)S(1)}, u32[]{:S(2)}, u32[]{:S(2)}) %collective-permute-start.8) | collective-permute-done | bytes 614432 | tf_op jit(solution)/shard_map/ppermute | solution.py:45
  58.8 2.4 collective-permute-start.12
  62.8 11.0 %qkv.1 = (bf16[2,512,512]{2,1,0:T(8,128)(2,1)S(1)}, bf16[3,512,1024]{2,1,0:T(8,128)(2,1)S(1)}, f32[8,1024]{1,0:T(8,128)S(1)}) custom-call(s32[7]{0:T(128)S(1)} %stack.61.meta_ref, bf16[512,1024]{1,0:T(8,128)(2,1)} %bitcast.190, bf16[256,3072]{1,0:T(8,128)(2,1)} %own_ref.7, bf16[3,64,3200]{2,1,0:T(8,128)(2,1)} %bitcast.184, bf16[3,64,3200]{2,1,0:T(8,128)(2,1)} %bitcast.180, ...), custom_call_target="tpu_custom_call" | custom-call | flops 3221225472 | bytes 11534336 | tf_op jit(solution)/shard_map/qkv/pallas_call | solution.py:360
  75.2 5.3 %collective-permute-done.12 = bf16[2,16,6400]{2,1,0:T(8,128)(2,1)S(1)} collective-permute-done((bf16[2,16,6400]{2,1,0:T(8,128)(2,1)}, bf16[2,16,6400]{2,1,0:T(8,128)(2,1)S(1)}, u32[]{:S(2)}, u32[]{:S(2)}) %collective-permute-start.12) | collective-permute-done | bytes 409632 | tf_op jit(solution)/shard_map/ppermute | solution.py:50
  83.6 4.6 %collective-permute-start.14 = (bf16[2,128,1024]{2,1,0:T(8,128)(2,1)S(1)}, bf16[2,128,1024]{2,1,0:T(8,128)(2,1)S(1)}, u32[]{:S(2)}, u32[]{:S(2)}) collective-permute-start(bf16[2,128,1024]{2,1,0:T(8,128)(2,1)S(1)} %bitcast.226), channel_id=1, source_target_pairs={{0,1},{1,2},{2,3},{4,5},{5,6},{6,7},{8,9},{9,10},{10,11},{12,13},{... | collective-permute-start | bytes 1572872 | tf_op jit(solution)/shard_map/ppermute | solution.py:208
  88.2 8.0 %collective-permute-done.16 = bf16[3,1,1,16,6400]{4,3,2,1,0:T(8,128)(2,1)S(1)} collective-permute-done((bf16[3,1,1,16,6400]{4,3,2,1,0:T(8,128)(2,1)S(1)}, bf16[3,1,1,16,6400]{4,3,2,1,0:T(8,128)(2,1)S(1)}, u32[]{:S(2)}, u32[]{:S(2)}) %collective-permute-start.16) | collective-permute-done | bytes 614432 | tf_op jit(solution)/shard_map/ppermute | solution.py:45
  99.5 2.5 collective-permute-start.19
  102.5 2.3 collective-permute-start.21
  106.3 11.3 %attend.1 = (bf16[512,1024]{1,0:T(8,128)(2,1)S(1)}, bf16[2,8,2,256,256]{4,3,2,1,0:T(8,128)(2,1)}) custom-call(s32[3]{0:T(128)S(1)} %pad_add_fusion.meta_ref, bf16[3,512,1024]{2,1,0:T(8,128)(2,1)S(1)} %get-tuple-element.289.q_ref.k_ref.v_ref, bf16[3,512,1024]{2,1,0:T(8,128)(2,1)S(1)} %get-tuple-element.289.q_ref.k_ref.v_ref, ...), custom_call_target="tpu_custom_call" | custom-call | flops 1073741824 | bytes 5242880 | tf_op jit(solution)/shard_map/attend/pallas_call | solution.py:452
  118.6 5.8 %collective-permute-done.18 = bf16[3,2,1,16,6400]{4,3,2,1,0:T(8,128)(2,1)S(1)} collective-permute-done((bf16[3,2,1,16,6400]{4,3,2,1,0:T(8,128)(2,1)S(1)}, bf16[3,2,1,16,6400]{4,3,2,1,0:T(8,128)(2,1)S(1)}, u32[]{:S(2)}, u32[]{:S(2)}) %collective-permute-start.18) | collective-permute-done | bytes 1228832 | tf_op jit(solution)/shard_map/ppermute | solution.py:45
  126.3 4.5 %collective-permute-done.17 = bf16[3,1,2,16,6400]{4,3,0,2,1:T(8,128)(2,1)S(1)} collective-permute-done((bf16[3,1,2,16,6400]{4,3,0,2,1:T(8,128)(2,1)S(1)}, bf16[3,1,2,16,6400]{4,3,0,2,1:T(8,128)(2,1)S(1)}, u32[]{:S(2)}, u32[]{:S(2)}) %collective-permute-start.17) | collective-permute-done | bytes 1228832 | tf_op jit(solution)/shard_map/ppermute | solution.py:45
  138.0 4.8 %collective-permute-done.25 = bf16[3,1,1,320,128]{4,3,0,2,1:T(8,128)(2,1)S(1)} collective-permute-done((bf16[3,1,1,320,128]{4,3,0,2,1:T(8,128)(2,1)S(1)}, bf16[3,1,1,320,128]{4,3,0,2,1:T(8,128)(2,1)S(1)}, u32[]{:S(2)}, u32[]{:S(2)}) %collective-permute-start.25) | collective-permute-done | bytes 245792 | tf_op jit(solution)/shard_map/ppermute | solution.py:45
  142.9 2.6 collective-permute-done.24
  146.4 5.8 %out_norm.1 = (f32[512,1024]{1,0:T(8,128)}, bf16[2,512,512]{2,1,0:T(8,128)(2,1)S(1)}, bf16[2,512,512]{2,1,0:T(8,128)(2,1)S(1)}) custom-call(s32[7]{0:T(128)S(1)} %stack.61.meta_ref, bf16[512,1024]{1,0:T(8,128)(2,1)S(1)} %copy-done.15, bf16[256,1024]{1,0:T(8,128)(2,1)} %out_own_ref.1, bf16[3,64,6400]{2,1,0:T(8,128)(2,1)} %bitcast.23.p0.q0.r0.s0, ...), custom_call_target="tpu_custom_call" | custom-call | flops 1073741824 | bytes 8388608 | tf_op jit(solution)/shard_map/out_norm/pallas_call | solution.py:579
  154.1 11.9 %gate.1 = (bf16[512,2688]{1,0:T(8,128)(2,1)}, bf16[512,2688]{1,0:T(8,128)(2,1)}, bf16[512,2688]{1,0:T(8,128)(2,1)}) custom-call(s32[7]{0:T(128)S(1)} %stack.61.meta_ref, bf16[2,512,512]{2,1,0:T(8,128)(2,1)S(1)} %get-tuple-element.310.n_ref.left_ref, bf16[256,2688]{1,0:T(8,128)(2,1)} %copy-done.33, bf16[3,64,6400]{2,1,0:T(8,128)(2,1)} %bitcast.23.p0.q0.r0.s0, ...), custom_call_target="tpu_custom_call" | custom-call | flops 5637144576 | bytes 19267584 | tf_op jit(solution)/shard_map/gate/pallas_call | solution.py:624
  168.5 3.4 collective-permute-done.32.p3
  173.2 9.2 %gate_back.1 = (bf16[2,512,2688]{2,1,0:T(8,128)(2,1)S(1)}, bf16[2688,1024]{1,0:T(8,128)(2,1)S(1)}) custom-call(s32[7]{0:T(128)S(1)} %stack.61.meta_ref, bf16[512,1024]{1,0:T(8,128)(2,1)} %copy-done.36, bf16[656,1024]{1,0:T(8,128)(2,1)} %own_ref.6, bf16[3,4,336,128]{3,2,1,0:T(8,128)(2,1)} %bitcast.204, bf16[3,4,320,128]{3,2,1,0:T(8,128)(2,1)} %bitcast.210, ...), custom_call_target="tpu_custom_call" | custom-call | flops 2818572288 | bytes 22020096 | tf_op jit(solution)/shard_map/gate_back/pallas_call | solution.py:710
  184.1 8.8 %down_sum.1 = (bf16[4,2,16,2688]{3,2,1,0:T(8,128)(2,1)}, bf16[4,2,16,2688]{3,2,1,0:T(8,128)(2,1)}, bf16[4,2,16,2688]{3,2,1,0:T(8,128)(2,1)}, bf16[4,2,16,2688]{3,2,1,0:T(8,128)(2,1)}) custom-call(s32[7]{0:T(128)S(1)} %stack.61.meta_ref, bf16[512,2688]{1,0:T(8,128)(2,1)} %get-tuple-element.330.m_ref, bf16[512,2688]{1,0:T(8,128)(2,1)} %copy-done.78, ...), custom_call_target="tpu_custom_call" | custom-call | flops 2751463424 | bytes 10158080 | tf_op jit(solution)/shard_map/down_sum/pallas_call | solution.py:790
  192.9 4.1 %add_convert_fusion.2 = bf16[512,1024]{1,0:T(8,128)(2,1)} fusion(f32[512,1024]{1,0:T(8,128)S(1)} %copy-done.41, f32[512]{0:T(512)S(1)} %bitcast.229, bf16[512,2688]{1,0:T(8,128)(2,1)S(1)} %copy-done.77, bf16[2688,1024]{1,0:T(8,128)(2,1)S(1)} %get-tuple-element.339), kind=kOutput, calls=%fused_computation.7 | convolution fusion | flops 2820145152 | bytes 11405312 | tf_op jit(solution)/shard_map/dot_general | solution.py:1224
  199.3 11.2 %sum_rows.3 = (bf16[4,2,16,2688]{3,2,1,0:T(8,128)(2,1)}, bf16[4,2,16,2688]{3,2,1,0:T(8,128)(2,1)}, bf16[4,2,16,2688]{3,2,1,0:T(8,128)(2,1)}, bf16[4,2,16,2688]{3...) custom-call(s32[7]{0:T(128)S(1)} %stack.61.meta_ref, ...), custom_call_target="tpu_custom_call" | custom-call | flops 5637144576 | bytes 22020096 | tf_op jit(solution)/shard_map/sum_rows/pallas_call | solution.py:850
  210.5 4.0 collective-permute-done.35.refs_1_
  216.8 2.9 fold.4
  222.9 16.0 %middle_back.1 = (f32[512,1024]{1,0:T(8,128)S(1)}, bf16[512,1024]{1,0:T(8,128)(2,1)S(1)}, bf16[512,1024]{1,0:T(8,128)(2,1)S(1)}) custom-call(s32[7]{0:T(128)S(1)} %stack.61.meta_ref, bf16[2,512,2688]{2,1,0:T(8,128)(2,1)S(1)} %get-tuple-element.365.right_ref.gu_ref, bf16[256,2688]{1,0:T(8,128)(2,1)} %copy-done.33, bf16[3,64,6400]{2,1,0:T(8,128)(2,1)} %bitcast.23.p0.q0.r0.s0, ...), custom_call_target="tpu_custom_call" | custom-call | flops 5637144576 | bytes 22806528 | tf_op jit(solution)/shard_map/middle_back/pallas_call | solution.py:1045
  243.1 3.1 fold.5
  251.9 17.4 %attend_back.1 = (bf16[512,1024]{1,0:T(8,128)(2,1)S(1)}, f32[512,1024]{1,0:T(8,128)S(1)}, f32[512,1024]{1,0:T(8,128)S(1)}, bf16[2,128,1024]{2,1,0:T(8,128)(2,1)S(1)}, bf16[2,128,1024]{2,1,0:T(8,128)(2,1)S(1)}) custom-call(bf16[3,512,1024]{2,1,0:T(8,128)(2,1)S(1)} %get-tuple-element.289.q_ref.k_ref.v_ref, ...), custom_call_target="tpu_custom_call" | custom-call | flops 2684354560 | bytes 10485760 | tf_op jit(solution)/shard_map/attend_back/pallas_call | solution.py:530
  271.0 4.6 %collective-permute-start.47 = (bf16[2,128,1024]{2,1,0:T(8,128)(2,1)S(1)}, bf16[2,128,1024]{2,1,0:T(8,128)(2,1)S(1)}, u32[]{:S(2)}, u32[]{:S(2)}) collective-permute-start(bf16[2,128,1024]{2,1,0:T(8,128)(2,1)S(1)} %get-tuple-element.403), channel_id=1, source_target_pairs={{0,1},{1,2},{2,3},{4,5},{5,6},{6,7},{8,9},{9,10},{10,11},{12,13},{... | collective-permute-start | bytes 1572872 | tf_op jit(solution)/shard_map/ppermute | solution.py:208
  275.6 2.9 fold.6
  281.6 3.1 sum_rows.4
  289.6 1.9 pad_maximum_fusion
  292.7 2.3 collective-permute-start.54
  299.3 1.9 copy-done.4
  301.2 6.6 %sum_rows.5 = (bf16[4,2,16,3072]{3,2,1,0:T(8,128)(2,1)}, bf16[4,2,16,3072]{3,2,1,0:T(8,128)(2,1)}, bf16[4,2,16,3072]{3,2,1,0:T(8,128)(2,1)}, bf16[4,2,16,3072]{3,2,1,0:T(8,128)(2,1)}) custom-call(s32[7]{0:T(128)S(1)} %stack.61.meta_ref, bf16[2,512,512]{2,1,0:T(8,128)(2,1)S(1)} %copy-done.20, bf16[512,512]{1,0:T(8,128)(2,1)S(1)} %copy-done.26, ...), custom_call_target="tpu_custom_call" | custom-call | flops 3221225472 | bytes 12582912 | tf_op jit(solution)/shard_map/sum_rows/pallas_call | solution.py:850
  314.8 2.8 collective-permute-start.60
  317.7 9.9 %input_back.1 = bf16[512,1024]{1,0:T(8,128)(2,1)} custom-call(s32[7]{0:T(128)S(1)} %stack.61.meta_ref, bf16[512,3072]{1,0:T(8,128)(2,1)S(1)} %get-tuple-element.449.gqkv_ref, bf16[256,3072]{1,0:T(8,128)(2,1)} %own_ref.7, bf16[3,64,3200]{2,1,0:T(8,128)(2,1)} %bitcast.186, bf16[3,64,3200]{2,1,0:T(8,128)(2,1)} %bitcast.182, ...), custom_call_target="tpu_custom_call" | custom-call | flops 3221225472 | bytes 13631488 | tf_op jit(solution)/shard_map/input_back/pallas_call | solution.py:1099
  329.1 3.9 fold.7
  341.8 2.0 collective-permute-done.63
  343.8 4.4 %collective-permute-done.64 = bf16[32,2688]{1,0:T(8,128)(2,1)S(1)} collective-permute-done((bf16[32,2688]{1,0:T(8,128)(2,1)S(1)}, bf16[32,2688]{1,0:T(8,128)(2,1)S(1)}, u32[]{:S(2)}, u32[]{:S(2)}) %collective-permute-start.64) | collective-permute-done | bytes 172064 | tf_op jit(solution)/shard_map/ppermute | solution.py:50
  352.7 4.2 %collective-permute-start.66 = (bf16[32,4096]{1,0:T(8,128)(2,1)S(1)}, bf16[32,4096]{1,0:T(8,128)(2,1)S(1)}, u32[]{:S(2)}, u32[]{:S(2)}) collective-permute-start(bf16[32,4096]{1,0:T(8,128)(2,1)S(1)} %get-tuple-element.535), channel_id=1, source_target_pairs={{0,1},{1,2},{2,3},{3,0},{4,5},{5,6},{6,7},{7,4},{8,9},{9,10},{10,1... | collective-permute-start | bytes 786440 | tf_op jit(solution)/shard_map/ppermute | solution.py:50
  358.9 6.2 %collective-permute-done.66 = bf16[32,4096]{1,0:T(8,128)(2,1)S(1)} collective-permute-done((bf16[32,4096]{1,0:T(8,128)(2,1)S(1)}, bf16[32,4096]{1,0:T(8,128)(2,1)S(1)}, u32[]{:S(2)}, u32[]{:S(2)}) %collective-permute-start.66) | collective-permute-done | bytes 262176 | tf_op jit(solution)/shard_map/ppermute | solution.py:50
  365.1 2.7 collective-permute-done.67
  370.0 10.5 %collective-permute-done.72 = bf16[2,1,16,8064]{3,2,1,0:T(8,128)(2,1)S(1)} collective-permute-done((bf16[2,1,16,8064]{3,2,1,0:T(8,128)(2,1)S(1)}, bf16[2,1,16,8064]{3,2,1,0:T(8,128)(2,1)S(1)}, u32[]{:S(2)}, u32[]{:S(2)}) %collective-permute-start.72) | collective-permute-done | bytes 516128 | tf_op jit(solution)/shard_map/ppermute | solution.py:45
  385.9 2.0 collective-permute-done.73
  391.5 8.7 %finish.1 = (f32[256,5248]{1,0:T(8,128)}, f32[4,1,64]{2,1,0:T(1,128)S(1)}, f32[656,1024]{1,0:T(8,128)}) custom-call(s32[7]{0:T(128)S(1)} %stack.61.meta_ref, bf16[64,8064]{1,0:T(8,128)(2,1)} %bitcast.208, bf16[64,8064]{1,0:T(8,128)(2,1)} %bitcast.206, bf16[64,8064]{1,0:T(8,128)(2,1)} %copy-done.49, bf16[64,8064]{1,0:T(8,128)(2,1)} %copy-done.50, ...), custom_call_target="tpu_custom_call" | custom-call | flops 5373952 | bytes 13434880 | tf_op jit(solution)/shard_map/finish/pallas_call | solution.py:949
  404.9 2.1 multiply_reduce_fusion
  (414 shorter events, 132.9 us)
Async XLA Ops:
  4.0 18.2 %collective-permute-start = (bf16[2,16,3200]{2,1,0:T(8,128)(2,1)}, bf16[2,16,3200]{2,1,0:T(8,128)(2,1)}, u32[]{:S(2)}, u32[]{:S(2)}) collective-permute-start(bf16[2,16,3200]{2,1,0:T(8,128)(2,1)} %maximum_bitcast_fusion.6), channel_id=1, source_target_pairs={{0,1},{1,2},{2,3},{3,0},{4,5},{5,6},{6,7},{7,4},{8,9},{9,10},{10,1... | collective-permute-start | bytes 614408 | tf_op jit(solution)/shard_map/ppermute | solution.py:50
  7.0 16.3 %collective-permute-start.1 = (bf16[2,16,3200]{2,1,0:T(8,128)(2,1)}, bf16[2,16,3200]{2,1,0:T(8,128)(2,1)}, u32[]{:S(2)}, u32[]{:S(2)}) collective-permute-start(bf16[2,16,3200]{2,1,0:T(8,128)(2,1)} %maximum_bitcast_fusion.6), channel_id=1, source_target_pairs={{0,2},{1,3},{2,0},{3,1},{4,6},{5,7},{6,4},{7,5},{8,10},{9,11},{10,... | collective-permute-start | bytes 614408 | tf_op jit(solution)/shard_map/ppermute | solution.py:50
  9.6 13.7 %collective-permute-start.2 = (bf16[2,16,3200]{2,1,0:T(8,128)(2,1)}, bf16[2,16,3200]{2,1,0:T(8,128)(2,1)}, u32[]{:S(2)}, u32[]{:S(2)}) collective-permute-start(bf16[2,16,3200]{2,1,0:T(8,128)(2,1)} %maximum_bitcast_fusion.6), channel_id=1, source_target_pairs={{0,3},{1,0},{2,1},{3,2},{4,7},{5,4},{6,5},{7,6},{8,11},{9,8},{10,9... | collective-permute-start | bytes 614408 | tf_op jit(solution)/shard_map/ppermute | solution.py:50
  29.4 14.1 %collective-permute-start.6 = (bf16[2,16,6400]{2,1,0:T(8,128)(2,1)}, bf16[2,16,6400]{2,1,0:T(8,128)(2,1)S(1)}, u32[]{:S(2)}, u32[]{:S(2)}) collective-permute-start(bf16[2,16,6400]{2,1,0:T(8,128)(2,1)} %maximum_bitcast_fusion.2), channel_id=1, source_target_pairs={{0,1},{1,2},{2,3},{3,0},{4,5},{5,6},{6,7},{7,4},{8,9},{9,10},{10,1... | collective-permute-start | bytes 1228808 | tf_op jit(solution)/shard_map/ppermute | solution.py:50
  43.6 13.7 %collective-permute-start.8 = (bf16[3,2,1,16,3200]{4,3,2,1,0:T(8,128)(2,1)S(1)}, bf16[3,2,1,16,3200]{4,3,2,1,0:T(8,128)(2,1)S(1)}, u32[]{:S(2)}, u32[]{:S(2)}) collective-permute-start(bf16[3,2,1,16,3200]{4,3,2,1,0:T(8,128)(2,1)S(1)} %pad_maximum_fusion.14), channel_id=1, source_target_pairs={{0,8},{4,12},{8,0},{12,4},{16,24},{20,28},{24,16},{28,20},{1,9},{5... | collective-permute-start | bytes 1843208 | tf_op jit(solution)/shard_map/ppermute | solution.py:45
  44.1 13.4 %collective-permute-start.7 = (bf16[3,1,2,16,3200]{4,3,0,2,1:T(8,128)(2,1)S(1)}, bf16[3,1,2,16,3200]{4,3,0,2,1:T(8,128)(2,1)S(1)}, u32[]{:S(2)}, u32[]{:S(2)}) collective-permute-start(bf16[3,1,2,16,3200]{4,3,0,2,1:T(8,128)(2,1)S(1)} %pad_maximum_fusion.13), channel_id=1, source_target_pairs={{0,16},{4,20},{8,24},{12,28},{16,0},{20,4},{24,8},{28,12},{1,17},{... | collective-permute-start | bytes 1843208 | tf_op jit(solution)/shard_map/ppermute | solution.py:45
  44.6 13.2 %collective-permute-start.9 = (bf16[2,16,6400]{2,1,0:T(8,128)(2,1)}, bf16[2,16,6400]{2,1,0:T(8,128)(2,1)S(1)}, u32[]{:S(2)}, u32[]{:S(2)}) collective-permute-start(bf16[2,16,6400]{2,1,0:T(8,128)(2,1)} %maximum_bitcast_fusion.2), channel_id=1, source_target_pairs={{0,3},{1,0},{2,1},{3,2},{4,7},{5,4},{6,5},{7,6},{8,11},{9,8},{10,9... | collective-permute-start | bytes 1228808 | tf_op jit(solution)/shard_map/ppermute | solution.py:50
  58.8 21.7 %collective-permute-start.12 = (bf16[2,16,6400]{2,1,0:T(8,128)(2,1)}, bf16[2,16,6400]{2,1,0:T(8,128)(2,1)S(1)}, u32[]{:S(2)}, u32[]{:S(2)}) collective-permute-start(bf16[2,16,6400]{2,1,0:T(8,128)(2,1)} %maximum_bitcast_fusion.2), channel_id=1, source_target_pairs={{0,2},{1,3},{2,0},{3,1},{4,6},{5,7},{6,4},{7,5},{8,10},{9,11},{10,... | collective-permute-start | bytes 1228808 | tf_op jit(solution)/shard_map/ppermute | solution.py:50
  80.7 15.5 %collective-permute-start.16 = (bf16[3,1,1,16,6400]{4,3,2,1,0:T(8,128)(2,1)S(1)}, bf16[3,1,1,16,6400]{4,3,2,1,0:T(8,128)(2,1)S(1)}, u32[]{:S(2)}, u32[]{:S(2)}) collective-permute-start(bf16[3,1,1,16,6400]{4,3,2,1,0:T(8,128)(2,1)S(1)} %maximum_bitcast_fusion.1), channel_id=1, source_target_pairs={{0,16},{4,20},{8,24},{12,28},{16,0},{20,4},{24,8},{28,12},{1,17},{... | collective-permute-start | bytes 1843208 | tf_op jit(solution)/shard_map/ppermute | solution.py:45
  81.3 15.2 %collective-permute-start.15 = (bf16[3,1,1,16,6400]{4,3,0,2,1:T(8,128)(2,1)S(1)}, bf16[3,1,1,16,6400]{4,3,0,2,1:T(8,128)(2,1)S(1)}, u32[]{:S(2)}, u32[]{:S(2)}) collective-permute-start(bf16[3,1,1,16,6400]{4,3,0,2,1:T(8,128)(2,1)S(1)} %maximum_bitcast_fusion), channel_id=1, source_target_pairs={{0,8},{4,12},{8,0},{12,4},{16,24},{20,28},{24,16},{28,20},{1,9},{5... | collective-permute-start | bytes 1843208 | tf_op jit(solution)/shard_map/ppermute | solution.py:45
  82.3 14.4 %collective-permute-start.13 = (bf16[2,128,1024]{2,1,0:T(8,128)(2,1)S(1)}, bf16[2,128,1024]{2,1,0:T(8,128)(2,1)S(1)}, u32[]{:S(2)}, u32[]{:S(2)}) collective-permute-start(bf16[2,128,1024]{2,1,0:T(8,128)(2,1)S(1)} %bitcast.227), channel_id=1, source_target_pairs={{1,0},{2,1},{3,2},{5,4},{6,5},{7,6},{9,8},{10,9},{11,10},{13,12},{... | collective-permute-start | bytes 1572872 | tf_op jit(solution)/shard_map/ppermute | solution.py:208
  83.6 14.2 %collective-permute-start.14 = (bf16[2,128,1024]{2,1,0:T(8,128)(2,1)S(1)}, bf16[2,128,1024]{2,1,0:T(8,128)(2,1)S(1)}, u32[]{:S(2)}, u32[]{:S(2)}) collective-permute-start(bf16[2,128,1024]{2,1,0:T(8,128)(2,1)S(1)} %bitcast.226), channel_id=1, source_target_pairs={{0,1},{1,2},{2,3},{4,5},{5,6},{6,7},{8,9},{9,10},{10,11},{12,13},{... | collective-permute-start | bytes 1572872 | tf_op jit(solution)/shard_map/ppermute | solution.py:208
  97.8 26.6 %collective-permute-start.18 = (bf16[3,2,1,16,6400]{4,3,2,1,0:T(8,128)(2,1)S(1)}, bf16[3,2,1,16,6400]{4,3,2,1,0:T(8,128)(2,1)S(1)}, u32[]{:S(2)}, u32[]{:S(2)}) collective-permute-start(bf16[3,2,1,16,6400]{4,3,2,1,0:T(8,128)(2,1)S(1)} %pad_maximum_fusion.7), channel_id=1, source_target_pairs={{0,8},{4,12},{8,0},{12,4},{16,24},{20,28},{24,16},{28,20},{1,9},{5... | collective-permute-start | bytes 3686408 | tf_op jit(solution)/shard_map/ppermute | solution.py:45
  99.5 31.7 %collective-permute-start.19 = (bf16[656,128]{1,0:T(8,128)(2,1)S(1)}, bf16[656,128]{1,0:T(8,128)(2,1)S(1)}, u32[]{:S(2)}, u32[]{:S(2)}) collective-permute-start(bf16[656,128]{1,0:T(8,128)(2,1)S(1)} %copy-done.71), channel_id=1, source_target_pairs={{0,1},{1,2},{2,3},{3,0},{4,5},{5,6},{6,7},{7,4},{8,9},{9,10},{10,1... | collective-permute-start | bytes 503816 | tf_op jit(solution)/shard_map/ppermute | solution.py:50
  102.0 29.3 %collective-permute-start.20 = (bf16[656,128]{1,0:T(8,128)(2,1)S(1)}, bf16[656,128]{1,0:T(8,128)(2,1)S(1)}, u32[]{:S(2)}, u32[]{:S(2)}) collective-permute-start(bf16[656,128]{1,0:T(8,128)(2,1)S(1)} %copy-done.71), channel_id=1, source_target_pairs={{0,2},{1,3},{2,0},{3,1},{4,6},{5,7},{6,4},{7,5},{8,10},{9,11},{10,... | collective-permute-start | bytes 503816 | tf_op jit(solution)/shard_map/ppermute | solution.py:50
  102.5 28.8 %collective-permute-start.21 = (bf16[656,128]{1,0:T(8,128)(2,1)S(1)}, bf16[656,128]{1,0:T(8,128)(2,1)S(1)}, u32[]{:S(2)}, u32[]{:S(2)}) collective-permute-start(bf16[656,128]{1,0:T(8,128)(2,1)S(1)} %copy-done.71), channel_id=1, source_target_pairs={{0,3},{1,0},{2,1},{3,2},{4,7},{5,4},{6,5},{7,6},{8,11},{9,8},{10,9... | collective-permute-start | bytes 503816 | tf_op jit(solution)/shard_map/ppermute | solution.py:50
  104.8 26.0 %collective-permute-start.17 = (bf16[3,1,2,16,6400]{4,3,0,2,1:T(8,128)(2,1)S(1)}, bf16[3,1,2,16,6400]{4,3,0,2,1:T(8,128)(2,1)S(1)}, u32[]{:S(2)}, u32[]{:S(2)}) collective-permute-start(bf16[3,1,2,16,6400]{4,3,0,2,1:T(8,128)(2,1)S(1)} %pad_maximum_fusion.6), channel_id=1, source_target_pairs={{0,16},{4,20},{8,24},{12,28},{16,0},{20,4},{24,8},{28,12},{1,17},{... | collective-permute-start | bytes 3686408 | tf_op jit(solution)/shard_map/ppermute | solution.py:45
  132.9 13.5 %collective-permute-start.22 = (bf16[3,64,6400]{2,1,0:T(8,128)(2,1)}, bf16[3,64,6400]{2,1,0:T(8,128)(2,1)}, u32[]{:S(2)}, u32[]{:S(2)}) collective-permute-start(bf16[3,64,6400]{2,1,0:T(8,128)(2,1)} %bitcast.23.p0.q0.r0.s0), channel_id=1, source_target_pairs={{0,4},{4,0},{8,12},{12,8},{16,20},{20,16},{24,28},{28,24},{1,5},{5... | collective-permute-start | bytes 7372808 | tf_op jit(solution)/shard_map/ppermute | solution.py:45
  133.0 13.4 %collective-permute-start.23 = (bf16[3,64,6400]{2,1,0:T(8,128)(2,1)}, bf16[3,64,6400]{2,1,0:T(8,128)(2,1)}, u32[]{:S(2)}, u32[]{:S(2)}) collective-permute-start(bf16[3,64,6400]{2,1,0:T(8,128)(2,1)} %bitcast.24.p1.q1.r1.s1), channel_id=1, source_target_pairs={{0,4},{4,0},{8,12},{12,8},{16,20},{20,16},{24,28},{28,24},{1,5},{5... | collective-permute-start | bytes 7372808 | tf_op jit(solution)/shard_map/ppermute | solution.py:45
  152.2 15.4 %collective-permute-start.29 = (bf16[512,512]{1,0:T(8,128)(2,1)S(1)}, bf16[512,512]{1,0:T(8,128)(2,1)S(1)}, u32[]{:S(2)}, u32[]{:S(2)}) collective-permute-start(bf16[512,512]{1,0:T(8,128)(2,1)S(1)} %dynamic-slice_bitcast_fusion.1), channel_id=1, source_target_pairs={{0,4},{4,0},{8,12},{12,8},{16,20},{20,16},{24,28},{28,24},{1,5},{5... | collective-permute-start | bytes 1572872 | tf_op jit(solution)/shard_map/ppermute | solution.py:45
  153.2 14.5 %collective-permute-start.30 = (bf16[512,512]{1,0:T(8,128)(2,1)S(1)}, bf16[512,512]{1,0:T(8,128)(2,1)S(1)}, u32[]{:S(2)}, u32[]{:S(2)}) collective-permute-start(bf16[512,512]{1,0:T(8,128)(2,1)S(1)} %dynamic-slice_bitcast_fusion), channel_id=1, source_target_pairs={{0,4},{4,0},{8,12},{12,8},{16,20},{20,16},{24,28},{28,24},{1,5},{5... | collective-permute-start | bytes 1572872 | tf_op jit(solution)/shard_map/ppermute | solution.py:45
  153.3 13.6 %collective-permute-start.28 = (bf16[3,2,1,320,128]{4,3,0,2,1:T(8,128)(2,1)S(1)}, bf16[3,2,1,320,128]{4,3,0,2,1:T(8,128)(2,1)S(1)}, u32[]{:S(2)}, u32[]{:S(2)}) collective-permute-start(bf16[3,2,1,320,128]{4,3,0,2,1:T(8,128)(2,1)S(1)} %pad_maximum_fusion.22), channel_id=1, source_target_pairs={{0,8},{4,12},{8,0},{12,4},{16,24},{20,28},{24,16},{28,20},{1,9},{5... | collective-permute-start | bytes 1474568 | tf_op jit(solution)/shard_map/ppermute | solution.py:45
  153.6 13.8 %collective-permute-start.27 = (bf16[3,1,2,336,128]{4,3,0,2,1:T(8,128)(2,1)S(1)}, bf16[3,1,2,336,128]{4,3,0,2,1:T(8,128)(2,1)S(1)}, u32[]{:S(2)}, u32[]{:S(2)}) collective-permute-start(bf16[3,1,2,336,128]{4,3,0,2,1:T(8,128)(2,1)S(1)} %pad_maximum_fusion.17), channel_id=1, source_target_pairs={{0,16},{4,20},{8,24},{12,28},{16,0},{20,4},{24,8},{28,12},{1,17},{... | collective-permute-start | bytes 1548296 | tf_op jit(solution)/shard_map/ppermute | solution.py:45
  182.4 14.6 %collective-permute-start.34 = (bf16[2,512,2688]{2,1,0:T(8,128)(2,1)S(1)}, bf16[2,512,2688]{2,1,0:T(8,128)(2,1)S(1)}, u32[]{:S(2)}, u32[]{:S(2)}) collective-permute-start(bf16[2,512,2688]{2,1,0:T(8,128)(2,1)S(1)} %get-tuple-element.365.right_ref.gu_ref), channel_id=1, source_target_pairs={{0,4},{4,0},{8,12},{12,8},{16,20},{20,16},{24,28},{28,24},{1,5},{5... | collective-permute-start | bytes 16515080 | tf_op jit(solution)/shard_map/ppermute | solution.py:45
  197.0 17.5 %collective-permute-start.35 = (bf16[4,2,16,2688]{3,2,1,0:T(8,128)(2,1)S(1)}, bf16[4,2,16,2688]{3,2,1,0:T(8,128)(2,1)S(1)}, u32[]{:S(2)}, u32[]{:S(2)}) collective-permute-start(bf16[4,2,16,2688]{3,2,1,0:T(8,128)(2,1)S(1)} %copy-done.80), channel_id=1, source_target_pairs={{0,8},{4,12},{8,0},{12,4},{16,24},{20,28},{24,16},{28,20},{1,9},{5... | collective-permute-start | bytes 2064392 | tf_op jit(solution)/shard_map/ppermute | solution.py:45
  198.7 17.2 %collective-permute-start.36 = (bf16[4,2,16,2688]{3,2,1,0:T(8,128)(2,1)S(1)}, bf16[4,2,16,2688]{3,2,1,0:T(8,128)(2,1)S(1)}, u32[]{:S(2)}, u32[]{:S(2)}) collective-permute-start(bf16[4,2,16,2688]{3,2,1,0:T(8,128)(2,1)S(1)} %copy-done.79), channel_id=1, source_target_pairs={{0,16},{4,20},{8,24},{12,28},{16,0},{20,4},{24,8},{28,12},{1,17},{... | collective-permute-start | bytes 2064392 | tf_op jit(solution)/shard_map/ppermute | solution.py:45
  216.0 26.2 %collective-permute-start.37 = (bf16[4,2,16,2688]{3,2,1,0:T(8,128)(2,1)}, bf16[4,2,16,2688]{3,2,1,0:T(8,128)(2,1)}, u32[]{:S(2)}, u32[]{:S(2)}) collective-permute-start(bf16[4,2,16,2688]{3,2,1,0:T(8,128)(2,1)} %get-tuple-element.358), channel_id=1, source_target_pairs={{0,8},{4,12},{8,0},{12,4},{16,24},{20,28},{24,16},{28,20},{1,9},{5... | collective-permute-start | bytes 2064392 | tf_op jit(solution)/shard_map/ppermute | solution.py:45
  216.3 25.9 %collective-permute-start.38 = (bf16[4,2,16,2688]{3,2,1,0:T(8,128)(2,1)}, bf16[4,2,16,2688]{3,2,1,0:T(8,128)(2,1)}, u32[]{:S(2)}, u32[]{:S(2)}) collective-permute-start(bf16[4,2,16,2688]{3,2,1,0:T(8,128)(2,1)} %get-tuple-element.360), channel_id=1, source_target_pairs={{0,16},{4,20},{8,24},{12,28},{16,0},{20,4},{24,8},{28,12},{1,17},{... | collective-permute-start | bytes 2064392 | tf_op jit(solution)/shard_map/ppermute | solution.py:45
  219.7 22.4 %collective-permute-start.39 = (bf16[4,1,16,2688]{3,2,1,0:T(8,128)(2,1)}, bf16[4,1,16,2688]{3,2,1,0:T(8,128)(2,1)}, u32[]{:S(2)}, u32[]{:S(2)}) collective-permute-start(bf16[4,1,16,2688]{3,2,1,0:T(8,128)(2,1)} %get-tuple-element.373), channel_id=1, source_target_pairs={{0,16},{4,20},{8,24},{12,28},{16,0},{20,4},{24,8},{28,12},{1,17},{... | collective-permute-start | bytes 1032200 | tf_op jit(solution)/shard_map/ppermute | solution.py:45
  221.3 20.9 %collective-permute-start.40 = (bf16[4,1,16,2688]{3,2,1,0:T(8,128)(2,1)}, bf16[4,1,16,2688]{3,2,1,0:T(8,128)(2,1)}, u32[]{:S(2)}, u32[]{:S(2)}) collective-permute-start(bf16[4,1,16,2688]{3,2,1,0:T(8,128)(2,1)} %get-tuple-element.375), channel_id=1, source_target_pairs={{0,8},{4,12},{8,0},{12,4},{16,24},{20,28},{24,16},{28,20},{1,9},{5... | collective-permute-start | bytes 1032200 | tf_op jit(solution)/shard_map/ppermute | solution.py:45
  242.2 27.2 %collective-permute-start.43 = (bf16[4,2,16,2688]{3,2,1,0:T(8,128)(2,1)}, bf16[4,2,16,2688]{3,2,1,0:T(8,128)(2,1)}, u32[]{:S(2)}, u32[]{:S(2)}) collective-permute-start(bf16[4,2,16,2688]{3,2,1,0:T(8,128)(2,1)} %get-tuple-element.385), channel_id=1, source_target_pairs={{0,8},{4,12},{8,0},{12,4},{16,24},{20,28},{24,16},{28,20},{1,9},{5... | collective-permute-start | bytes 2064392 | tf_op jit(solution)/shard_map/ppermute | solution.py:45
  242.6 26.8 %collective-permute-start.44 = (bf16[4,2,16,2688]{3,2,1,0:T(8,128)(2,1)}, bf16[4,2,16,2688]{3,2,1,0:T(8,128)(2,1)}, u32[]{:S(2)}, u32[]{:S(2)}) collective-permute-start(bf16[4,2,16,2688]{3,2,1,0:T(8,128)(2,1)} %get-tuple-element.387), channel_id=1, source_target_pairs={{0,16},{4,20},{8,24},{12,28},{16,0},{20,4},{24,8},{28,12},{1,17},{... | collective-permute-start | bytes 2064392 | tf_op jit(solution)/shard_map/ppermute | solution.py:45
  246.2 23.2 %collective-permute-start.41 = (bf16[4,1,16,2688]{3,2,1,0:T(8,128)(2,1)}, bf16[4,1,16,2688]{3,2,1,0:T(8,128)(2,1)S(1)}, u32[]{:S(2)}, u32[]{:S(2)}) collective-permute-start(bf16[4,1,16,2688]{3,2,1,0:T(8,128)(2,1)} %get-tuple-element.381), channel_id=1, source_target_pairs={{0,16},{4,20},{8,24},{12,28},{16,0},{20,4},{24,8},{28,12},{1,17},{... | collective-permute-start | bytes 1032200 | tf_op jit(solution)/shard_map/ppermute | solution.py:45
  247.7 21.7 %collective-permute-start.42 = (bf16[4,1,16,2688]{3,2,1,0:T(8,128)(2,1)}, bf16[4,1,16,2688]{3,2,1,0:T(8,128)(2,1)S(1)}, u32[]{:S(2)}, u32[]{:S(2)}) collective-permute-start(bf16[4,1,16,2688]{3,2,1,0:T(8,128)(2,1)} %get-tuple-element.383), channel_id=1, source_target_pairs={{0,8},{4,12},{8,0},{12,4},{16,24},{20,28},{24,16},{28,20},{1,9},{5... | collective-permute-start | bytes 1032200 | tf_op jit(solution)/shard_map/ppermute | solution.py:45
  251.8 17.6 %collective-permute-start.45 = (bf16[32,2688]{1,0:T(8,128)(2,1)S(1)}, bf16[32,2688]{1,0:T(8,128)(2,1)S(1)}, u32[]{:S(2)}, u32[]{:S(2)}) collective-permute-start(bf16[32,2688]{1,0:T(8,128)(2,1)S(1)} %dynamic-slice_bitcast_fusion.15), channel_id=1, source_target_pairs={{0,1},{1,2},{2,3},{3,0},{4,5},{5,6},{6,7},{7,4},{8,9},{9,10},{10,1... | collective-permute-start | bytes 516104 | tf_op jit(solution)/shard_map/ppermute | solution.py:50
  269.5 16.2 %collective-permute-start.46 = (bf16[2,128,1024]{2,1,0:T(8,128)(2,1)S(1)}, bf16[2,128,1024]{2,1,0:T(8,128)(2,1)S(1)}, u32[]{:S(2)}, u32[]{:S(2)}) collective-permute-start(bf16[2,128,1024]{2,1,0:T(8,128)(2,1)S(1)} %get-tuple-element.402), channel_id=1, source_target_pairs={{1,0},{2,1},{3,2},{5,4},{6,5},{7,6},{9,8},{10,9},{11,10},{13,12},{... | collective-permute-start | bytes 1572872 | tf_op jit(solution)/shard_map/ppermute | solution.py:208
  271.0 16.0 %collective-permute-start.47 = (bf16[2,128,1024]{2,1,0:T(8,128)(2,1)S(1)}, bf16[2,128,1024]{2,1,0:T(8,128)(2,1)S(1)}, u32[]{:S(2)}, u32[]{:S(2)}) collective-permute-start(bf16[2,128,1024]{2,1,0:T(8,128)(2,1)S(1)} %get-tuple-element.403), channel_id=1, source_target_pairs={{0,1},{1,2},{2,3},{4,5},{5,6},{6,7},{8,9},{9,10},{10,11},{12,13},{... | collective-permute-start | bytes 1572872 | tf_op jit(solution)/shard_map/ppermute | solution.py:208
  292.7 15.1 %collective-permute-start.54 = (bf16[32,2688]{1,0:T(8,128)(2,1)S(1)}, bf16[32,2688]{1,0:T(8,128)(2,1)S(1)}, u32[]{:S(2)}, u32[]{:S(2)}) collective-permute-start(bf16[32,2688]{1,0:T(8,128)(2,1)S(1)} %get-tuple-element.557), channel_id=1, source_target_pairs={{0,3},{1,0},{2,1},{3,2},{4,7},{5,4},{6,5},{7,6},{8,11},{9,8},{10,9... | collective-permute-start | bytes 516104 | tf_op jit(solution)/shard_map/ppermute | solution.py:50
  295.0 12.8 %collective-permute-start.55 = (bf16[32,2688]{1,0:T(8,128)(2,1)S(1)}, bf16[32,2688]{1,0:T(8,128)(2,1)S(1)}, u32[]{:S(2)}, u32[]{:S(2)}) collective-permute-start(bf16[32,2688]{1,0:T(8,128)(2,1)S(1)} %get-tuple-element.556), channel_id=1, source_target_pairs={{0,2},{1,3},{2,0},{3,1},{4,6},{5,7},{6,4},{7,5},{8,10},{9,11},{10,... | collective-permute-start | bytes 516104 | tf_op jit(solution)/shard_map/ppermute | solution.py:50
  295.4 13.0 %collective-permute-start.53 = (bf16[4,2,16,1024]{3,2,1,0:T(8,128)(2,1)}, bf16[4,2,16,1024]{3,2,1,0:T(8,128)(2,1)}, u32[]{:S(2)}, u32[]{:S(2)}) collective-permute-start(bf16[4,2,16,1024]{3,2,1,0:T(8,128)(2,1)} %get-tuple-element.437), channel_id=1, source_target_pairs={{0,16},{4,20},{8,24},{12,28},{16,0},{20,4},{24,8},{28,12},{1,17},{... | collective-permute-start | bytes 786440 | tf_op jit(solution)/shard_map/ppermute | solution.py:45
  308.5 19.1 %collective-permute-start.56 = (bf16[4,2,16,3072]{3,2,1,0:T(8,128)(2,1)}, bf16[4,2,16,3072]{3,2,1,0:T(8,128)(2,1)}, u32[]{:S(2)}, u32[]{:S(2)}) collective-permute-start(bf16[4,2,16,3072]{3,2,1,0:T(8,128)(2,1)} %get-tuple-element.446), channel_id=1, source_target_pairs={{0,8},{4,12},{8,0},{12,4},{16,24},{20,28},{24,16},{28,20},{1,9},{5... | collective-permute-start | bytes 2359304 | tf_op jit(solution)/shard_map/ppermute | solution.py:45
  310.2 18.9 %collective-permute-start.57 = (bf16[4,2,16,3072]{3,2,1,0:T(8,128)(2,1)}, bf16[4,2,16,3072]{3,2,1,0:T(8,128)(2,1)}, u32[]{:S(2)}, u32[]{:S(2)}) collective-permute-start(bf16[4,2,16,3072]{3,2,1,0:T(8,128)(2,1)} %get-tuple-element.448), channel_id=1, source_target_pairs={{0,16},{4,20},{8,24},{12,28},{16,0},{20,4},{24,8},{28,12},{1,17},{... | collective-permute-start | bytes 2359304 | tf_op jit(solution)/shard_map/ppermute | solution.py:45
  311.8 15.8 %collective-permute-start.58 = (bf16[32,2688]{1,0:T(8,128)(2,1)S(1)}, bf16[32,2688]{1,0:T(8,128)(2,1)S(1)}, u32[]{:S(2)}, u32[]{:S(2)}) collective-permute-start(bf16[32,2688]{1,0:T(8,128)(2,1)S(1)} %get-tuple-element.555), channel_id=1, source_target_pairs={{0,1},{1,2},{2,3},{3,0},{4,5},{5,6},{6,7},{7,4},{8,9},{9,10},{10,1... | collective-permute-start | bytes 516104 | tf_op jit(solution)/shard_map/ppermute | solution.py:50
  313.5 14.1 %collective-permute-start.59 = (bf16[32,2688]{1,0:T(8,128)(2,1)S(1)}, bf16[32,2688]{1,0:T(8,128)(2,1)S(1)}, u32[]{:S(2)}, u32[]{:S(2)}) collective-permute-start(bf16[32,2688]{1,0:T(8,128)(2,1)S(1)} %get-tuple-element.554), channel_id=1, source_target_pairs={{0,2},{1,3},{2,0},{3,1},{4,6},{5,7},{6,4},{7,5},{8,10},{9,11},{10,... | collective-permute-start | bytes 516104 | tf_op jit(solution)/shard_map/ppermute | solution.py:50
  314.8 12.8 %collective-permute-start.60 = (bf16[32,2688]{1,0:T(8,128)(2,1)S(1)}, bf16[32,2688]{1,0:T(8,128)(2,1)S(1)}, u32[]{:S(2)}, u32[]{:S(2)}) collective-permute-start(bf16[32,2688]{1,0:T(8,128)(2,1)S(1)} %get-tuple-element.553), channel_id=1, source_target_pairs={{0,3},{1,0},{2,1},{3,2},{4,7},{5,4},{6,5},{7,6},{8,11},{9,8},{10,9... | collective-permute-start | bytes 516104 | tf_op jit(solution)/shard_map/ppermute | solution.py:50
  332.9 15.2 %collective-permute-start.61 = (bf16[4,1,16,4096]{3,2,1,0:T(8,128)(2,1)}, bf16[4,1,16,4096]{3,2,1,0:T(8,128)(2,1)S(1)}, u32[]{:S(2)}, u32[]{:S(2)}) collective-permute-start(bf16[4,1,16,4096]{3,2,1,0:T(8,128)(2,1)} %get-tuple-element.467), channel_id=1, source_target_pairs={{0,16},{4,20},{8,24},{12,28},{16,0},{20,4},{24,8},{28,12},{1,17},{... | collective-permute-start | bytes 1572872 | tf_op jit(solution)/shard_map/ppermute | solution.py:45
  333.7 14.5 %collective-permute-start.62 = (bf16[4,1,16,4096]{3,2,1,0:T(8,128)(2,1)}, bf16[4,1,16,4096]{3,2,1,0:T(8,128)(2,1)S(1)}, u32[]{:S(2)}, u32[]{:S(2)}) collective-permute-start(bf16[4,1,16,4096]{3,2,1,0:T(8,128)(2,1)} %get-tuple-element.469), channel_id=1, source_target_pairs={{0,8},{4,12},{8,0},{12,4},{16,24},{20,28},{24,16},{28,20},{1,9},{5... | collective-permute-start | bytes 1572872 | tf_op jit(solution)/shard_map/ppermute | solution.py:45
  369.4 13.3 %collective-permute-start.70 = (bf16[32,4096]{1,0:T(8,128)(2,1)S(1)}, bf16[32,4096]{1,0:T(8,128)(2,1)S(1)}, u32[]{:S(2)}, u32[]{:S(2)}) collective-permute-start(bf16[32,4096]{1,0:T(8,128)(2,1)S(1)} %dynamic-slice_bitcast_fusion.3), channel_id=1, source_target_pairs={{0,2},{1,3},{2,0},{3,1},{4,6},{5,7},{6,4},{7,5},{8,10},{9,11},{10,... | collective-permute-start | bytes 786440 | tf_op jit(solution)/shard_map/ppermute | solution.py:50
  (113 other events, 697.9 us)

commit v5 on v4

--- a/solution.py
+++ b/solution.py
@@ -397,19 +397,19 @@
 
 
 def score_bias(first_row, length):
-    shape = (BLOCK_Q, BLOCK_Q + 2 * WIN)
-    query = first_row + lax.broadcasted_iota(jnp.int32, shape, 0)
-    key = first_row - WIN + lax.broadcasted_iota(jnp.int32, shape, 1)
+    shape = (BLOCK_Q + 2 * WIN, BLOCK_Q)
+    key = first_row - WIN + lax.broadcasted_iota(jnp.int32, shape, 0)
+    query = first_row + lax.broadcasted_iota(jnp.int32, shape, 1)
     near = jnp.abs(query - key) <= WIN
     live = (key >= 0) & (key < length)
     bias = jnp.where(near & (live | (query == key)), 0.0, -1e30).astype(f32)
-    return jnp.concatenate([bias, bias], axis=0)
+    return jnp.concatenate([bias, bias], axis=1)
 
 
 def softmax_of(queries, keys, bias):
-    scores = dot_nt(queries, keys) * (HEAD_DIM**-0.5) + bias
-    exponent = jnp.exp(scores - jnp.max(scores, axis=-1, keepdims=True))
-    return exponent / jnp.sum(exponent, axis=-1, keepdims=True)
+    scores = dot_nt(keys, queries) * (HEAD_DIM**-0.5) + bias
+    exponent = jnp.exp(scores - jnp.max(scores, axis=0, keepdims=True))
+    return exponent / jnp.sum(exponent, axis=0, keepdims=True)
 
 
 def attend_kernel(
@@ -428,7 +428,7 @@
             queries = two_heads(q_ref[0, top : top + BLOCK_Q, lanes], low_mask, high_mask)
             probs = softmax_of(queries, keys[span], bias).astype(bf16)
             probs_ref[0, lane // LANES, top // BLOCK_Q] = probs
-            result = dot_nn(probs, values[span])
+            result = tokens_dot(probs, values[span])
             out_ref[top : top + BLOCK_Q, lanes] = jnp.where(
                 first_head, result[:BLOCK_Q], result[BLOCK_Q:]
             ).astype(bf16)
@@ -438,7 +438,7 @@
     own = lambda plane: pl.BlockSpec((1, seq_rows, block), lambda s, h: (plane, s, h))
     rim = lambda plane: pl.BlockSpec((1, WIN, block), lambda s, h: (plane, s, h))
     flat = pl.BlockSpec((seq_rows, block), lambda s, h: (s, h))
-    inner = (seq_rows // BLOCK_Q, 2 * BLOCK_Q, BLOCK_Q + 2 * WIN)
+    inner = (seq_rows // BLOCK_Q, BLOCK_Q + 2 * WIN, 2 * BLOCK_Q)
     probs = pl.BlockSpec((1, block // LANES) + inner, lambda s, h: (s, h, 0, 0, 0))
     probs_shape = pltpu.HBM((seqs, width // LANES) + inner, bf16)
     return own, rim, flat, probs, probs_shape
@@ -478,8 +478,6 @@
     gv_ref,
     up_ref,
     down_ref,
-    gk_acc,
-    gv_acc,
 ):
     rows, width = q_ref.shape[1:]
     scale = HEAD_DIM**-0.5
@@ -492,25 +490,31 @@
         lanes = slice(lane, lane + LANES)
         keys = jnp.concatenate([k_up_ref[0, :, lanes], k_ref[0, :, lanes], k_down_ref[0, :, lanes]], 0)
         values = jnp.concatenate([v_up_ref[0, :, lanes], v_ref[0, :, lanes], v_down_ref[0, :, lanes]], 0)
-        gk_acc[...] = jnp.zeros_like(gk_acc)
-        gv_acc[...] = jnp.zeros_like(gv_acc)
+        key_parts, value_parts = [], []
         for top in range(0, rows, BLOCK_Q):
             span = slice(top, top + BLOCK_Q + 2 * WIN)
             queries = two_heads(q_ref[0, top : top + BLOCK_Q, lanes], low_mask, high_mask)
             grads = two_heads(go_ref[top : top + BLOCK_Q, lanes], low_mask, high_mask)
             probs_low = probs_ref[0, lane // LANES, top // BLOCK_Q]
             probs = probs_low.astype(f32)
-            grad_probs = dot_nt(grads, values[span])
-            delta = jnp.sum(probs * grad_probs, axis=-1, keepdims=True)
+            grad_probs = dot_nt(values[span], grads)
+            delta = jnp.sum(probs * grad_probs, axis=0, keepdims=True)
             grad_scores = (probs * (grad_probs - delta)).astype(bf16)
-            result = dot_nn(grad_scores, keys[span])
+            result = tokens_dot(grad_scores, keys[span])
             result = jnp.where(first_head, result[:BLOCK_Q], result[BLOCK_Q:]) * scale
             own = slice(WIN + top, WIN + top + BLOCK_Q)
             gq_ref[top : top + BLOCK_Q, lanes] = turned_back(result, own).astype(bf16)
-            gk_acc[span, :] += tokens_dot(grad_scores, queries)
-            gv_acc[span, :] += tokens_dot(probs_low, grads)
-        grad_keys = turned_back(gk_acc[...] * scale, slice(None))
-        grad_values = gv_acc[...]
+            key_parts.append(dot_nn(grad_scores, queries))
+            value_parts.append(dot_nn(probs_low, grads))
+
+        def laid_out(parts):
+            pieces = [parts[0][:BLOCK_Q]]
+            for before, part in zip(parts, parts[1:]):
+                pieces.append(before[BLOCK_Q:] + part[:BLOCK_Q])
+            return jnp.concatenate(pieces + [parts[-1][BLOCK_Q:]], axis=0)
+
+        grad_keys = turned_back(laid_out(key_parts) * scale, slice(None))
+        grad_values = laid_out(value_parts)
         up_ref[0, :, lanes] = grad_keys[:WIN].astype(bf16)
         up_ref[1, :, lanes] = grad_values[:WIN].astype(bf16)
         down_ref[0, :, lanes] = grad_keys[WIN + rows :].astype(bf16)
@@ -541,10 +545,6 @@
             jax.ShapeDtypeStruct((rows, width), f32),
             edge_shape,
             edge_shape,
-        ],
-        scratch_shapes=[
-            pltpu.VMEM((seq_rows + 2 * WIN, LANES), f32),
-            pltpu.VMEM((seq_rows + 2 * WIN, LANES), f32),
         ],
         compiler_params=params(16, "arbitrary", "arbitrary"),
         cost_estimate=cost(20 * rows * width * (BLOCK_Q + 2 * WIN), 20 * rows * width),
@@ -825,7 +825,7 @@
         pl.when(pl.program_id(0) // steps == plane)(functools.partial(put, rest[4 * plane : 4 * plane + 4]))
 
 
-def sum_call(meta, left, left_other, right, right_other, block):
+def sum_call(meta, left, left_other, right, right_other, block, outside=False):
     _, tokens, height = left.shape
     planes, _, width = right.shape
     size = lax.axis_size("fsdp")
@@ -857,7 +857,7 @@
         compiler_params=params(22, "arbitrary"),
         cost_estimate=cost(4 * tokens * height * width * planes, 4 * planes * (height + tokens) * width),
         name="sum_rows",
-    )(meta, left, left_other, right, right_other)
+    )(meta, *far(left, left_other), *(far(right, right_other) if outside else [right] + far(right_other)))
     return [[(out[k], out[k + 1]), (out[k + 2], out[k + 3])] for k in range(0, 4 * planes, 4)]
 
 
@@ -1053,7 +1053,7 @@
         + stretch_specs(parts, 2 * hidden, block)
         + [whole, whole, once(rows, 1), once(8, width)],
         out_specs=[whole, whole, whole],
-        out_shape=[jax.ShapeDtypeStruct((rows, width), f32), flat_low, flat_low],
+        out_shape=[pltpu.HBM((rows, width), f32), flat_low, flat_low],
         scratch_shapes=[
             pltpu.VMEM((rows, width), f32),
             pltpu.VMEM((width, block), bf16),
@@ -1112,7 +1112,7 @@
         compiler_params=params(24, "arbitrary"),
         cost_estimate=cost(6 * rows * width * width, 6 * width * width + 14 * rows * width),
         name="input_back",
-    )(meta, grad_joint, *far(own, *parts, x, grad_middle), gains)
+    )(meta, *far(grad_joint, own, *parts, x, grad_middle), gains)
 
 
 def rope_tables(positions):
@@ -1221,9 +1221,7 @@
 
     hidden_other = flip(grad_hidden, 0)
     down = down_call(meta, mixed, mixed_other, grad_result, grad_other, hidden, block)
-    result = jnp.dot(mixed, whole_down, preferred_element_type=f32)
-    output = (middle + valid * result).astype(bf16)
-    down, hidden_other, grad_hidden, output = after((down, hidden_other, grad_hidden, output))
+    down, hidden_other, grad_hidden = after((down, hidden_other, grad_hidden))
 
     down = swap(down, 0)
     one, two = sum_call(meta, normed_second, second_other, grad_hidden, hidden_other, block)
@@ -1279,7 +1277,7 @@
     down_came = down_came + turned_slots(down_slots, far) + turned_slots(down_slots, middle_way)
     grad_joint = jnp.concatenate([grad_q, with_edges(grad_k, 0), with_edges(grad_v, 1)], axis=1)
     joint_other = flip(grad_joint, 0)
-    (last,) = sum_call(meta, normed_first, first_other, grad_joint[None], joint_other[None], width)
+    (last,) = sum_call(meta, normed_first, first_other, grad_joint[None], joint_other[None], width, True)
     two_slots = fold_last(two)
     last, grad_joint, outs, one_slots, two_slots, down_came, down_slots = after(
         (last, grad_joint, outs, one_slots, two_slots, down_came, down_slots)
@@ -1288,8 +1286,8 @@
     last = swap(last, 0)
     one_came = turned_slots(one_slots, range(1, size))
     grad_inputs = input_back_call(meta, grad_joint, w_qkv, parts_one, x, grad_middle, gains_all)
-    last, grad_inputs, one_came, one_slots, two_slots, down_came, down_slots = after(
-        (last, grad_inputs, one_came, one_slots, two_slots, down_came, down_slots)
+    last, grad_inputs, one_came, one_slots, two_slots, down_came, down_slots, mixed = after(
+        (last, grad_inputs, one_came, one_slots, two_slots, down_came, down_slots, mixed)
     )
 
     last = [last, outs]
@@ -1297,7 +1295,9 @@
         last = [swap(fold_next(meta, last, done), done)]
     two_came = turned_slots(two_slots, range(1, size))
     owned = [slot_sum(one_slots, one_came), slot_sum(down_slots, down_came)]
-    last, two_came, two_slots, owned = after((last, two_came, two_slots, owned))
+    result = jnp.dot(mixed, whole_down, preferred_element_type=f32)
+    output = (middle + valid * result).astype(bf16)
+    last, two_came, two_slots, owned, output = after((last, two_came, two_slots, owned, output))
 
     last_slots = fold_last(last[0])
     last_came = turned_slots(last_slots, near) + turned_slots(last_slots, far)

time: 417 us -> 413 us (level)
  local copies, waits for them, and re-layouts: 35.1 us -> 26.3 us
    unnamed x168 -> x164, local copies, waits for them, and re-layouts: 22 us -> 14.3 us
    ppermute x55, waiting for transfers between devices: 69.2 us -> 74.7 us  [flip(): return lax.ppermute(value, 'rep', [(i, i ^ 1 << bit) for i in range(size)])]
    ppermute x21, starting transfers between devices: 41.3 us -> 36.8 us  [turn(): lax.ppermute(value, 'fsdp', [(i, (i + steps) % size) for i in range(size)])]
    ppermute x55, starting transfers between devices: 39.6 us -> 43.9 us  [flip(): return lax.ppermute(value, 'rep', [(i, i ^ 1 << bit) for i in range(size)])]
  transfers between devices with their start and end apart: 80 -> 80, of which waited for: 35 -> 34; matrix products, arithmetic and copies ran while one was open for 7% -> 6% of each run, Pallas kernels for 34% -> 37%
where the time goes in v5:
time: 413 us; the launch traced here: 405 us
  Pallas kernels  153 us (37%)
  waiting for transfers between devices  103 us (25%)
  starting transfers between devices  92.6 us (22%)
  local copies, waits for them, and re-layouts  26.3 us (6%)
  other arithmetic  23.1 us (6%)
    ppermute x55, waiting for transfers between devices, flip(): return lax.ppermute(value, 'rep', [(i, i ^ 1 << bit) for i in range(size)])  74.7 us
    ppermute x55, starting transfers between devices, flip(): return lax.ppermute(value, 'rep', [(i, i ^ 1 << bit) for i in range(size)])  43.9 us
    ppermute x21, starting transfers between devices, turn(): lax.ppermute(value, 'fsdp', [(i, (i + steps) % size) for i in range(size)])  36.8 us
    ppermute x21, waiting for transfers between devices, turn(): lax.ppermute(value, 'fsdp', [(i, (i + steps) % size) for i in range(size)])  28.1 us
    pallas_call x3, Pallas kernels, sum_call(): pl.pallas_call(functools.partial(sum_kernel, size=size, links=links, plac...  23.7 us
    pallas_call x1, Pallas kernels, middle_back_call(): pl.pallas_call(middle_back_kernel, grid=(hidden // block,), in_specs=[SME...  17.3 us
    pallas_call x1, Pallas kernels, attend_back_call(): pl.pallas_call(attend_back_kernel, grid=(seqs, width // block), in_specs=...  15.2 us
    unnamed x164, local copies, waits for them, and re-layouts  14.3 us
  transfers between devices with their start and end apart: 80, of which 34 were waited for; matrix products, arithmetic and copies ran while one was open for 6% of the time, Pallas kernels for 37%

profile of v5, /device:TPU:0, one launch (start us, length us, event | category | flops | bytes accessed | tf_op | source)
XLA Modules:
  0.0 405.0 jit_solution(12006626711119006264)
XLA Ops:
  4.0 3.0 collective-permute-start
  7.0 2.6 collective-permute-start.1
  11.7 2.4 multiply_convert_fusion.g_ref
  14.1 1.9 constant_dynamic-slice_fusion
  29.5 4.8 %collective-permute-start.6 = (bf16[2,16,6400]{2,1,0:T(8,128)(2,1)}, bf16[2,16,6400]{2,1,0:T(8,128)(2,1)S(1)}, u32[]{:S(2)}, u32[]{:S(2)}) collective-permute-start(bf16[2,16,6400]{2,1,0:T(8,128)(2,1)} %maximum_bitcast_fusion.2), channel_id=1, source_target_pairs={{0,1},{1,2},{2,3},{3,0},{4,5},{5,6},{6,7},{7,4},{8,9},{9,10},{10,1... | collective-permute-start | bytes 1228808 | tf_op jit(solution)/shard_map/ppermute | solution.py:50
  37.5 6.1 %collective-permute-done.6 = bf16[2,16,6400]{2,1,0:T(8,128)(2,1)S(1)} collective-permute-done((bf16[2,16,6400]{2,1,0:T(8,128)(2,1)}, bf16[2,16,6400]{2,1,0:T(8,128)(2,1)S(1)}, u32[]{:S(2)}, u32[]{:S(2)}) %collective-permute-start.6) | collective-permute-done | bytes 409632 | tf_op jit(solution)/shard_map/ppermute | solution.py:50
  46.4 10.9 %collective-permute-done.7 = bf16[3,1,2,16,3200]{4,3,0,2,1:T(8,128)(2,1)S(1)} collective-permute-done((bf16[3,1,2,16,3200]{4,3,0,2,1:T(8,128)(2,1)S(1)}, bf16[3,1,2,16,3200]{4,3,0,2,1:T(8,128)(2,1)S(1)}, u32[]{:S(2)}, u32[]{:S(2)}) %collective-permute-start.7) | collective-permute-done | bytes 614432 | tf_op jit(solution)/shard_map/ppermute | solution.py:45
  58.7 2.4 collective-permute-start.12
  62.8 11.0 %qkv.1 = (bf16[2,512,512]{2,1,0:T(8,128)(2,1)S(1)}, bf16[3,512,1024]{2,1,0:T(8,128)(2,1)S(1)}, f32[8,1024]{1,0:T(8,128)S(1)}) custom-call(s32[7]{0:T(128)S(1)} %stack.61.meta_ref, bf16[512,1024]{1,0:T(8,128)(2,1)} %bitcast.191, bf16[256,3072]{1,0:T(8,128)(2,1)} %own_ref.7, bf16[3,64,3200]{2,1,0:T(8,128)(2,1)} %bitcast.185, bf16[3,64,3200]{2,1,0:T(8,128)(2,1)} %bitcast.181, ...), custom_call_target="tpu_custom_call" | custom-call | flops 3221225472 | bytes 11534336 | tf_op jit(solution)/shard_map/qkv/pallas_call | solution.py:360
  75.1 4.8 %collective-permute-done.12 = bf16[2,16,6400]{2,1,0:T(8,128)(2,1)S(1)} collective-permute-done((bf16[2,16,6400]{2,1,0:T(8,128)(2,1)}, bf16[2,16,6400]{2,1,0:T(8,128)(2,1)S(1)}, u32[]{:S(2)}, u32[]{:S(2)}) %collective-permute-start.12) | collective-permute-done | bytes 409632 | tf_op jit(solution)/shard_map/ppermute | solution.py:50
  81.2 4.6 %collective-permute-start.14 = (bf16[2,128,1024]{2,1,0:T(8,128)(2,1)S(1)}, bf16[2,128,1024]{2,1,0:T(8,128)(2,1)S(1)}, u32[]{:S(2)}, u32[]{:S(2)}) collective-permute-start(bf16[2,128,1024]{2,1,0:T(8,128)(2,1)S(1)} %bitcast.227), channel_id=1, source_target_pairs={{0,1},{1,2},{2,3},{4,5},{5,6},{6,7},{8,9},{9,10},{10,11},{12,13},{... | collective-permute-start | bytes 1572872 | tf_op jit(solution)/shard_map/ppermute | solution.py:208
  88.2 12.2 %collective-permute-done.15 = bf16[3,1,1,16,6400]{4,3,0,2,1:T(8,128)(2,1)S(1)} collective-permute-done((bf16[3,1,1,16,6400]{4,3,0,2,1:T(8,128)(2,1)S(1)}, bf16[3,1,1,16,6400]{4,3,0,2,1:T(8,128)(2,1)S(1)}, u32[]{:S(2)}, u32[]{:S(2)}) %collective-permute-start.15) | collective-permute-done | bytes 614432 | tf_op jit(solution)/shard_map/ppermute | solution.py:45
  103.4 3.3 collective-permute-start.21
  108.2 11.3 %attend.1 = (bf16[512,1024]{1,0:T(8,128)(2,1)S(1)}, bf16[2,8,2,256,256]{4,3,2,1,0:T(8,128)(2,1)}) custom-call(s32[3]{0:T(128)S(1)} %pad_add_fusion.meta_ref, bf16[3,512,1024]{2,1,0:T(8,128)(2,1)S(1)} %get-tuple-element.289.q_ref.k_ref.v_ref, bf16[3,512,1024]{2,1,0:T(8,128)(2,1)S(1)} %get-tuple-element.289.q_ref.k_ref.v_ref, ...), custom_call_target="tpu_custom_call" | custom-call | flops 1073741824 | bytes 5242880 | tf_op jit(solution)/shard_map/attend/pallas_call | solution.py:452
  120.5 7.1 %collective-permute-done.17 = bf16[3,1,2,16,6400]{4,3,0,2,1:T(8,128)(2,1)S(1)} collective-permute-done((bf16[3,1,2,16,6400]{4,3,0,2,1:T(8,128)(2,1)S(1)}, bf16[3,1,2,16,6400]{4,3,0,2,1:T(8,128)(2,1)S(1)}, u32[]{:S(2)}, u32[]{:S(2)}) %collective-permute-start.17) | collective-permute-done | bytes 1228832 | tf_op jit(solution)/shard_map/ppermute | solution.py:45
  128.0 4.4 %collective-permute-done.18 = bf16[3,2,1,16,6400]{4,3,2,1,0:T(8,128)(2,1)S(1)} collective-permute-done((bf16[3,2,1,16,6400]{4,3,2,1,0:T(8,128)(2,1)S(1)}, bf16[3,2,1,16,6400]{4,3,2,1,0:T(8,128)(2,1)S(1)}, u32[]{:S(2)}, u32[]{:S(2)}) %collective-permute-start.18) | collective-permute-done | bytes 1228832 | tf_op jit(solution)/shard_map/ppermute | solution.py:45
  141.1 4.7 %collective-permute-done.25 = bf16[3,1,1,320,128]{4,3,0,2,1:T(8,128)(2,1)S(1)} collective-permute-done((bf16[3,1,1,320,128]{4,3,0,2,1:T(8,128)(2,1)S(1)}, bf16[3,1,1,320,128]{4,3,0,2,1:T(8,128)(2,1)S(1)}, u32[]{:S(2)}, u32[]{:S(2)}) %collective-permute-start.25) | collective-permute-done | bytes 245792 | tf_op jit(solution)/shard_map/ppermute | solution.py:45
  150.5 5.8 %out_norm.1 = (f32[512,1024]{1,0:T(8,128)}, bf16[2,512,512]{2,1,0:T(8,128)(2,1)S(1)}, bf16[2,512,512]{2,1,0:T(8,128)(2,1)S(1)}) custom-call(s32[7]{0:T(128)S(1)} %stack.61.meta_ref, bf16[512,1024]{1,0:T(8,128)(2,1)S(1)} %copy-done.12, bf16[256,1024]{1,0:T(8,128)(2,1)} %out_own_ref.1, bf16[3,64,6400]{2,1,0:T(8,128)(2,1)} %bitcast.23.p0.q0.r0.s0, ...), custom_call_target="tpu_custom_call" | custom-call | flops 1073741824 | bytes 8388608 | tf_op jit(solution)/shard_map/out_norm/pallas_call | solution.py:579
  157.1 11.9 %gate.1 = (bf16[512,2688]{1,0:T(8,128)(2,1)}, bf16[512,2688]{1,0:T(8,128)(2,1)}, bf16[512,2688]{1,0:T(8,128)(2,1)}) custom-call(s32[7]{0:T(128)S(1)} %stack.61.meta_ref, bf16[2,512,512]{2,1,0:T(8,128)(2,1)S(1)} %get-tuple-element.312.n_ref.left_ref, bf16[256,2688]{1,0:T(8,128)(2,1)} %copy-done.25, bf16[3,64,6400]{2,1,0:T(8,128)(2,1)} %bitcast.23.p0.q0.r0.s0, ...), custom_call_target="tpu_custom_call" | custom-call | flops 5637144576 | bytes 19267584 | tf_op jit(solution)/shard_map/gate/pallas_call | solution.py:624
  170.3 3.3 collective-permute-done.32.p3
  174.9 9.2 %gate_back.1 = (bf16[2,512,2688]{2,1,0:T(8,128)(2,1)S(1)}, bf16[2688,1024]{1,0:T(8,128)(2,1)S(1)}) custom-call(s32[7]{0:T(128)S(1)} %stack.61.meta_ref, bf16[512,1024]{1,0:T(8,128)(2,1)} %multiply_convert_fusion.g_ref, bf16[656,1024]{1,0:T(8,128)(2,1)} %own_ref.6, bf16[3,4,336,128]{3,2,1,0:T(8,128)(2,1)} %bitcast.205, bf16[3,4,320,128]{3,2,1,0:T(8,128)(2,1)} %bitcast.211, ...), custom_call_target="tpu_custom_call" | custom-call | flops 2818572288 | bytes 22020096 | tf_op jit(solution)/shard_map/gate_back/pallas_call | solution.py:710
  185.7 9.1 %down_sum.1 = (bf16[4,2,16,2688]{3,2,1,0:T(8,128)(2,1)}, bf16[4,2,16,2688]{3,2,1,0:T(8,128)(2,1)}, bf16[4,2,16,2688]{3,2,1,0:T(8,128)(2,1)}, bf16[4,2,16,2688]{3,2,1,0:T(8,128)(2,1)}) custom-call(s32[7]{0:T(128)S(1)} %stack.61.meta_ref, bf16[512,2688]{1,0:T(8,128)(2,1)} %get-tuple-element.477.m_ref, bf16[512,2688]{1,0:T(8,128)(2,1)} %copy-done.72, ...), custom_call_target="tpu_custom_call" | custom-call | flops 2751463424 | bytes 10158080 | tf_op jit(solution)/shard_map/down_sum/pallas_call | solution.py:790
  197.3 12.0 %sum_rows.3 = (bf16[4,2,16,2688]{3,2,1,0:T(8,128)(2,1)}, bf16[4,2,16,2688]{3,2,1,0:T(8,128)(2,1)}, bf16[4,2,16,2688]{3,2,1,0:T(8,128)(2,1)}, bf16[4,2,16,2688]{3...) custom-call(s32[7]{0:T(128)S(1)} %stack.61.meta_ref, ...), custom_call_target="tpu_custom_call" | custom-call | flops 5637144576 | bytes 22020096 | tf_op jit(solution)/shard_map/sum_rows/pallas_call | solution.py:850
  209.3 3.3 collective-permute-done.35.refs_1_
  214.9 2.9 fold.4
  220.0 17.3 %middle_back.1 = (f32[512,1024]{1,0:T(8,128)}, bf16[512,1024]{1,0:T(8,128)(2,1)S(1)}, bf16[512,1024]{1,0:T(8,128)(2,1)S(1)}) custom-call(s32[7]{0:T(128)S(1)} %stack.61.meta_ref, bf16[2,512,2688]{2,1,0:T(8,128)(2,1)S(1)} %get-tuple-element.363.right_ref.gu_ref, bf16[256,2688]{1,0:T(8,128)(2,1)} %copy-done.25, bf16[3,64,6400]{2,1,0:T(8,128)(2,1)} %bitcast.23.p0.q0.r0.s0, ...), custom_call_target="tpu_custom_call" | custom-call | flops 5637144576 | bytes 22806528 | tf_op jit(solution)/shard_map/middle_back/pallas_call | solution.py:1045
  241.2 3.1 fold.5
  248.7 15.2 %attend_back.1 = (bf16[512,1024]{1,0:T(8,128)(2,1)S(1)}, f32[512,1024]{1,0:T(8,128)S(1)}, f32[512,1024]{1,0:T(8,128)S(1)}, bf16[2,128,1024]{2,1,0:T(8,128)(2,1)S(1)}, bf16[2,128,1024]{2,1,0:T(8,128)(2,1)S(1)}) custom-call(bf16[3,512,1024]{2,1,0:T(8,128)(2,1)S(1)} %get-tuple-element.289.q_ref.k_ref.v_ref, ...), custom_call_target="tpu_custom_call" | custom-call | flops 2684354560 | bytes 10485760 | tf_op jit(solution)/shard_map/attend_back/pallas_call | solution.py:534
  265.4 4.8 %collective-permute-start.47 = (bf16[2,128,1024]{2,1,0:T(8,128)(2,1)S(1)}, bf16[2,128,1024]{2,1,0:T(8,128)(2,1)S(1)}, u32[]{:S(2)}, u32[]{:S(2)}) collective-permute-start(bf16[2,128,1024]{2,1,0:T(8,128)(2,1)S(1)} %get-tuple-element.402), channel_id=1, source_target_pairs={{0,1},{1,2},{2,3},{4,5},{5,6},{6,7},{8,9},{9,10},{10,11},{12,13},{... | collective-permute-start | bytes 1572872 | tf_op jit(solution)/shard_map/ppermute | solution.py:208
  270.2 3.3 fold.6
  276.8 4.0 sum_rows.4
  281.5 2.1 collective-permute-done.49.refs_1_
  285.1 3.1 pad_maximum_fusion
  289.2 2.2 collective-permute-start.55
  295.4 7.7 %sum_rows.5 = (bf16[4,2,16,3072]{3,2,1,0:T(8,128)(2,1)}, bf16[4,2,16,3072]{3,2,1,0:T(8,128)(2,1)}, bf16[4,2,16,3072]{3,2,1,0:T(8,128)(2,1)}, bf16[4,2,16,3072]{3,2,1,0:T(8,128)(2,1)}) custom-call(s32[7]{0:T(128)S(1)} %stack.61.meta_ref, bf16[2,512,512]{2,1,0:T(8,128)(2,1)} %copy-done.15, bf16[512,512]{1,0:T(8,128)(2,1)} %copy-done.74, ...), custom_call_target="tpu_custom_call" | custom-call | flops 3221225472 | bytes 12582912 | tf_op jit(solution)/shard_map/sum_rows/pallas_call | solution.py:850
  308.7 2.0 collective-permute-start.60
  310.7 10.4 %input_back.1 = bf16[512,1024]{1,0:T(8,128)(2,1)} custom-call(s32[7]{0:T(128)S(1)} %stack.61.meta_ref, bf16[512,3072]{1,0:T(8,128)(2,1)} %get-tuple-element.448.gqkv_ref, bf16[256,3072]{1,0:T(8,128)(2,1)} %own_ref.7, bf16[3,64,3200]{2,1,0:T(8,128)(2,1)} %bitcast.187, bf16[3,64,3200]{2,1,0:T(8,128)(2,1)} %bitcast.183, ...), custom_call_target="tpu_custom_call" | custom-call | flops 3221225472 | bytes 13631488 | tf_op jit(solution)/shard_map/input_back/pallas_call | solution.py:1099
  321.7 1.9 collective-permute-done.56.refs_1_
  324.5 3.9 fold.7
  334.9 4.1 %add_convert_fusion = bf16[512,1024]{1,0:T(8,128)(2,1)} fusion(f32[512,1024]{1,0:T(8,128)S(1)} %copy-done.32, f32[512]{0:T(512)S(1)} %bitcast.230, bf16[512,2688]{1,0:T(8,128)(2,1)S(1)} %copy-done.71, bf16[2688,1024]{1,0:T(8,128)(2,1)S(1)} %bitcast.178), kind=kOutput, calls=%fused_computation.5 | convolution fusion | flops 2820145152 | bytes 11405312 | tf_op jit(solution)/shard_map/dot_general | solution.py:1298
  340.2 4.9 %collective-permute-done.64 = bf16[32,2688]{1,0:T(8,128)(2,1)S(1)} collective-permute-done((bf16[32,2688]{1,0:T(8,128)(2,1)S(1)}, bf16[32,2688]{1,0:T(8,128)(2,1)S(1)}, u32[]{:S(2)}, u32[]{:S(2)}) %collective-permute-start.64) | collective-permute-done | bytes 172064 | tf_op jit(solution)/shard_map/ppermute | solution.py:50
  348.6 4.2 %collective-permute-start.66 = (bf16[32,4096]{1,0:T(8,128)(2,1)S(1)}, bf16[32,4096]{1,0:T(8,128)(2,1)S(1)}, u32[]{:S(2)}, u32[]{:S(2)}) collective-permute-start(bf16[32,4096]{1,0:T(8,128)(2,1)S(1)} %get-tuple-element.537), channel_id=1, source_target_pairs={{0,1},{1,2},{2,3},{3,0},{4,5},{5,6},{6,7},{7,4},{8,9},{9,10},{10,1... | collective-permute-start | bytes 786440 | tf_op jit(solution)/shard_map/ppermute | solution.py:50
  353.9 6.3 %collective-permute-done.66 = bf16[32,4096]{1,0:T(8,128)(2,1)S(1)} collective-permute-done((bf16[32,4096]{1,0:T(8,128)(2,1)S(1)}, bf16[32,4096]{1,0:T(8,128)(2,1)S(1)}, u32[]{:S(2)}, u32[]{:S(2)}) %collective-permute-start.66) | collective-permute-done | bytes 262176 | tf_op jit(solution)/shard_map/ppermute | solution.py:50
  360.2 3.5 collective-permute-done.67
  366.3 10.8 %collective-permute-done.71 = bf16[1,2,16,8064]{3,2,1,0:T(8,128)(2,1)S(1)} collective-permute-done((bf16[1,2,16,8064]{3,2,1,0:T(8,128)(2,1)S(1)}, bf16[1,2,16,8064]{3,2,1,0:T(8,128)(2,1)S(1)}, u32[]{:S(2)}, u32[]{:S(2)}) %collective-permute-start.71) | collective-permute-done | bytes 516128 | tf_op jit(solution)/shard_map/ppermute | solution.py:45
  382.0 2.7 collective-permute-done.74
  387.7 8.7 %finish.1 = (f32[256,5248]{1,0:T(8,128)}, f32[4,1,64]{2,1,0:T(1,128)S(1)}, f32[656,1024]{1,0:T(8,128)}) custom-call(s32[7]{0:T(128)S(1)} %stack.61.meta_ref, bf16[64,8064]{1,0:T(8,128)(2,1)} %bitcast.207, bf16[64,8064]{1,0:T(8,128)(2,1)} %bitcast.209, bf16[64,8064]{1,0:T(8,128)(2,1)} %copy-done.40, bf16[64,8064]{1,0:T(8,128)(2,1)} %copy-done.41, ...), custom_call_target="tpu_custom_call" | custom-call | flops 5373952 | bytes 13434880 | tf_op jit(solution)/shard_map/finish/pallas_call | solution.py:949
  401.0 2.1 multiply_reduce_fusion
  (411 shorter events, 119.4 us)
Async XLA Ops:
  4.0 19.4 %collective-permute-start = (bf16[2,16,3200]{2,1,0:T(8,128)(2,1)}, bf16[2,16,3200]{2,1,0:T(8,128)(2,1)}, u32[]{:S(2)}, u32[]{:S(2)}) collective-permute-start(bf16[2,16,3200]{2,1,0:T(8,128)(2,1)} %maximum_bitcast_fusion.6), channel_id=1, source_target_pairs={{0,1},{1,2},{2,3},{3,0},{4,5},{5,6},{6,7},{7,4},{8,9},{9,10},{10,1... | collective-permute-start | bytes 614408 | tf_op jit(solution)/shard_map/ppermute | solution.py:50
  7.0 16.3 %collective-permute-start.1 = (bf16[2,16,3200]{2,1,0:T(8,128)(2,1)}, bf16[2,16,3200]{2,1,0:T(8,128)(2,1)}, u32[]{:S(2)}, u32[]{:S(2)}) collective-permute-start(bf16[2,16,3200]{2,1,0:T(8,128)(2,1)} %maximum_bitcast_fusion.6), channel_id=1, source_target_pairs={{0,2},{1,3},{2,0},{3,1},{4,6},{5,7},{6,4},{7,5},{8,10},{9,11},{10,... | collective-permute-start | bytes 614408 | tf_op jit(solution)/shard_map/ppermute | solution.py:50
  9.6 13.8 %collective-permute-start.2 = (bf16[2,16,3200]{2,1,0:T(8,128)(2,1)}, bf16[2,16,3200]{2,1,0:T(8,128)(2,1)}, u32[]{:S(2)}, u32[]{:S(2)}) collective-permute-start(bf16[2,16,3200]{2,1,0:T(8,128)(2,1)} %maximum_bitcast_fusion.6), channel_id=1, source_target_pairs={{0,3},{1,0},{2,1},{3,2},{4,7},{5,4},{6,5},{7,6},{8,11},{9,8},{10,9... | collective-permute-start | bytes 614408 | tf_op jit(solution)/shard_map/ppermute | solution.py:50
  29.5 14.1 %collective-permute-start.6 = (bf16[2,16,6400]{2,1,0:T(8,128)(2,1)}, bf16[2,16,6400]{2,1,0:T(8,128)(2,1)S(1)}, u32[]{:S(2)}, u32[]{:S(2)}) collective-permute-start(bf16[2,16,6400]{2,1,0:T(8,128)(2,1)} %maximum_bitcast_fusion.2), channel_id=1, source_target_pairs={{0,1},{1,2},{2,3},{3,0},{4,5},{5,6},{6,7},{7,4},{8,9},{9,10},{10,1... | collective-permute-start | bytes 1228808 | tf_op jit(solution)/shard_map/ppermute | solution.py:50
  43.6 13.7 %collective-permute-start.7 = (bf16[3,1,2,16,3200]{4,3,0,2,1:T(8,128)(2,1)S(1)}, bf16[3,1,2,16,3200]{4,3,0,2,1:T(8,128)(2,1)S(1)}, u32[]{:S(2)}, u32[]{:S(2)}) collective-permute-start(bf16[3,1,2,16,3200]{4,3,0,2,1:T(8,128)(2,1)S(1)} %pad_maximum_fusion.13), channel_id=1, source_target_pairs={{0,16},{4,20},{8,24},{12,28},{16,0},{20,4},{24,8},{28,12},{1,17},{... | collective-permute-start | bytes 1843208 | tf_op jit(solution)/shard_map/ppermute | solution.py:45
  44.1 13.4 %collective-permute-start.8 = (bf16[3,2,1,16,3200]{4,3,2,1,0:T(8,128)(2,1)S(1)}, bf16[3,2,1,16,3200]{4,3,2,1,0:T(8,128)(2,1)S(1)}, u32[]{:S(2)}, u32[]{:S(2)}) collective-permute-start(bf16[3,2,1,16,3200]{4,3,2,1,0:T(8,128)(2,1)S(1)} %pad_maximum_fusion.14), channel_id=1, source_target_pairs={{0,8},{4,12},{8,0},{12,4},{16,24},{20,28},{24,16},{28,20},{1,9},{5... | collective-permute-start | bytes 1843208 | tf_op jit(solution)/shard_map/ppermute | solution.py:45
  44.6 13.2 %collective-permute-start.9 = (bf16[2,16,6400]{2,1,0:T(8,128)(2,1)}, bf16[2,16,6400]{2,1,0:T(8,128)(2,1)S(1)}, u32[]{:S(2)}, u32[]{:S(2)}) collective-permute-start(bf16[2,16,6400]{2,1,0:T(8,128)(2,1)} %maximum_bitcast_fusion.2), channel_id=1, source_target_pairs={{0,3},{1,0},{2,1},{3,2},{4,7},{5,4},{6,5},{7,6},{8,11},{9,8},{10,9... | collective-permute-start | bytes 1228808 | tf_op jit(solution)/shard_map/ppermute | solution.py:50
  58.7 21.2 %collective-permute-start.12 = (bf16[2,16,6400]{2,1,0:T(8,128)(2,1)}, bf16[2,16,6400]{2,1,0:T(8,128)(2,1)S(1)}, u32[]{:S(2)}, u32[]{:S(2)}) collective-permute-start(bf16[2,16,6400]{2,1,0:T(8,128)(2,1)} %maximum_bitcast_fusion.2), channel_id=1, source_target_pairs={{0,2},{1,3},{2,0},{3,1},{4,6},{5,7},{6,4},{7,5},{8,10},{9,11},{10,... | collective-permute-start | bytes 1228808 | tf_op jit(solution)/shard_map/ppermute | solution.py:50
  79.9 21.1 %collective-permute-start.13 = (bf16[2,128,1024]{2,1,0:T(8,128)(2,1)S(1)}, bf16[2,128,1024]{2,1,0:T(8,128)(2,1)S(1)}, u32[]{:S(2)}, u32[]{:S(2)}) collective-permute-start(bf16[2,128,1024]{2,1,0:T(8,128)(2,1)S(1)} %bitcast.228), channel_id=1, source_target_pairs={{1,0},{2,1},{3,2},{5,4},{6,5},{7,6},{9,8},{10,9},{11,10},{13,12},{... | collective-permute-start | bytes 1572872 | tf_op jit(solution)/shard_map/ppermute | solution.py:208
  81.2 19.8 %collective-permute-start.14 = (bf16[2,128,1024]{2,1,0:T(8,128)(2,1)S(1)}, bf16[2,128,1024]{2,1,0:T(8,128)(2,1)S(1)}, u32[]{:S(2)}, u32[]{:S(2)}) collective-permute-start(bf16[2,128,1024]{2,1,0:T(8,128)(2,1)S(1)} %bitcast.227), channel_id=1, source_target_pairs={{0,1},{1,2},{2,3},{4,5},{5,6},{6,7},{8,9},{9,10},{10,11},{12,13},{... | collective-permute-start | bytes 1572872 | tf_op jit(solution)/shard_map/ppermute | solution.py:208
  86.0 14.4 %collective-permute-start.15 = (bf16[3,1,1,16,6400]{4,3,0,2,1:T(8,128)(2,1)S(1)}, bf16[3,1,1,16,6400]{4,3,0,2,1:T(8,128)(2,1)S(1)}, u32[]{:S(2)}, u32[]{:S(2)}) collective-permute-start(bf16[3,1,1,16,6400]{4,3,0,2,1:T(8,128)(2,1)S(1)} %maximum_bitcast_fusion), channel_id=1, source_target_pairs={{0,8},{4,12},{8,0},{12,4},{16,24},{20,28},{24,16},{28,20},{1,9},{5... | collective-permute-start | bytes 1843208 | tf_op jit(solution)/shard_map/ppermute | solution.py:45
  86.7 14.1 %collective-permute-start.16 = (bf16[3,1,1,16,6400]{4,3,2,1,0:T(8,128)(2,1)S(1)}, bf16[3,1,1,16,6400]{4,3,2,1,0:T(8,128)(2,1)S(1)}, u32[]{:S(2)}, u32[]{:S(2)}) collective-permute-start(bf16[3,1,1,16,6400]{4,3,2,1,0:T(8,128)(2,1)S(1)} %maximum_bitcast_fusion.1), channel_id=1, source_target_pairs={{0,16},{4,20},{8,24},{12,28},{16,0},{20,4},{24,8},{28,12},{1,17},{... | collective-permute-start | bytes 1843208 | tf_op jit(solution)/shard_map/ppermute | solution.py:45
  101.1 26.5 %collective-permute-start.17 = (bf16[3,1,2,16,6400]{4,3,0,2,1:T(8,128)(2,1)S(1)}, bf16[3,1,2,16,6400]{4,3,0,2,1:T(8,128)(2,1)S(1)}, u32[]{:S(2)}, u32[]{:S(2)}) collective-permute-start(bf16[3,1,2,16,6400]{4,3,0,2,1:T(8,128)(2,1)S(1)} %pad_maximum_fusion.6), channel_id=1, source_target_pairs={{0,16},{4,20},{8,24},{12,28},{16,0},{20,4},{24,8},{28,12},{1,17},{... | collective-permute-start | bytes 3686408 | tf_op jit(solution)/shard_map/ppermute | solution.py:45
  102.7 31.5 %collective-permute-start.19 = (bf16[656,128]{1,0:T(8,128)(2,1)S(1)}, bf16[656,128]{1,0:T(8,128)(2,1)S(1)}, u32[]{:S(2)}, u32[]{:S(2)}) collective-permute-start(bf16[656,128]{1,0:T(8,128)(2,1)S(1)} %copy-done.64), channel_id=1, source_target_pairs={{0,1},{1,2},{2,3},{3,0},{4,5},{5,6},{6,7},{7,4},{8,9},{9,10},{10,1... | collective-permute-start | bytes 503816 | tf_op jit(solution)/shard_map/ppermute | solution.py:50
  103.0 31.2 %collective-permute-start.20 = (bf16[656,128]{1,0:T(8,128)(2,1)S(1)}, bf16[656,128]{1,0:T(8,128)(2,1)S(1)}, u32[]{:S(2)}, u32[]{:S(2)}) collective-permute-start(bf16[656,128]{1,0:T(8,128)(2,1)S(1)} %copy-done.64), channel_id=1, source_target_pairs={{0,2},{1,3},{2,0},{3,1},{4,6},{5,7},{6,4},{7,5},{8,10},{9,11},{10,... | collective-permute-start | bytes 503816 | tf_op jit(solution)/shard_map/ppermute | solution.py:50
  103.4 30.8 %collective-permute-start.21 = (bf16[656,128]{1,0:T(8,128)(2,1)S(1)}, bf16[656,128]{1,0:T(8,128)(2,1)S(1)}, u32[]{:S(2)}, u32[]{:S(2)}) collective-permute-start(bf16[656,128]{1,0:T(8,128)(2,1)S(1)} %copy-done.64), channel_id=1, source_target_pairs={{0,3},{1,0},{2,1},{3,2},{4,7},{5,4},{6,5},{7,6},{8,11},{9,8},{10,9... | collective-permute-start | bytes 503816 | tf_op jit(solution)/shard_map/ppermute | solution.py:50
  106.7 25.6 %collective-permute-start.18 = (bf16[3,2,1,16,6400]{4,3,2,1,0:T(8,128)(2,1)S(1)}, bf16[3,2,1,16,6400]{4,3,2,1,0:T(8,128)(2,1)S(1)}, u32[]{:S(2)}, u32[]{:S(2)}) collective-permute-start(bf16[3,2,1,16,6400]{4,3,2,1,0:T(8,128)(2,1)S(1)} %pad_maximum_fusion.7), channel_id=1, source_target_pairs={{0,8},{4,12},{8,0},{12,4},{16,24},{20,28},{24,16},{28,20},{1,9},{5... | collective-permute-start | bytes 3686408 | tf_op jit(solution)/shard_map/ppermute | solution.py:45
  147.9 21.3 %collective-permute-start.27 = (bf16[3,1,2,336,128]{4,3,0,2,1:T(8,128)(2,1)S(1)}, bf16[3,1,2,336,128]{4,3,0,2,1:T(8,128)(2,1)S(1)}, u32[]{:S(2)}, u32[]{:S(2)}) collective-permute-start(bf16[3,1,2,336,128]{4,3,0,2,1:T(8,128)(2,1)S(1)} %pad_maximum_fusion.17), channel_id=1, source_target_pairs={{0,16},{4,20},{8,24},{12,28},{16,0},{20,4},{24,8},{28,12},{1,17},{... | collective-permute-start | bytes 1548296 | tf_op jit(solution)/shard_map/ppermute | solution.py:45
  149.2 19.8 %collective-permute-start.28 = (bf16[3,2,1,320,128]{4,3,0,2,1:T(8,128)(2,1)S(1)}, bf16[3,2,1,320,128]{4,3,0,2,1:T(8,128)(2,1)S(1)}, u32[]{:S(2)}, u32[]{:S(2)}) collective-permute-start(bf16[3,2,1,320,128]{4,3,0,2,1:T(8,128)(2,1)S(1)} %pad_maximum_fusion.22), channel_id=1, source_target_pairs={{0,8},{4,12},{8,0},{12,4},{16,24},{20,28},{24,16},{28,20},{1,9},{5... | collective-permute-start | bytes 1474568 | tf_op jit(solution)/shard_map/ppermute | solution.py:45
  156.4 13.0 %collective-permute-start.29 = (bf16[512,512]{1,0:T(8,128)(2,1)S(1)}, bf16[512,512]{1,0:T(8,128)(2,1)S(1)}, u32[]{:S(2)}, u32[]{:S(2)}) collective-permute-start(bf16[512,512]{1,0:T(8,128)(2,1)S(1)} %dynamic-slice_bitcast_fusion.1), channel_id=1, source_target_pairs={{0,4},{4,0},{8,12},{12,8},{16,20},{20,16},{24,28},{28,24},{1,5},{5... | collective-permute-start | bytes 1572872 | tf_op jit(solution)/shard_map/ppermute | solution.py:45
  156.5 12.9 %collective-permute-start.30 = (bf16[512,512]{1,0:T(8,128)(2,1)S(1)}, bf16[512,512]{1,0:T(8,128)(2,1)S(1)}, u32[]{:S(2)}, u32[]{:S(2)}) collective-permute-start(bf16[512,512]{1,0:T(8,128)(2,1)S(1)} %dynamic-slice_bitcast_fusion), channel_id=1, source_target_pairs={{0,4},{4,0},{8,12},{12,8},{16,20},{20,16},{24,28},{28,24},{1,5},{5... | collective-permute-start | bytes 1572872 | tf_op jit(solution)/shard_map/ppermute | solution.py:45
  194.8 17.7 %collective-permute-start.35 = (bf16[4,2,16,2688]{3,2,1,0:T(8,128)(2,1)}, bf16[4,2,16,2688]{3,2,1,0:T(8,128)(2,1)S(1)}, u32[]{:S(2)}, u32[]{:S(2)}) collective-permute-start(bf16[4,2,16,2688]{3,2,1,0:T(8,128)(2,1)} %get-tuple-element.341), channel_id=1, source_target_pairs={{0,8},{4,12},{8,0},{12,4},{16,24},{20,28},{24,16},{28,20},{1,9},{5... | collective-permute-start | bytes 2064392 | tf_op jit(solution)/shard_map/ppermute | solution.py:45
  195.6 17.4 %collective-permute-start.36 = (bf16[4,2,16,2688]{3,2,1,0:T(8,128)(2,1)}, bf16[4,2,16,2688]{3,2,1,0:T(8,128)(2,1)S(1)}, u32[]{:S(2)}, u32[]{:S(2)}) collective-permute-start(bf16[4,2,16,2688]{3,2,1,0:T(8,128)(2,1)} %get-tuple-element.343), channel_id=1, source_target_pairs={{0,16},{4,20},{8,24},{12,28},{16,0},{20,4},{24,8},{28,12},{1,17},{... | collective-permute-start | bytes 2064392 | tf_op jit(solution)/shard_map/ppermute | solution.py:45
  213.0 26.3 %collective-permute-start.37 = (bf16[4,2,16,2688]{3,2,1,0:T(8,128)(2,1)}, bf16[4,2,16,2688]{3,2,1,0:T(8,128)(2,1)}, u32[]{:S(2)}, u32[]{:S(2)}) collective-permute-start(bf16[4,2,16,2688]{3,2,1,0:T(8,128)(2,1)} %get-tuple-element.356), channel_id=1, source_target_pairs={{0,8},{4,12},{8,0},{12,4},{16,24},{20,28},{24,16},{28,20},{1,9},{5... | collective-permute-start | bytes 2064392 | tf_op jit(solution)/shard_map/ppermute | solution.py:45
  214.3 24.9 %collective-permute-start.38 = (bf16[4,2,16,2688]{3,2,1,0:T(8,128)(2,1)}, bf16[4,2,16,2688]{3,2,1,0:T(8,128)(2,1)}, u32[]{:S(2)}, u32[]{:S(2)}) collective-permute-start(bf16[4,2,16,2688]{3,2,1,0:T(8,128)(2,1)} %get-tuple-element.358), channel_id=1, source_target_pairs={{0,16},{4,20},{8,24},{12,28},{16,0},{20,4},{24,8},{28,12},{1,17},{... | collective-permute-start | bytes 2064392 | tf_op jit(solution)/shard_map/ppermute | solution.py:45
  217.8 21.4 %collective-permute-start.39 = (bf16[4,1,16,2688]{3,2,1,0:T(8,128)(2,1)}, bf16[4,1,16,2688]{3,2,1,0:T(8,128)(2,1)}, u32[]{:S(2)}, u32[]{:S(2)}) collective-permute-start(bf16[4,1,16,2688]{3,2,1,0:T(8,128)(2,1)} %get-tuple-element.372), channel_id=1, source_target_pairs={{0,16},{4,20},{8,24},{12,28},{16,0},{20,4},{24,8},{28,12},{1,17},{... | collective-permute-start | bytes 1032200 | tf_op jit(solution)/shard_map/ppermute | solution.py:45
  219.3 19.9 %collective-permute-start.40 = (bf16[4,1,16,2688]{3,2,1,0:T(8,128)(2,1)}, bf16[4,1,16,2688]{3,2,1,0:T(8,128)(2,1)}, u32[]{:S(2)}, u32[]{:S(2)}) collective-permute-start(bf16[4,1,16,2688]{3,2,1,0:T(8,128)(2,1)} %get-tuple-element.374), channel_id=1, source_target_pairs={{0,8},{4,12},{8,0},{12,4},{16,24},{20,28},{24,16},{28,20},{1,9},{5... | collective-permute-start | bytes 1032200 | tf_op jit(solution)/shard_map/ppermute | solution.py:45
  239.3 24.7 %collective-permute-start.43 = (bf16[4,2,16,2688]{3,2,1,0:T(8,128)(2,1)}, bf16[4,2,16,2688]{3,2,1,0:T(8,128)(2,1)}, u32[]{:S(2)}, u32[]{:S(2)}) collective-permute-start(bf16[4,2,16,2688]{3,2,1,0:T(8,128)(2,1)} %get-tuple-element.384), channel_id=1, source_target_pairs={{0,8},{4,12},{8,0},{12,4},{16,24},{20,28},{24,16},{28,20},{1,9},{5... | collective-permute-start | bytes 2064392 | tf_op jit(solution)/shard_map/ppermute | solution.py:45
  240.7 23.3 %collective-permute-start.44 = (bf16[4,2,16,2688]{3,2,1,0:T(8,128)(2,1)}, bf16[4,2,16,2688]{3,2,1,0:T(8,128)(2,1)}, u32[]{:S(2)}, u32[]{:S(2)}) collective-permute-start(bf16[4,2,16,2688]{3,2,1,0:T(8,128)(2,1)} %get-tuple-element.386), channel_id=1, source_target_pairs={{0,16},{4,20},{8,24},{12,28},{16,0},{20,4},{24,8},{28,12},{1,17},{... | collective-permute-start | bytes 2064392 | tf_op jit(solution)/shard_map/ppermute | solution.py:45
  244.3 19.6 %collective-permute-start.41 = (bf16[4,1,16,2688]{3,2,1,0:T(8,128)(2,1)}, bf16[4,1,16,2688]{3,2,1,0:T(8,128)(2,1)S(1)}, u32[]{:S(2)}, u32[]{:S(2)}) collective-permute-start(bf16[4,1,16,2688]{3,2,1,0:T(8,128)(2,1)} %get-tuple-element.380), channel_id=1, source_target_pairs={{0,16},{4,20},{8,24},{12,28},{16,0},{20,4},{24,8},{28,12},{1,17},{... | collective-permute-start | bytes 1032200 | tf_op jit(solution)/shard_map/ppermute | solution.py:45
  245.8 18.2 %collective-permute-start.42 = (bf16[4,1,16,2688]{3,2,1,0:T(8,128)(2,1)}, bf16[4,1,16,2688]{3,2,1,0:T(8,128)(2,1)S(1)}, u32[]{:S(2)}, u32[]{:S(2)}) collective-permute-start(bf16[4,1,16,2688]{3,2,1,0:T(8,128)(2,1)} %get-tuple-element.382), channel_id=1, source_target_pairs={{0,8},{4,12},{8,0},{12,4},{16,24},{20,28},{24,16},{28,20},{1,9},{5... | collective-permute-start | bytes 1032200 | tf_op jit(solution)/shard_map/ppermute | solution.py:45
  248.0 16.0 %collective-permute-start.45 = (bf16[32,2688]{1,0:T(8,128)(2,1)S(1)}, bf16[32,2688]{1,0:T(8,128)(2,1)S(1)}, u32[]{:S(2)}, u32[]{:S(2)}) collective-permute-start(bf16[32,2688]{1,0:T(8,128)(2,1)S(1)} %dynamic-slice_bitcast_fusion.15), channel_id=1, source_target_pairs={{0,1},{1,2},{2,3},{3,0},{4,5},{5,6},{6,7},{7,4},{8,9},{9,10},{10,1... | collective-permute-start | bytes 516104 | tf_op jit(solution)/shard_map/ppermute | solution.py:50
  264.1 16.8 %collective-permute-start.46 = (bf16[2,128,1024]{2,1,0:T(8,128)(2,1)S(1)}, bf16[2,128,1024]{2,1,0:T(8,128)(2,1)S(1)}, u32[]{:S(2)}, u32[]{:S(2)}) collective-permute-start(bf16[2,128,1024]{2,1,0:T(8,128)(2,1)S(1)} %get-tuple-element.401), channel_id=1, source_target_pairs={{1,0},{2,1},{3,2},{5,4},{6,5},{7,6},{9,8},{10,9},{11,10},{13,12},{... | collective-permute-start | bytes 1572872 | tf_op jit(solution)/shard_map/ppermute | solution.py:208
  265.4 16.1 %collective-permute-start.47 = (bf16[2,128,1024]{2,1,0:T(8,128)(2,1)S(1)}, bf16[2,128,1024]{2,1,0:T(8,128)(2,1)S(1)}, u32[]{:S(2)}, u32[]{:S(2)}) collective-permute-start(bf16[2,128,1024]{2,1,0:T(8,128)(2,1)S(1)} %get-tuple-element.402), channel_id=1, source_target_pairs={{0,1},{1,2},{2,3},{4,5},{5,6},{6,7},{8,9},{9,10},{10,11},{12,13},{... | collective-permute-start | bytes 1572872 | tf_op jit(solution)/shard_map/ppermute | solution.py:208
  288.2 14.9 %collective-permute-start.54 = (bf16[32,2688]{1,0:T(8,128)(2,1)S(1)}, bf16[32,2688]{1,0:T(8,128)(2,1)S(1)}, u32[]{:S(2)}, u32[]{:S(2)}) collective-permute-start(bf16[32,2688]{1,0:T(8,128)(2,1)S(1)} %get-tuple-element.559), channel_id=1, source_target_pairs={{0,3},{1,0},{2,1},{3,2},{4,7},{5,4},{6,5},{7,6},{8,11},{9,8},{10,9... | collective-permute-start | bytes 516104 | tf_op jit(solution)/shard_map/ppermute | solution.py:50
  289.2 14.3 %collective-permute-start.55 = (bf16[32,2688]{1,0:T(8,128)(2,1)S(1)}, bf16[32,2688]{1,0:T(8,128)(2,1)S(1)}, u32[]{:S(2)}, u32[]{:S(2)}) collective-permute-start(bf16[32,2688]{1,0:T(8,128)(2,1)S(1)} %get-tuple-element.558), channel_id=1, source_target_pairs={{0,2},{1,3},{2,0},{3,1},{4,6},{5,7},{6,4},{7,5},{8,10},{9,11},{10,... | collective-permute-start | bytes 516104 | tf_op jit(solution)/shard_map/ppermute | solution.py:50
  291.4 12.1 %collective-permute-start.52 = (bf16[4,2,16,1024]{3,2,1,0:T(8,128)(2,1)}, bf16[4,2,16,1024]{3,2,1,0:T(8,128)(2,1)S(1)}, u32[]{:S(2)}, u32[]{:S(2)}) collective-permute-start(bf16[4,2,16,1024]{3,2,1,0:T(8,128)(2,1)} %get-tuple-element.434), channel_id=1, source_target_pairs={{0,8},{4,12},{8,0},{12,4},{16,24},{20,28},{24,16},{28,20},{1,9},{5... | collective-permute-start | bytes 786440 | tf_op jit(solution)/shard_map/ppermute | solution.py:45
  304.2 19.4 %collective-permute-start.56 = (bf16[4,2,16,3072]{3,2,1,0:T(8,128)(2,1)}, bf16[4,2,16,3072]{3,2,1,0:T(8,128)(2,1)S(1)}, u32[]{:S(2)}, u32[]{:S(2)}) collective-permute-start(bf16[4,2,16,3072]{3,2,1,0:T(8,128)(2,1)} %get-tuple-element.445), channel_id=1, source_target_pairs={{0,8},{4,12},{8,0},{12,4},{16,24},{20,28},{24,16},{28,20},{1,9},{5... | collective-permute-start | bytes 2359304 | tf_op jit(solution)/shard_map/ppermute | solution.py:45
  305.3 19.2 %collective-permute-start.57 = (bf16[4,2,16,3072]{3,2,1,0:T(8,128)(2,1)}, bf16[4,2,16,3072]{3,2,1,0:T(8,128)(2,1)}, u32[]{:S(2)}, u32[]{:S(2)}) collective-permute-start(bf16[4,2,16,3072]{3,2,1,0:T(8,128)(2,1)} %get-tuple-element.447), channel_id=1, source_target_pairs={{0,16},{4,20},{8,24},{12,28},{16,0},{20,4},{24,8},{28,12},{1,17},{... | collective-permute-start | bytes 2359304 | tf_op jit(solution)/shard_map/ppermute | solution.py:45
  306.8 14.3 %collective-permute-start.58 = (bf16[32,2688]{1,0:T(8,128)(2,1)S(1)}, bf16[32,2688]{1,0:T(8,128)(2,1)S(1)}, u32[]{:S(2)}, u32[]{:S(2)}) collective-permute-start(bf16[32,2688]{1,0:T(8,128)(2,1)S(1)} %get-tuple-element.557), channel_id=1, source_target_pairs={{0,1},{1,2},{2,3},{3,0},{4,5},{5,6},{6,7},{7,4},{8,9},{9,10},{10,1... | collective-permute-start | bytes 516104 | tf_op jit(solution)/shard_map/ppermute | solution.py:50
  306.9 14.8 %collective-permute-start.59 = (bf16[32,2688]{1,0:T(8,128)(2,1)S(1)}, bf16[32,2688]{1,0:T(8,128)(2,1)S(1)}, u32[]{:S(2)}, u32[]{:S(2)}) collective-permute-start(bf16[32,2688]{1,0:T(8,128)(2,1)S(1)} %get-tuple-element.556), channel_id=1, source_target_pairs={{0,2},{1,3},{2,0},{3,1},{4,6},{5,7},{6,4},{7,5},{8,10},{9,11},{10,... | collective-permute-start | bytes 516104 | tf_op jit(solution)/shard_map/ppermute | solution.py:50
  308.7 13.0 %collective-permute-start.60 = (bf16[32,2688]{1,0:T(8,128)(2,1)S(1)}, bf16[32,2688]{1,0:T(8,128)(2,1)S(1)}, u32[]{:S(2)}, u32[]{:S(2)}) collective-permute-start(bf16[32,2688]{1,0:T(8,128)(2,1)S(1)} %get-tuple-element.555), channel_id=1, source_target_pairs={{0,3},{1,0},{2,1},{3,2},{4,7},{5,4},{6,5},{7,6},{8,11},{9,8},{10,9... | collective-permute-start | bytes 516104 | tf_op jit(solution)/shard_map/ppermute | solution.py:50
  328.4 16.7 %collective-permute-start.61 = (bf16[4,1,16,4096]{3,2,1,0:T(8,128)(2,1)}, bf16[4,1,16,4096]{3,2,1,0:T(8,128)(2,1)S(1)}, u32[]{:S(2)}, u32[]{:S(2)}) collective-permute-start(bf16[4,1,16,4096]{3,2,1,0:T(8,128)(2,1)} %get-tuple-element.465), channel_id=1, source_target_pairs={{0,16},{4,20},{8,24},{12,28},{16,0},{20,4},{24,8},{28,12},{1,17},{... | collective-permute-start | bytes 1572872 | tf_op jit(solution)/shard_map/ppermute | solution.py:45
  329.9 15.2 %collective-permute-start.62 = (bf16[4,1,16,4096]{3,2,1,0:T(8,128)(2,1)}, bf16[4,1,16,4096]{3,2,1,0:T(8,128)(2,1)S(1)}, u32[]{:S(2)}, u32[]{:S(2)}) collective-permute-start(bf16[4,1,16,4096]{3,2,1,0:T(8,128)(2,1)} %get-tuple-element.467), channel_id=1, source_target_pairs={{0,8},{4,12},{8,0},{12,4},{16,24},{20,28},{24,16},{28,20},{1,9},{5... | collective-permute-start | bytes 1572872 | tf_op jit(solution)/shard_map/ppermute | solution.py:45
  331.5 13.6 %collective-permute-start.64 = (bf16[32,2688]{1,0:T(8,128)(2,1)S(1)}, bf16[32,2688]{1,0:T(8,128)(2,1)S(1)}, u32[]{:S(2)}, u32[]{:S(2)}) collective-permute-start(bf16[32,2688]{1,0:T(8,128)(2,1)S(1)} %get-tuple-element.553), channel_id=1, source_target_pairs={{0,2},{1,3},{2,0},{3,1},{4,6},{5,7},{6,4},{7,5},{8,10},{9,11},{10,... | collective-permute-start | bytes 516104 | tf_op jit(solution)/shard_map/ppermute | solution.py:50
  363.6 13.4 %collective-permute-start.71 = (bf16[1,2,16,8064]{3,2,1,0:T(8,128)(2,1)S(1)}, bf16[1,2,16,8064]{3,2,1,0:T(8,128)(2,1)S(1)}, u32[]{:S(2)}, u32[]{:S(2)}) collective-permute-start(bf16[1,2,16,8064]{3,2,1,0:T(8,128)(2,1)S(1)} %pad_maximum_fusion.19), channel_id=1, source_target_pairs={{0,16},{4,20},{8,24},{12,28},{16,0},{20,4},{24,8},{28,12},{1,17},{... | collective-permute-start | bytes 1548296 | tf_op jit(solution)/shard_map/ppermute | solution.py:45
  364.8 14.4 %collective-permute-start.70 = (bf16[32,4096]{1,0:T(8,128)(2,1)S(1)}, bf16[32,4096]{1,0:T(8,128)(2,1)S(1)}, u32[]{:S(2)}, u32[]{:S(2)}) collective-permute-start(bf16[32,4096]{1,0:T(8,128)(2,1)S(1)} %dynamic-slice_bitcast_fusion.3), channel_id=1, source_target_pairs={{0,2},{1,3},{2,0},{3,1},{4,6},{5,7},{6,4},{7,5},{8,10},{9,11},{10,... | collective-permute-start | bytes 786440 | tf_op jit(solution)/shard_map/ppermute | solution.py:50
  365.5 12.8 %collective-permute-start.72 = (bf16[2,1,16,8064]{3,2,1,0:T(8,128)(2,1)S(1)}, bf16[2,1,16,8064]{3,2,1,0:T(8,128)(2,1)S(1)}, u32[]{:S(2)}, u32[]{:S(2)}) collective-permute-start(bf16[2,1,16,8064]{3,2,1,0:T(8,128)(2,1)S(1)} %pad_maximum_fusion.20), channel_id=1, source_target_pairs={{0,8},{4,12},{8,0},{12,4},{16,24},{20,28},{24,16},{28,20},{1,9},{5... | collective-permute-start | bytes 1548296 | tf_op jit(solution)/shard_map/ppermute | solution.py:45
  (111 other events, 753.4 us)

commit v6 on v5

--- a/solution.py
+++ b/solution.py
@@ -852,7 +852,7 @@
         grid=(planes * steps,),
         in_specs=[SMEM_SPEC, once(2, tokens, height), once(tokens, height), right_spec, right_spec],
         out_specs=[out_spec(plane) for plane in range(planes) for _ in range(4)],
-        out_shape=[pltpu.HBM(shape, bf16)] * (4 * planes),
+        out_shape=[jax.ShapeDtypeStruct(shape, bf16) if outside else pltpu.HBM(shape, bf16)] * (4 * planes),
         scratch_shapes=[pltpu.VMEM((height, block), bf16)],
         compiler_params=params(22, "arbitrary"),
         cost_estimate=cost(4 * tokens * height * width * planes, 4 * planes * (height + tokens) * width),
@@ -880,7 +880,7 @@
             start += width
 
 
-def fold_next(meta, blocks, done):
+def fold_next(meta, blocks, done, near_by=False):
     size = blocks[0][0][0].shape[0]
     places = [left.index(bit) for left, bit in zip(bits_left(done), link_orders()[done])]
     flat = [array for block in blocks for pair in block for array in pair]
@@ -900,21 +900,26 @@
         grid=(1,),
         in_specs=[SMEM_SPEC] + [once(*array.shape) for array in flat],
         out_specs=[fixed(*shape) for shape in shapes],
-        out_shape=[pltpu.HBM(shape, bf16) for shape in shapes],
+        out_shape=[jax.ShapeDtypeStruct(shape, bf16) if near_by else pltpu.HBM(shape, bf16) for shape in shapes],
         compiler_params=params(16, "arbitrary"),
         cost_estimate=cost(0, 3 * sum(array.size for array in flat)),
         name="fold",
-    )(meta, *far(*flat))
+    )(meta, *(flat if near_by else far(*flat)))
     return [(out[0], out[1]), (out[2], out[3])]
 
 
-def finish_kernel(meta_ref, m0, m1, g0, g1, w_ref, out_ref, norm_ref, *down_refs, padded, links):
+def finish_kernel(meta_ref, m0, m1, g0, g1, w_ref, out_ref, norm_ref, *rest, padded, links):
     step = pl.program_id(0)
     mine = (step < 2) == (meta_ref[2] == 0)
     first = step % 2 == 0
-    own = jnp.where(first, m0[...].astype(f32), m1[...].astype(f32))
-    got = jnp.where(first, g0[...].astype(f32), g1[...].astype(f32))
-    value = jnp.where(mine, own, got)
+    down_refs, rows_ref = rest[:-1], rest[-1]
+    for source, own, even in ((m0, True, True), (m1, True, False), (g0, False, True), (g1, False, False)):
+
+        @pl.when((mine == own) & (first == even))
+        def _(source=source):
+            rows_ref[...] = source[...]
+
+    value = rows_ref[...].astype(f32)
     hidden = out_ref.shape[1] // 2
     out_ref[:, :hidden] = value[:, :hidden]
     out_ref[:, hidden:] = value[:, padded : padded + hidden]
@@ -959,6 +964,7 @@
         + [fixed(shard, model)] * fast,
         out_shape=[jax.ShapeDtypeStruct((rows, columns), f32), jax.ShapeDtypeStruct((4, 1, quarter), f32)]
         + [jax.ShapeDtypeStruct((shard, model), f32)] * fast,
+        scratch_shapes=[pltpu.VMEM((quarter, width), bf16)],
         compiler_params=params(30, "arbitrary"),
         cost_estimate=cost(4 * rows * columns, 10 * rows * columns),
         name="finish",
@@ -981,7 +987,7 @@
         out_ref[place, cut:, :] = added(k1[place, 0], g1[place, 0])
 
 
-def fold_last(parts):
+def fold_last(parts, near_by=False):
     (k0, g0), (k1, g1) = parts
     size, _, cut, width = k0.shape
     rows = cut + k1.shape[2]
@@ -996,7 +1002,7 @@
         compiler_params=params(16, "arbitrary"),
         cost_estimate=cost(0, 6 * size * rows * width),
         name="fold_last",
-    )(*far(k0, g0, k1, g1))
+    )(*((k0, g0, k1, g1) if near_by else far(k0, g0, k1, g1)))
 
 
 def middle_back_kernel(
@@ -1292,14 +1298,14 @@
 
     last = [last, outs]
     for done in range(1, len(steps)):
-        last = [swap(fold_next(meta, last, done), done)]
+        last = [swap(fold_next(meta, last, done, True), done)]
     two_came = turned_slots(two_slots, range(1, size))
     owned = [slot_sum(one_slots, one_came), slot_sum(down_slots, down_came)]
     result = jnp.dot(mixed, whole_down, preferred_element_type=f32)
     output = (middle + valid * result).astype(bf16)
     last, two_came, two_slots, owned, output = after((last, two_came, two_slots, owned, output))
 
-    last_slots = fold_last(last[0])
+    last_slots = fold_last(last[0], True)
     last_came = turned_slots(last_slots, near) + turned_slots(last_slots, far)
     spread_in = widen(
         spread_start(jnp.concatenate([owned[0], slot_sum(two_slots, two_came), owned[1]], axis=1)), steps[0], 0

time: 413 us -> 408 us (0.988)
  Pallas kernels: 153 us -> 148 us
    unnamed x164 -> x170, local copies, waits for them, and re-layouts: 14.3 us -> 15.2 us
  transfers between devices with their start and end apart: 80 -> 80, of which waited for: 34 -> 33; matrix products, arithmetic and copies ran while one was open for 6% -> 6% of each run, Pallas kernels for 37% -> 37%
where the time goes in v6:
time: 408 us; the launch traced here: 400 us
  Pallas kernels  148 us (36%)
  waiting for transfers between devices  102 us (25%)
  starting transfers between devices  92.9 us (23%)
  local copies, waits for them, and re-layouts  27.2 us (7%)
  other arithmetic  23.1 us (6%)
  matrix products  4.12 us (1%)
    ppermute x55, waiting for transfers between devices, flip(): return lax.ppermute(value, 'rep', [(i, i ^ 1 << bit) for i in range(size)])  75.5 us
    ppermute x55, starting transfers between devices, flip(): return lax.ppermute(value, 'rep', [(i, i ^ 1 << bit) for i in range(size)])  43.7 us
    ppermute x21, starting transfers between devices, turn(): lax.ppermute(value, 'fsdp', [(i, (i + steps) % size) for i in range(size)])  37.3 us
    ppermute x21, waiting for transfers between devices, turn(): lax.ppermute(value, 'fsdp', [(i, (i + steps) % size) for i in range(size)])  25.9 us
    pallas_call x3, Pallas kernels, sum_call(): pl.pallas_call(functools.partial(sum_kernel, size=size, links=links, plac...  23.4 us
    pallas_call x1, Pallas kernels, middle_back_call(): pl.pallas_call(middle_back_kernel, grid=(hidden // block,), in_specs=[SME...  17.3 us
    pallas_call x1, Pallas kernels, attend_back_call(): pl.pallas_call(attend_back_kernel, grid=(seqs, width // block), in_specs=...  15.2 us
    unnamed x170, local copies, waits for them, and re-layouts  15.2 us
  transfers between devices with their start and end apart: 80, of which 33 were waited for; matrix products, arithmetic and copies ran while one was open for 6% of the time, Pallas kernels for 37%

profile of v6, /device:TPU:0, one launch (start us, length us, event | category | flops | bytes accessed | tf_op | source)
XLA Modules:
  0.0 400.2 jit_solution(11729351543928105591)
XLA Ops:
  4.0 3.0 collective-permute-start
  7.0 2.6 collective-permute-start.1
  11.7 2.4 multiply_convert_fusion.g_ref
  14.1 1.9 constant_dynamic-slice_fusion
  29.5 4.8 %collective-permute-start.6 = (bf16[2,16,6400]{2,1,0:T(8,128)(2,1)}, bf16[2,16,6400]{2,1,0:T(8,128)(2,1)S(1)}, u32[]{:S(2)}, u32[]{:S(2)}) collective-permute-start(bf16[2,16,6400]{2,1,0:T(8,128)(2,1)} %maximum_bitcast_fusion.2), channel_id=1, source_target_pairs={{0,1},{1,2},{2,3},{3,0},{4,5},{5,6},{6,7},{7,4},{8,9},{9,10},{10,1... | collective-permute-start | bytes 1228808 | tf_op jit(solution)/shard_map/ppermute | solution.py:50
  37.6 6.0 %collective-permute-done.6 = bf16[2,16,6400]{2,1,0:T(8,128)(2,1)S(1)} collective-permute-done((bf16[2,16,6400]{2,1,0:T(8,128)(2,1)}, bf16[2,16,6400]{2,1,0:T(8,128)(2,1)S(1)}, u32[]{:S(2)}, u32[]{:S(2)}) %collective-permute-start.6) | collective-permute-done | bytes 409632 | tf_op jit(solution)/shard_map/ppermute | solution.py:50
  46.4 10.9 %collective-permute-done.7 = bf16[3,1,2,16,3200]{4,3,0,2,1:T(8,128)(2,1)S(1)} collective-permute-done((bf16[3,1,2,16,3200]{4,3,0,2,1:T(8,128)(2,1)S(1)}, bf16[3,1,2,16,3200]{4,3,0,2,1:T(8,128)(2,1)S(1)}, u32[]{:S(2)}, u32[]{:S(2)}) %collective-permute-start.7) | collective-permute-done | bytes 614432 | tf_op jit(solution)/shard_map/ppermute | solution.py:45
  58.7 2.4 collective-permute-start.12
  62.8 11.0 %qkv.1 = (bf16[2,512,512]{2,1,0:T(8,128)(2,1)S(1)}, bf16[3,512,1024]{2,1,0:T(8,128)(2,1)S(1)}, f32[8,1024]{1,0:T(8,128)S(1)}) custom-call(s32[7]{0:T(128)S(1)} %stack.61.meta_ref, bf16[512,1024]{1,0:T(8,128)(2,1)} %bitcast.191, bf16[256,3072]{1,0:T(8,128)(2,1)} %own_ref.7, bf16[3,64,3200]{2,1,0:T(8,128)(2,1)} %bitcast.185, bf16[3,64,3200]{2,1,0:T(8,128)(2,1)} %bitcast.181, ...), custom_call_target="tpu_custom_call" | custom-call | flops 3221225472 | bytes 11534336 | tf_op jit(solution)/shard_map/qkv/pallas_call | solution.py:360
  75.1 4.8 %collective-permute-done.12 = bf16[2,16,6400]{2,1,0:T(8,128)(2,1)S(1)} collective-permute-done((bf16[2,16,6400]{2,1,0:T(8,128)(2,1)}, bf16[2,16,6400]{2,1,0:T(8,128)(2,1)S(1)}, u32[]{:S(2)}, u32[]{:S(2)}) %collective-permute-start.12) | collective-permute-done | bytes 409632 | tf_op jit(solution)/shard_map/ppermute | solution.py:50
  81.2 4.6 %collective-permute-start.14 = (bf16[2,128,1024]{2,1,0:T(8,128)(2,1)S(1)}, bf16[2,128,1024]{2,1,0:T(8,128)(2,1)S(1)}, u32[]{:S(2)}, u32[]{:S(2)}) collective-permute-start(bf16[2,128,1024]{2,1,0:T(8,128)(2,1)S(1)} %bitcast.227), channel_id=1, source_target_pairs={{0,1},{1,2},{2,3},{4,5},{5,6},{6,7},{8,9},{9,10},{10,11},{12,13},{... | collective-permute-start | bytes 1572872 | tf_op jit(solution)/shard_map/ppermute | solution.py:208
  88.2 12.2 %collective-permute-done.15 = bf16[3,1,1,16,6400]{4,3,0,2,1:T(8,128)(2,1)S(1)} collective-permute-done((bf16[3,1,1,16,6400]{4,3,0,2,1:T(8,128)(2,1)S(1)}, bf16[3,1,1,16,6400]{4,3,0,2,1:T(8,128)(2,1)S(1)}, u32[]{:S(2)}, u32[]{:S(2)}) %collective-permute-start.15) | collective-permute-done | bytes 614432 | tf_op jit(solution)/shard_map/ppermute | solution.py:45
  103.4 3.3 collective-permute-start.21
  108.2 11.3 %attend.1 = (bf16[512,1024]{1,0:T(8,128)(2,1)S(1)}, bf16[2,8,2,256,256]{4,3,2,1,0:T(8,128)(2,1)}) custom-call(s32[3]{0:T(128)S(1)} %pad_add_fusion.meta_ref, bf16[3,512,1024]{2,1,0:T(8,128)(2,1)S(1)} %get-tuple-element.289.q_ref.k_ref.v_ref, bf16[3,512,1024]{2,1,0:T(8,128)(2,1)S(1)} %get-tuple-element.289.q_ref.k_ref.v_ref, ...), custom_call_target="tpu_custom_call" | custom-call | flops 1073741824 | bytes 5242880 | tf_op jit(solution)/shard_map/attend/pallas_call | solution.py:452
  120.5 7.1 %collective-permute-done.17 = bf16[3,1,2,16,6400]{4,3,0,2,1:T(8,128)(2,1)S(1)} collective-permute-done((bf16[3,1,2,16,6400]{4,3,0,2,1:T(8,128)(2,1)S(1)}, bf16[3,1,2,16,6400]{4,3,0,2,1:T(8,128)(2,1)S(1)}, u32[]{:S(2)}, u32[]{:S(2)}) %collective-permute-start.17) | collective-permute-done | bytes 1228832 | tf_op jit(solution)/shard_map/ppermute | solution.py:45
  128.0 4.4 %collective-permute-done.18 = bf16[3,2,1,16,6400]{4,3,2,1,0:T(8,128)(2,1)S(1)} collective-permute-done((bf16[3,2,1,16,6400]{4,3,2,1,0:T(8,128)(2,1)S(1)}, bf16[3,2,1,16,6400]{4,3,2,1,0:T(8,128)(2,1)S(1)}, u32[]{:S(2)}, u32[]{:S(2)}) %collective-permute-start.18) | collective-permute-done | bytes 1228832 | tf_op jit(solution)/shard_map/ppermute | solution.py:45
  141.1 4.7 %collective-permute-done.25 = bf16[3,1,1,320,128]{4,3,0,2,1:T(8,128)(2,1)S(1)} collective-permute-done((bf16[3,1,1,320,128]{4,3,0,2,1:T(8,128)(2,1)S(1)}, bf16[3,1,1,320,128]{4,3,0,2,1:T(8,128)(2,1)S(1)}, u32[]{:S(2)}, u32[]{:S(2)}) %collective-permute-start.25) | collective-permute-done | bytes 245792 | tf_op jit(solution)/shard_map/ppermute | solution.py:45
  150.5 5.8 %out_norm.1 = (f32[512,1024]{1,0:T(8,128)}, bf16[2,512,512]{2,1,0:T(8,128)(2,1)S(1)}, bf16[2,512,512]{2,1,0:T(8,128)(2,1)S(1)}) custom-call(s32[7]{0:T(128)S(1)} %stack.61.meta_ref, bf16[512,1024]{1,0:T(8,128)(2,1)S(1)} %copy-done.12, bf16[256,1024]{1,0:T(8,128)(2,1)} %out_own_ref.1, bf16[3,64,6400]{2,1,0:T(8,128)(2,1)} %bitcast.23.p0.q0.r0.s0, ...), custom_call_target="tpu_custom_call" | custom-call | flops 1073741824 | bytes 8388608 | tf_op jit(solution)/shard_map/out_norm/pallas_call | solution.py:579
  157.1 11.9 %gate.1 = (bf16[512,2688]{1,0:T(8,128)(2,1)}, bf16[512,2688]{1,0:T(8,128)(2,1)}, bf16[512,2688]{1,0:T(8,128)(2,1)}) custom-call(s32[7]{0:T(128)S(1)} %stack.61.meta_ref, bf16[2,512,512]{2,1,0:T(8,128)(2,1)S(1)} %get-tuple-element.312.n_ref.left_ref, bf16[256,2688]{1,0:T(8,128)(2,1)} %copy-done.33, bf16[3,64,6400]{2,1,0:T(8,128)(2,1)} %bitcast.23.p0.q0.r0.s0, ...), custom_call_target="tpu_custom_call" | custom-call | flops 5637144576 | bytes 19267584 | tf_op jit(solution)/shard_map/gate/pallas_call | solution.py:624
  170.2 3.4 collective-permute-done.32.p3
  174.9 9.2 %gate_back.1 = (bf16[2,512,2688]{2,1,0:T(8,128)(2,1)S(1)}, bf16[2688,1024]{1,0:T(8,128)(2,1)S(1)}) custom-call(s32[7]{0:T(128)S(1)} %stack.61.meta_ref, bf16[512,1024]{1,0:T(8,128)(2,1)} %multiply_convert_fusion.g_ref, bf16[656,1024]{1,0:T(8,128)(2,1)} %own_ref.6, bf16[3,4,336,128]{3,2,1,0:T(8,128)(2,1)} %bitcast.205, bf16[3,4,320,128]{3,2,1,0:T(8,128)(2,1)} %bitcast.211, ...), custom_call_target="tpu_custom_call" | custom-call | flops 2818572288 | bytes 22020096 | tf_op jit(solution)/shard_map/gate_back/pallas_call | solution.py:710
  185.7 9.1 %down_sum.1 = (bf16[4,2,16,2688]{3,2,1,0:T(8,128)(2,1)}, bf16[4,2,16,2688]{3,2,1,0:T(8,128)(2,1)}, bf16[4,2,16,2688]{3,2,1,0:T(8,128)(2,1)}, bf16[4,2,16,2688]{3,2,1,0:T(8,128)(2,1)}) custom-call(s32[7]{0:T(128)S(1)} %stack.61.meta_ref, bf16[512,2688]{1,0:T(8,128)(2,1)} %get-tuple-element.477.m_ref, bf16[512,2688]{1,0:T(8,128)(2,1)} %copy-done.75, ...), custom_call_target="tpu_custom_call" | custom-call | flops 2751463424 | bytes 10158080 | tf_op jit(solution)/shard_map/down_sum/pallas_call | solution.py:790
  197.3 12.0 %sum_rows.3 = (bf16[4,2,16,2688]{3,2,1,0:T(8,128)(2,1)}, bf16[4,2,16,2688]{3,2,1,0:T(8,128)(2,1)}, bf16[4,2,16,2688]{3,2,1,0:T(8,128)(2,1)}, bf16[4,2,16,2688]{3...) custom-call(s32[7]{0:T(128)S(1)} %stack.61.meta_ref, ...), custom_call_target="tpu_custom_call" | custom-call | flops 5637144576 | bytes 22020096 | tf_op jit(solution)/shard_map/sum_rows/pallas_call | solution.py:850
  209.3 3.3 collective-permute-done.35.refs_1_
  214.9 2.9 fold.4
  220.0 17.3 %middle_back.1 = (f32[512,1024]{1,0:T(8,128)}, bf16[512,1024]{1,0:T(8,128)(2,1)S(1)}, bf16[512,1024]{1,0:T(8,128)(2,1)S(1)}) custom-call(s32[7]{0:T(128)S(1)} %stack.61.meta_ref, bf16[2,512,2688]{2,1,0:T(8,128)(2,1)S(1)} %get-tuple-element.363.right_ref.gu_ref, bf16[256,2688]{1,0:T(8,128)(2,1)} %copy-done.33, bf16[3,64,6400]{2,1,0:T(8,128)(2,1)} %bitcast.23.p0.q0.r0.s0, ...), custom_call_target="tpu_custom_call" | custom-call | flops 5637144576 | bytes 22806528 | tf_op jit(solution)/shard_map/middle_back/pallas_call | solution.py:1051
  241.2 3.1 fold.5
  248.7 15.2 %attend_back.1 = (bf16[512,1024]{1,0:T(8,128)(2,1)S(1)}, f32[512,1024]{1,0:T(8,128)S(1)}, f32[512,1024]{1,0:T(8,128)S(1)}, bf16[2,128,1024]{2,1,0:T(8,128)(2,1)S(1)}, bf16[2,128,1024]{2,1,0:T(8,128)(2,1)S(1)}) custom-call(bf16[3,512,1024]{2,1,0:T(8,128)(2,1)S(1)} %get-tuple-element.289.q_ref.k_ref.v_ref, ...), custom_call_target="tpu_custom_call" | custom-call | flops 2684354560 | bytes 10485760 | tf_op jit(solution)/shard_map/attend_back/pallas_call | solution.py:534
  265.4 4.8 %collective-permute-start.47 = (bf16[2,128,1024]{2,1,0:T(8,128)(2,1)S(1)}, bf16[2,128,1024]{2,1,0:T(8,128)(2,1)S(1)}, u32[]{:S(2)}, u32[]{:S(2)}) collective-permute-start(bf16[2,128,1024]{2,1,0:T(8,128)(2,1)S(1)} %get-tuple-element.402), channel_id=1, source_target_pairs={{0,1},{1,2},{2,3},{4,5},{5,6},{6,7},{8,9},{9,10},{10,11},{12,13},{... | collective-permute-start | bytes 1572872 | tf_op jit(solution)/shard_map/ppermute | solution.py:208
  270.2 3.3 fold.6
  276.8 4.0 %sum_rows.4 = (bf16[4,2,16,1024]{3,2,1,0:T(8,128)(2,1)}, bf16[4,2,16,1024]{3,2,1,0:T(8,128)(2,1)}, bf16[4,2,16,1024]{3,2,1,0:T(8,128)(2,1)}, bf16[4,2,16,1024]{3,2,1,0:T(8,128)(2,1)}) custom-call(s32[7]{0:T(128)S(1)} %stack.61.meta_ref, bf16[2,512,512]{2,1,0:T(8,128)(2,1)} %copy-done.25, bf16[512,512]{1,0:T(8,128)(2,1)} %copy-done.78, ...), custom_call_target="tpu_custom_call" | custom-call | flops 1073741824 | bytes 4194304 | tf_op jit(solution)/shard_map/sum_rows/pallas_call | solution.py:850
  281.5 2.1 collective-permute-done.49.refs_1_
  285.0 3.1 pad_maximum_fusion
  289.2 2.2 collective-permute-start.55
  295.4 7.4 %sum_rows.5 = (bf16[4,2,16,3072]{3,2,1,0:T(8,128)(2,1)S(1)}, bf16[4,2,16,3072]{3,2,1,0:T(8,128)(2,1)}, bf16[4,2,16,3072]{3,2,1,0:T(8,128)(2,1)S(1)}, bf16[4,2,16,3072]{3,2,1,0:T(8,128)(2,1)}) custom-call(s32[7]{0:T(128)S(1)} %stack.61.meta_ref, bf16[2,512,512]{2,1,0:T(8,128)(2,1)} %copy-done.23, bf16[512,512]{1,0:T(8,128)(2,1)} %copy-done.77, ...), custom_call_target="tpu_custom_call" | custom-call | flops 3221225472 | bytes 12582912 | tf_op jit(solution)/shard_map/sum_rows/pallas_call | solution.py:850
  308.7 2.0 collective-permute-start.60
  310.8 10.7 %input_back.1 = bf16[512,1024]{1,0:T(8,128)(2,1)} custom-call(s32[7]{0:T(128)S(1)} %stack.61.meta_ref, bf16[512,3072]{1,0:T(8,128)(2,1)} %get-tuple-element.448.gqkv_ref, bf16[256,3072]{1,0:T(8,128)(2,1)} %own_ref.7, bf16[3,64,3200]{2,1,0:T(8,128)(2,1)} %bitcast.187, bf16[3,64,3200]{2,1,0:T(8,128)(2,1)} %bitcast.183, ...), custom_call_target="tpu_custom_call" | custom-call | flops 3221225472 | bytes 13631488 | tf_op jit(solution)/shard_map/input_back/pallas_call | solution.py:1105
  321.6 2.0 collective-permute-done.56.refs_1_
  324.5 1.9 fold.7
  332.6 4.1 %add_convert_fusion = bf16[512,1024]{1,0:T(8,128)(2,1)} fusion(f32[512,1024]{1,0:T(8,128)S(1)} %copy-done.40, f32[512]{0:T(512)S(1)} %bitcast.230, bf16[512,2688]{1,0:T(8,128)(2,1)S(1)} %copy-done.74, bf16[2688,1024]{1,0:T(8,128)(2,1)S(1)} %bitcast.178), kind=kOutput, calls=%fused_computation.5 | convolution fusion | flops 2820145152 | bytes 11405312 | tf_op jit(solution)/shard_map/dot_general | solution.py:1304
  337.9 4.4 %collective-permute-done.64 = bf16[32,2688]{1,0:T(8,128)(2,1)S(1)} collective-permute-done((bf16[32,2688]{1,0:T(8,128)(2,1)S(1)}, bf16[32,2688]{1,0:T(8,128)(2,1)S(1)}, u32[]{:S(2)}, u32[]{:S(2)}) %collective-permute-start.64) | collective-permute-done | bytes 172064 | tf_op jit(solution)/shard_map/ppermute | solution.py:50
  344.8 4.2 %collective-permute-start.66 = (bf16[32,4096]{1,0:T(8,128)(2,1)S(1)}, bf16[32,4096]{1,0:T(8,128)(2,1)S(1)}, u32[]{:S(2)}, u32[]{:S(2)}) collective-permute-start(bf16[32,4096]{1,0:T(8,128)(2,1)S(1)} %get-tuple-element.537), channel_id=1, source_target_pairs={{0,1},{1,2},{2,3},{3,0},{4,5},{5,6},{6,7},{7,4},{8,9},{9,10},{10,1... | collective-permute-start | bytes 786440 | tf_op jit(solution)/shard_map/ppermute | solution.py:50
  351.1 5.8 %collective-permute-done.66 = bf16[32,4096]{1,0:T(8,128)(2,1)S(1)} collective-permute-done((bf16[32,4096]{1,0:T(8,128)(2,1)S(1)}, bf16[32,4096]{1,0:T(8,128)(2,1)S(1)}, u32[]{:S(2)}, u32[]{:S(2)}) %collective-permute-start.66) | collective-permute-done | bytes 262176 | tf_op jit(solution)/shard_map/ppermute | solution.py:50
  356.9 2.9 collective-permute-done.67
  362.6 10.3 %collective-permute-done.71 = bf16[1,2,16,8064]{3,2,1,0:T(8,128)(2,1)S(1)} collective-permute-done((bf16[1,2,16,8064]{3,2,1,0:T(8,128)(2,1)S(1)}, bf16[1,2,16,8064]{3,2,1,0:T(8,128)(2,1)S(1)}, u32[]{:S(2)}, u32[]{:S(2)}) %collective-permute-start.71) | collective-permute-done | bytes 516128 | tf_op jit(solution)/shard_map/ppermute | solution.py:45
  377.2 3.5 collective-permute-done.74
  383.9 7.7 %finish.1 = (f32[256,5248]{1,0:T(8,128)}, f32[4,1,64]{2,1,0:T(1,128)S(1)}, f32[656,1024]{1,0:T(8,128)}) custom-call(s32[7]{0:T(128)S(1)} %stack.61.meta_ref, bf16[64,8064]{1,0:T(8,128)(2,1)} %bitcast.207, bf16[64,8064]{1,0:T(8,128)(2,1)} %bitcast.209, bf16[64,8064]{1,0:T(8,128)(2,1)} %copy-done.48, bf16[64,8064]{1,0:T(8,128)(2,1)} %copy-done.49, ...), custom_call_target="tpu_custom_call" | custom-call | flops 5373952 | bytes 13434880 | tf_op jit(solution)/shard_map/finish/pallas_call | solution.py:954
  396.3 2.1 multiply_reduce_fusion
  (417 shorter events, 118.7 us)
Async XLA Ops:
  4.0 19.4 %collective-permute-start = (bf16[2,16,3200]{2,1,0:T(8,128)(2,1)}, bf16[2,16,3200]{2,1,0:T(8,128)(2,1)}, u32[]{:S(2)}, u32[]{:S(2)}) collective-permute-start(bf16[2,16,3200]{2,1,0:T(8,128)(2,1)} %maximum_bitcast_fusion.6), channel_id=1, source_target_pairs={{0,1},{1,2},{2,3},{3,0},{4,5},{5,6},{6,7},{7,4},{8,9},{9,10},{10,1... | collective-permute-start | bytes 614408 | tf_op jit(solution)/shard_map/ppermute | solution.py:50
  7.0 16.3 %collective-permute-start.1 = (bf16[2,16,3200]{2,1,0:T(8,128)(2,1)}, bf16[2,16,3200]{2,1,0:T(8,128)(2,1)}, u32[]{:S(2)}, u32[]{:S(2)}) collective-permute-start(bf16[2,16,3200]{2,1,0:T(8,128)(2,1)} %maximum_bitcast_fusion.6), channel_id=1, source_target_pairs={{0,2},{1,3},{2,0},{3,1},{4,6},{5,7},{6,4},{7,5},{8,10},{9,11},{10,... | collective-permute-start | bytes 614408 | tf_op jit(solution)/shard_map/ppermute | solution.py:50
  9.6 13.8 %collective-permute-start.2 = (bf16[2,16,3200]{2,1,0:T(8,128)(2,1)}, bf16[2,16,3200]{2,1,0:T(8,128)(2,1)}, u32[]{:S(2)}, u32[]{:S(2)}) collective-permute-start(bf16[2,16,3200]{2,1,0:T(8,128)(2,1)} %maximum_bitcast_fusion.6), channel_id=1, source_target_pairs={{0,3},{1,0},{2,1},{3,2},{4,7},{5,4},{6,5},{7,6},{8,11},{9,8},{10,9... | collective-permute-start | bytes 614408 | tf_op jit(solution)/shard_map/ppermute | solution.py:50
  29.5 14.1 %collective-permute-start.6 = (bf16[2,16,6400]{2,1,0:T(8,128)(2,1)}, bf16[2,16,6400]{2,1,0:T(8,128)(2,1)S(1)}, u32[]{:S(2)}, u32[]{:S(2)}) collective-permute-start(bf16[2,16,6400]{2,1,0:T(8,128)(2,1)} %maximum_bitcast_fusion.2), channel_id=1, source_target_pairs={{0,1},{1,2},{2,3},{3,0},{4,5},{5,6},{6,7},{7,4},{8,9},{9,10},{10,1... | collective-permute-start | bytes 1228808 | tf_op jit(solution)/shard_map/ppermute | solution.py:50
  43.6 13.7 %collective-permute-start.7 = (bf16[3,1,2,16,3200]{4,3,0,2,1:T(8,128)(2,1)S(1)}, bf16[3,1,2,16,3200]{4,3,0,2,1:T(8,128)(2,1)S(1)}, u32[]{:S(2)}, u32[]{:S(2)}) collective-permute-start(bf16[3,1,2,16,3200]{4,3,0,2,1:T(8,128)(2,1)S(1)} %pad_maximum_fusion.13), channel_id=1, source_target_pairs={{0,16},{4,20},{8,24},{12,28},{16,0},{20,4},{24,8},{28,12},{1,17},{... | collective-permute-start | bytes 1843208 | tf_op jit(solution)/shard_map/ppermute | solution.py:45
  44.1 13.4 %collective-permute-start.8 = (bf16[3,2,1,16,3200]{4,3,2,1,0:T(8,128)(2,1)S(1)}, bf16[3,2,1,16,3200]{4,3,2,1,0:T(8,128)(2,1)S(1)}, u32[]{:S(2)}, u32[]{:S(2)}) collective-permute-start(bf16[3,2,1,16,3200]{4,3,2,1,0:T(8,128)(2,1)S(1)} %pad_maximum_fusion.14), channel_id=1, source_target_pairs={{0,8},{4,12},{8,0},{12,4},{16,24},{20,28},{24,16},{28,20},{1,9},{5... | collective-permute-start | bytes 1843208 | tf_op jit(solution)/shard_map/ppermute | solution.py:45
  44.6 13.2 %collective-permute-start.9 = (bf16[2,16,6400]{2,1,0:T(8,128)(2,1)}, bf16[2,16,6400]{2,1,0:T(8,128)(2,1)S(1)}, u32[]{:S(2)}, u32[]{:S(2)}) collective-permute-start(bf16[2,16,6400]{2,1,0:T(8,128)(2,1)} %maximum_bitcast_fusion.2), channel_id=1, source_target_pairs={{0,3},{1,0},{2,1},{3,2},{4,7},{5,4},{6,5},{7,6},{8,11},{9,8},{10,9... | collective-permute-start | bytes 1228808 | tf_op jit(solution)/shard_map/ppermute | solution.py:50
  58.7 21.2 %collective-permute-start.12 = (bf16[2,16,6400]{2,1,0:T(8,128)(2,1)}, bf16[2,16,6400]{2,1,0:T(8,128)(2,1)S(1)}, u32[]{:S(2)}, u32[]{:S(2)}) collective-permute-start(bf16[2,16,6400]{2,1,0:T(8,128)(2,1)} %maximum_bitcast_fusion.2), channel_id=1, source_target_pairs={{0,2},{1,3},{2,0},{3,1},{4,6},{5,7},{6,4},{7,5},{8,10},{9,11},{10,... | collective-permute-start | bytes 1228808 | tf_op jit(solution)/shard_map/ppermute | solution.py:50
  79.9 21.1 %collective-permute-start.13 = (bf16[2,128,1024]{2,1,0:T(8,128)(2,1)S(1)}, bf16[2,128,1024]{2,1,0:T(8,128)(2,1)S(1)}, u32[]{:S(2)}, u32[]{:S(2)}) collective-permute-start(bf16[2,128,1024]{2,1,0:T(8,128)(2,1)S(1)} %bitcast.228), channel_id=1, source_target_pairs={{1,0},{2,1},{3,2},{5,4},{6,5},{7,6},{9,8},{10,9},{11,10},{13,12},{... | collective-permute-start | bytes 1572872 | tf_op jit(solution)/shard_map/ppermute | solution.py:208
  81.2 19.8 %collective-permute-start.14 = (bf16[2,128,1024]{2,1,0:T(8,128)(2,1)S(1)}, bf16[2,128,1024]{2,1,0:T(8,128)(2,1)S(1)}, u32[]{:S(2)}, u32[]{:S(2)}) collective-permute-start(bf16[2,128,1024]{2,1,0:T(8,128)(2,1)S(1)} %bitcast.227), channel_id=1, source_target_pairs={{0,1},{1,2},{2,3},{4,5},{5,6},{6,7},{8,9},{9,10},{10,11},{12,13},{... | collective-permute-start | bytes 1572872 | tf_op jit(solution)/shard_map/ppermute | solution.py:208
  86.0 14.4 %collective-permute-start.15 = (bf16[3,1,1,16,6400]{4,3,0,2,1:T(8,128)(2,1)S(1)}, bf16[3,1,1,16,6400]{4,3,0,2,1:T(8,128)(2,1)S(1)}, u32[]{:S(2)}, u32[]{:S(2)}) collective-permute-start(bf16[3,1,1,16,6400]{4,3,0,2,1:T(8,128)(2,1)S(1)} %maximum_bitcast_fusion), channel_id=1, source_target_pairs={{0,8},{4,12},{8,0},{12,4},{16,24},{20,28},{24,16},{28,20},{1,9},{5... | collective-permute-start | bytes 1843208 | tf_op jit(solution)/shard_map/ppermute | solution.py:45
  86.7 14.1 %collective-permute-start.16 = (bf16[3,1,1,16,6400]{4,3,2,1,0:T(8,128)(2,1)S(1)}, bf16[3,1,1,16,6400]{4,3,2,1,0:T(8,128)(2,1)S(1)}, u32[]{:S(2)}, u32[]{:S(2)}) collective-permute-start(bf16[3,1,1,16,6400]{4,3,2,1,0:T(8,128)(2,1)S(1)} %maximum_bitcast_fusion.1), channel_id=1, source_target_pairs={{0,16},{4,20},{8,24},{12,28},{16,0},{20,4},{24,8},{28,12},{1,17},{... | collective-permute-start | bytes 1843208 | tf_op jit(solution)/shard_map/ppermute | solution.py:45
  101.1 26.5 %collective-permute-start.17 = (bf16[3,1,2,16,6400]{4,3,0,2,1:T(8,128)(2,1)S(1)}, bf16[3,1,2,16,6400]{4,3,0,2,1:T(8,128)(2,1)S(1)}, u32[]{:S(2)}, u32[]{:S(2)}) collective-permute-start(bf16[3,1,2,16,6400]{4,3,0,2,1:T(8,128)(2,1)S(1)} %pad_maximum_fusion.6), channel_id=1, source_target_pairs={{0,16},{4,20},{8,24},{12,28},{16,0},{20,4},{24,8},{28,12},{1,17},{... | collective-permute-start | bytes 3686408 | tf_op jit(solution)/shard_map/ppermute | solution.py:45
  102.7 31.5 %collective-permute-start.19 = (bf16[656,128]{1,0:T(8,128)(2,1)S(1)}, bf16[656,128]{1,0:T(8,128)(2,1)S(1)}, u32[]{:S(2)}, u32[]{:S(2)}) collective-permute-start(bf16[656,128]{1,0:T(8,128)(2,1)S(1)} %copy-done.67), channel_id=1, source_target_pairs={{0,1},{1,2},{2,3},{3,0},{4,5},{5,6},{6,7},{7,4},{8,9},{9,10},{10,1... | collective-permute-start | bytes 503816 | tf_op jit(solution)/shard_map/ppermute | solution.py:50
  103.0 31.2 %collective-permute-start.20 = (bf16[656,128]{1,0:T(8,128)(2,1)S(1)}, bf16[656,128]{1,0:T(8,128)(2,1)S(1)}, u32[]{:S(2)}, u32[]{:S(2)}) collective-permute-start(bf16[656,128]{1,0:T(8,128)(2,1)S(1)} %copy-done.67), channel_id=1, source_target_pairs={{0,2},{1,3},{2,0},{3,1},{4,6},{5,7},{6,4},{7,5},{8,10},{9,11},{10,... | collective-permute-start | bytes 503816 | tf_op jit(solution)/shard_map/ppermute | solution.py:50
  103.4 30.8 %collective-permute-start.21 = (bf16[656,128]{1,0:T(8,128)(2,1)S(1)}, bf16[656,128]{1,0:T(8,128)(2,1)S(1)}, u32[]{:S(2)}, u32[]{:S(2)}) collective-permute-start(bf16[656,128]{1,0:T(8,128)(2,1)S(1)} %copy-done.67), channel_id=1, source_target_pairs={{0,3},{1,0},{2,1},{3,2},{4,7},{5,4},{6,5},{7,6},{8,11},{9,8},{10,9... | collective-permute-start | bytes 503816 | tf_op jit(solution)/shard_map/ppermute | solution.py:50
  106.7 25.6 %collective-permute-start.18 = (bf16[3,2,1,16,6400]{4,3,2,1,0:T(8,128)(2,1)S(1)}, bf16[3,2,1,16,6400]{4,3,2,1,0:T(8,128)(2,1)S(1)}, u32[]{:S(2)}, u32[]{:S(2)}) collective-permute-start(bf16[3,2,1,16,6400]{4,3,2,1,0:T(8,128)(2,1)S(1)} %pad_maximum_fusion.7), channel_id=1, source_target_pairs={{0,8},{4,12},{8,0},{12,4},{16,24},{20,28},{24,16},{28,20},{1,9},{5... | collective-permute-start | bytes 3686408 | tf_op jit(solution)/shard_map/ppermute | solution.py:45
  147.9 21.3 %collective-permute-start.27 = (bf16[3,1,2,336,128]{4,3,0,2,1:T(8,128)(2,1)S(1)}, bf16[3,1,2,336,128]{4,3,0,2,1:T(8,128)(2,1)S(1)}, u32[]{:S(2)}, u32[]{:S(2)}) collective-permute-start(bf16[3,1,2,336,128]{4,3,0,2,1:T(8,128)(2,1)S(1)} %pad_maximum_fusion.17), channel_id=1, source_target_pairs={{0,16},{4,20},{8,24},{12,28},{16,0},{20,4},{24,8},{28,12},{1,17},{... | collective-permute-start | bytes 1548296 | tf_op jit(solution)/shard_map/ppermute | solution.py:45
  149.2 19.8 %collective-permute-start.28 = (bf16[3,2,1,320,128]{4,3,0,2,1:T(8,128)(2,1)S(1)}, bf16[3,2,1,320,128]{4,3,0,2,1:T(8,128)(2,1)S(1)}, u32[]{:S(2)}, u32[]{:S(2)}) collective-permute-start(bf16[3,2,1,320,128]{4,3,0,2,1:T(8,128)(2,1)S(1)} %pad_maximum_fusion.22), channel_id=1, source_target_pairs={{0,8},{4,12},{8,0},{12,4},{16,24},{20,28},{24,16},{28,20},{1,9},{5... | collective-permute-start | bytes 1474568 | tf_op jit(solution)/shard_map/ppermute | solution.py:45
  156.4 13.0 %collective-permute-start.29 = (bf16[512,512]{1,0:T(8,128)(2,1)S(1)}, bf16[512,512]{1,0:T(8,128)(2,1)S(1)}, u32[]{:S(2)}, u32[]{:S(2)}) collective-permute-start(bf16[512,512]{1,0:T(8,128)(2,1)S(1)} %dynamic-slice_bitcast_fusion.1), channel_id=1, source_target_pairs={{0,4},{4,0},{8,12},{12,8},{16,20},{20,16},{24,28},{28,24},{1,5},{5... | collective-permute-start | bytes 1572872 | tf_op jit(solution)/shard_map/ppermute | solution.py:45
  156.5 12.9 %collective-permute-start.30 = (bf16[512,512]{1,0:T(8,128)(2,1)S(1)}, bf16[512,512]{1,0:T(8,128)(2,1)S(1)}, u32[]{:S(2)}, u32[]{:S(2)}) collective-permute-start(bf16[512,512]{1,0:T(8,128)(2,1)S(1)} %dynamic-slice_bitcast_fusion), channel_id=1, source_target_pairs={{0,4},{4,0},{8,12},{12,8},{16,20},{20,16},{24,28},{28,24},{1,5},{5... | collective-permute-start | bytes 1572872 | tf_op jit(solution)/shard_map/ppermute | solution.py:45
  194.8 17.8 %collective-permute-start.35 = (bf16[4,2,16,2688]{3,2,1,0:T(8,128)(2,1)}, bf16[4,2,16,2688]{3,2,1,0:T(8,128)(2,1)S(1)}, u32[]{:S(2)}, u32[]{:S(2)}) collective-permute-start(bf16[4,2,16,2688]{3,2,1,0:T(8,128)(2,1)} %get-tuple-element.341), channel_id=1, source_target_pairs={{0,8},{4,12},{8,0},{12,4},{16,24},{20,28},{24,16},{28,20},{1,9},{5... | collective-permute-start | bytes 2064392 | tf_op jit(solution)/shard_map/ppermute | solution.py:45
  195.6 17.4 %collective-permute-start.36 = (bf16[4,2,16,2688]{3,2,1,0:T(8,128)(2,1)}, bf16[4,2,16,2688]{3,2,1,0:T(8,128)(2,1)S(1)}, u32[]{:S(2)}, u32[]{:S(2)}) collective-permute-start(bf16[4,2,16,2688]{3,2,1,0:T(8,128)(2,1)} %get-tuple-element.343), channel_id=1, source_target_pairs={{0,16},{4,20},{8,24},{12,28},{16,0},{20,4},{24,8},{28,12},{1,17},{... | collective-permute-start | bytes 2064392 | tf_op jit(solution)/shard_map/ppermute | solution.py:45
  213.0 26.2 %collective-permute-start.37 = (bf16[4,2,16,2688]{3,2,1,0:T(8,128)(2,1)}, bf16[4,2,16,2688]{3,2,1,0:T(8,128)(2,1)}, u32[]{:S(2)}, u32[]{:S(2)}) collective-permute-start(bf16[4,2,16,2688]{3,2,1,0:T(8,128)(2,1)} %get-tuple-element.356), channel_id=1, source_target_pairs={{0,8},{4,12},{8,0},{12,4},{16,24},{20,28},{24,16},{28,20},{1,9},{5... | collective-permute-start | bytes 2064392 | tf_op jit(solution)/shard_map/ppermute | solution.py:45
  214.3 24.9 %collective-permute-start.38 = (bf16[4,2,16,2688]{3,2,1,0:T(8,128)(2,1)}, bf16[4,2,16,2688]{3,2,1,0:T(8,128)(2,1)}, u32[]{:S(2)}, u32[]{:S(2)}) collective-permute-start(bf16[4,2,16,2688]{3,2,1,0:T(8,128)(2,1)} %get-tuple-element.358), channel_id=1, source_target_pairs={{0,16},{4,20},{8,24},{12,28},{16,0},{20,4},{24,8},{28,12},{1,17},{... | collective-permute-start | bytes 2064392 | tf_op jit(solution)/shard_map/ppermute | solution.py:45
  217.8 21.4 %collective-permute-start.39 = (bf16[4,1,16,2688]{3,2,1,0:T(8,128)(2,1)}, bf16[4,1,16,2688]{3,2,1,0:T(8,128)(2,1)}, u32[]{:S(2)}, u32[]{:S(2)}) collective-permute-start(bf16[4,1,16,2688]{3,2,1,0:T(8,128)(2,1)} %get-tuple-element.372), channel_id=1, source_target_pairs={{0,16},{4,20},{8,24},{12,28},{16,0},{20,4},{24,8},{28,12},{1,17},{... | collective-permute-start | bytes 1032200 | tf_op jit(solution)/shard_map/ppermute | solution.py:45
  219.3 19.9 %collective-permute-start.40 = (bf16[4,1,16,2688]{3,2,1,0:T(8,128)(2,1)}, bf16[4,1,16,2688]{3,2,1,0:T(8,128)(2,1)}, u32[]{:S(2)}, u32[]{:S(2)}) collective-permute-start(bf16[4,1,16,2688]{3,2,1,0:T(8,128)(2,1)} %get-tuple-element.374), channel_id=1, source_target_pairs={{0,8},{4,12},{8,0},{12,4},{16,24},{20,28},{24,16},{28,20},{1,9},{5... | collective-permute-start | bytes 1032200 | tf_op jit(solution)/shard_map/ppermute | solution.py:45
  239.3 24.8 %collective-permute-start.43 = (bf16[4,2,16,2688]{3,2,1,0:T(8,128)(2,1)}, bf16[4,2,16,2688]{3,2,1,0:T(8,128)(2,1)}, u32[]{:S(2)}, u32[]{:S(2)}) collective-permute-start(bf16[4,2,16,2688]{3,2,1,0:T(8,128)(2,1)} %get-tuple-element.384), channel_id=1, source_target_pairs={{0,8},{4,12},{8,0},{12,4},{16,24},{20,28},{24,16},{28,20},{1,9},{5... | collective-permute-start | bytes 2064392 | tf_op jit(solution)/shard_map/ppermute | solution.py:45
  240.7 23.4 %collective-permute-start.44 = (bf16[4,2,16,2688]{3,2,1,0:T(8,128)(2,1)}, bf16[4,2,16,2688]{3,2,1,0:T(8,128)(2,1)}, u32[]{:S(2)}, u32[]{:S(2)}) collective-permute-start(bf16[4,2,16,2688]{3,2,1,0:T(8,128)(2,1)} %get-tuple-element.386), channel_id=1, source_target_pairs={{0,16},{4,20},{8,24},{12,28},{16,0},{20,4},{24,8},{28,12},{1,17},{... | collective-permute-start | bytes 2064392 | tf_op jit(solution)/shard_map/ppermute | solution.py:45
  244.3 19.7 %collective-permute-start.41 = (bf16[4,1,16,2688]{3,2,1,0:T(8,128)(2,1)}, bf16[4,1,16,2688]{3,2,1,0:T(8,128)(2,1)S(1)}, u32[]{:S(2)}, u32[]{:S(2)}) collective-permute-start(bf16[4,1,16,2688]{3,2,1,0:T(8,128)(2,1)} %get-tuple-element.380), channel_id=1, source_target_pairs={{0,16},{4,20},{8,24},{12,28},{16,0},{20,4},{24,8},{28,12},{1,17},{... | collective-permute-start | bytes 1032200 | tf_op jit(solution)/shard_map/ppermute | solution.py:45
  245.8 18.2 %collective-permute-start.42 = (bf16[4,1,16,2688]{3,2,1,0:T(8,128)(2,1)}, bf16[4,1,16,2688]{3,2,1,0:T(8,128)(2,1)S(1)}, u32[]{:S(2)}, u32[]{:S(2)}) collective-permute-start(bf16[4,1,16,2688]{3,2,1,0:T(8,128)(2,1)} %get-tuple-element.382), channel_id=1, source_target_pairs={{0,8},{4,12},{8,0},{12,4},{16,24},{20,28},{24,16},{28,20},{1,9},{5... | collective-permute-start | bytes 1032200 | tf_op jit(solution)/shard_map/ppermute | solution.py:45
  248.0 16.0 %collective-permute-start.45 = (bf16[32,2688]{1,0:T(8,128)(2,1)S(1)}, bf16[32,2688]{1,0:T(8,128)(2,1)S(1)}, u32[]{:S(2)}, u32[]{:S(2)}) collective-permute-start(bf16[32,2688]{1,0:T(8,128)(2,1)S(1)} %dynamic-slice_bitcast_fusion.15), channel_id=1, source_target_pairs={{0,1},{1,2},{2,3},{3,0},{4,5},{5,6},{6,7},{7,4},{8,9},{9,10},{10,1... | collective-permute-start | bytes 516104 | tf_op jit(solution)/shard_map/ppermute | solution.py:50
  264.1 16.8 %collective-permute-start.46 = (bf16[2,128,1024]{2,1,0:T(8,128)(2,1)S(1)}, bf16[2,128,1024]{2,1,0:T(8,128)(2,1)S(1)}, u32[]{:S(2)}, u32[]{:S(2)}) collective-permute-start(bf16[2,128,1024]{2,1,0:T(8,128)(2,1)S(1)} %get-tuple-element.401), channel_id=1, source_target_pairs={{1,0},{2,1},{3,2},{5,4},{6,5},{7,6},{9,8},{10,9},{11,10},{13,12},{... | collective-permute-start | bytes 1572872 | tf_op jit(solution)/shard_map/ppermute | solution.py:208
  265.4 16.1 %collective-permute-start.47 = (bf16[2,128,1024]{2,1,0:T(8,128)(2,1)S(1)}, bf16[2,128,1024]{2,1,0:T(8,128)(2,1)S(1)}, u32[]{:S(2)}, u32[]{:S(2)}) collective-permute-start(bf16[2,128,1024]{2,1,0:T(8,128)(2,1)S(1)} %get-tuple-element.402), channel_id=1, source_target_pairs={{0,1},{1,2},{2,3},{4,5},{5,6},{6,7},{8,9},{9,10},{10,11},{12,13},{... | collective-permute-start | bytes 1572872 | tf_op jit(solution)/shard_map/ppermute | solution.py:208
  288.2 15.5 %collective-permute-start.54 = (bf16[32,2688]{1,0:T(8,128)(2,1)S(1)}, bf16[32,2688]{1,0:T(8,128)(2,1)S(1)}, u32[]{:S(2)}, u32[]{:S(2)}) collective-permute-start(bf16[32,2688]{1,0:T(8,128)(2,1)S(1)} %get-tuple-element.559), channel_id=1, source_target_pairs={{0,3},{1,0},{2,1},{3,2},{4,7},{5,4},{6,5},{7,6},{8,11},{9,8},{10,9... | collective-permute-start | bytes 516104 | tf_op jit(solution)/shard_map/ppermute | solution.py:50
  289.2 14.5 %collective-permute-start.55 = (bf16[32,2688]{1,0:T(8,128)(2,1)S(1)}, bf16[32,2688]{1,0:T(8,128)(2,1)S(1)}, u32[]{:S(2)}, u32[]{:S(2)}) collective-permute-start(bf16[32,2688]{1,0:T(8,128)(2,1)S(1)} %get-tuple-element.558), channel_id=1, source_target_pairs={{0,2},{1,3},{2,0},{3,1},{4,6},{5,7},{6,4},{7,5},{8,10},{9,11},{10,... | collective-permute-start | bytes 516104 | tf_op jit(solution)/shard_map/ppermute | solution.py:50
  291.3 12.3 %collective-permute-start.52 = (bf16[4,2,16,1024]{3,2,1,0:T(8,128)(2,1)}, bf16[4,2,16,1024]{3,2,1,0:T(8,128)(2,1)S(1)}, u32[]{:S(2)}, u32[]{:S(2)}) collective-permute-start(bf16[4,2,16,1024]{3,2,1,0:T(8,128)(2,1)} %get-tuple-element.434), channel_id=1, source_target_pairs={{0,8},{4,12},{8,0},{12,4},{16,24},{20,28},{24,16},{28,20},{1,9},{5... | collective-permute-start | bytes 786440 | tf_op jit(solution)/shard_map/ppermute | solution.py:45
  304.4 19.2 %collective-permute-start.56 = (bf16[4,2,16,3072]{3,2,1,0:T(8,128)(2,1)}, bf16[4,2,16,3072]{3,2,1,0:T(8,128)(2,1)}, u32[]{:S(2)}, u32[]{:S(2)}) collective-permute-start(bf16[4,2,16,3072]{3,2,1,0:T(8,128)(2,1)} %get-tuple-element.445), channel_id=1, source_target_pairs={{0,8},{4,12},{8,0},{12,4},{16,24},{20,28},{24,16},{28,20},{1,9},{5... | collective-permute-start | bytes 2359304 | tf_op jit(solution)/shard_map/ppermute | solution.py:45
  305.3 19.2 %collective-permute-start.57 = (bf16[4,2,16,3072]{3,2,1,0:T(8,128)(2,1)}, bf16[4,2,16,3072]{3,2,1,0:T(8,128)(2,1)}, u32[]{:S(2)}, u32[]{:S(2)}) collective-permute-start(bf16[4,2,16,3072]{3,2,1,0:T(8,128)(2,1)} %get-tuple-element.447), channel_id=1, source_target_pairs={{0,16},{4,20},{8,24},{12,28},{16,0},{20,4},{24,8},{28,12},{1,17},{... | collective-permute-start | bytes 2359304 | tf_op jit(solution)/shard_map/ppermute | solution.py:45
  306.8 14.7 %collective-permute-start.58 = (bf16[32,2688]{1,0:T(8,128)(2,1)S(1)}, bf16[32,2688]{1,0:T(8,128)(2,1)S(1)}, u32[]{:S(2)}, u32[]{:S(2)}) collective-permute-start(bf16[32,2688]{1,0:T(8,128)(2,1)S(1)} %get-tuple-element.557), channel_id=1, source_target_pairs={{0,1},{1,2},{2,3},{3,0},{4,5},{5,6},{6,7},{7,4},{8,9},{9,10},{10,1... | collective-permute-start | bytes 516104 | tf_op jit(solution)/shard_map/ppermute | solution.py:50
  307.4 14.1 %collective-permute-start.59 = (bf16[32,2688]{1,0:T(8,128)(2,1)S(1)}, bf16[32,2688]{1,0:T(8,128)(2,1)S(1)}, u32[]{:S(2)}, u32[]{:S(2)}) collective-permute-start(bf16[32,2688]{1,0:T(8,128)(2,1)S(1)} %get-tuple-element.556), channel_id=1, source_target_pairs={{0,2},{1,3},{2,0},{3,1},{4,6},{5,7},{6,4},{7,5},{8,10},{9,11},{10,... | collective-permute-start | bytes 516104 | tf_op jit(solution)/shard_map/ppermute | solution.py:50
  308.7 12.9 %collective-permute-start.60 = (bf16[32,2688]{1,0:T(8,128)(2,1)S(1)}, bf16[32,2688]{1,0:T(8,128)(2,1)S(1)}, u32[]{:S(2)}, u32[]{:S(2)}) collective-permute-start(bf16[32,2688]{1,0:T(8,128)(2,1)S(1)} %get-tuple-element.555), channel_id=1, source_target_pairs={{0,3},{1,0},{2,1},{3,2},{4,7},{5,4},{6,5},{7,6},{8,11},{9,8},{10,9... | collective-permute-start | bytes 516104 | tf_op jit(solution)/shard_map/ppermute | solution.py:50
  326.4 15.9 %collective-permute-start.61 = (bf16[4,1,16,4096]{3,2,1,0:T(8,128)(2,1)S(1)}, bf16[4,1,16,4096]{3,2,1,0:T(8,128)(2,1)S(1)}, u32[]{:S(2)}, u32[]{:S(2)}) collective-permute-start(bf16[4,1,16,4096]{3,2,1,0:T(8,128)(2,1)S(1)} %get-tuple-element.465), channel_id=1, source_target_pairs={{0,16},{4,20},{8,24},{12,28},{16,0},{20,4},{24,8},{28,12},{1,17},{... | collective-permute-start | bytes 1572872 | tf_op jit(solution)/shard_map/ppermute | solution.py:45
  327.9 14.4 %collective-permute-start.62 = (bf16[4,1,16,4096]{3,2,1,0:T(8,128)(2,1)S(1)}, bf16[4,1,16,4096]{3,2,1,0:T(8,128)(2,1)S(1)}, u32[]{:S(2)}, u32[]{:S(2)}) collective-permute-start(bf16[4,1,16,4096]{3,2,1,0:T(8,128)(2,1)S(1)} %get-tuple-element.467), channel_id=1, source_target_pairs={{0,8},{4,12},{8,0},{12,4},{16,24},{20,28},{24,16},{28,20},{1,9},{5... | collective-permute-start | bytes 1572872 | tf_op jit(solution)/shard_map/ppermute | solution.py:45
  329.7 12.6 %collective-permute-start.64 = (bf16[32,2688]{1,0:T(8,128)(2,1)S(1)}, bf16[32,2688]{1,0:T(8,128)(2,1)S(1)}, u32[]{:S(2)}, u32[]{:S(2)}) collective-permute-start(bf16[32,2688]{1,0:T(8,128)(2,1)S(1)} %get-tuple-element.553), channel_id=1, source_target_pairs={{0,2},{1,3},{2,0},{3,1},{4,6},{5,7},{6,4},{7,5},{8,10},{9,11},{10,... | collective-permute-start | bytes 516104 | tf_op jit(solution)/shard_map/ppermute | solution.py:50
  359.8 13.1 %collective-permute-start.71 = (bf16[1,2,16,8064]{3,2,1,0:T(8,128)(2,1)S(1)}, bf16[1,2,16,8064]{3,2,1,0:T(8,128)(2,1)S(1)}, u32[]{:S(2)}, u32[]{:S(2)}) collective-permute-start(bf16[1,2,16,8064]{3,2,1,0:T(8,128)(2,1)S(1)} %pad_maximum_fusion.19), channel_id=1, source_target_pairs={{0,16},{4,20},{8,24},{12,28},{16,0},{20,4},{24,8},{28,12},{1,17},{... | collective-permute-start | bytes 1548296 | tf_op jit(solution)/shard_map/ppermute | solution.py:45
  361.3 14.2 %collective-permute-start.70 = (bf16[32,4096]{1,0:T(8,128)(2,1)S(1)}, bf16[32,4096]{1,0:T(8,128)(2,1)S(1)}, u32[]{:S(2)}, u32[]{:S(2)}) collective-permute-start(bf16[32,4096]{1,0:T(8,128)(2,1)S(1)} %dynamic-slice_bitcast_fusion.3), channel_id=1, source_target_pairs={{0,2},{1,3},{2,0},{3,1},{4,6},{5,7},{6,4},{7,5},{8,10},{9,11},{10,... | collective-permute-start | bytes 786440 | tf_op jit(solution)/shard_map/ppermute | solution.py:50
  361.9 12.6 %collective-permute-start.72 = (bf16[2,1,16,8064]{3,2,1,0:T(8,128)(2,1)S(1)}, bf16[2,1,16,8064]{3,2,1,0:T(8,128)(2,1)S(1)}, u32[]{:S(2)}, u32[]{:S(2)}) collective-permute-start(bf16[2,1,16,8064]{3,2,1,0:T(8,128)(2,1)S(1)} %pad_maximum_fusion.20), channel_id=1, source_target_pairs={{0,8},{4,12},{8,0},{12,4},{16,24},{20,28},{24,16},{28,20},{1,9},{5... | collective-permute-start | bytes 1548296 | tf_op jit(solution)/shard_map/ppermute | solution.py:45
  (114 other events, 787.7 us)

commit v7 on v6

--- a/solution.py
+++ b/solution.py
@@ -799,7 +799,7 @@
         compiler_params=params(24, "arbitrary"),
         cost_estimate=cost(2 * rows * width * hidden, width * hidden + 4 * rows * (hidden + width)),
         name="down_sum",
-    )(meta, *far(mixed, mixed_other, grad_result, grad_other))
+    )(meta, *far(mixed), mixed_other, *far(grad_result), grad_other)
     return [(out[0], out[1]), (out[2], out[3])]
 
 
@@ -1144,7 +1144,7 @@
     steps = link_orders()
     near, far, middle_way = runs()
 
-    gains = jnp.pad(jnp.stack([norm_first, norm_second], axis=1), ((0, 0), (0, LANES - 2)))
+    gains = jnp.pad(jnp.stack([norm_first, norm_second]).T, ((0, 0), (0, LANES - 2)))
     came_one = turned_before(row_piece([w_qkv, gains]), range(1, size))
     own_in = [jnp.pad(w_in[:, half * hidden :][:, :hidden], ((0, 0), (0, pad))) for half in range(2)]
     piece_two = row_piece([own_in[0], own_in[1], w_out])

time: 408 us -> 407 us (level)
    unnamed x170 -> x172, local copies, waits for them, and re-layouts: 15.2 us -> 13.9 us
where the time goes in v7:
time: 407 us; the launch traced here: 399 us
  Pallas kernels  148 us (36%)
  waiting for transfers between devices  102 us (25%)
  starting transfers between devices  93.3 us (23%)
  local copies, waits for them, and re-layouts  26.1 us (6%)
  other arithmetic  23.1 us (6%)
  matrix products  4.2 us (1%)
    ppermute x55, waiting for transfers between devices, flip(): return lax.ppermute(value, 'rep', [(i, i ^ 1 << bit) for i in range(size)])  75.4 us
    ppermute x55, starting transfers between devices, flip(): return lax.ppermute(value, 'rep', [(i, i ^ 1 << bit) for i in range(size)])  44.1 us
    ppermute x21, starting transfers between devices, turn(): lax.ppermute(value, 'fsdp', [(i, (i + steps) % size) for i in range(size)])  37.3 us
    ppermute x21, waiting for transfers between devices, turn(): lax.ppermute(value, 'fsdp', [(i, (i + steps) % size) for i in range(size)])  25.8 us
    pallas_call x3, Pallas kernels, sum_call(): pl.pallas_call(functools.partial(sum_kernel, size=size, links=links, plac...  23.4 us
    pallas_call x1, Pallas kernels, middle_back_call(): pl.pallas_call(middle_back_kernel, grid=(hidden // block,), in_specs=[SME...  17.3 us
    pallas_call x1, Pallas kernels, attend_back_call(): pl.pallas_call(attend_back_kernel, grid=(seqs, width // block), in_specs=...  15.1 us
    unnamed x172, local copies, waits for them, and re-layouts  13.9 us
  transfers between devices with their start and end apart: 80, of which 33 were waited for; matrix products, arithmetic and copies ran while one was open for 6% of the time, Pallas kernels for 37%

profile of v7, /device:TPU:0, one launch (start us, length us, event | category | flops | bytes accessed | tf_op | source)
XLA Modules:
  0.0 399.4 jit_solution(17275448839694614352)
XLA Ops:
  4.0 3.0 collective-permute-start
  7.0 2.6 collective-permute-start.1
  11.7 2.4 multiply_convert_fusion.g_ref
  14.1 1.9 constant_dynamic-slice_fusion
  29.7 4.8 %collective-permute-start.6 = (bf16[2,16,6400]{2,1,0:T(8,128)(2,1)}, bf16[2,16,6400]{2,1,0:T(8,128)(2,1)S(1)}, u32[]{:S(2)}, u32[]{:S(2)}) collective-permute-start(bf16[2,16,6400]{2,1,0:T(8,128)(2,1)} %maximum_bitcast_fusion.2), channel_id=1, source_target_pairs={{0,1},{1,2},{2,3},{3,0},{4,5},{5,6},{6,7},{7,4},{8,9},{9,10},{10,1... | collective-permute-start | bytes 1228808 | tf_op jit(solution)/shard_map/ppermute | solution.py:50
  37.8 6.0 %collective-permute-done.6 = bf16[2,16,6400]{2,1,0:T(8,128)(2,1)S(1)} collective-permute-done((bf16[2,16,6400]{2,1,0:T(8,128)(2,1)}, bf16[2,16,6400]{2,1,0:T(8,128)(2,1)S(1)}, u32[]{:S(2)}, u32[]{:S(2)}) %collective-permute-start.6) | collective-permute-done | bytes 409632 | tf_op jit(solution)/shard_map/ppermute | solution.py:50
  46.6 10.9 %collective-permute-done.7 = bf16[3,1,2,16,3200]{4,3,0,2,1:T(8,128)(2,1)S(1)} collective-permute-done((bf16[3,1,2,16,3200]{4,3,0,2,1:T(8,128)(2,1)S(1)}, bf16[3,1,2,16,3200]{4,3,0,2,1:T(8,128)(2,1)S(1)}, u32[]{:S(2)}, u32[]{:S(2)}) %collective-permute-start.7) | collective-permute-done | bytes 614432 | tf_op jit(solution)/shard_map/ppermute | solution.py:45
  58.9 2.4 collective-permute-start.12
  63.0 10.9 %qkv.1 = (bf16[2,512,512]{2,1,0:T(8,128)(2,1)S(1)}, bf16[3,512,1024]{2,1,0:T(8,128)(2,1)S(1)}, f32[8,1024]{1,0:T(8,128)S(1)}) custom-call(s32[7]{0:T(128)S(1)} %stack.61.meta_ref, bf16[512,1024]{1,0:T(8,128)(2,1)} %bitcast.192, bf16[256,3072]{1,0:T(8,128)(2,1)} %own_ref.7, bf16[3,64,3200]{2,1,0:T(8,128)(2,1)} %bitcast.186, bf16[3,64,3200]{2,1,0:T(8,128)(2,1)} %bitcast.182, ...), custom_call_target="tpu_custom_call" | custom-call | flops 3221225472 | bytes 11534336 | tf_op jit(solution)/shard_map/qkv/pallas_call | solution.py:360
  75.2 4.9 %collective-permute-done.12 = bf16[2,16,6400]{2,1,0:T(8,128)(2,1)S(1)} collective-permute-done((bf16[2,16,6400]{2,1,0:T(8,128)(2,1)}, bf16[2,16,6400]{2,1,0:T(8,128)(2,1)S(1)}, u32[]{:S(2)}, u32[]{:S(2)}) %collective-permute-start.12) | collective-permute-done | bytes 409632 | tf_op jit(solution)/shard_map/ppermute | solution.py:50
  81.4 4.6 %collective-permute-start.14 = (bf16[2,128,1024]{2,1,0:T(8,128)(2,1)S(1)}, bf16[2,128,1024]{2,1,0:T(8,128)(2,1)S(1)}, u32[]{:S(2)}, u32[]{:S(2)}) collective-permute-start(bf16[2,128,1024]{2,1,0:T(8,128)(2,1)S(1)} %bitcast.228), channel_id=1, source_target_pairs={{0,1},{1,2},{2,3},{4,5},{5,6},{6,7},{8,9},{9,10},{10,11},{12,13},{... | collective-permute-start | bytes 1572872 | tf_op jit(solution)/shard_map/ppermute | solution.py:208
  88.4 12.2 %collective-permute-done.15 = bf16[3,1,1,16,6400]{4,3,0,2,1:T(8,128)(2,1)S(1)} collective-permute-done((bf16[3,1,1,16,6400]{4,3,0,2,1:T(8,128)(2,1)S(1)}, bf16[3,1,1,16,6400]{4,3,0,2,1:T(8,128)(2,1)S(1)}, u32[]{:S(2)}, u32[]{:S(2)}) %collective-permute-start.15) | collective-permute-done | bytes 614432 | tf_op jit(solution)/shard_map/ppermute | solution.py:45
  103.6 3.3 collective-permute-start.21
  108.4 11.3 %attend.1 = (bf16[512,1024]{1,0:T(8,128)(2,1)S(1)}, bf16[2,8,2,256,256]{4,3,2,1,0:T(8,128)(2,1)}) custom-call(s32[3]{0:T(128)S(1)} %pad_add_fusion.meta_ref, bf16[3,512,1024]{2,1,0:T(8,128)(2,1)S(1)} %get-tuple-element.289.q_ref.k_ref.v_ref, bf16[3,512,1024]{2,1,0:T(8,128)(2,1)S(1)} %get-tuple-element.289.q_ref.k_ref.v_ref, ...), custom_call_target="tpu_custom_call" | custom-call | flops 1073741824 | bytes 5242880 | tf_op jit(solution)/shard_map/attend/pallas_call | solution.py:452
  120.6 7.1 %collective-permute-done.17 = bf16[3,1,2,16,6400]{4,3,0,2,1:T(8,128)(2,1)S(1)} collective-permute-done((bf16[3,1,2,16,6400]{4,3,0,2,1:T(8,128)(2,1)S(1)}, bf16[3,1,2,16,6400]{4,3,0,2,1:T(8,128)(2,1)S(1)}, u32[]{:S(2)}, u32[]{:S(2)}) %collective-permute-start.17) | collective-permute-done | bytes 1228832 | tf_op jit(solution)/shard_map/ppermute | solution.py:45
  128.2 4.4 %collective-permute-done.18 = bf16[3,2,1,16,6400]{4,3,2,1,0:T(8,128)(2,1)S(1)} collective-permute-done((bf16[3,2,1,16,6400]{4,3,2,1,0:T(8,128)(2,1)S(1)}, bf16[3,2,1,16,6400]{4,3,2,1,0:T(8,128)(2,1)S(1)}, u32[]{:S(2)}, u32[]{:S(2)}) %collective-permute-start.18) | collective-permute-done | bytes 1228832 | tf_op jit(solution)/shard_map/ppermute | solution.py:45
  141.2 4.7 %collective-permute-done.25 = bf16[3,1,1,320,128]{4,3,0,2,1:T(8,128)(2,1)S(1)} collective-permute-done((bf16[3,1,1,320,128]{4,3,0,2,1:T(8,128)(2,1)S(1)}, bf16[3,1,1,320,128]{4,3,0,2,1:T(8,128)(2,1)S(1)}, u32[]{:S(2)}, u32[]{:S(2)}) %collective-permute-start.25) | collective-permute-done | bytes 245792 | tf_op jit(solution)/shard_map/ppermute | solution.py:45
  150.6 5.7 %out_norm.1 = (f32[512,1024]{1,0:T(8,128)}, bf16[2,512,512]{2,1,0:T(8,128)(2,1)S(1)}, bf16[2,512,512]{2,1,0:T(8,128)(2,1)S(1)}) custom-call(s32[7]{0:T(128)S(1)} %stack.61.meta_ref, bf16[512,1024]{1,0:T(8,128)(2,1)S(1)} %copy-done.12, bf16[256,1024]{1,0:T(8,128)(2,1)} %out_own_ref.1, bf16[3,64,6400]{2,1,0:T(8,128)(2,1)} %bitcast.24.p0.q0.r0.s0, ...), custom_call_target="tpu_custom_call" | custom-call | flops 1073741824 | bytes 8388608 | tf_op jit(solution)/shard_map/out_norm/pallas_call | solution.py:579
  157.1 11.9 %gate.1 = (bf16[512,2688]{1,0:T(8,128)(2,1)}, bf16[512,2688]{1,0:T(8,128)(2,1)}, bf16[512,2688]{1,0:T(8,128)(2,1)}) custom-call(s32[7]{0:T(128)S(1)} %stack.61.meta_ref, bf16[2,512,512]{2,1,0:T(8,128)(2,1)S(1)} %get-tuple-element.312.n_ref.left_ref, bf16[256,2688]{1,0:T(8,128)(2,1)} %copy-done.35, bf16[3,64,6400]{2,1,0:T(8,128)(2,1)} %bitcast.24.p0.q0.r0.s0, ...), custom_call_target="tpu_custom_call" | custom-call | flops 5637144576 | bytes 19267584 | tf_op jit(solution)/shard_map/gate/pallas_call | solution.py:624
  170.3 3.4 collective-permute-done.32.p3
  175.0 9.2 %gate_back.1 = (bf16[2,512,2688]{2,1,0:T(8,128)(2,1)S(1)}, bf16[2688,1024]{1,0:T(8,128)(2,1)S(1)}) custom-call(s32[7]{0:T(128)S(1)} %stack.61.meta_ref, bf16[512,1024]{1,0:T(8,128)(2,1)} %multiply_convert_fusion.g_ref, bf16[656,1024]{1,0:T(8,128)(2,1)} %own_ref.6, bf16[3,4,336,128]{3,2,1,0:T(8,128)(2,1)} %bitcast.206, bf16[3,4,320,128]{3,2,1,0:T(8,128)(2,1)} %bitcast.212, ...), custom_call_target="tpu_custom_call" | custom-call | flops 2818572288 | bytes 22020096 | tf_op jit(solution)/shard_map/gate_back/pallas_call | solution.py:710
  184.4 9.2 %down_sum.1 = (bf16[4,2,16,2688]{3,2,1,0:T(8,128)(2,1)}, bf16[4,2,16,2688]{3,2,1,0:T(8,128)(2,1)}, bf16[4,2,16,2688]{3,2,1,0:T(8,128)(2,1)}, bf16[4,2,16,2688]{3,2,1,0:T(8,128)(2,1)}) custom-call(s32[7]{0:T(128)S(1)} %stack.61.meta_ref, bf16[512,2688]{1,0:T(8,128)(2,1)} %get-tuple-element.477.m_ref, bf16[512,2688]{1,0:T(8,128)(2,1)S(1)} %collective-permute-done.33.n_ref, ...), custom_call_target="tpu_custom_call" | custom-call | flops 2751463424 | bytes 10158080 | tf_op jit(solution)/shard_map/down_sum/pallas_call | solution.py:790
  196.1 12.0 %sum_rows.3 = (bf16[4,2,16,2688]{3,2,1,0:T(8,128)(2,1)}, bf16[4,2,16,2688]{3,2,1,0:T(8,128)(2,1)}, bf16[4,2,16,2688]{3,2,1,0:T(8,128)(2,1)}, bf16[4,2,16,2688]{3...) custom-call(s32[7]{0:T(128)S(1)} %stack.61.meta_ref, ...), custom_call_target="tpu_custom_call" | custom-call | flops 5637144576 | bytes 22020096 | tf_op jit(solution)/shard_map/sum_rows/pallas_call | solution.py:850
  208.1 3.2 collective-permute-done.35.refs_1_
  213.7 2.9 fold.4
  218.8 17.3 %middle_back.1 = (f32[512,1024]{1,0:T(8,128)}, bf16[512,1024]{1,0:T(8,128)(2,1)S(1)}, bf16[512,1024]{1,0:T(8,128)(2,1)S(1)}) custom-call(s32[7]{0:T(128)S(1)} %stack.61.meta_ref, bf16[2,512,2688]{2,1,0:T(8,128)(2,1)S(1)} %get-tuple-element.363.right_ref.gu_ref, bf16[256,2688]{1,0:T(8,128)(2,1)} %copy-done.35, bf16[3,64,6400]{2,1,0:T(8,128)(2,1)} %bitcast.24.p0.q0.r0.s0, ...), custom_call_target="tpu_custom_call" | custom-call | flops 5637144576 | bytes 22806528 | tf_op jit(solution)/shard_map/middle_back/pallas_call | solution.py:1051
  240.0 3.0 fold.5
  247.4 15.1 %attend_back.1 = (bf16[512,1024]{1,0:T(8,128)(2,1)S(1)}, f32[512,1024]{1,0:T(8,128)S(1)}, f32[512,1024]{1,0:T(8,128)S(1)}, bf16[2,128,1024]{2,1,0:T(8,128)(2,1)S(1)}, bf16[2,128,1024]{2,1,0:T(8,128)(2,1)S(1)}) custom-call(bf16[3,512,1024]{2,1,0:T(8,128)(2,1)S(1)} %get-tuple-element.289.q_ref.k_ref.v_ref, ...), custom_call_target="tpu_custom_call" | custom-call | flops 2684354560 | bytes 10485760 | tf_op jit(solution)/shard_map/attend_back/pallas_call | solution.py:534
  264.5 4.8 %collective-permute-start.47 = (bf16[2,128,1024]{2,1,0:T(8,128)(2,1)S(1)}, bf16[2,128,1024]{2,1,0:T(8,128)(2,1)S(1)}, u32[]{:S(2)}, u32[]{:S(2)}) collective-permute-start(bf16[2,128,1024]{2,1,0:T(8,128)(2,1)S(1)} %get-tuple-element.402), channel_id=1, source_target_pairs={{0,1},{1,2},{2,3},{4,5},{5,6},{6,7},{8,9},{9,10},{10,11},{12,13},{... | collective-permute-start | bytes 1572872 | tf_op jit(solution)/shard_map/ppermute | solution.py:208
  269.3 3.3 fold.6
  275.9 4.0 %sum_rows.4 = (bf16[4,2,16,1024]{3,2,1,0:T(8,128)(2,1)}, bf16[4,2,16,1024]{3,2,1,0:T(8,128)(2,1)}, bf16[4,2,16,1024]{3,2,1,0:T(8,128)(2,1)}, bf16[4,2,16,1024]{3,2,1,0:T(8,128)(2,1)}) custom-call(s32[7]{0:T(128)S(1)} %stack.61.meta_ref, bf16[2,512,512]{2,1,0:T(8,128)(2,1)} %copy-done.25, bf16[512,512]{1,0:T(8,128)(2,1)} %copy-done.79, ...), custom_call_target="tpu_custom_call" | custom-call | flops 1073741824 | bytes 4194304 | tf_op jit(solution)/shard_map/sum_rows/pallas_call | solution.py:850
  280.6 2.1 collective-permute-done.49.refs_1_
  284.1 3.1 pad_maximum_fusion
  288.5 2.0 collective-permute-start.55
  294.5 7.4 %sum_rows.5 = (bf16[4,2,16,3072]{3,2,1,0:T(8,128)(2,1)S(1)}, bf16[4,2,16,3072]{3,2,1,0:T(8,128)(2,1)}, bf16[4,2,16,3072]{3,2,1,0:T(8,128)(2,1)S(1)}, bf16[4,2,16,3072]{3,2,1,0:T(8,128)(2,1)}) custom-call(s32[7]{0:T(128)S(1)} %stack.61.meta_ref, bf16[2,512,512]{2,1,0:T(8,128)(2,1)} %copy-done.23, bf16[512,512]{1,0:T(8,128)(2,1)} %copy-done.78, ...), custom_call_target="tpu_custom_call" | custom-call | flops 3221225472 | bytes 12582912 | tf_op jit(solution)/shard_map/sum_rows/pallas_call | solution.py:850
  307.8 2.0 collective-permute-start.60
  309.9 10.7 %input_back.1 = bf16[512,1024]{1,0:T(8,128)(2,1)} custom-call(s32[7]{0:T(128)S(1)} %stack.61.meta_ref, bf16[512,3072]{1,0:T(8,128)(2,1)} %get-tuple-element.448.gqkv_ref, bf16[256,3072]{1,0:T(8,128)(2,1)} %own_ref.7, bf16[3,64,3200]{2,1,0:T(8,128)(2,1)} %bitcast.188, bf16[3,64,3200]{2,1,0:T(8,128)(2,1)} %bitcast.184, ...), custom_call_target="tpu_custom_call" | custom-call | flops 3221225472 | bytes 13631488 | tf_op jit(solution)/shard_map/input_back/pallas_call | solution.py:1105
  320.7 2.0 collective-permute-done.56.refs_1_
  323.6 1.9 fold.7
  331.7 4.2 %add_convert_fusion = bf16[512,1024]{1,0:T(8,128)(2,1)} fusion(f32[512,1024]{1,0:T(8,128)S(1)} %copy-done.42, f32[512]{0:T(512)S(1)} %bitcast.232, bf16[512,2688]{1,0:T(8,128)(2,1)S(1)} %copy-done.76, bf16[2688,1024]{1,0:T(8,128)(2,1)S(1)} %bitcast.179), kind=kOutput, calls=%fused_computation.5 | convolution fusion | flops 2820145152 | bytes 11405312 | tf_op jit(solution)/shard_map/dot_general | solution.py:1304
  337.0 4.4 %collective-permute-done.64 = bf16[32,2688]{1,0:T(8,128)(2,1)S(1)} collective-permute-done((bf16[32,2688]{1,0:T(8,128)(2,1)S(1)}, bf16[32,2688]{1,0:T(8,128)(2,1)S(1)}, u32[]{:S(2)}, u32[]{:S(2)}) %collective-permute-start.64) | collective-permute-done | bytes 172064 | tf_op jit(solution)/shard_map/ppermute | solution.py:50
  343.8 4.2 %collective-permute-start.66 = (bf16[32,4096]{1,0:T(8,128)(2,1)S(1)}, bf16[32,4096]{1,0:T(8,128)(2,1)S(1)}, u32[]{:S(2)}, u32[]{:S(2)}) collective-permute-start(bf16[32,4096]{1,0:T(8,128)(2,1)S(1)} %get-tuple-element.537), channel_id=1, source_target_pairs={{0,1},{1,2},{2,3},{3,0},{4,5},{5,6},{6,7},{7,4},{8,9},{9,10},{10,1... | collective-permute-start | bytes 786440 | tf_op jit(solution)/shard_map/ppermute | solution.py:50
  350.2 5.8 %collective-permute-done.66 = bf16[32,4096]{1,0:T(8,128)(2,1)S(1)} collective-permute-done((bf16[32,4096]{1,0:T(8,128)(2,1)S(1)}, bf16[32,4096]{1,0:T(8,128)(2,1)S(1)}, u32[]{:S(2)}, u32[]{:S(2)}) %collective-permute-start.66) | collective-permute-done | bytes 262176 | tf_op jit(solution)/shard_map/ppermute | solution.py:50
  356.0 2.9 collective-permute-done.67
  361.7 10.3 %collective-permute-done.71 = bf16[1,2,16,8064]{3,2,1,0:T(8,128)(2,1)S(1)} collective-permute-done((bf16[1,2,16,8064]{3,2,1,0:T(8,128)(2,1)S(1)}, bf16[1,2,16,8064]{3,2,1,0:T(8,128)(2,1)S(1)}, u32[]{:S(2)}, u32[]{:S(2)}) %collective-permute-start.71) | collective-permute-done | bytes 516128 | tf_op jit(solution)/shard_map/ppermute | solution.py:45
  376.4 3.5 collective-permute-done.74
  383.0 7.7 %finish.1 = (f32[256,5248]{1,0:T(8,128)}, f32[4,1,64]{2,1,0:T(1,128)S(1)}, f32[656,1024]{1,0:T(8,128)}) custom-call(s32[7]{0:T(128)S(1)} %stack.61.meta_ref, bf16[64,8064]{1,0:T(8,128)(2,1)} %bitcast.208, bf16[64,8064]{1,0:T(8,128)(2,1)} %bitcast.210, bf16[64,8064]{1,0:T(8,128)(2,1)} %copy-done.50, bf16[64,8064]{1,0:T(8,128)(2,1)} %copy-done.51, ...), custom_call_target="tpu_custom_call" | custom-call | flops 5373952 | bytes 13434880 | tf_op jit(solution)/shard_map/finish/pallas_call | solution.py:954
  395.4 2.1 multiply_reduce_fusion
  (419 shorter events, 118.1 us)
Async XLA Ops:
  4.0 19.4 %collective-permute-start = (bf16[2,16,3200]{2,1,0:T(8,128)(2,1)}, bf16[2,16,3200]{2,1,0:T(8,128)(2,1)}, u32[]{:S(2)}, u32[]{:S(2)}) collective-permute-start(bf16[2,16,3200]{2,1,0:T(8,128)(2,1)} %maximum_bitcast_fusion.6), channel_id=1, source_target_pairs={{0,1},{1,2},{2,3},{3,0},{4,5},{5,6},{6,7},{7,4},{8,9},{9,10},{10,1... | collective-permute-start | bytes 614408 | tf_op jit(solution)/shard_map/ppermute | solution.py:50
  7.0 16.4 %collective-permute-start.1 = (bf16[2,16,3200]{2,1,0:T(8,128)(2,1)}, bf16[2,16,3200]{2,1,0:T(8,128)(2,1)}, u32[]{:S(2)}, u32[]{:S(2)}) collective-permute-start(bf16[2,16,3200]{2,1,0:T(8,128)(2,1)} %maximum_bitcast_fusion.6), channel_id=1, source_target_pairs={{0,2},{1,3},{2,0},{3,1},{4,6},{5,7},{6,4},{7,5},{8,10},{9,11},{10,... | collective-permute-start | bytes 614408 | tf_op jit(solution)/shard_map/ppermute | solution.py:50
  9.6 13.8 %collective-permute-start.2 = (bf16[2,16,3200]{2,1,0:T(8,128)(2,1)}, bf16[2,16,3200]{2,1,0:T(8,128)(2,1)}, u32[]{:S(2)}, u32[]{:S(2)}) collective-permute-start(bf16[2,16,3200]{2,1,0:T(8,128)(2,1)} %maximum_bitcast_fusion.6), channel_id=1, source_target_pairs={{0,3},{1,0},{2,1},{3,2},{4,7},{5,4},{6,5},{7,6},{8,11},{9,8},{10,9... | collective-permute-start | bytes 614408 | tf_op jit(solution)/shard_map/ppermute | solution.py:50
  29.7 14.1 %collective-permute-start.6 = (bf16[2,16,6400]{2,1,0:T(8,128)(2,1)}, bf16[2,16,6400]{2,1,0:T(8,128)(2,1)S(1)}, u32[]{:S(2)}, u32[]{:S(2)}) collective-permute-start(bf16[2,16,6400]{2,1,0:T(8,128)(2,1)} %maximum_bitcast_fusion.2), channel_id=1, source_target_pairs={{0,1},{1,2},{2,3},{3,0},{4,5},{5,6},{6,7},{7,4},{8,9},{9,10},{10,1... | collective-permute-start | bytes 1228808 | tf_op jit(solution)/shard_map/ppermute | solution.py:50
  43.8 13.7 %collective-permute-start.7 = (bf16[3,1,2,16,3200]{4,3,0,2,1:T(8,128)(2,1)S(1)}, bf16[3,1,2,16,3200]{4,3,0,2,1:T(8,128)(2,1)S(1)}, u32[]{:S(2)}, u32[]{:S(2)}) collective-permute-start(bf16[3,1,2,16,3200]{4,3,0,2,1:T(8,128)(2,1)S(1)} %pad_maximum_fusion.13), channel_id=1, source_target_pairs={{0,16},{4,20},{8,24},{12,28},{16,0},{20,4},{24,8},{28,12},{1,17},{... | collective-permute-start | bytes 1843208 | tf_op jit(solution)/shard_map/ppermute | solution.py:45
  44.3 13.4 %collective-permute-start.8 = (bf16[3,2,1,16,3200]{4,3,2,1,0:T(8,128)(2,1)S(1)}, bf16[3,2,1,16,3200]{4,3,2,1,0:T(8,128)(2,1)S(1)}, u32[]{:S(2)}, u32[]{:S(2)}) collective-permute-start(bf16[3,2,1,16,3200]{4,3,2,1,0:T(8,128)(2,1)S(1)} %pad_maximum_fusion.14), channel_id=1, source_target_pairs={{0,8},{4,12},{8,0},{12,4},{16,24},{20,28},{24,16},{28,20},{1,9},{5... | collective-permute-start | bytes 1843208 | tf_op jit(solution)/shard_map/ppermute | solution.py:45
  44.8 13.2 %collective-permute-start.9 = (bf16[2,16,6400]{2,1,0:T(8,128)(2,1)}, bf16[2,16,6400]{2,1,0:T(8,128)(2,1)S(1)}, u32[]{:S(2)}, u32[]{:S(2)}) collective-permute-start(bf16[2,16,6400]{2,1,0:T(8,128)(2,1)} %maximum_bitcast_fusion.2), channel_id=1, source_target_pairs={{0,3},{1,0},{2,1},{3,2},{4,7},{5,4},{6,5},{7,6},{8,11},{9,8},{10,9... | collective-permute-start | bytes 1228808 | tf_op jit(solution)/shard_map/ppermute | solution.py:50
  58.9 21.2 %collective-permute-start.12 = (bf16[2,16,6400]{2,1,0:T(8,128)(2,1)}, bf16[2,16,6400]{2,1,0:T(8,128)(2,1)S(1)}, u32[]{:S(2)}, u32[]{:S(2)}) collective-permute-start(bf16[2,16,6400]{2,1,0:T(8,128)(2,1)} %maximum_bitcast_fusion.2), channel_id=1, source_target_pairs={{0,2},{1,3},{2,0},{3,1},{4,6},{5,7},{6,4},{7,5},{8,10},{9,11},{10,... | collective-permute-start | bytes 1228808 | tf_op jit(solution)/shard_map/ppermute | solution.py:50
  80.1 21.1 %collective-permute-start.13 = (bf16[2,128,1024]{2,1,0:T(8,128)(2,1)S(1)}, bf16[2,128,1024]{2,1,0:T(8,128)(2,1)S(1)}, u32[]{:S(2)}, u32[]{:S(2)}) collective-permute-start(bf16[2,128,1024]{2,1,0:T(8,128)(2,1)S(1)} %bitcast.229), channel_id=1, source_target_pairs={{1,0},{2,1},{3,2},{5,4},{6,5},{7,6},{9,8},{10,9},{11,10},{13,12},{... | collective-permute-start | bytes 1572872 | tf_op jit(solution)/shard_map/ppermute | solution.py:208
  81.4 19.8 %collective-permute-start.14 = (bf16[2,128,1024]{2,1,0:T(8,128)(2,1)S(1)}, bf16[2,128,1024]{2,1,0:T(8,128)(2,1)S(1)}, u32[]{:S(2)}, u32[]{:S(2)}) collective-permute-start(bf16[2,128,1024]{2,1,0:T(8,128)(2,1)S(1)} %bitcast.228), channel_id=1, source_target_pairs={{0,1},{1,2},{2,3},{4,5},{5,6},{6,7},{8,9},{9,10},{10,11},{12,13},{... | collective-permute-start | bytes 1572872 | tf_op jit(solution)/shard_map/ppermute | solution.py:208
  86.2 14.4 %collective-permute-start.15 = (bf16[3,1,1,16,6400]{4,3,0,2,1:T(8,128)(2,1)S(1)}, bf16[3,1,1,16,6400]{4,3,0,2,1:T(8,128)(2,1)S(1)}, u32[]{:S(2)}, u32[]{:S(2)}) collective-permute-start(bf16[3,1,1,16,6400]{4,3,0,2,1:T(8,128)(2,1)S(1)} %maximum_bitcast_fusion), channel_id=1, source_target_pairs={{0,8},{4,12},{8,0},{12,4},{16,24},{20,28},{24,16},{28,20},{1,9},{5... | collective-permute-start | bytes 1843208 | tf_op jit(solution)/shard_map/ppermute | solution.py:45
  86.9 14.1 %collective-permute-start.16 = (bf16[3,1,1,16,6400]{4,3,2,1,0:T(8,128)(2,1)S(1)}, bf16[3,1,1,16,6400]{4,3,2,1,0:T(8,128)(2,1)S(1)}, u32[]{:S(2)}, u32[]{:S(2)}) collective-permute-start(bf16[3,1,1,16,6400]{4,3,2,1,0:T(8,128)(2,1)S(1)} %maximum_bitcast_fusion.1), channel_id=1, source_target_pairs={{0,16},{4,20},{8,24},{12,28},{16,0},{20,4},{24,8},{28,12},{1,17},{... | collective-permute-start | bytes 1843208 | tf_op jit(solution)/shard_map/ppermute | solution.py:45
  101.3 26.5 %collective-permute-start.17 = (bf16[3,1,2,16,6400]{4,3,0,2,1:T(8,128)(2,1)S(1)}, bf16[3,1,2,16,6400]{4,3,0,2,1:T(8,128)(2,1)S(1)}, u32[]{:S(2)}, u32[]{:S(2)}) collective-permute-start(bf16[3,1,2,16,6400]{4,3,0,2,1:T(8,128)(2,1)S(1)} %pad_maximum_fusion.6), channel_id=1, source_target_pairs={{0,16},{4,20},{8,24},{12,28},{16,0},{20,4},{24,8},{28,12},{1,17},{... | collective-permute-start | bytes 3686408 | tf_op jit(solution)/shard_map/ppermute | solution.py:45
  102.9 31.5 %collective-permute-start.19 = (bf16[656,128]{1,0:T(8,128)(2,1)S(1)}, bf16[656,128]{1,0:T(8,128)(2,1)S(1)}, u32[]{:S(2)}, u32[]{:S(2)}) collective-permute-start(bf16[656,128]{1,0:T(8,128)(2,1)S(1)} %copy-done.69), channel_id=1, source_target_pairs={{0,1},{1,2},{2,3},{3,0},{4,5},{5,6},{6,7},{7,4},{8,9},{9,10},{10,1... | collective-permute-start | bytes 503816 | tf_op jit(solution)/shard_map/ppermute | solution.py:50
  103.1 31.2 %collective-permute-start.20 = (bf16[656,128]{1,0:T(8,128)(2,1)S(1)}, bf16[656,128]{1,0:T(8,128)(2,1)S(1)}, u32[]{:S(2)}, u32[]{:S(2)}) collective-permute-start(bf16[656,128]{1,0:T(8,128)(2,1)S(1)} %copy-done.69), channel_id=1, source_target_pairs={{0,2},{1,3},{2,0},{3,1},{4,6},{5,7},{6,4},{7,5},{8,10},{9,11},{10,... | collective-permute-start | bytes 503816 | tf_op jit(solution)/shard_map/ppermute | solution.py:50
  103.6 30.8 %collective-permute-start.21 = (bf16[656,128]{1,0:T(8,128)(2,1)S(1)}, bf16[656,128]{1,0:T(8,128)(2,1)S(1)}, u32[]{:S(2)}, u32[]{:S(2)}) collective-permute-start(bf16[656,128]{1,0:T(8,128)(2,1)S(1)} %copy-done.69), channel_id=1, source_target_pairs={{0,3},{1,0},{2,1},{3,2},{4,7},{5,4},{6,5},{7,6},{8,11},{9,8},{10,9... | collective-permute-start | bytes 503816 | tf_op jit(solution)/shard_map/ppermute | solution.py:50
  106.9 25.6 %collective-permute-start.18 = (bf16[3,2,1,16,6400]{4,3,2,1,0:T(8,128)(2,1)S(1)}, bf16[3,2,1,16,6400]{4,3,2,1,0:T(8,128)(2,1)S(1)}, u32[]{:S(2)}, u32[]{:S(2)}) collective-permute-start(bf16[3,2,1,16,6400]{4,3,2,1,0:T(8,128)(2,1)S(1)} %pad_maximum_fusion.7), channel_id=1, source_target_pairs={{0,8},{4,12},{8,0},{12,4},{16,24},{20,28},{24,16},{28,20},{1,9},{5... | collective-permute-start | bytes 3686408 | tf_op jit(solution)/shard_map/ppermute | solution.py:45
  148.0 21.3 %collective-permute-start.27 = (bf16[3,1,2,336,128]{4,3,0,2,1:T(8,128)(2,1)S(1)}, bf16[3,1,2,336,128]{4,3,0,2,1:T(8,128)(2,1)S(1)}, u32[]{:S(2)}, u32[]{:S(2)}) collective-permute-start(bf16[3,1,2,336,128]{4,3,0,2,1:T(8,128)(2,1)S(1)} %pad_maximum_fusion.17), channel_id=1, source_target_pairs={{0,16},{4,20},{8,24},{12,28},{16,0},{20,4},{24,8},{28,12},{1,17},{... | collective-permute-start | bytes 1548296 | tf_op jit(solution)/shard_map/ppermute | solution.py:45
  149.3 19.7 %collective-permute-start.28 = (bf16[3,2,1,320,128]{4,3,0,2,1:T(8,128)(2,1)S(1)}, bf16[3,2,1,320,128]{4,3,0,2,1:T(8,128)(2,1)S(1)}, u32[]{:S(2)}, u32[]{:S(2)}) collective-permute-start(bf16[3,2,1,320,128]{4,3,0,2,1:T(8,128)(2,1)S(1)} %pad_maximum_fusion.22), channel_id=1, source_target_pairs={{0,8},{4,12},{8,0},{12,4},{16,24},{20,28},{24,16},{28,20},{1,9},{5... | collective-permute-start | bytes 1474568 | tf_op jit(solution)/shard_map/ppermute | solution.py:45
  156.4 13.0 %collective-permute-start.29 = (bf16[512,512]{1,0:T(8,128)(2,1)S(1)}, bf16[512,512]{1,0:T(8,128)(2,1)S(1)}, u32[]{:S(2)}, u32[]{:S(2)}) collective-permute-start(bf16[512,512]{1,0:T(8,128)(2,1)S(1)} %dynamic-slice_bitcast_fusion.1), channel_id=1, source_target_pairs={{0,4},{4,0},{8,12},{12,8},{16,20},{20,16},{24,28},{28,24},{1,5},{5... | collective-permute-start | bytes 1572872 | tf_op jit(solution)/shard_map/ppermute | solution.py:45
  156.6 12.9 %collective-permute-start.30 = (bf16[512,512]{1,0:T(8,128)(2,1)S(1)}, bf16[512,512]{1,0:T(8,128)(2,1)S(1)}, u32[]{:S(2)}, u32[]{:S(2)}) collective-permute-start(bf16[512,512]{1,0:T(8,128)(2,1)S(1)} %dynamic-slice_bitcast_fusion), channel_id=1, source_target_pairs={{0,4},{4,0},{8,12},{12,8},{16,20},{20,16},{24,28},{28,24},{1,5},{5... | collective-permute-start | bytes 1572872 | tf_op jit(solution)/shard_map/ppermute | solution.py:45
  193.6 17.7 %collective-permute-start.35 = (bf16[4,2,16,2688]{3,2,1,0:T(8,128)(2,1)}, bf16[4,2,16,2688]{3,2,1,0:T(8,128)(2,1)S(1)}, u32[]{:S(2)}, u32[]{:S(2)}) collective-permute-start(bf16[4,2,16,2688]{3,2,1,0:T(8,128)(2,1)} %get-tuple-element.341), channel_id=1, source_target_pairs={{0,8},{4,12},{8,0},{12,4},{16,24},{20,28},{24,16},{28,20},{1,9},{5... | collective-permute-start | bytes 2064392 | tf_op jit(solution)/shard_map/ppermute | solution.py:45
  194.4 17.4 %collective-permute-start.36 = (bf16[4,2,16,2688]{3,2,1,0:T(8,128)(2,1)}, bf16[4,2,16,2688]{3,2,1,0:T(8,128)(2,1)S(1)}, u32[]{:S(2)}, u32[]{:S(2)}) collective-permute-start(bf16[4,2,16,2688]{3,2,1,0:T(8,128)(2,1)} %get-tuple-element.343), channel_id=1, source_target_pairs={{0,16},{4,20},{8,24},{12,28},{16,0},{20,4},{24,8},{28,12},{1,17},{... | collective-permute-start | bytes 2064392 | tf_op jit(solution)/shard_map/ppermute | solution.py:45
  211.8 26.2 %collective-permute-start.37 = (bf16[4,2,16,2688]{3,2,1,0:T(8,128)(2,1)}, bf16[4,2,16,2688]{3,2,1,0:T(8,128)(2,1)}, u32[]{:S(2)}, u32[]{:S(2)}) collective-permute-start(bf16[4,2,16,2688]{3,2,1,0:T(8,128)(2,1)} %get-tuple-element.356), channel_id=1, source_target_pairs={{0,8},{4,12},{8,0},{12,4},{16,24},{20,28},{24,16},{28,20},{1,9},{5... | collective-permute-start | bytes 2064392 | tf_op jit(solution)/shard_map/ppermute | solution.py:45
  213.1 24.9 %collective-permute-start.38 = (bf16[4,2,16,2688]{3,2,1,0:T(8,128)(2,1)}, bf16[4,2,16,2688]{3,2,1,0:T(8,128)(2,1)}, u32[]{:S(2)}, u32[]{:S(2)}) collective-permute-start(bf16[4,2,16,2688]{3,2,1,0:T(8,128)(2,1)} %get-tuple-element.358), channel_id=1, source_target_pairs={{0,16},{4,20},{8,24},{12,28},{16,0},{20,4},{24,8},{28,12},{1,17},{... | collective-permute-start | bytes 2064392 | tf_op jit(solution)/shard_map/ppermute | solution.py:45
  216.6 21.4 %collective-permute-start.39 = (bf16[4,1,16,2688]{3,2,1,0:T(8,128)(2,1)}, bf16[4,1,16,2688]{3,2,1,0:T(8,128)(2,1)}, u32[]{:S(2)}, u32[]{:S(2)}) collective-permute-start(bf16[4,1,16,2688]{3,2,1,0:T(8,128)(2,1)} %get-tuple-element.372), channel_id=1, source_target_pairs={{0,16},{4,20},{8,24},{12,28},{16,0},{20,4},{24,8},{28,12},{1,17},{... | collective-permute-start | bytes 1032200 | tf_op jit(solution)/shard_map/ppermute | solution.py:45
  218.1 19.9 %collective-permute-start.40 = (bf16[4,1,16,2688]{3,2,1,0:T(8,128)(2,1)}, bf16[4,1,16,2688]{3,2,1,0:T(8,128)(2,1)}, u32[]{:S(2)}, u32[]{:S(2)}) collective-permute-start(bf16[4,1,16,2688]{3,2,1,0:T(8,128)(2,1)} %get-tuple-element.374), channel_id=1, source_target_pairs={{0,8},{4,12},{8,0},{12,4},{16,24},{20,28},{24,16},{28,20},{1,9},{5... | collective-permute-start | bytes 1032200 | tf_op jit(solution)/shard_map/ppermute | solution.py:45
  238.0 24.6 %collective-permute-start.43 = (bf16[4,2,16,2688]{3,2,1,0:T(8,128)(2,1)}, bf16[4,2,16,2688]{3,2,1,0:T(8,128)(2,1)}, u32[]{:S(2)}, u32[]{:S(2)}) collective-permute-start(bf16[4,2,16,2688]{3,2,1,0:T(8,128)(2,1)} %get-tuple-element.384), channel_id=1, source_target_pairs={{0,8},{4,12},{8,0},{12,4},{16,24},{20,28},{24,16},{28,20},{1,9},{5... | collective-permute-start | bytes 2064392 | tf_op jit(solution)/shard_map/ppermute | solution.py:45
  239.4 23.2 %collective-permute-start.44 = (bf16[4,2,16,2688]{3,2,1,0:T(8,128)(2,1)}, bf16[4,2,16,2688]{3,2,1,0:T(8,128)(2,1)}, u32[]{:S(2)}, u32[]{:S(2)}) collective-permute-start(bf16[4,2,16,2688]{3,2,1,0:T(8,128)(2,1)} %get-tuple-element.386), channel_id=1, source_target_pairs={{0,16},{4,20},{8,24},{12,28},{16,0},{20,4},{24,8},{28,12},{1,17},{... | collective-permute-start | bytes 2064392 | tf_op jit(solution)/shard_map/ppermute | solution.py:45
  243.0 19.5 %collective-permute-start.41 = (bf16[4,1,16,2688]{3,2,1,0:T(8,128)(2,1)}, bf16[4,1,16,2688]{3,2,1,0:T(8,128)(2,1)S(1)}, u32[]{:S(2)}, u32[]{:S(2)}) collective-permute-start(bf16[4,1,16,2688]{3,2,1,0:T(8,128)(2,1)} %get-tuple-element.380), channel_id=1, source_target_pairs={{0,16},{4,20},{8,24},{12,28},{16,0},{20,4},{24,8},{28,12},{1,17},{... | collective-permute-start | bytes 1032200 | tf_op jit(solution)/shard_map/ppermute | solution.py:45
  244.5 18.1 %collective-permute-start.42 = (bf16[4,1,16,2688]{3,2,1,0:T(8,128)(2,1)}, bf16[4,1,16,2688]{3,2,1,0:T(8,128)(2,1)S(1)}, u32[]{:S(2)}, u32[]{:S(2)}) collective-permute-start(bf16[4,1,16,2688]{3,2,1,0:T(8,128)(2,1)} %get-tuple-element.382), channel_id=1, source_target_pairs={{0,8},{4,12},{8,0},{12,4},{16,24},{20,28},{24,16},{28,20},{1,9},{5... | collective-permute-start | bytes 1032200 | tf_op jit(solution)/shard_map/ppermute | solution.py:45
  246.7 15.8 %collective-permute-start.45 = (bf16[32,2688]{1,0:T(8,128)(2,1)S(1)}, bf16[32,2688]{1,0:T(8,128)(2,1)S(1)}, u32[]{:S(2)}, u32[]{:S(2)}) collective-permute-start(bf16[32,2688]{1,0:T(8,128)(2,1)S(1)} %dynamic-slice_bitcast_fusion.15), channel_id=1, source_target_pairs={{0,1},{1,2},{2,3},{3,0},{4,5},{5,6},{6,7},{7,4},{8,9},{9,10},{10,1... | collective-permute-start | bytes 516104 | tf_op jit(solution)/shard_map/ppermute | solution.py:50
  263.2 16.7 %collective-permute-start.46 = (bf16[2,128,1024]{2,1,0:T(8,128)(2,1)S(1)}, bf16[2,128,1024]{2,1,0:T(8,128)(2,1)S(1)}, u32[]{:S(2)}, u32[]{:S(2)}) collective-permute-start(bf16[2,128,1024]{2,1,0:T(8,128)(2,1)S(1)} %get-tuple-element.401), channel_id=1, source_target_pairs={{1,0},{2,1},{3,2},{5,4},{6,5},{7,6},{9,8},{10,9},{11,10},{13,12},{... | collective-permute-start | bytes 1572872 | tf_op jit(solution)/shard_map/ppermute | solution.py:208
  264.5 16.1 %collective-permute-start.47 = (bf16[2,128,1024]{2,1,0:T(8,128)(2,1)S(1)}, bf16[2,128,1024]{2,1,0:T(8,128)(2,1)S(1)}, u32[]{:S(2)}, u32[]{:S(2)}) collective-permute-start(bf16[2,128,1024]{2,1,0:T(8,128)(2,1)S(1)} %get-tuple-element.402), channel_id=1, source_target_pairs={{0,1},{1,2},{2,3},{4,5},{5,6},{6,7},{8,9},{9,10},{10,11},{12,13},{... | collective-permute-start | bytes 1572872 | tf_op jit(solution)/shard_map/ppermute | solution.py:208
  287.3 15.5 %collective-permute-start.54 = (bf16[32,2688]{1,0:T(8,128)(2,1)S(1)}, bf16[32,2688]{1,0:T(8,128)(2,1)S(1)}, u32[]{:S(2)}, u32[]{:S(2)}) collective-permute-start(bf16[32,2688]{1,0:T(8,128)(2,1)S(1)} %get-tuple-element.559), channel_id=1, source_target_pairs={{0,3},{1,0},{2,1},{3,2},{4,7},{5,4},{6,5},{7,6},{8,11},{9,8},{10,9... | collective-permute-start | bytes 516104 | tf_op jit(solution)/shard_map/ppermute | solution.py:50
  288.5 14.3 %collective-permute-start.55 = (bf16[32,2688]{1,0:T(8,128)(2,1)S(1)}, bf16[32,2688]{1,0:T(8,128)(2,1)S(1)}, u32[]{:S(2)}, u32[]{:S(2)}) collective-permute-start(bf16[32,2688]{1,0:T(8,128)(2,1)S(1)} %get-tuple-element.558), channel_id=1, source_target_pairs={{0,2},{1,3},{2,0},{3,1},{4,6},{5,7},{6,4},{7,5},{8,10},{9,11},{10,... | collective-permute-start | bytes 516104 | tf_op jit(solution)/shard_map/ppermute | solution.py:50
  290.5 12.3 %collective-permute-start.52 = (bf16[4,2,16,1024]{3,2,1,0:T(8,128)(2,1)}, bf16[4,2,16,1024]{3,2,1,0:T(8,128)(2,1)S(1)}, u32[]{:S(2)}, u32[]{:S(2)}) collective-permute-start(bf16[4,2,16,1024]{3,2,1,0:T(8,128)(2,1)} %get-tuple-element.434), channel_id=1, source_target_pairs={{0,8},{4,12},{8,0},{12,4},{16,24},{20,28},{24,16},{28,20},{1,9},{5... | collective-permute-start | bytes 786440 | tf_op jit(solution)/shard_map/ppermute | solution.py:45
  303.5 19.2 %collective-permute-start.56 = (bf16[4,2,16,3072]{3,2,1,0:T(8,128)(2,1)}, bf16[4,2,16,3072]{3,2,1,0:T(8,128)(2,1)}, u32[]{:S(2)}, u32[]{:S(2)}) collective-permute-start(bf16[4,2,16,3072]{3,2,1,0:T(8,128)(2,1)} %get-tuple-element.445), channel_id=1, source_target_pairs={{0,8},{4,12},{8,0},{12,4},{16,24},{20,28},{24,16},{28,20},{1,9},{5... | collective-permute-start | bytes 2359304 | tf_op jit(solution)/shard_map/ppermute | solution.py:45
  304.4 19.2 %collective-permute-start.57 = (bf16[4,2,16,3072]{3,2,1,0:T(8,128)(2,1)}, bf16[4,2,16,3072]{3,2,1,0:T(8,128)(2,1)}, u32[]{:S(2)}, u32[]{:S(2)}) collective-permute-start(bf16[4,2,16,3072]{3,2,1,0:T(8,128)(2,1)} %get-tuple-element.447), channel_id=1, source_target_pairs={{0,16},{4,20},{8,24},{12,28},{16,0},{20,4},{24,8},{28,12},{1,17},{... | collective-permute-start | bytes 2359304 | tf_op jit(solution)/shard_map/ppermute | solution.py:45
  305.9 14.7 %collective-permute-start.58 = (bf16[32,2688]{1,0:T(8,128)(2,1)S(1)}, bf16[32,2688]{1,0:T(8,128)(2,1)S(1)}, u32[]{:S(2)}, u32[]{:S(2)}) collective-permute-start(bf16[32,2688]{1,0:T(8,128)(2,1)S(1)} %get-tuple-element.557), channel_id=1, source_target_pairs={{0,1},{1,2},{2,3},{3,0},{4,5},{5,6},{6,7},{7,4},{8,9},{9,10},{10,1... | collective-permute-start | bytes 516104 | tf_op jit(solution)/shard_map/ppermute | solution.py:50
  306.6 14.1 %collective-permute-start.59 = (bf16[32,2688]{1,0:T(8,128)(2,1)S(1)}, bf16[32,2688]{1,0:T(8,128)(2,1)S(1)}, u32[]{:S(2)}, u32[]{:S(2)}) collective-permute-start(bf16[32,2688]{1,0:T(8,128)(2,1)S(1)} %get-tuple-element.556), channel_id=1, source_target_pairs={{0,2},{1,3},{2,0},{3,1},{4,6},{5,7},{6,4},{7,5},{8,10},{9,11},{10,... | collective-permute-start | bytes 516104 | tf_op jit(solution)/shard_map/ppermute | solution.py:50
  307.8 12.9 %collective-permute-start.60 = (bf16[32,2688]{1,0:T(8,128)(2,1)S(1)}, bf16[32,2688]{1,0:T(8,128)(2,1)S(1)}, u32[]{:S(2)}, u32[]{:S(2)}) collective-permute-start(bf16[32,2688]{1,0:T(8,128)(2,1)S(1)} %get-tuple-element.555), channel_id=1, source_target_pairs={{0,3},{1,0},{2,1},{3,2},{4,7},{5,4},{6,5},{7,6},{8,11},{9,8},{10,9... | collective-permute-start | bytes 516104 | tf_op jit(solution)/shard_map/ppermute | solution.py:50
  325.5 15.9 %collective-permute-start.61 = (bf16[4,1,16,4096]{3,2,1,0:T(8,128)(2,1)S(1)}, bf16[4,1,16,4096]{3,2,1,0:T(8,128)(2,1)S(1)}, u32[]{:S(2)}, u32[]{:S(2)}) collective-permute-start(bf16[4,1,16,4096]{3,2,1,0:T(8,128)(2,1)S(1)} %get-tuple-element.465), channel_id=1, source_target_pairs={{0,16},{4,20},{8,24},{12,28},{16,0},{20,4},{24,8},{28,12},{1,17},{... | collective-permute-start | bytes 1572872 | tf_op jit(solution)/shard_map/ppermute | solution.py:45
  327.0 14.4 %collective-permute-start.62 = (bf16[4,1,16,4096]{3,2,1,0:T(8,128)(2,1)S(1)}, bf16[4,1,16,4096]{3,2,1,0:T(8,128)(2,1)S(1)}, u32[]{:S(2)}, u32[]{:S(2)}) collective-permute-start(bf16[4,1,16,4096]{3,2,1,0:T(8,128)(2,1)S(1)} %get-tuple-element.467), channel_id=1, source_target_pairs={{0,8},{4,12},{8,0},{12,4},{16,24},{20,28},{24,16},{28,20},{1,9},{5... | collective-permute-start | bytes 1572872 | tf_op jit(solution)/shard_map/ppermute | solution.py:45
  328.8 12.6 %collective-permute-start.64 = (bf16[32,2688]{1,0:T(8,128)(2,1)S(1)}, bf16[32,2688]{1,0:T(8,128)(2,1)S(1)}, u32[]{:S(2)}, u32[]{:S(2)}) collective-permute-start(bf16[32,2688]{1,0:T(8,128)(2,1)S(1)} %get-tuple-element.553), channel_id=1, source_target_pairs={{0,2},{1,3},{2,0},{3,1},{4,6},{5,7},{6,4},{7,5},{8,10},{9,11},{10,... | collective-permute-start | bytes 516104 | tf_op jit(solution)/shard_map/ppermute | solution.py:50
  358.9 13.1 %collective-permute-start.71 = (bf16[1,2,16,8064]{3,2,1,0:T(8,128)(2,1)S(1)}, bf16[1,2,16,8064]{3,2,1,0:T(8,128)(2,1)S(1)}, u32[]{:S(2)}, u32[]{:S(2)}) collective-permute-start(bf16[1,2,16,8064]{3,2,1,0:T(8,128)(2,1)S(1)} %pad_maximum_fusion.19), channel_id=1, source_target_pairs={{0,16},{4,20},{8,24},{12,28},{16,0},{20,4},{24,8},{28,12},{1,17},{... | collective-permute-start | bytes 1548296 | tf_op jit(solution)/shard_map/ppermute | solution.py:45
  360.4 14.2 %collective-permute-start.70 = (bf16[32,4096]{1,0:T(8,128)(2,1)S(1)}, bf16[32,4096]{1,0:T(8,128)(2,1)S(1)}, u32[]{:S(2)}, u32[]{:S(2)}) collective-permute-start(bf16[32,4096]{1,0:T(8,128)(2,1)S(1)} %dynamic-slice_bitcast_fusion.3), channel_id=1, source_target_pairs={{0,2},{1,3},{2,0},{3,1},{4,6},{5,7},{6,4},{7,5},{8,10},{9,11},{10,... | collective-permute-start | bytes 786440 | tf_op jit(solution)/shard_map/ppermute | solution.py:50
  361.0 12.6 %collective-permute-start.72 = (bf16[2,1,16,8064]{3,2,1,0:T(8,128)(2,1)S(1)}, bf16[2,1,16,8064]{3,2,1,0:T(8,128)(2,1)S(1)}, u32[]{:S(2)}, u32[]{:S(2)}) collective-permute-start(bf16[2,1,16,8064]{3,2,1,0:T(8,128)(2,1)S(1)} %pad_maximum_fusion.20), channel_id=1, source_target_pairs={{0,8},{4,12},{8,0},{12,4},{16,24},{20,28},{24,16},{28,20},{1,9},{5... | collective-permute-start | bytes 1548296 | tf_op jit(solution)/shard_map/ppermute | solution.py:45
  (115 other events, 812.4 us)
